TPU v7x, 32 devices: a whole 2x2x4 slice. The times are simulated.
32 devices in a mesh: seq: 16 (over z, y, x), fsdp: 2 (over core).
Axes of the slice: x: 2, y: 2, z: 4, core: 2. Of those that a mesh axis runs over, the one named last changes fastest.
Arguments:
- tokens: bfloat16 [2, 2048, 640], P('fsdp', 'seq'), may hold values from -6 to 6
- segments: int32 [2, 2048], P('fsdp', 'seq'), may hold values from 0 to 2, as said below
- positions: int32 [2, 2048], P('fsdp', 'seq'), may hold values from 0 to 2047, as said below
- w_query: bfloat16 [640, 1024], P('fsdp'), may hold values from -0.25 to 0.25
- w_key: bfloat16 [640, 256], P('fsdp'), may hold values from -0.25 to 0.25
- w_value: bfloat16 [640, 256], P('fsdp'), may hold values from -0.25 to 0.25
- w_out: bfloat16 [1024, 640], P('fsdp'), may hold values from -0.1875 to 0.1875
- w_gate: bfloat16 [640, 2048], P('fsdp'), may hold values from -0.25 to 0.25
- w_up: bfloat16 [640, 2048], P('fsdp'), may hold values from -0.25 to 0.25
- w_down: bfloat16 [2048, 640], P('fsdp'), may hold values from -0.125 to 0.125
- norm_gains: bfloat16 [3072], P('fsdp'), may hold values from 0.25 to 1.75
- cotangent: bfloat16 [2, 2048, 640], P('fsdp', 'seq'), may hold values from -6 to 6
Outputs:
- mixed: bfloat16 [2, 2048, 640], P('fsdp', 'seq')
- input_grad: float32 [2, 2048, 640], P('fsdp', 'seq')
- grad_query: float32 [655360], P(('seq', 'fsdp'))
- grad_key: float32 [163840], P(('seq', 'fsdp'))
- grad_value: float32 [163840], P(('seq', 'fsdp'))
- grad_out: float32 [655360], P(('seq', 'fsdp'))
- grad_gate: float32 [1310720], P(('seq', 'fsdp'))
- grad_up: float32 [1310720], P(('seq', 'fsdp'))
- grad_down: float32 [1310720], P(('seq', 'fsdp'))
- grad_gains: float32 [3072], P(('seq', 'fsdp'))
Inputs may be any that keep to these rules, and one draw needn't show every extreme that they name: `segments`: segment ids never fall along a row. Segment 0 starts each row and ends within its first 128 tokens; segment 2 fills the last 1 to 127 tokens; segment 1 lies between. Within a segment positions rise by one from token to token; each row starts at position 0 and ends at position 2047.
All inputs are finite; a program needn't handle non-finite values.
Results may differ from a plain program's by a relative error of at most 0.017.
Values may be sent and summed in bfloat16 or wider, within the bound.
No kernel may reach another device: no remote copies, remote signals or barrier semaphores. Data moves between devices by JAX's collectives and lax.ppermute only.
A program may use at most 128 MiB of HBM per device.

v0:
```python
import math

import jax
import jax.numpy as jnp
from jax import lax
from jax.sharding import PartitionSpec as P

WINDOW = 512


EPS = 1e-06


def shifted(x, axis, by):
    peers = lax.axis_size(axis)
    pairs = [(i, i + by) for i in range(peers) if 0 <= i + by < peers]
    return lax.ppermute(x, axis, pairs)


def norm_rows(value, gain):
    return value * lax.rsqrt(jnp.mean(value * value, axis=-1, keepdims=True) + EPS) * gain


def rotate(value, cosine, sine):
    half = value.shape[-1] // 2
    first = value[..., :half]
    second = value[..., half:]
    return jnp.concatenate(
        [first * cosine - second * sine, second * cosine + first * sine], axis=-1
    )


def angles(positions, size):
    freq = jnp.exp(jnp.arange(size // 2, dtype=jnp.float32) * (-2.0 * math.log(10000.0) / size))
    turn = positions.astype(jnp.float32)[..., None] * freq
    return (jnp.cos(turn), jnp.sin(turn))


def product(form, left, right):
    return jnp.einsum(form, left, right, preferred_element_type=jnp.float32)


def on_device(
    tokens,
    segments,
    positions,
    w_query,
    w_key,
    w_value,
    w_out,
    w_gate,
    w_up,
    w_down,
    norm_gains,
    cotangent,
):
    tok_rows = tokens.shape[1]
    width = tokens.shape[2]
    head_size = w_key.shape[1]
    head_count = w_query.shape[1] // head_size
    reach = (WINDOW - 1 + tok_rows - 1) // tok_rows
    scale = head_size ** (-0.5)
    gathered = (
        lax.all_gather(w_query, "fsdp", axis=0, tiled=True),
        lax.all_gather(w_key, "fsdp", axis=0, tiled=True),
        lax.all_gather(w_value, "fsdp", axis=0, tiled=True),
        lax.all_gather(w_out, "fsdp", axis=0, tiled=True),
        lax.all_gather(w_gate, "fsdp", axis=0, tiled=True),
        lax.all_gather(w_up, "fsdp", axis=0, tiled=True),
        lax.all_gather(w_down, "fsdp", axis=0, tiled=True),
        lax.all_gather(norm_gains, "fsdp", axis=0, tiled=True),
    )
    query_full, key_full, value_full, out_full, gate_full, up_full, down_full, gains_full = gathered
    gains = gains_full.astype(jnp.float32)
    gain_in = gains[:width]
    gain_q = gains[width : width + head_size]
    gain_k = gains[width + head_size : width + 2 * head_size]
    gain_pa = gains[width + 2 * head_size : 2 * width + 2 * head_size]
    gain_pf = gains[2 * width + 2 * head_size : 3 * width + 2 * head_size]
    gain_pff = gains[3 * width + 2 * head_size :]
    hidden_in = tokens[0].astype(jnp.float32)
    segment = segments[0]
    cosine, sine = angles(positions[0], head_size)
    normed, first_back = jax.vjp(norm_rows, hidden_in, gain_in)
    normed_low = normed.astype(jnp.bfloat16)
    query_raw = jnp.dot(normed_low, query_full, preferred_element_type=jnp.float32)
    key_raw = jnp.dot(normed_low, key_full, preferred_element_type=jnp.float32)
    value_low = jnp.dot(normed_low, value_full, preferred_element_type=jnp.float32).astype(
        jnp.bfloat16
    )

    def turn(query, key, gain_query, gain_key):
        query = norm_rows(query.reshape(tok_rows, head_count, head_size), gain_query)
        query = rotate(query, cosine[:, None, :], sine[:, None, :]) * scale
        key = rotate(norm_rows(key, gain_key), cosine, sine)
        return (query, key)

    (query_rot, key_rot), turn_back = jax.vjp(turn, query_raw, key_raw, gain_q, gain_k)
    query_low = query_rot.astype(jnp.bfloat16)
    packed = jnp.concatenate([key_rot.astype(jnp.bfloat16), value_low], axis=1)
    pieces = [packed]
    seg_pieces = [segment]
    for distance in range(1, reach + 1):
        far_pack, far_seg = shifted((packed, segment), "seq", distance)
        pieces.insert(0, far_pack)
        seg_pieces.insert(0, far_seg)
    keys_all = jnp.concatenate(pieces, axis=0)
    seg_all = jnp.concatenate(seg_pieces, axis=0)
    key_part = keys_all[:, :head_size]
    value_part = keys_all[:, head_size:]
    place = lax.axis_index("seq")
    query_index = place * tok_rows + jnp.arange(tok_rows, dtype=jnp.int32)
    key_index = (place - reach) * tok_rows + jnp.arange((reach + 1) * tok_rows, dtype=jnp.int32)
    spacing = query_index[:, None] - key_index[None, :]
    allowed = (
        (segment[:, None] == seg_all[None, :])
        & (spacing >= 0)
        & (spacing < WINDOW)
        & (key_index[None, :] >= 0)
    )
    scores = product("qhd,kd->hqk", query_low, key_part)
    masked = jnp.where(allowed[None], scores, -1e30)
    top = jnp.max(masked, axis=-1, keepdims=True)
    expd = jnp.exp(masked - top)
    total = jnp.sum(expd, axis=-1, keepdims=True)
    probs_low = (expd / total).astype(jnp.bfloat16)
    log_total = top + jnp.log(total)
    mixed_heads = (
        product("hqk,kd->qhd", probs_low, value_part)
        .reshape(tok_rows, head_count * head_size)
        .astype(jnp.bfloat16)
    )
    attn_out = jnp.dot(mixed_heads, out_full, preferred_element_type=jnp.float32)

    def middle(resid, branch, gain_a, gain_b):
        after = resid + norm_rows(branch, gain_a)
        return (after, norm_rows(after, gain_b))

    (after, normed_ff), middle_back = jax.vjp(middle, hidden_in, attn_out, gain_pa, gain_pf)
    ff_low = normed_ff.astype(jnp.bfloat16)
    gate = jnp.dot(ff_low, gate_full, preferred_element_type=jnp.float32)
    up_value = jnp.dot(ff_low, up_full, preferred_element_type=jnp.float32)

    def mixer(gate_in, up_in):
        return jax.nn.gelu(gate_in, approximate=True) * up_in

    inner, mixer_back = jax.vjp(mixer, gate, up_value)
    inner_low = inner.astype(jnp.bfloat16)
    down = jnp.dot(inner_low, down_full, preferred_element_type=jnp.float32)

    def finish(resid, branch, gain):
        return resid + norm_rows(branch, gain)

    result, finish_back = jax.vjp(finish, after, down, gain_pff)
    again = (
        lax.all_gather(w_query, "fsdp", axis=0, tiled=True),
        lax.all_gather(w_key, "fsdp", axis=0, tiled=True),
        lax.all_gather(w_value, "fsdp", axis=0, tiled=True),
        lax.all_gather(w_out, "fsdp", axis=0, tiled=True),
        lax.all_gather(w_gate, "fsdp", axis=0, tiled=True),
        lax.all_gather(w_up, "fsdp", axis=0, tiled=True),
        lax.all_gather(w_down, "fsdp", axis=0, tiled=True),
    )
    query_back, key_back, value_back, out_back, gate_back, up_back, down_back = again
    grad_result = cotangent[0].astype(jnp.float32)
    grad_after, grad_down, grad_gpff = finish_back(grad_result)
    down_grad_low = grad_down.astype(jnp.bfloat16)
    grad_w_down = product("tf,td->fd", inner_low, down_grad_low)
    grad_inner = product("td,fd->tf", down_grad_low, down_back)
    grad_gate, grad_upv = mixer_back(grad_inner)
    gate_grad_low = grad_gate.astype(jnp.bfloat16)
    up_grad_low = grad_upv.astype(jnp.bfloat16)
    grad_w_gate = product("td,tf->df", ff_low, gate_grad_low)
    grad_w_up = product("td,tf->df", ff_low, up_grad_low)
    grad_normed_ff = product("tf,df->td", gate_grad_low, gate_back) + product(
        "tf,df->td", up_grad_low, up_back
    )
    grad_resid, grad_branch, grad_gpa, grad_gpf = middle_back((grad_after, grad_normed_ff))
    branch_grad_low = grad_branch.astype(jnp.bfloat16)
    grad_w_out = product("ta,td->ad", mixed_heads, branch_grad_low)
    grad_heads = (
        product("td,ad->ta", branch_grad_low, out_back)
        .astype(jnp.bfloat16)
        .reshape(tok_rows, head_count, head_size)
    )
    scores_again = product("qhd,kd->hqk", query_low, key_part)
    probs = jnp.exp(jnp.where(allowed[None], scores_again, -1e30) - log_total)
    probs_again = probs.astype(jnp.bfloat16)
    grad_probs = product("qhd,kd->hqk", grad_heads, value_part)
    grad_scores = (
        probs * (grad_probs - jnp.sum(probs * grad_probs, axis=-1, keepdims=True))
    ).astype(jnp.bfloat16)
    grad_query_rot = product("hqk,kd->qhd", grad_scores, key_part)
    grad_keys = product("hqk,qhd->kd", grad_scores, query_low)
    grad_values = product("hqk,qhd->kd", probs_again, grad_heads)
    grad_packed = jnp.concatenate([grad_keys, grad_values], axis=1)
    collected = grad_packed[reach * tok_rows :]
    for distance in range(1, reach + 1):
        begin = (reach - distance) * tok_rows
        collected = collected + shifted(
            grad_packed[begin : begin + tok_rows].astype(jnp.bfloat16), "seq", -distance
        ).astype(jnp.float32)
    grad_key_rot = collected[:, :head_size]
    value_grad_low = collected[:, head_size:].astype(jnp.bfloat16)
    grad_q_raw, grad_k_raw, grad_gq, grad_gk = turn_back((grad_query_rot, grad_key_rot))
    query_grad_low = grad_q_raw.astype(jnp.bfloat16)
    key_grad_low = grad_k_raw.astype(jnp.bfloat16)
    grad_w_query = product("td,te->de", normed_low, query_grad_low)
    grad_w_key = product("td,te->de", normed_low, key_grad_low)
    grad_w_value = product("td,te->de", normed_low, value_grad_low)
    grad_normed = (
        product("te,de->td", query_grad_low, query_back)
        + product("te,de->td", key_grad_low, key_back)
        + product("te,de->td", value_grad_low, value_back)
    )
    grad_in, grad_gin = first_back(grad_normed)
    input_grad = (grad_resid + grad_in)[None]
    grad_gains = jnp.concatenate([grad_gin, grad_gq, grad_gk, grad_gpa, grad_gpf, grad_gpff])
    flat_query = grad_w_query.reshape(-1)
    flat_key = grad_w_key.reshape(-1)
    flat_value = grad_w_value.reshape(-1)
    flat_out = grad_w_out.reshape(-1)
    flat_gate = grad_w_gate.reshape(-1)
    flat_up = grad_w_up.reshape(-1)
    flat_down = grad_w_down.reshape(-1)
    owned = (
        lax.psum_scatter(flat_query, ("seq", "fsdp"), scatter_dimension=0, tiled=True),
        lax.psum_scatter(flat_key, ("seq", "fsdp"), scatter_dimension=0, tiled=True),
        lax.psum_scatter(flat_value, ("seq", "fsdp"), scatter_dimension=0, tiled=True),
        lax.psum_scatter(flat_out, ("seq", "fsdp"), scatter_dimension=0, tiled=True),
        lax.psum_scatter(flat_gate, ("seq", "fsdp"), scatter_dimension=0, tiled=True),
        lax.psum_scatter(flat_up, ("seq", "fsdp"), scatter_dimension=0, tiled=True),
        lax.psum_scatter(flat_down, ("seq", "fsdp"), scatter_dimension=0, tiled=True),
        lax.psum_scatter(grad_gains, ("seq", "fsdp"), scatter_dimension=0, tiled=True),
    )
    own_query, own_key, own_value, own_out, own_gate, own_up, own_down, own_gains = owned
    return (
        result.astype(jnp.bfloat16)[None],
        input_grad,
        own_query,
        own_key,
        own_value,
        own_out,
        own_gate,
        own_up,
        own_down,
        own_gains,
    )


def solution(mesh):
    placed = (
        P("fsdp", "seq", None),
        P("fsdp", "seq"),
        P("fsdp", "seq"),
        P("fsdp", None),
        P("fsdp", None),
        P("fsdp", None),
        P("fsdp", None),
        P("fsdp", None),
        P("fsdp", None),
        P("fsdp", None),
        P("fsdp"),
        P("fsdp", "seq", None),
    )
    return jax.shard_map(
        on_device,
        mesh=mesh,
        in_specs=placed,
        out_specs=(
            P("fsdp", "seq", None),
            P("fsdp", "seq", None),
            P(("seq", "fsdp")),
            P(("seq", "fsdp")),
            P(("seq", "fsdp")),
            P(("seq", "fsdp")),
            P(("seq", "fsdp")),
            P(("seq", "fsdp")),
            P(("seq", "fsdp")),
            P(("seq", "fsdp")),
        ),
        check_vma=False,
    )
```

profile of v0, /device:TPU:0, one launch (start us, length us, event | category | flops | bytes accessed | tf_op | source)
XLA Modules:
  0.0 526.7 jit_solution(410115597185445806)
XLA Ops:
  10.1 4.8 collective-permute-start.7
  14.9 3.4 collective-permute-start.6
  18.4 4.4 collective-permute-start.5
  22.7 3.5 collective-permute-start.4
  26.3 1.8 all-gather
  28.1 2.0 all_gather.32
  30.2 2.0 all_gather.33
  34.0 2.5 collective-permute-start.3
  36.7 3.4 collective-permute-start.2
  40.2 3.8 collective-permute-start.1
  43.9 1.9 collective-permute-start
  46.2 2.1 collective-permute-done
  48.6 1.9 copy.49
  52.6 1.9 multiply_reduce_fusion.10
  54.9 3.4 fusion.88
  58.3 3.8 all-gather.13.cloned.1.call-done
  62.0 3.8 multiply_convert_fusion.2
  65.8 10.2 %all-gather.15.cloned.1.call-done = bf16[2048,640]{1,0:T(8,128)(2,1)} async-done(((bf16[1024,640]{1,0:T(8,128)(2,1)}), bf16[2048,640]{1,0:T(8,128)(2,1)}) %all-gather.15.cloned.1.call-update) | async-done | bytes 2621456 | tf_op jit(solution)/shard_map/all_gather | solution.py:70
  76.0 2.6 multiply_reduce_fusion.8
  90.4 2.0 fusion.91
  92.4 3.2 convolution_bitcast_fusion
  95.6 3.2 fusion.92
  105.4 3.7 reshape.361
  109.8 2.1 copy.78
  111.9 3.5 copy.82
  116.3 3.6 copy.81
  119.9 6.6 %reshape.364 = f32[1310720]{0:T(1024)} reshape(f32[2048,640]{1,0:T(8,128)} %fusion.92) | data formatting | bytes 10485760 | tf_op jit(solution)/shard_map/reshape | solution.py:225
  133.5 49.0 %all-reduce.11 = f32[3072]{0:T(1024)S(1)} all-reduce(f32[3072]{0:T(1024)S(1)} %constant_dynamic-update-slice_fusion.11), channel_id=9, replica_groups=mesh['seq'=16,'fsdp'=2] {'seq','fsdp'}, use_global_device_ids=true, to_apply=%region_28.29.clone | all-reduce | flops 3072 | bytes 24576
  184.0 325.4 %all-reduce.15.cloned.1.call-done = (f32[655360]{0:T(1024)}, f32[163840]{0:T(1024)}, f32[163840]{0:T(1024)}, f32[655360]{0:T(1024)}, f32[1310720]{0:T(1024)}, /*index=5*/f32[1310720]{0:T(1024)}, f32[1310720]{0:T(1024)}) async-done(((f32[655360]{0:T(1024)}, f32[163840]{0:T(1024)}, f32[163840]{0:T(1024)}, f32[655360]{0:T(1024)}, f32[1310720]{0:T(1024)}, /*index=5*/f32[1310720]{0:T(1024)}, f32[1310720]{0:T(1024)}), ...) | async-done | bytes 22282256
  515.1 1.6 dynamic-slice.4
  516.7 1.6 dynamic-slice.5
  518.3 1.6 dynamic-slice.6
  (233 shorter events, 41.2 us)
Async XLA Ops:
  7.2 41.4 %all-gather.7.cloned.1.call-start = ((), (), s32[]{:S(2)}) async-start(), calls=%async_computation | async-start | bytes 1966080 | tf_op jit(solution)/shard_map/all_gather | solution.py:64
  7.9 44.7 %all-gather.9.cloned.1.call-start = ((), (), s32[]{:S(2)}) async-start(), calls=%async_computation.1 | async-start | bytes 1966080 | tf_op jit(solution)/shard_map/all_gather | solution.py:67
  8.7 17.6 %copy-start.41 = (bf16[1536]{0:T(1024)(128)(2,1)S(1)}, bf16[1536]{0:T(1024)(128)(2,1)}, u32[]{:S(2)}) copy-start(bf16[1536]{0:T(1024)(128)(2,1)} %param.22) | copy-start | bytes 9220
  8.7 19.4 %copy-start.38 = (bf16[320,256]{1,0:T(8,128)(2,1)S(1)}, bf16[320,256]{1,0:T(8,128)(2,1)}, u32[]{:S(2)}) copy-start(bf16[320,256]{1,0:T(8,128)(2,1)} %param.16) | copy-start | bytes 491524
  8.7 21.5 %copy-start.39 = (bf16[320,256]{1,0:T(8,128)(2,1)S(1)}, bf16[320,256]{1,0:T(8,128)(2,1)}, u32[]{:S(2)}) copy-start(bf16[320,256]{1,0:T(8,128)(2,1)} %param.17) | copy-start | bytes 491524
  8.7 46.2 %all-gather.11.cloned.1.call-start = ((), (), s32[]{:S(2)}) async-start(), calls=%async_computation.2 | async-start | bytes 3932160 | tf_op jit(solution)/shard_map/all_gather | solution.py:68
  9.4 22.8 %copy-start.2 = (bf16[1,128,640]{2,1,0:T(8,128)(2,1)S(1)}, bf16[1,128,640]{2,1,0:T(8,128)(2,1)}, u32[]{:S(2)}) copy-start(bf16[1,128,640]{2,1,0:T(8,128)(2,1)} %param.12) | copy-start | bytes 491524
  9.4 22.9 %copy-start.49 = (s32[1,128]{1,0:T(1,128)S(1)}, s32[1,128]{1,0:T(1,128)}, u32[]{:S(2)}) copy-start(s32[1,128]{1,0:T(1,128)} %param.14) | copy-start | bytes 1540
  9.5 52.6 %all-gather.13.cloned.1.call-start = ((), (), s32[]{:S(2)}) async-start(), calls=%async_computation.3 | async-start | bytes 3932160 | tf_op jit(solution)/shard_map/all_gather | solution.py:69
  10.0 66.0 %all-gather.15.cloned.1.call-start = ((), (), s32[]{:S(2)}) async-start(), calls=%async_computation.4 | async-start | bytes 3932160 | tf_op jit(solution)/shard_map/all_gather | solution.py:70
  10.1 35.8 %collective-permute-start.7 = (s32[128]{0:T(128)S(1)}, s32[128]{0:T(128)S(1)}, u32[]{:S(2)}, u32[]{:S(2)}) collective-permute-start(s32[128]{0:T(128)S(1)} %bitcast.164), channel_id=1, source_target_pairs={{0,2},{2,4},{4,6},{6,8},{8,10},{10,12},{12,14},{14,16},{16,18},{18... | collective-permute-start | bytes 1544 | tf_op jit(solution)/shard_map/ppermute | solution.py:17
  14.9 29.0 %collective-permute-start.6 = (s32[128]{0:T(128)S(1)}, s32[128]{0:T(128)S(1)}, u32[]{:S(2)}, u32[]{:S(2)}) collective-permute-start(s32[128]{0:T(128)S(1)} %bitcast.165), channel_id=1, source_target_pairs={{0,4},{2,6},{4,8},{6,10},{8,12},{10,14},{12,16},{14,18},{16,20},{1... | collective-permute-start | bytes 1544 | tf_op jit(solution)/shard_map/ppermute | solution.py:17
  18.4 21.8 %collective-permute-start.5 = (s32[128]{0:T(128)S(1)}, s32[128]{0:T(128)S(1)}, u32[]{:S(2)}, u32[]{:S(2)}) collective-permute-start(s32[128]{0:T(128)S(1)} %bitcast.166), channel_id=1, source_target_pairs={{0,6},{2,8},{4,10},{6,12},{8,14},{10,16},{12,18},{14,20},{16,22},{... | collective-permute-start | bytes 1544 | tf_op jit(solution)/shard_map/ppermute | solution.py:17
  22.7 13.9 %collective-permute-start.4 = (s32[128]{0:T(128)S(1)}, s32[128]{0:T(128)S(1)}, u32[]{:S(2)}, u32[]{:S(2)}) collective-permute-start(s32[128]{0:T(128)S(1)} %bitcast.167), channel_id=1, source_target_pairs={{0,8},{2,10},{4,12},{6,14},{8,16},{10,18},{12,20},{14,22},{16,24},... | collective-permute-start | bytes 1544 | tf_op jit(solution)/shard_map/ppermute | solution.py:17
  32.2 4.3 copy-start.42
  33.7 17.6 %copy-start.34 = (f32[128,128]{1,0:T(8,128)}, f32[128,128]{1,0:T(8,128)S(1)}, u32[]{:S(2)}) copy-start(f32[128,128]{1,0:T(8,128)S(1)} %get-tuple-element.54) | copy-start | bytes 196612
  33.7 17.6 %copy-start.36 = (f32[128,128]{1,0:T(8,128)}, f32[128,128]{1,0:T(8,128)S(1)}, u32[]{:S(2)}) copy-start(f32[128,128]{1,0:T(8,128)S(1)} %get-tuple-element.55) | copy-start | bytes 196612
  34.0 14.4 %collective-permute-start.3 = (bf16[128,512]{1,0:T(8,128)(2,1)S(1)}, bf16[128,512]{1,0:T(8,128)(2,1)S(1)}, u32[]{:S(2)}, u32[]{:S(2)}) collective-permute-start(bf16[128,512]{1,0:T(8,128)(2,1)S(1)} %pad_maximum_fusion.1), channel_id=1, source_target_pairs={{0,2},{2,4},{4,6},{6,8},{8,10},{10,12},{12,14},{14,16},{16,18},{18... | collective-permute-start | bytes 393224 | tf_op jit(solution)/shard_map/ppermute | solution.py:17
  36.6 472.8 %all-reduce.15.cloned.1.call-start = ((), (), s32[]{:S(2)}) async-start(), calls=%async_computation.5 | async-start | bytes 44564480
  36.7 11.7 %collective-permute-start.2 = (bf16[128,512]{1,0:T(8,128)(2,1)S(1)}, bf16[128,512]{1,0:T(8,128)(2,1)S(1)}, u32[]{:S(2)}, u32[]{:S(2)}) collective-permute-start(bf16[128,512]{1,0:T(8,128)(2,1)S(1)} %pad_maximum_fusion.1), channel_id=1, source_target_pairs={{0,4},{2,6},{4,8},{6,10},{8,12},{10,14},{12,16},{14,18},{16,20},{1... | collective-permute-start | bytes 393224 | tf_op jit(solution)/shard_map/ppermute | solution.py:17
  40.2 8.3 %collective-permute-start.1 = (bf16[128,512]{1,0:T(8,128)(2,1)S(1)}, bf16[128,512]{1,0:T(8,128)(2,1)S(1)}, u32[]{:S(2)}, u32[]{:S(2)}) collective-permute-start(bf16[128,512]{1,0:T(8,128)(2,1)S(1)} %pad_maximum_fusion.1), channel_id=1, source_target_pairs={{0,6},{2,8},{4,10},{6,12},{8,14},{10,16},{12,18},{14,20},{16,22},{... | collective-permute-start | bytes 393224 | tf_op jit(solution)/shard_map/ppermute | solution.py:17
  43.9 4.5 collective-permute-start
  54.5 30.0 %copy-start.40 = (f32[128]{0:T(128)}, f32[128]{0:T(128)S(1)}, u32[]{:S(2)}) copy-start(f32[128]{0:T(128)S(1)} %fusion.71) | copy-start | bytes 1540
  90.3 9.1 %copy-start.4 = (f32[640,256]{1,0:T(8,128)}, f32[640,256]{1,0:T(8,128)S(1)}, u32[]{:S(2)}) copy-start(f32[640,256]{1,0:T(8,128)S(1)} %convolution_bitcast_fusion.6) | copy-start | bytes 1966084
  100.0 26.5 %collective-permute-start.8 = (bf16[128,512]{1,0:T(8,128)(2,1)S(1)}, bf16[128,512]{1,0:T(8,128)(2,1)S(1)}, u32[]{:S(2)}, u32[]{:S(2)}) collective-permute-start(bf16[128,512]{1,0:T(8,128)(2,1)S(1)} %get-tuple-element.34), channel_id=1, source_target_pairs={{2,0},{4,2},{6,4},{8,6},{10,8},{12,10},{14,12},{16,14},{18,16},{20... | collective-permute-start | bytes 393224 | tf_op jit(solution)/shard_map/ppermute | solution.py:17
  101.5 24.9 %collective-permute-start.11 = (bf16[128,512]{1,0:T(8,128)(2,1)S(1)}, bf16[128,512]{1,0:T(8,128)(2,1)S(1)}, u32[]{:S(2)}, u32[]{:S(2)}) collective-permute-start(bf16[128,512]{1,0:T(8,128)(2,1)S(1)} %get-tuple-element.35), channel_id=1, source_target_pairs={{8,0},{10,2},{12,4},{14,6},{16,8},{18,10},{20,12},{22,14},{24,16},... | collective-permute-start | bytes 393224 | tf_op jit(solution)/shard_map/ppermute | solution.py:17
  102.8 23.7 %collective-permute-start.10 = (bf16[128,512]{1,0:T(8,128)(2,1)S(1)}, bf16[128,512]{1,0:T(8,128)(2,1)S(1)}, u32[]{:S(2)}, u32[]{:S(2)}) collective-permute-start(bf16[128,512]{1,0:T(8,128)(2,1)S(1)} %get-tuple-element.36), channel_id=1, source_target_pairs={{6,0},{8,2},{10,4},{12,6},{14,8},{16,10},{18,12},{20,14},{22,16},{... | collective-permute-start | bytes 393224 | tf_op jit(solution)/shard_map/ppermute | solution.py:17
  104.1 22.4 %collective-permute-start.9 = (bf16[128,512]{1,0:T(8,128)(2,1)S(1)}, bf16[128,512]{1,0:T(8,128)(2,1)S(1)}, u32[]{:S(2)}, u32[]{:S(2)}) collective-permute-start(bf16[128,512]{1,0:T(8,128)(2,1)S(1)} %get-tuple-element.37), channel_id=1, source_target_pairs={{4,0},{6,2},{8,4},{10,6},{12,8},{14,10},{16,12},{18,14},{20,16},{2... | collective-permute-start | bytes 393224 | tf_op jit(solution)/shard_map/ppermute | solution.py:17
  105.4 6.5 %slice-start = ((s8[5242880]{0:T(1024)(128)(4,1)}), s8[1048576]{0:T(1024)(128)(4,1)S(1)}, s32[]{:S(2)}) async-start(s8[5242880]{0:T(1024)(128)(4,1)} %bitcast.147), calls=%async_computation.6 | async-start | bytes 2097152
  119.9 6.6 %copy-start.5 = (f32[640,256]{1,0:T(8,128)S(1)}, f32[640,256]{1,0:T(8,128)}, u32[]{:S(2)}) copy-start(f32[640,256]{1,0:T(8,128)} %copy-done.4) | copy-start | bytes 1966084
  132.7 50.5 %copy-start.48 = (f32[128]{0:T(128)S(1)}, f32[128]{0:T(128)}, u32[]{:S(2)}) copy-start(f32[128]{0:T(128)} %copy-done.47) | copy-start | bytes 1540
  132.7 50.5 %copy-start.10 = (f32[128,640]{1,0:T(8,128)S(1)}, f32[128,640]{1,0:T(8,128)}, u32[]{:S(2)}) copy-start(f32[128,640]{1,0:T(8,128)} %copy-done.9) | copy-start | bytes 983044
  (40 other events, 77.1 us)
Sparse Core Ops, SparseCore 0:
  9.6 12.1 all-gather.6
  23.2 10.6 all-gather.8
  35.5 12.5 all-gather.10
  49.5 12.5 all-gather.12
  63.4 12.5 all-gather.14
  130.9 378.3 all-reduce.14
where the time goes:
time: 528 us; the launch traced here: 527 us
  waiting for transfers between devices  344 us (65%)
  blocking collectives  54.9 us (10%)
  local copies, waits for them, and re-layouts  41.3 us (8%)
  starting transfers between devices  33.3 us (6%)
  matrix products  31.6 us (6%)
  between operations  15.3 us (3%)
  other arithmetic  6.17 us (1%)
    unnamed x7, waiting for transfers between devices  328 us
    unnamed x1, blocking collectives  49 us
    ppermute x12, starting transfers between devices, shifted(): return lax.ppermute(x, axis, pairs)  33.1 us
    unnamed x135, local copies, waits for them, and re-layouts  28.7 us
    dot_general x20, matrix products, product(): return jnp.einsum(form, left, right, preferred_element_type=jnp.float32)  18.8 us
  transfers between devices with their start and end apart: 18, of which 4 were waited for; matrix products, arithmetic and copies ran while one was open for 7% of the time, Pallas kernels for 0%

commit v1 on v0

--- a/solution.py
+++ b/solution.py
@@ -1,14 +1,20 @@
+import functools
 import math
 
 import jax
 import jax.numpy as jnp
+import numpy as np
 from jax import lax
+from jax.experimental import pallas as pl
+from jax.experimental.pallas import tpu as pltpu
 from jax.sharding import PartitionSpec as P
 
 WINDOW = 512
-
-
 EPS = 1e-06
+LANES = 128
+F32 = jnp.float32
+BF16 = jnp.bfloat16
+MIB = 1 << 20
 
 
 def shifted(x, axis, by):
@@ -40,7 +46,7 @@
     return jnp.einsum(form, left, right, preferred_element_type=jnp.float32)
 
 
-def on_device(
+def general(
     tokens,
     segments,
     positions,
@@ -60,15 +66,9 @@
     head_count = w_query.shape[1] // head_size
     reach = (WINDOW - 1 + tok_rows - 1) // tok_rows
     scale = head_size ** (-0.5)
-    gathered = (
-        lax.all_gather(w_query, "fsdp", axis=0, tiled=True),
-        lax.all_gather(w_key, "fsdp", axis=0, tiled=True),
-        lax.all_gather(w_value, "fsdp", axis=0, tiled=True),
-        lax.all_gather(w_out, "fsdp", axis=0, tiled=True),
-        lax.all_gather(w_gate, "fsdp", axis=0, tiled=True),
-        lax.all_gather(w_up, "fsdp", axis=0, tiled=True),
-        lax.all_gather(w_down, "fsdp", axis=0, tiled=True),
-        lax.all_gather(norm_gains, "fsdp", axis=0, tiled=True),
+    gathered = tuple(
+        lax.all_gather(w, "fsdp", axis=0, tiled=True)
+        for w in (w_query, w_key, w_value, w_out, w_gate, w_up, w_down, norm_gains)
     )
     query_full, key_full, value_full, out_full, gate_full, up_full, down_full, gains_full = gathered
     gains = gains_full.astype(jnp.float32)
@@ -152,34 +152,24 @@
         return resid + norm_rows(branch, gain)
 
     result, finish_back = jax.vjp(finish, after, down, gain_pff)
-    again = (
-        lax.all_gather(w_query, "fsdp", axis=0, tiled=True),
-        lax.all_gather(w_key, "fsdp", axis=0, tiled=True),
-        lax.all_gather(w_value, "fsdp", axis=0, tiled=True),
-        lax.all_gather(w_out, "fsdp", axis=0, tiled=True),
-        lax.all_gather(w_gate, "fsdp", axis=0, tiled=True),
-        lax.all_gather(w_up, "fsdp", axis=0, tiled=True),
-        lax.all_gather(w_down, "fsdp", axis=0, tiled=True),
-    )
-    query_back, key_back, value_back, out_back, gate_back, up_back, down_back = again
     grad_result = cotangent[0].astype(jnp.float32)
     grad_after, grad_down, grad_gpff = finish_back(grad_result)
     down_grad_low = grad_down.astype(jnp.bfloat16)
     grad_w_down = product("tf,td->fd", inner_low, down_grad_low)
-    grad_inner = product("td,fd->tf", down_grad_low, down_back)
+    grad_inner = product("td,fd->tf", down_grad_low, down_full)
     grad_gate, grad_upv = mixer_back(grad_inner)
     gate_grad_low = grad_gate.astype(jnp.bfloat16)
     up_grad_low = grad_upv.astype(jnp.bfloat16)
     grad_w_gate = product("td,tf->df", ff_low, gate_grad_low)
     grad_w_up = product("td,tf->df", ff_low, up_grad_low)
-    grad_normed_ff = product("tf,df->td", gate_grad_low, gate_back) + product(
-        "tf,df->td", up_grad_low, up_back
+    grad_normed_ff = product("tf,df->td", gate_grad_low, gate_full) + product(
+        "tf,df->td", up_grad_low, up_full
     )
     grad_resid, grad_branch, grad_gpa, grad_gpf = middle_back((grad_after, grad_normed_ff))
     branch_grad_low = grad_branch.astype(jnp.bfloat16)
     grad_w_out = product("ta,td->ad", mixed_heads, branch_grad_low)
     grad_heads = (
-        product("td,ad->ta", branch_grad_low, out_back)
+        product("td,ad->ta", branch_grad_low, out_full)
         .astype(jnp.bfloat16)
         .reshape(tok_rows, head_count, head_size)
     )
@@ -209,34 +199,777 @@
     grad_w_key = product("td,te->de", normed_low, key_grad_low)
     grad_w_value = product("td,te->de", normed_low, value_grad_low)
     grad_normed = (
-        product("te,de->td", query_grad_low, query_back)
-        + product("te,de->td", key_grad_low, key_back)
-        + product("te,de->td", value_grad_low, value_back)
+        product("te,de->td", query_grad_low, query_full)
+        + product("te,de->td", key_grad_low, key_full)
+        + product("te,de->td", value_grad_low, value_full)
     )
     grad_in, grad_gin = first_back(grad_normed)
     input_grad = (grad_resid + grad_in)[None]
     grad_gains = jnp.concatenate([grad_gin, grad_gq, grad_gk, grad_gpa, grad_gpf, grad_gpff])
-    flat_query = grad_w_query.reshape(-1)
-    flat_key = grad_w_key.reshape(-1)
-    flat_value = grad_w_value.reshape(-1)
-    flat_out = grad_w_out.reshape(-1)
-    flat_gate = grad_w_gate.reshape(-1)
-    flat_up = grad_w_up.reshape(-1)
-    flat_down = grad_w_down.reshape(-1)
-    owned = (
-        lax.psum_scatter(flat_query, ("seq", "fsdp"), scatter_dimension=0, tiled=True),
-        lax.psum_scatter(flat_key, ("seq", "fsdp"), scatter_dimension=0, tiled=True),
-        lax.psum_scatter(flat_value, ("seq", "fsdp"), scatter_dimension=0, tiled=True),
-        lax.psum_scatter(flat_out, ("seq", "fsdp"), scatter_dimension=0, tiled=True),
-        lax.psum_scatter(flat_gate, ("seq", "fsdp"), scatter_dimension=0, tiled=True),
-        lax.psum_scatter(flat_up, ("seq", "fsdp"), scatter_dimension=0, tiled=True),
-        lax.psum_scatter(flat_down, ("seq", "fsdp"), scatter_dimension=0, tiled=True),
-        lax.psum_scatter(grad_gains, ("seq", "fsdp"), scatter_dimension=0, tiled=True),
-    )
-    own_query, own_key, own_value, own_out, own_gate, own_up, own_down, own_gains = owned
+    own = tuple(
+        lax.psum_scatter(g.reshape(-1), ("seq", "fsdp"), scatter_dimension=0, tiled=True)
+        for g in (
+            grad_w_query,
+            grad_w_key,
+            grad_w_value,
+            grad_w_out,
+            grad_w_gate,
+            grad_w_up,
+            grad_w_down,
+            grad_gains,
+        )
+    )
+    return (result.astype(jnp.bfloat16)[None], input_grad) + own
+
+
+XY = 4
+LINE = 4
+
+
+def vmem(count):
+    return [pl.BlockSpec(memory_space=pltpu.VMEM)] * count
+
+
+def anywhere(count):
+    return [pl.BlockSpec(memory_space=pl.ANY)] * count
+
+
+def mm(a, b):
+    return lax.dot_general(a, b, (((1,), (0,)), ((), ())), preferred_element_type=F32)
+
+
+def mm_nt(a, b):
+    return lax.dot_general(a, b, (((1,), (1,)), ((), ())), preferred_element_type=F32)
+
+
+def mm_tn(a, b):
+    return lax.dot_general(a, b, (((0,), (0,)), ((), ())), preferred_element_type=F32)
+
+
+def inverse_rms(x):
+    return lax.rsqrt(jnp.mean(x * x, axis=-1, keepdims=True) + EPS)
+
+
+def norm_back(hat, inv, gain, grad):
+    scaled = grad * gain
+    return inv * (scaled - hat * jnp.mean(hat * scaled, axis=-1, keepdims=True))
+
+
+def turn_fwd(x, cosine, sine):
+    half = x.shape[1] // 2
+    a, b = x[:, :half], x[:, half:]
+    return jnp.concatenate([a * cosine - b * sine, b * cosine + a * sine], axis=1)
+
+
+def turn_bwd(x, cosine, sine):
+    half = x.shape[1] // 2
+    a, b = x[:, :half], x[:, half:]
+    return jnp.concatenate([a * cosine + b * sine, b * cosine - a * sine], axis=1)
+
+
+def assemble(core, pairs, sems):
+    copies = []
+    for n, (mine, theirs, full) in enumerate(pairs):
+        rows = mine.shape[0]
+        for side, (part, at) in enumerate(((mine, core), (theirs, 1 - core))):
+            begin = pl.multiple_of(at * rows, 16)
+            copy = pltpu.make_async_copy(part, full.at[pl.ds(begin, rows)], sems.at[n, side])
+            copy.start()
+            copies.append(copy)
+    return copies
+
+
+def attention_kernel(
+    reach,
+    meta,
+    *refs,
+):
+    halo = refs[: reach + 1]
+    (
+        gains,
+        cos_ref,
+        sin_ref,
+        wq_a,
+        wq_b,
+        wk_a,
+        wk_b,
+        wv_a,
+        wv_b,
+        n1_out,
+        qraw_out,
+        q_out,
+        kraw_out,
+        k_out,
+        v_out,
+        p_out,
+        ao_out,
+        wq,
+        wk,
+        wv,
+        sems,
+    ) = refs[reach + 1 :]
+    rows = halo[0].shape[0]
+    width = n1_out.shape[1]
+    size = k_out.shape[1]
+    heads = q_out.shape[1] // size
+    scale = size ** (-0.5)
+    place, core = meta[0], meta[1]
+    copies = assemble(core, ((wk_a, wk_b, wk), (wv_a, wv_b, wv), (wq_a, wq_b, wq)), sems)
+    g_in = gains[:, :width]
+    g_q = gains[:, width : width + size]
+    g_k = gains[:, width + size : width + 2 * size]
+    for block in range(reach + 1):
+        x = halo[block][:, :width].astype(F32)
+        n1_out[block * rows : (block + 1) * rows, :] = (x * inverse_rms(x) * g_in).astype(BF16)
+    for copy in copies[:4]:
+        copy.wait()
+    n1 = n1_out[...]
+    kraw = mm(n1, wk[...])
+    kraw_out[...] = kraw
+    k = turn_fwd(kraw * inverse_rms(kraw) * g_k, cos_ref[...], sin_ref[...]).astype(BF16)
+    k_out[...] = k
+    v = mm(n1, wv[...]).astype(BF16)
+    v_out[...] = v
+    for copy in copies[4:]:
+        copy.wait()
+    keys = (reach + 1) * rows
+    lane = lax.broadcasted_iota(jnp.int32, (rows, LANES), 1)
+    pick = jnp.where(lane == 0, 1.0, 0.0).astype(BF16)
+    seg_keys = jnp.concatenate([mm_nt(pick, halo[b][:, width:]) for b in range(reach + 1)], axis=1)
+    seg_own = halo[reach][:, width : width + 1].astype(F32)
+    at_query = reach * rows + lax.broadcasted_iota(jnp.int32, (rows, keys), 0)
+    at_key = lax.broadcasted_iota(jnp.int32, (rows, keys), 1)
+    gap = at_query - at_key
+    allowed = (
+        (seg_keys == seg_own)
+        & (gap >= 0)
+        & (gap < WINDOW)
+        & (at_key >= (reach - place) * rows)
+    )
+    cos_own, sin_own = cos_ref[reach * rows :, :], sin_ref[reach * rows :, :]
+    for h in range(heads):
+        cols = slice(h * size, (h + 1) * size)
+        qraw = mm(n1_out[reach * rows :, :], wq[:, cols])
+        qraw_out[:, cols] = qraw
+        q = turn_fwd(qraw * inverse_rms(qraw) * g_q, cos_own, sin_own) * scale
+        q = q.astype(BF16)
+        q_out[:, cols] = q
+        s = jnp.where(allowed, mm_nt(q, k), -1e30)
+        e = jnp.exp(s - jnp.max(s, axis=-1, keepdims=True))
+        p = e / jnp.sum(e, axis=-1, keepdims=True)
+        p_out[h] = p
+        ao_out[:, cols] = mm(p.astype(BF16), v).astype(BF16)
+
+
+def pick_half(core, unit, width):
+    row = lax.broadcasted_iota(jnp.int32, (LANES, width), 0)
+    col = lax.broadcasted_iota(jnp.int32, (LANES, width), 1)
+    want = (lax.div(row, unit) * 2 + core) * unit + lax.rem(row, unit)
+    return jnp.where(col == want, 1.0, 0.0).astype(BF16)
+
+
+def store_lanes(ref, base, value):
+    rows = value.shape[0]
+    for b in range(value.shape[1] // LANES):
+        ref[base + b * rows : base + (b + 1) * rows, :] = value[:, b * LANES : (b + 1) * LANES]
+    return base + rows * (value.shape[1] // LANES)
+
+
+def feed_kernel(
+    meta,
+    tok,
+    ct,
+    gains,
+    order,
+    ao_ref,
+    wo_a,
+    wo_b,
+    wg_a,
+    wg_b,
+    wu_a,
+    wu_b,
+    wd_a,
+    wd_b,
+    mixed_out,
+    dx_out,
+    dao_out,
+    dg_out,
+    keep,
+    send,
+    wo,
+    wg,
+    wu,
+    wd,
+    gate_s,
+    up_s,
+    hid_s,
+    dg_s,
+    du_s,
+    sems,
+):
+    core = meta[1]
+    rows, width = ct.shape
+    size2 = gains.shape[1] - 4 * width
+    ff = wg.shape[1]
+    copies = assemble(
+        core, ((wo_a, wo_b, wo), (wg_a, wg_b, wg), (wu_a, wu_b, wu), (wd_a, wd_b, wd)), sems
+    )
+    base = width + size2
+    g_pa = gains[:, base : base + width]
+    g_pf = gains[:, base + width : base + 2 * width]
+    g_pff = gains[:, base + 2 * width :]
+    x = tok[:, :width].astype(F32)
+    c = ct[...].astype(F32)
+    for copy in copies[:2]:
+        copy.wait()
+    ya = mm(ao_ref[...], wo[...])
+    inv_a = inverse_rms(ya)
+    hat_a = ya * inv_a
+    x2 = x + hat_a * g_pa
+    inv_f = inverse_rms(x2)
+    hat_f = x2 * inv_f
+    n2 = (hat_f * g_pf).astype(BF16)
+    for copy in copies[2:]:
+        copy.wait()
+    part = 512
+    root = math.sqrt(2.0 / math.pi)
+    f = jnp.zeros((rows, width), F32)
+    for at in range(0, ff, part):
+        cols = slice(at, at + part)
+        gate = mm(n2, wg[:, cols])
+        up = mm(n2, wu[:, cols])
+        gate_s[:, cols] = gate
+        up_s[:, cols] = up
+        t = jnp.tanh(root * (gate + 0.044715 * (gate * gate * gate)))
+        hid = (0.5 * gate * (1.0 + t) * up).astype(BF16)
+        hid_s[:, cols] = hid
+        f = f + mm(hid, wd[cols, :])
+    inv_d = inverse_rms(f)
+    hat_d = f * inv_d
+    mixed_out[...] = (x2 + hat_d * g_pff).astype(BF16)
+    df = norm_back(hat_d, inv_d, g_pff, c).astype(BF16)
+    dn2 = jnp.zeros((rows, width), F32)
+    for at in range(0, ff, part):
+        cols = slice(at, at + part)
+        dhid = mm_nt(df, wd[cols, :])
+        gate = gate_s[:, cols]
+        up = up_s[:, cols]
+        t = jnp.tanh(root * (gate + 0.044715 * (gate * gate * gate)))
+        act = 0.5 * gate * (1.0 + t)
+        slope = 0.5 * (1.0 + t) + 0.5 * gate * (1.0 - t * t) * (
+            root * (1.0 + 3.0 * 0.044715 * (gate * gate))
+        )
+        dgate = (dhid * up * slope).astype(BF16)
+        dup = (dhid * act).astype(BF16)
+        dg_s[:, cols] = dgate
+        du_s[:, cols] = dup
+        dn2 = dn2 + mm_nt(dgate, wg[:, cols]) + mm_nt(dup, wu[:, cols])
+    dx2 = c + norm_back(hat_f, inv_f, g_pf, dn2)
+    dx_out[...] = dx2
+    dya = norm_back(hat_a, inv_a, g_pa, dx2).astype(BF16)
+    dao_out[...] = mm_nt(dya, wo[...]).astype(BF16)
+    dg_out[:, :width] = jnp.sum(dx2 * hat_a, axis=0, keepdims=True)
+    dg_out[:, width : 2 * width] = jnp.sum(dn2 * hat_f, axis=0, keepdims=True)
+    dg_out[:, 2 * width :] = jnp.sum(c * hat_d, axis=0, keepdims=True)
+    ranks = lax.broadcasted_iota(jnp.int32, (width, width), 1)
+    perm = jnp.where(ranks == order[...], 1.0, 0.0).astype(BF16)
+    n2_t = mm_nt(perm, n2).astype(BF16)
+    half = width // 2
+    keep[:half, :] = n2_t[:half]
+    send[:half, :] = n2_t[half:]
+    at = half
+    for source, unit in ((hid_s, ff // 32), (ao_ref, ao_ref.shape[1] // 32)):
+        for ref, side in ((keep, core), (send, 1 - core)):
+            pick = pick_half(side, unit, 2 * LANES)
+            for b in range(source.shape[1] // (2 * LANES)):
+                block = source[:, 2 * b * LANES : 2 * (b + 1) * LANES]
+                ref[at + b * LANES : at + (b + 1) * LANES, :] = mm_nt(pick, block).astype(BF16)
+        at += source.shape[1] // 2
+    for ref in (keep, send):
+        base = store_lanes(ref, at, dg_s[...])
+        base = store_lanes(ref, base, du_s[...])
+        base = store_lanes(ref, base, df)
+        store_lanes(ref, base, dya)
+
+
+def load_lanes(ref, base, rows, cols):
+    blocks = [ref[base + b * rows : base + (b + 1) * rows, :] for b in range(cols // LANES)]
+    return jnp.concatenate(blocks, axis=1), base + rows * (cols // LANES)
+
+
+def put(xk, xs, first, plane, at, value):
+    x_bit, y_bit = plane & 1, plane >> 1
+    lead, other = (x_bit, y_bit) if first == "x" else (y_bit, x_bit)
+    ref = xs if lead else xk
+    ref[other, at : at + value.shape[0], :] = value
+
+
+def grads_kernel(
+    meta, width, ff, attn, mine, recv, gk, gs, uk, us, dk, ds, ok, os, left_s, right_s, prod_s
+):
+    place = meta[0]
+    half = width // 2
+    rows = LANES
+
+    def both(base, count):
+        left_s[:count, :rows] = mine[base : base + count, :]
+        left_s[:count, rows:] = recv[base : base + count, :]
+        return left_s[:count, :]
+
+    def right(base, cols):
+        for side, ref in enumerate((mine, recv)):
+            for b in range(cols // LANES):
+                right_s[side * rows : (side + 1) * rows, b * LANES : (b + 1) * LANES] = ref[
+                    base + b * rows : base + (b + 1) * rows, :
+                ]
+
+    at_hid = half
+    at_ao = at_hid + ff // 2
+    at_gate = at_ao + attn // 2
+    at_up = at_gate + ff
+    at_df = at_up + ff
+    at_dya = at_df + width
+    per = half // XY
+    n2 = both(0, half)
+    for base, (keep, send), first in ((at_gate, (gk, gs), "x"), (at_up, (uk, us), "y")):
+        right(base, ff)
+        for col in range(0, ff, 512):
+            out = mm(n2, right_s[:, col : col + 512]).astype(BF16)
+            for plane in range(XY):
+                for b in range(4):
+                    put(
+                        keep,
+                        send,
+                        first,
+                        plane,
+                        (col // LANES + b) * per,
+                        out[plane * per : (plane + 1) * per, b * LANES : (b + 1) * LANES],
+                    )
+    for base, at_left, count, (keep, send), first in (
+        (at_df, at_hid, ff // 2, (dk, ds), "x"),
+        (at_dya, at_ao, attn // 2, (ok, os), "y"),
+    ):
+        left = both(at_left, count)
+        right(base, width)
+        prod_s[:count, :] = mm(left, right_s[:, :width])
+        unit = count // (XY * LINE)
+        for plane in range(XY):
+            for line in range(LINE):
+                whose = (place ^ (line * XY + plane)) * unit
+                block = prod_s[pl.ds(pl.multiple_of(whose, unit), unit), :].astype(BF16)
+                for b in range(width // LANES):
+                    put(
+                        keep,
+                        send,
+                        first,
+                        plane,
+                        b * unit * LINE + line * unit,
+                        block[:, b * LANES : (b + 1) * LANES],
+                    )
+
+
+def back_kernel(
+    reach,
+    meta,
+    *refs,
+):
+    halo = refs[: reach + 1]
+    (
+        gains,
+        order,
+        cos_ref,
+        sin_ref,
+        n1_ref,
+        qraw_ref,
+        q_ref,
+        kraw_ref,
+        k_ref,
+        v_ref,
+        p_ref,
+        dao_ref,
+        wq_a,
+        wq_b,
+        wk_a,
+        wk_b,
+        wv_a,
+        wv_b,
+        keep,
+        send,
+        dn1_own,
+        dn1_far,
+        dg_out,
+        wq,
+        wk,
+        wv,
+        dqr_s,
+        dkv_s,
+        sems,
+    ) = refs[reach + 1 :]
+    core = meta[1]
+    rows = halo[0].shape[0]
+    width = n1_ref.shape[1]
+    size = k_ref.shape[1]
+    heads = q_ref.shape[1] // size
+    scale = size ** (-0.5)
+    copies = assemble(core, ((wk_a, wk_b, wk), (wv_a, wv_b, wv), (wq_a, wq_b, wq)), sems)
+    g_in = gains[:, :width]
+    g_q = gains[:, width : width + size]
+    g_k = gains[:, width + size : width + 2 * size]
+    k = k_ref[...]
+    v = v_ref[...]
+    keys = (reach + 1) * rows
+    cos_own, sin_own = cos_ref[reach * rows :, :], sin_ref[reach * rows :, :]
+    dk = jnp.zeros((keys, size), F32)
+    dv = jnp.zeros((keys, size), F32)
+    dgq = jnp.zeros((1, size), F32)
+    for h in range(heads):
+        cols = slice(h * size, (h + 1) * size)
+        p = p_ref[h]
+        dao = dao_ref[:, cols]
+        dp = mm_nt(dao, v)
+        ds = (p * (dp - jnp.sum(p * dp, axis=-1, keepdims=True))).astype(BF16)
+        dv = dv + mm_tn(p.astype(BF16), dao)
+        dk = dk + mm_tn(ds, q_ref[:, cols])
+        dq = turn_bwd(mm(ds, k) * scale, cos_own, sin_own)
+        qraw = qraw_ref[:, cols]
+        inv = inverse_rms(qraw)
+        hat = qraw * inv
+        dgq = dgq + jnp.sum(dq * hat, axis=0, keepdims=True)
+        dqr_s[:, cols] = norm_back(hat, inv, g_q, dq).astype(BF16)
+    dk = turn_bwd(dk, cos_ref[...], sin_ref[...])
+    kraw = kraw_ref[...]
+    inv = inverse_rms(kraw)
+    hat = kraw * inv
+    dg_out[:, width : width + size] = dgq
+    dg_out[:, width + size :] = jnp.sum(dk * hat, axis=0, keepdims=True)
+    dkv_s[:, :size] = norm_back(hat, inv, g_k, dk).astype(BF16)
+    dkv_s[:, size:] = dv.astype(BF16)
+    ranks = lax.broadcasted_iota(jnp.int32, (width, width), 1)
+    perm = jnp.where(ranks == order[...], 1.0, 0.0).astype(BF16)
+    n1_t = mm_nt(perm, n1_ref[...]).astype(BF16)
+    half = width // 2
+    per = half // XY
+    attn = heads * size
+    for ref, begin in ((send, half), (keep, 0)):
+        left = n1_t[begin : begin + half]
+        own = left[:, reach * rows :]
+        at = 0
+        for value, left_part, total in (
+            (dqr_s, own, attn),
+            (dkv_s, left, 2 * size),
+        ):
+            for col in range(0, total, 512):
+                out = mm(left_part, value[:, col : col + 512]).astype(BF16)
+                for plane in range(XY):
+                    for b in range(4):
+                        ref[
+                            plane,
+                            at + (col // LANES + b) * per : at + (col // LANES + b + 1) * per,
+                            :,
+                        ] = out[plane * per : (plane + 1) * per, b * LANES : (b + 1) * LANES]
+            at += total // LANES * per
+    for copy in copies:
+        copy.wait()
+    dgi = jnp.zeros((1, width), F32)
+    for block in range(reach + 1):
+        span = slice(block * rows, (block + 1) * rows)
+        dn1 = mm_nt(dkv_s[span, :size], wk[...]) + mm_nt(dkv_s[span, size:], wv[...])
+        if block == reach:
+            dn1 = dn1 + mm_nt(dqr_s[...], wq[...])
+        x = halo[block][:, :width].astype(F32)
+        dgi = dgi + jnp.sum(dn1 * (x * inverse_rms(x)), axis=0, keepdims=True)
+        if block == reach:
+            dn1_own[...] = dn1
+        else:
+            dn1_far[block] = dn1.astype(BF16)
+    dg_out[:, :width] = dgi
+
+
+def call(kernel, meta, args, specs, outs, scratch, limit, flops):
+    return pl.pallas_call(
+        kernel,
+        out_shape=outs,
+        in_specs=[pl.BlockSpec(memory_space=pltpu.SMEM)] + specs,
+        out_specs=vmem(len(outs)),
+        scratch_shapes=scratch,
+        compiler_params=pltpu.CompilerParams(vmem_limit_bytes=limit * MIB),
+        cost_estimate=pl.CostEstimate(flops=flops, bytes_accessed=8 * MIB, transcendentals=0),
+    )(meta, *args)
+
+
+def shape(dims, dtype):
+    return jax.ShapeDtypeStruct(dims, dtype)
+
+
+def fast(
+    tokens,
+    segments,
+    positions,
+    w_query,
+    w_key,
+    w_value,
+    w_out,
+    w_gate,
+    w_up,
+    w_down,
+    norm_gains,
+    cotangent,
+):
+    rows, width = tokens.shape[1:]
+    size = w_key.shape[1]
+    attn = w_query.shape[1]
+    heads = attn // size
+    ff = w_gate.shape[1]
+    count = norm_gains.shape[0] * 2
+    reach = (WINDOW - 1 + rows - 1) // rows
+    keys = (reach + 1) * rows
+    place = lax.axis_index("seq")
+    core = lax.axis_index("fsdp")
+    meta = jnp.stack([place, core]).astype(jnp.int32)
+
+    def partner(value):
+        return lax.ppermute(value, "fsdp", [(0, 1), (1, 0)])
+
+    def across(value, bits):
+        return lax.ppermute(value, "seq", [(i, i ^ bits) for i in range(XY * LINE)])
+
+    weights = (w_query, w_key, w_value, w_out, w_gate, w_up, w_down)
+    other = [partner(w) for w in weights]
+    gains_far = partner(norm_gains)
+    seg_cols = jnp.broadcast_to(segments[0].astype(BF16)[:, None], (rows, LANES))
+    tok = jnp.concatenate([tokens[0], seg_cols], axis=1)
+    halo = [shifted(tok, "seq", distance) for distance in range(reach, 0, -1)] + [tok]
+
+    gains = jnp.where(
+        core == 0,
+        jnp.concatenate([norm_gains, gains_far]),
+        jnp.concatenate([gains_far, norm_gains]),
+    ).astype(F32)[None]
+    unit = width // (2 * XY * LINE)
+    new = np.arange(width) // unit
+    core_bit, plane, line = new // (XY * LINE), new // LINE % XY, new % LINE
+    owner = (jnp.asarray(line * XY + plane, jnp.int32) ^ place) * 2 + (
+        jnp.asarray(core_bit, jnp.int32) ^ core
+    )
+    order = (owner * unit + jnp.asarray(np.arange(width) % unit, jnp.int32))[:, None]
+    freq = np.exp(np.arange(size // 2, dtype=np.float64) * (-2.0 * math.log(10000.0) / size))
+    turn = np.arange(keys, dtype=np.float64)[:, None] * freq
+    cosine = jnp.asarray(np.cos(turn).astype(np.float32))
+    sine = jnp.asarray(np.sin(turn).astype(np.float32))
+
+    n1, qraw, q, kraw, k, v, p, ao = call(
+        functools.partial(attention_kernel, reach),
+        meta,
+        (*halo, gains, cosine, sine, w_query, other[0], w_key, other[1], w_value, other[2]),
+        vmem(reach + 4) + anywhere(6),
+        [
+            shape((keys, width), BF16),
+            shape((rows, attn), F32),
+            shape((rows, attn), BF16),
+            shape((keys, size), F32),
+            shape((keys, size), BF16),
+            shape((keys, size), BF16),
+            shape((heads, rows, keys), F32),
+            shape((rows, attn), BF16),
+        ],
+        [
+            pltpu.VMEM((width, attn), BF16),
+            pltpu.VMEM((width, size), BF16),
+            pltpu.VMEM((width, size), BF16),
+            pltpu.SemaphoreType.DMA((3, 2)),
+        ],
+        24,
+        3 * 10**9,
+    )
+
+    pack = width // 2 + ff // 2 + attn // 2 + 2 * ff + 2 * width
+    mixed, dx, dao, dg_post, mlp_keep, mlp_send = call(
+        feed_kernel,
+        meta,
+        (
+            tok,
+            cotangent[0],
+            gains,
+            order,
+            ao,
+            w_out,
+            other[3],
+            w_gate,
+            other[4],
+            w_up,
+            other[5],
+            w_down,
+            other[6],
+        ),
+        vmem(5) + anywhere(8),
+        [
+            shape((rows, width), BF16),
+            shape((rows, width), F32),
+            shape((rows, attn), BF16),
+            shape((1, 3 * width), F32),
+            shape((pack, LANES), BF16),
+            shape((pack, LANES), BF16),
+        ],
+        [
+            pltpu.VMEM((attn, width), BF16),
+            pltpu.VMEM((width, ff), BF16),
+            pltpu.VMEM((width, ff), BF16),
+            pltpu.VMEM((ff, width), BF16),
+            pltpu.VMEM((rows, ff), F32),
+            pltpu.VMEM((rows, ff), F32),
+            pltpu.VMEM((rows, ff), BF16),
+            pltpu.VMEM((rows, ff), BF16),
+            pltpu.VMEM((rows, ff), BF16),
+            pltpu.SemaphoreType.DMA((4, 2)),
+        ],
+        36,
+        4 * 10**9,
+    )
+    mlp_recv = partner(mlp_send)
+
+    per_ff = width // 2 // XY * ff // LANES
+    per_down = ff // 2 // XY * width // LANES
+    per_out = attn // 2 // XY * width // LANES
+    halves = []
+    for per in (per_ff, per_ff, per_down, per_out):
+        halves += [shape((2, per, LANES), BF16)] * 2
+    gk, gs, uk, us, dk, ds, ok, os = call(
+        lambda meta_ref, *refs: grads_kernel(meta_ref, width, ff, attn, *refs),
+        meta,
+        (mlp_keep, mlp_recv),
+        vmem(2),
+        halves,
+        [
+            pltpu.VMEM((ff // 2, 2 * LANES), BF16),
+            pltpu.VMEM((2 * LANES, ff), BF16),
+            pltpu.VMEM((ff // 2, width), F32),
+        ],
+        32,
+        10**9,
+    )
+
+    per_q = width // 2 // XY * attn // LANES
+    per_k = width // 2 // XY * size // LANES
+    per_back = per_q + 2 * per_k
+    back_keep, back_send, dn1_own, dn1_far, dg_pre = call(
+        functools.partial(back_kernel, reach),
+        meta,
+        (
+            *halo,
+            gains,
+            order,
+            cosine,
+            sine,
+            n1,
+            qraw,
+            q,
+            kraw,
+            k,
+            v,
+            p,
+            dao,
+            w_query,
+            other[0],
+            w_key,
+            other[1],
+            w_value,
+            other[2],
+        ),
+        vmem(reach + 13) + anywhere(6),
+        [
+            shape((XY, per_back + 16, LANES), BF16),
+            shape((XY, per_back + 16, LANES), BF16),
+            shape((rows, width), F32),
+            shape((reach, rows, width), BF16),
+            shape((1, width + 2 * size), F32),
+        ],
+        [
+            pltpu.VMEM((width, attn), BF16),
+            pltpu.VMEM((width, size), BF16),
+            pltpu.VMEM((width, size), BF16),
+            pltpu.VMEM((rows, attn), BF16),
+            pltpu.VMEM((keys, 2 * size), BF16),
+            pltpu.SemaphoreType.DMA((3, 2)),
+        ],
+        32,
+        4 * 10**9,
+    )
+    share = count // (2 * XY * LINE)
+    dg = jnp.concatenate([dg_pre, dg_post], axis=1).reshape(2 * XY * LINE, share)
+    new = np.arange(2 * XY * LINE)
+    core_bit, plane, line = new // (XY * LINE), new // LINE % XY, new % LINE
+    owner = (jnp.asarray(line * XY + plane, jnp.int32) ^ place) * 2 + (
+        jnp.asarray(core_bit, jnp.int32) ^ core
+    )
+    dg = jnp.take(dg, owner, axis=0).reshape(2, XY, LINE, share).astype(BF16)
+    dg = jnp.pad(dg, ((0, 0), (0, 0), (0, 16 - LINE), (0, LANES - share)))
+    back_keep = lax.dynamic_update_slice(back_keep, dg[0], (0, per_back, 0))
+    back_send = lax.dynamic_update_slice(back_send, dg[1], (0, per_back, 0))
+    back_recv = partner(back_send)
+
+    def add(a, b):
+        return (a.astype(F32) + b.astype(F32)).astype(BF16)
+
+    def plane_sum(keep, send, bits):
+        keep = add(keep, across(send, bits))
+        return add(keep[0], across(keep[1], 3 - bits))
+
+    def line_sum(parts):
+        total = parts[0].astype(F32)
+        for step in range(1, LINE):
+            total = total + across(parts[step], step * XY).astype(F32)
+        return total
+
+    def by_line(value, blocks):
+        unit = value.shape[0] // (blocks * LINE)
+        return value.reshape(blocks, LINE, unit, LANES).transpose(1, 0, 2, 3)
+
+    def flat(total, blocks):
+        unit = total.shape[0] // blocks
+        return total.reshape(blocks, unit, LANES).transpose(1, 0, 2).reshape(-1)
+
+    gate_sum = plane_sum(gk, gs, 1)
+    up_sum = plane_sum(uk, us, 2)
+    down_sum = plane_sum(dk, ds, 1)
+    out_sum = plane_sum(ok, os, 2)
+    mid = per_q // 2 + per_k
+    both = add(back_keep, back_recv)
+    back_x = plane_sum(both[0::2, :mid], both[1::2, :mid], 1)
+    back_y = plane_sum(both[:2, mid:], both[2:, mid:], 2)
+    back_sum = jnp.concatenate([back_x, back_y], axis=0)
+
+    def joined(*pieces):
+        return jnp.concatenate([by_line(v, b).reshape(LINE, -1, LANES) for v, b in pieces], axis=1)
+
+    wide = ff // LANES
+    narrow = width // LANES
+    first = line_sum(joined((gate_sum, wide), (up_sum, wide)))
+    second = line_sum(joined((down_sum, narrow), (out_sum, narrow)))
+    scales = back_sum[per_back : per_back + LINE].reshape(LINE, 1, LANES)
+    third = line_sum(
+        jnp.concatenate(
+            [joined((back_sum[:per_back], (attn + 2 * size) // LANES)), scales], axis=1
+        )
+    )
+    own_gate = flat(first[: per_ff // LINE], wide)
+    own_up = flat(first[per_ff // LINE :], wide)
+    own_down = flat(second[: per_down // LINE], narrow)
+    own_out = flat(second[per_down // LINE :], narrow)
+    a, b = per_q // LINE, (per_q + per_k) // LINE
+    own_query = flat(third[:a], attn // LANES)
+    own_key = flat(third[a:b], size // LANES)
+    own_value = flat(third[b : per_back // LINE], size // LANES)
+    own_gains = third[per_back // LINE, :share]
+
+    dn1 = dn1_own
+    for index in range(reach):
+        dn1 = dn1 + shifted(dn1_far[index], "seq", index - reach).astype(F32)
+    x = tokens[0].astype(F32)
+    inv = inverse_rms(x)
+    input_grad = dx + norm_back(x * inv, inv, gains[:, :width], dn1)
     return (
-        result.astype(jnp.bfloat16)[None],
-        input_grad,
+        mixed[None],
+        input_grad[None],
         own_query,
         own_key,
         own_value,
@@ -263,8 +996,9 @@
         P("fsdp"),
         P("fsdp", "seq", None),
     )
+    small = mesh.shape["seq"] == XY * LINE and mesh.shape["fsdp"] == 2
     return jax.shard_map(
-        on_device,
+        fast if small else general,
         mesh=mesh,
         in_specs=placed,
         out_specs=(

time: 528 us -> 190 us (0.36)
  waiting for transfers between devices: 344 us -> 56.8 us
  blocking collectives: 54.9 us -> 0 us
  matrix products: 31.6 us -> 0 us
  starting transfers between devices: 33.3 us -> 62 us
  Pallas kernels: 0 us -> 26.6 us
  local copies, waits for them, and re-layouts: 41.3 us -> 27.4 us
  between operations: 15.3 us -> 1.63 us
  other arithmetic: 6.17 us -> 14.4 us
    unnamed x7 -> x0, waiting for transfers between devices: 328 us -> none
    unnamed x1 -> x0, blocking collectives: 49 us -> none
    ppermute x0 -> x31, waiting for transfers between devices: none -> 43.2 us  [the longest x21 43.1 us: across(): return lax.ppermute(value, 'seq', [(i, i ^ bits) for i in range(XY * LINE)])]
    ppermute x0 -> x31, starting transfers between devices: none -> 41.7 us  [the longest x21 39.5 us: across(): return lax.ppermute(value, 'seq', [(i, i ^ bits) for i in range(XY * LINE)])]
    dot_general x27 -> x0, matrix products: 31.6 us -> none  [the longest x20 18.8 us: product(): return jnp.einsum(form, left, right, preferred_element_type=jnp.float32)]
    pallas_call x0 -> x4, Pallas kernels: none -> 26.6 us  [call(): pl.pallas_call(kernel, out_shape=outs, in_specs=[pl.BlockSpec(memory_spac...]
    all_gather x5 -> x0, waiting for transfers between devices: 14 us -> none  [the longest x1 10.2 us: on_device(): lax.all_gather(w_down, 'fsdp', axis=0, tiled=True)]
    ppermute x12 -> x8, starting transfers between devices: 33.1 us -> 20.4 us  [shifted(): return lax.ppermute(x, axis, pairs)]
  transfers between devices with their start and end apart: 18 -> 39, of which waited for: 4 -> 17; matrix products, arithmetic and copies ran while one was open for 7% -> 10% of each run, Pallas kernels for 0% -> 5%
where the time goes in v1:
time: 190 us; the launch traced here: 189 us
  starting transfers between devices  62 us (33%)
  waiting for transfers between devices  56.8 us (30%)
  local copies, waits for them, and re-layouts  27.4 us (14%)
  Pallas kernels  26.6 us (14%)
  other arithmetic  14.4 us (8%)
    ppermute x21, waiting for transfers between devices, across(): return lax.ppermute(value, 'seq', [(i, i ^ bits) for i in range(XY * LINE)])  43.1 us
    ppermute x21, starting transfers between devices, across(): return lax.ppermute(value, 'seq', [(i, i ^ bits) for i in range(XY * LINE)])  39.5 us
    pallas_call x4, Pallas kernels, call(): pl.pallas_call(kernel, out_shape=outs, in_specs=[pl.BlockSpec(memory_spac...  26.6 us
    ppermute x8, starting transfers between devices, shifted(): return lax.ppermute(x, axis, pairs)  20.4 us
    unnamed x108, local copies, waits for them, and re-layouts  19 us
    ppermute x8, waiting for transfers between devices, shifted(): return lax.ppermute(x, axis, pairs)  13.7 us
    convert_element_type x13, other arithmetic, add(): return (a.astype(F32) + b.astype(F32)).astype(BF16)  4.33 us
    concatenate x1, other arithmetic, joined(): jnp.concatenate([by_line(v, b).reshape(LINE, -1, LANES) for v, b in piece...  4.01 us
  transfers between devices with their start and end apart: 39, of which 17 were waited for; matrix products, arithmetic and copies ran while one was open for 10% of the time, Pallas kernels for 5%

profile of v1, /device:TPU:0, one launch (start us, length us, event | category | flops | bytes accessed | tf_op | source)
XLA Modules:
  0.0 188.9 jit_solution(321763828725309833)
XLA Ops:
  2.9 4.9 %collective-permute-start.1 = (bf16[128,768]{1,0:T(8,128)(2,1)S(1)}, bf16[128,768]{1,0:T(8,128)(2,1)S(1)}, u32[]{:S(2)}, u32[]{:S(2)}) collective-permute-start(bf16[128,768]{1,0:T(8,128)(2,1)S(1)} %pad_maximum_fusion.2.refs_4_.tok), channel_id=1, source_target_pairs={{0,8},{2,10},{4,12},{6,14},{8,16},{10,18},{12,20},{14,22},{16,24},... | collective-permute-start | bytes 589832 | tf_op jit(solution)/shard_map/ppermute | solution.py:23
  11.0 4.4 %collective-permute-start.2 = (bf16[128,768]{1,0:T(8,128)(2,1)S(1)}, bf16[128,768]{1,0:T(8,128)(2,1)S(1)}, u32[]{:S(2)}, u32[]{:S(2)}) collective-permute-start(bf16[128,768]{1,0:T(8,128)(2,1)S(1)} %pad_maximum_fusion.2.refs_4_.tok), channel_id=1, source_target_pairs={{0,6},{2,8},{4,10},{6,12},{8,14},{10,16},{12,18},{14,20},{16,22},{... | collective-permute-start | bytes 589832 | tf_op jit(solution)/shard_map/ppermute | solution.py:23
  15.4 3.4 %collective-permute-start.3 = (bf16[128,768]{1,0:T(8,128)(2,1)S(1)}, bf16[128,768]{1,0:T(8,128)(2,1)S(1)}, u32[]{:S(2)}, u32[]{:S(2)}) collective-permute-start(bf16[128,768]{1,0:T(8,128)(2,1)S(1)} %pad_maximum_fusion.2.refs_4_.tok), channel_id=1, source_target_pairs={{0,4},{2,6},{4,8},{6,10},{8,12},{10,14},{12,16},{14,18},{16,20},{1... | collective-permute-start | bytes 589832 | tf_op jit(solution)/shard_map/ppermute | solution.py:23
  19.9 2.5 %collective-permute-start.4 = (bf16[128,768]{1,0:T(8,128)(2,1)S(1)}, bf16[128,768]{1,0:T(8,128)(2,1)S(1)}, u32[]{:S(2)}, u32[]{:S(2)}) collective-permute-start(bf16[128,768]{1,0:T(8,128)(2,1)S(1)} %pad_maximum_fusion.2.refs_4_.tok), channel_id=1, source_target_pairs={{0,2},{2,4},{4,6},{6,8},{8,10},{10,12},{12,14},{14,16},{16,18},{18... | collective-permute-start | bytes 589832 | tf_op jit(solution)/shard_map/ppermute | solution.py:23
  23.7 2.5 %collective-permute-done.4.refs_3_ = bf16[128,768]{1,0:T(8,128)(2,1)S(1)} collective-permute-done((bf16[128,768]{1,0:T(8,128)(2,1)S(1)}, bf16[128,768]{1,0:T(8,128)(2,1)S(1)}, u32[]{:S(2)}, u32[]{:S(2)}) %collective-permute-start.4) | collective-permute-done | bytes 196640 | tf_op jit(solution)/shard_map/ppermute | solution.py:23
  34.4 5.4 %shard_map.249 = (bf16[640,640]{1,0:T(8,128)(2,1)S(1)}, f32[128,1024]{1,0:T(8,128)S(1)}, bf16[128,1024]{1,0:T(8,128)(2,1)S(1)}, f32[640,256]{1,0:T(8,128)S(1)}, ...) custom-call(s32[2]{0:T(128)S(1)} %pad_add_fusion.meta.meta_ref, ...), custom_call_target="tpu_custom_call" | custom-call | flops 3000000000 | bytes 8388608 | tf_op jit(solution)/shard_map/pallas_call | solution.py:689
  42.5 9.1 %shard_map.250 = (bf16[128,640]{1,0:T(8,128)(2,1)}, f32[128,640]{1,0:T(8,128)S(1)}, bf16[128,1024]{1,0:T(8,128)(2,1)S(1)}, f32[1,1920]{1,0:T(1,128)S(1)}, bf16[7...) custom-call(s32[2]{0:T(128)S(1)} %pad_add_fusion.meta.meta_ref, ...), custom_call_target="tpu_custom_call" | custom-call | flops 4000000000 | bytes 8388608 | tf_op jit(solution)/shard_map/pallas_call | solution.py:689
  54.5 7.8 %shard_map.251 = (bf16[4,976,128]{2,1,0:T(8,128)(2,1)S(1)}, bf16[4,976,128]{2,1,0:T(8,128)(2,1)S(1)}, f32[128,640]{1,0:T(8,128)S(1)}, bf16[4,128,640]{2,1,0:T(8,128)(2,1)S(1)}, f32[1,1152]{1,0:T(1,128)S(1)}) custom-call(s32[2]{0:T(128)S(1)} %pad_add_fusion.meta.meta_ref, bf16[128,768]{1,0:T(8,128)(2,1)S(1)} %copy-done.28, bf16[128,768]{1,0:T(8,128)(2,1)S(1)} %copy-done.30, ...), custom_call_target="tpu_custom_call" | custom-call | flops 4000000000 | bytes 8388608 | tf_op jit(solution)/shard_map/pallas_call | solution.py:689
  71.3 7.9 %collective-permute-done.12 = bf16[128,640]{1,0:T(8,128)(2,1)S(1)} collective-permute-done((bf16[128,640]{1,0:T(8,128)(2,1)S(1)}, bf16[128,640]{1,0:T(8,128)(2,1)S(1)}, u32[]{:S(2)}, u32[]{:S(2)}) %collective-permute-start.12) | collective-permute-done | bytes 163872 | tf_op jit(solution)/shard_map/ppermute | solution.py:23
  79.2 2.8 %collective-permute-done.14 = bf16[128,640]{1,0:T(8,128)(2,1)S(1)} collective-permute-done((bf16[128,640]{1,0:T(8,128)(2,1)S(1)}, bf16[128,640]{1,0:T(8,128)(2,1)S(1)}, u32[]{:S(2)}, u32[]{:S(2)}) %collective-permute-start.14) | collective-permute-done | bytes 163872 | tf_op jit(solution)/shard_map/ppermute | solution.py:23
  82.5 4.3 %collective-permute-start.17 = (bf16[2,480,128]{2,1,0:T(8,128)(2,1)S(1)}, bf16[2,480,128]{2,1,0:T(8,128)(2,1)S(1)}, u32[]{:S(2)}, u32[]{:S(2)}) collective-permute-start(bf16[2,480,128]{2,1,0:T(8,128)(2,1)S(1)} %slice.143), channel_id=1, source_target_pairs={{0,2},{2,0},{4,6},{6,4},{8,10},{10,8},{12,14},{14,12},{16,18},{18,... | collective-permute-start | bytes 737288 | tf_op jit(solution)/shard_map/ppermute | solution.py:734
  87.7 6.7 %collective-permute-start.19 = (bf16[2,496,128]{2,1,0:T(8,128)(2,1)S(1)}, bf16[2,496,128]{2,1,0:T(8,128)(2,1)S(1)}, u32[]{:S(2)}, u32[]{:S(2)}) collective-permute-start(bf16[2,496,128]{2,1,0:T(8,128)(2,1)S(1)} %slice.186), channel_id=1, source_target_pairs={{0,4},{2,6},{4,0},{6,2},{8,12},{10,14},{12,8},{14,10},{16,20},{18,... | collective-permute-start | bytes 761864 | tf_op jit(solution)/shard_map/ppermute | solution.py:734
  94.5 4.6 %collective-permute-start.18 = (bf16[480,128]{1,0:T(8,128)(2,1)S(1)}, bf16[480,128]{1,0:T(8,128)(2,1)S(1)}, u32[]{:S(2)}, u32[]{:S(2)}) collective-permute-start(bf16[480,128]{1,0:T(8,128)(2,1)S(1)} %slice_bitcast_fusion.14), channel_id=1, source_target_pairs={{0,4},{2,6},{4,0},{6,2},{8,12},{10,14},{12,8},{14,10},{16,20},{18,... | collective-permute-start | bytes 368648 | tf_op jit(solution)/shard_map/ppermute | solution.py:734
  99.1 1.7 collective-permute-done.19
  102.5 3.4 %collective-permute-done.20 = bf16[496,128]{1,0:T(8,128)(2,1)S(1)} collective-permute-done((bf16[496,128]{1,0:T(8,128)(2,1)S(1)}, bf16[496,128]{1,0:T(8,128)(2,1)S(1)}, u32[]{:S(2)}, u32[]{:S(2)}) %collective-permute-start.20) | collective-permute-done | bytes 127008 | tf_op jit(solution)/shard_map/ppermute | solution.py:734
  106.6 1.8 collective-permute-start.21
  109.5 1.7 collective-permute-start.23
  111.2 4.3 %shard_map.252 = (bf16[2,1280,128]{2,1,0:T(8,128)(2,1)S(1)}, bf16[2,1280,128]{2,1,0:T(8,128)(2,1)S(1)}, bf16[2,1280,128]{2,1,0:T(8,128)(2,1)S(1)}, bf16[2,1280,1...) custom-call(s32[2]{0:T(128)S(1)} %pad_add_fusion.meta.meta_ref, ...), custom_call_target="tpu_custom_call" | custom-call | flops 1000000000 | bytes 8388608 | tf_op jit(solution)/shard_map/pallas_call | solution.py:689
  118.9 1.7 collective-permute-start.27
  122.9 6.9 %collective-permute-done.27 = bf16[2,640,128]{2,1,0:T(8,128)(2,1)} collective-permute-done((bf16[2,640,128]{2,1,0:T(8,128)(2,1)}, bf16[2,640,128]{2,1,0:T(8,128)(2,1)}, u32[]{:S(2)}, u32[]{:S(2)}) %collective-permute-start.27) | collective-permute-done | bytes 327712 | tf_op jit(solution)/shard_map/ppermute | solution.py:734
  131.8 1.7 collective-permute-start.32
  133.9 4.3 %collective-permute-done.28 = bf16[640,128]{1,0:T(8,128)(2,1)S(1)} collective-permute-done((bf16[640,128]{1,0:T(8,128)(2,1)S(1)}, bf16[640,128]{1,0:T(8,128)(2,1)S(1)}, u32[]{:S(2)}, u32[]{:S(2)}) %collective-permute-start.28) | collective-permute-done | bytes 163872 | tf_op jit(solution)/shard_map/ppermute | solution.py:734
  138.9 2.1 %collective-permute-start.35 = (bf16[1280,128]{1,0:T(8,128)(2,1)S(1)}, bf16[1280,128]{1,0:T(8,128)(2,1)S(1)}, u32[]{:S(2)}, u32[]{:S(2)}) collective-permute-start(bf16[1280,128]{1,0:T(8,128)(2,1)S(1)} %slice_bitcast_fusion), channel_id=1, source_target_pairs={{0,2},{2,0},{4,6},{6,4},{8,10},{10,8},{12,14},{14,12},{16,18},{18,... | collective-permute-start | bytes 983048 | tf_op jit(solution)/shard_map/ppermute | solution.py:734
  141.0 11.2 %collective-permute-done.32 = bf16[2,1280,128]{2,1,0:T(8,128)(2,1)S(1)} collective-permute-done((bf16[2,1280,128]{2,1,0:T(8,128)(2,1)S(1)}, bf16[2,1280,128]{2,1,0:T(8,128)(2,1)S(1)}, u32[]{:S(2)}, u32[]{:S(2)}) %collective-permute-start.32) | collective-permute-done | bytes 655392 | tf_op jit(solution)/shard_map/ppermute | solution.py:734
  152.4 1.8 collective-permute-start.33
  154.2 5.7 %collective-permute-done.25 = bf16[2,1280,128]{2,1,0:T(8,128)(2,1)S(1)} collective-permute-done((bf16[2,1280,128]{2,1,0:T(8,128)(2,1)S(1)}, bf16[2,1280,128]{2,1,0:T(8,128)(2,1)S(1)}, u32[]{:S(2)}, u32[]{:S(2)}) %collective-permute-start.25) | collective-permute-done | bytes 655392 | tf_op jit(solution)/shard_map/ppermute | solution.py:734
  161.6 1.8 collective-permute-done.35
  165.0 2.4 %collective-permute-done.26 = bf16[1280,128]{1,0:T(8,128)(2,1)} collective-permute-done((bf16[1280,128]{1,0:T(8,128)(2,1)S(1)}, bf16[1280,128]{1,0:T(8,128)(2,1)}, u32[]{:S(2)}, u32[]{:S(2)}) %collective-permute-start.26) | collective-permute-done | bytes 327712 | tf_op jit(solution)/shard_map/ppermute | solution.py:734
  169.1 2.4 %collective-permute-start.30 = (bf16[480,128]{1,0:T(8,128)(2,1)S(1)}, bf16[480,128]{1,0:T(8,128)(2,1)S(1)}, u32[]{:S(2)}, u32[]{:S(2)}) collective-permute-start(bf16[480,128]{1,0:T(8,128)(2,1)S(1)} %get-tuple-element.78), channel_id=1, source_target_pairs={{0,16},{2,18},{4,20},{6,22},{8,24},{10,26},{12,28},{14,30},{16,0},... | collective-permute-start | bytes 368648 | tf_op jit(solution)/shard_map/ppermute | solution.py:734
  172.9 4.0 %fusion.13 = (bf16[1,640,128]{2,0,1:T(2,128)(2,1)S(1)}, f32[1,640,128]{2,0,1:T(1,128)S(1)}, bf16[1,640,128]{2,0,1:T(2,128)(2,1)S(1)}, bf16[1,640,128]{2,0,1:T(2,128)(2,1)S(1)}) fusion(bf16[4,320,128]{2,0,1:T(4,128)(2,1)S(1)} %bitcast.155, bf16[4,320,128]{2,0,1:T(4,128)(2,1)S(1)} %bitcast.154), kind=kLoop, calls=%fused_computation.41 | loop fusion | flops 1310720 | bytes 1474560 | tf_op jit(solution)/shard_map/concatenate | solution.py:942
  177.1 3.0 %collective-permute-start.37 = (bf16[640,128]{1,0:T(8,128)(2,1)S(1)}, bf16[640,128]{1,0:T(8,128)(2,1)S(1)}, u32[]{:S(2)}, u32[]{:S(2)}) collective-permute-start(bf16[640,128]{1,0:T(8,128)(2,1)S(1)} %bitcast.170), channel_id=1, source_target_pairs={{0,16},{2,18},{4,20},{6,22},{8,24},{10,26},{12,28},{14,30},{16,0},... | collective-permute-start | bytes 491528 | tf_op jit(solution)/shard_map/ppermute | solution.py:734
  185.2 2.2 %collective-permute-done.38 = bf16[640,128]{1,0:T(8,128)(2,1)S(1)} collective-permute-done((bf16[640,128]{1,0:T(8,128)(2,1)S(1)}, bf16[640,128]{1,0:T(8,128)(2,1)S(1)}, u32[]{:S(2)}, u32[]{:S(2)}) %collective-permute-start.38) | collective-permute-done | bytes 163872 | tf_op jit(solution)/shard_map/ppermute | solution.py:734
  (239 shorter events, 56.9 us)
Async XLA Ops:
  0.6 7.8 %collective-permute-start = (bf16[1536]{0:T(1024)(128)(2,1)}, bf16[1536]{0:T(1024)(128)(2,1)S(1)}, u32[]{:S(2)}, u32[]{:S(2)}) collective-permute-start(bf16[1536]{0:T(1024)(128)(2,1)} %param.28), channel_id=1, source_target_pairs={{0,1},{1,0},{2,3},{3,2},{4,5},{5,4},{6,7},{7,6},{8,9},{9,8},{10,11... | collective-permute-start | bytes 9224 | tf_op jit(solution)/shard_map/ppermute | solution.py:731
  1.2 7.4 %collective-permute-start.6 = (bf16[320,256]{1,0:T(8,128)(2,1)}, bf16[320,256]{1,0:T(8,128)(2,1)S(1)}, u32[]{:S(2)}, u32[]{:S(2)}) collective-permute-start(bf16[320,256]{1,0:T(8,128)(2,1)} %refs_19_.1), channel_id=1, source_target_pairs={{0,1},{1,0},{2,3},{3,2},{4,5},{5,4},{6,7},{7,6},{8,9},{9,8},{10,11... | collective-permute-start | bytes 491528 | tf_op jit(solution)/shard_map/ppermute | solution.py:731
  2.9 12.4 %collective-permute-start.1 = (bf16[128,768]{1,0:T(8,128)(2,1)S(1)}, bf16[128,768]{1,0:T(8,128)(2,1)S(1)}, u32[]{:S(2)}, u32[]{:S(2)}) collective-permute-start(bf16[128,768]{1,0:T(8,128)(2,1)S(1)} %pad_maximum_fusion.2.refs_4_.tok), channel_id=1, source_target_pairs={{0,8},{2,10},{4,12},{6,14},{8,16},{10,18},{12,20},{14,22},{16,24},... | collective-permute-start | bytes 589832 | tf_op jit(solution)/shard_map/ppermute | solution.py:23
  7.9 32.0 %collective-permute-start.10 = (bf16[320,2048]{1,0:T(8,128)(2,1)}, bf16[320,2048]{1,0:T(8,128)(2,1)S(1)}, u32[]{:S(2)}, u32[]{:S(2)}) collective-permute-start(bf16[320,2048]{1,0:T(8,128)(2,1)} %wu_a.1), channel_id=1, source_target_pairs={{0,1},{1,0},{2,3},{3,2},{4,5},{5,4},{6,7},{7,6},{8,9},{9,8},{10,11... | collective-permute-start | bytes 3932168 | tf_op jit(solution)/shard_map/ppermute | solution.py:731
  8.4 32.5 %collective-permute-start.11 = (bf16[1024,640]{1,0:T(8,128)(2,1)}, bf16[1024,640]{1,0:T(8,128)(2,1)}, u32[]{:S(2)}, u32[]{:S(2)}) collective-permute-start(bf16[1024,640]{1,0:T(8,128)(2,1)} %wd_a.1), channel_id=1, source_target_pairs={{0,1},{1,0},{2,3},{3,2},{4,5},{5,4},{6,7},{7,6},{8,9},{9,8},{10,11... | collective-permute-start | bytes 3932168 | tf_op jit(solution)/shard_map/ppermute | solution.py:731
  9.2 31.8 %collective-permute-start.9 = (bf16[320,2048]{1,0:T(8,128)(2,1)}, bf16[320,2048]{1,0:T(8,128)(2,1)}, u32[]{:S(2)}, u32[]{:S(2)}) collective-permute-start(bf16[320,2048]{1,0:T(8,128)(2,1)} %wg_a.1), channel_id=1, source_target_pairs={{0,1},{1,0},{2,3},{3,2},{4,5},{5,4},{6,7},{7,6},{8,9},{9,8},{10,11... | collective-permute-start | bytes 3932168 | tf_op jit(solution)/shard_map/ppermute | solution.py:731
  11.0 8.9 %collective-permute-start.2 = (bf16[128,768]{1,0:T(8,128)(2,1)S(1)}, bf16[128,768]{1,0:T(8,128)(2,1)S(1)}, u32[]{:S(2)}, u32[]{:S(2)}) collective-permute-start(bf16[128,768]{1,0:T(8,128)(2,1)S(1)} %pad_maximum_fusion.2.refs_4_.tok), channel_id=1, source_target_pairs={{0,6},{2,8},{4,10},{6,12},{8,14},{10,16},{12,18},{14,20},{16,22},{... | collective-permute-start | bytes 589832 | tf_op jit(solution)/shard_map/ppermute | solution.py:23
  15.4 7.5 %collective-permute-start.3 = (bf16[128,768]{1,0:T(8,128)(2,1)S(1)}, bf16[128,768]{1,0:T(8,128)(2,1)S(1)}, u32[]{:S(2)}, u32[]{:S(2)}) collective-permute-start(bf16[128,768]{1,0:T(8,128)(2,1)S(1)} %pad_maximum_fusion.2.refs_4_.tok), channel_id=1, source_target_pairs={{0,4},{2,6},{4,8},{6,10},{8,12},{10,14},{12,16},{14,18},{16,20},{1... | collective-permute-start | bytes 589832 | tf_op jit(solution)/shard_map/ppermute | solution.py:23
  26.2 13.7 %collective-permute-start.8 = (bf16[512,640]{1,0:T(8,128)(2,1)}, bf16[512,640]{1,0:T(8,128)(2,1)}, u32[]{:S(2)}, u32[]{:S(2)}) collective-permute-start(bf16[512,640]{1,0:T(8,128)(2,1)} %wo_a.1), channel_id=1, source_target_pairs={{0,1},{1,0},{2,3},{3,2},{4,5},{5,4},{6,7},{7,6},{8,9},{9,8},{10,11... | collective-permute-start | bytes 1966088 | tf_op jit(solution)/shard_map/ppermute | solution.py:731
  65.5 16.7 %collective-permute-start.16 = (bf16[4,976,128]{2,1,0:T(8,128)(2,1)}, bf16[4,976,128]{2,1,0:T(8,128)(2,1)S(1)}, u32[]{:S(2)}, u32[]{:S(2)}) collective-permute-start(bf16[4,976,128]{2,1,0:T(8,128)(2,1)} %get-tuple-element.88), channel_id=1, source_target_pairs={{0,1},{1,0},{2,3},{3,2},{4,5},{5,4},{6,7},{7,6},{8,9},{9,8},{10,11... | collective-permute-start | bytes 2998280 | tf_op jit(solution)/shard_map/ppermute | solution.py:731
  66.0 13.1 %collective-permute-start.12 = (bf16[128,640]{1,0:T(8,128)(2,1)S(1)}, bf16[128,640]{1,0:T(8,128)(2,1)S(1)}, u32[]{:S(2)}, u32[]{:S(2)}) collective-permute-start(bf16[128,640]{1,0:T(8,128)(2,1)S(1)} %get-tuple-element.72), channel_id=1, source_target_pairs={{8,0},{10,2},{12,4},{14,6},{16,8},{18,10},{20,12},{22,14},{24,16},... | collective-permute-start | bytes 491528 | tf_op jit(solution)/shard_map/ppermute | solution.py:23
  67.3 11.8 %collective-permute-start.13 = (bf16[128,640]{1,0:T(8,128)(2,1)S(1)}, bf16[128,640]{1,0:T(8,128)(2,1)S(1)}, u32[]{:S(2)}, u32[]{:S(2)}) collective-permute-start(bf16[128,640]{1,0:T(8,128)(2,1)S(1)} %get-tuple-element.75), channel_id=1, source_target_pairs={{6,0},{8,2},{10,4},{12,6},{14,8},{16,10},{18,12},{20,14},{22,16},{... | collective-permute-start | bytes 491528 | tf_op jit(solution)/shard_map/ppermute | solution.py:23
  68.6 13.3 %collective-permute-start.14 = (bf16[128,640]{1,0:T(8,128)(2,1)S(1)}, bf16[128,640]{1,0:T(8,128)(2,1)S(1)}, u32[]{:S(2)}, u32[]{:S(2)}) collective-permute-start(bf16[128,640]{1,0:T(8,128)(2,1)S(1)} %get-tuple-element.74), channel_id=1, source_target_pairs={{4,0},{6,2},{8,4},{10,6},{12,8},{14,10},{16,12},{18,14},{20,16},{2... | collective-permute-start | bytes 491528 | tf_op jit(solution)/shard_map/ppermute | solution.py:23
  69.9 12.0 %collective-permute-start.15 = (bf16[128,640]{1,0:T(8,128)(2,1)S(1)}, bf16[128,640]{1,0:T(8,128)(2,1)S(1)}, u32[]{:S(2)}, u32[]{:S(2)}) collective-permute-start(bf16[128,640]{1,0:T(8,128)(2,1)S(1)} %get-tuple-element.73), channel_id=1, source_target_pairs={{2,0},{4,2},{6,4},{8,6},{10,8},{12,10},{14,12},{16,14},{18,16},{20... | collective-permute-start | bytes 491528 | tf_op jit(solution)/shard_map/ppermute | solution.py:23
  79.2 32.0 %collective-permute-start.24 = (bf16[7232,128]{1,0:T(8,128)(2,1)}, bf16[7232,128]{1,0:T(8,128)(2,1)}, u32[]{:S(2)}, u32[]{:S(2)}) collective-permute-start(bf16[7232,128]{1,0:T(8,128)(2,1)} %copy-done.10), channel_id=1, source_target_pairs={{0,1},{1,0},{2,3},{3,2},{4,5},{5,4},{6,7},{7,6},{8,9},{9,8},{10,11... | collective-permute-start | bytes 5554184 | tf_op jit(solution)/shard_map/ppermute | solution.py:731
  82.5 11.9 %collective-permute-start.17 = (bf16[2,480,128]{2,1,0:T(8,128)(2,1)S(1)}, bf16[2,480,128]{2,1,0:T(8,128)(2,1)S(1)}, u32[]{:S(2)}, u32[]{:S(2)}) collective-permute-start(bf16[2,480,128]{2,1,0:T(8,128)(2,1)S(1)} %slice.143), channel_id=1, source_target_pairs={{0,2},{2,0},{4,6},{6,4},{8,10},{10,8},{12,14},{14,12},{16,18},{18,... | collective-permute-start | bytes 737288 | tf_op jit(solution)/shard_map/ppermute | solution.py:734
  87.7 13.1 %collective-permute-start.19 = (bf16[2,496,128]{2,1,0:T(8,128)(2,1)S(1)}, bf16[2,496,128]{2,1,0:T(8,128)(2,1)S(1)}, u32[]{:S(2)}, u32[]{:S(2)}) collective-permute-start(bf16[2,496,128]{2,1,0:T(8,128)(2,1)S(1)} %slice.186), channel_id=1, source_target_pairs={{0,4},{2,6},{4,0},{6,2},{8,12},{10,14},{12,8},{14,10},{16,20},{18,... | collective-permute-start | bytes 761864 | tf_op jit(solution)/shard_map/ppermute | solution.py:734
  94.5 7.9 %collective-permute-start.18 = (bf16[480,128]{1,0:T(8,128)(2,1)S(1)}, bf16[480,128]{1,0:T(8,128)(2,1)S(1)}, u32[]{:S(2)}, u32[]{:S(2)}) collective-permute-start(bf16[480,128]{1,0:T(8,128)(2,1)S(1)} %slice_bitcast_fusion.14), channel_id=1, source_target_pairs={{0,4},{2,6},{4,0},{6,2},{8,12},{10,14},{12,8},{14,10},{16,20},{18,... | collective-permute-start | bytes 368648 | tf_op jit(solution)/shard_map/ppermute | solution.py:734
  106.6 14.1 %collective-permute-start.21 = (bf16[241,128]{1,0:T(8,128)(2,1)S(1)}, bf16[241,128]{1,0:T(8,128)(2,1)S(1)}, u32[]{:S(2)}, u32[]{:S(2)}) collective-permute-start(bf16[241,128]{1,0:T(8,128)(2,1)S(1)} %bitcast.175), channel_id=1, source_target_pairs={{0,8},{2,10},{4,12},{6,14},{8,0},{10,2},{12,4},{14,6},{16,24},{18,... | collective-permute-start | bytes 185096 | tf_op jit(solution)/shard_map/ppermute | solution.py:734
  108.4 12.2 %collective-permute-start.22 = (bf16[241,128]{1,0:T(8,128)(2,1)S(1)}, bf16[241,128]{1,0:T(8,128)(2,1)S(1)}, u32[]{:S(2)}, u32[]{:S(2)}) collective-permute-start(bf16[241,128]{1,0:T(8,128)(2,1)S(1)} %bitcast.176), channel_id=1, source_target_pairs={{0,16},{2,18},{4,20},{6,22},{8,24},{10,26},{12,28},{14,30},{16,0},... | collective-permute-start | bytes 185096 | tf_op jit(solution)/shard_map/ppermute | solution.py:734
  109.5 11.2 %collective-permute-start.23 = (bf16[241,128]{1,0:T(8,128)(2,1)S(1)}, bf16[241,128]{1,0:T(8,128)(2,1)S(1)}, u32[]{:S(2)}, u32[]{:S(2)}) collective-permute-start(bf16[241,128]{1,0:T(8,128)(2,1)S(1)} %bitcast.177), channel_id=1, source_target_pairs={{0,24},{2,26},{4,28},{6,30},{8,16},{10,18},{12,20},{14,22},{16,8},... | collective-permute-start | bytes 185096 | tf_op jit(solution)/shard_map/ppermute | solution.py:734
  118.9 11.0 %collective-permute-start.27 = (bf16[2,640,128]{2,1,0:T(8,128)(2,1)}, bf16[2,640,128]{2,1,0:T(8,128)(2,1)}, u32[]{:S(2)}, u32[]{:S(2)}) collective-permute-start(bf16[2,640,128]{2,1,0:T(8,128)(2,1)} %get-tuple-element.59), channel_id=1, source_target_pairs={{0,4},{2,6},{4,0},{6,2},{8,12},{10,14},{12,8},{14,10},{16,20},{18,... | collective-permute-start | bytes 983048 | tf_op jit(solution)/shard_map/ppermute | solution.py:734
  122.6 16.0 %collective-permute-start.34 = (bf16[2,1280,128]{2,1,0:T(8,128)(2,1)}, bf16[2,1280,128]{2,1,0:T(8,128)(2,1)S(1)}, u32[]{:S(2)}, u32[]{:S(2)}) collective-permute-start(bf16[2,1280,128]{2,1,0:T(8,128)(2,1)} %copy-done.24), channel_id=1, source_target_pairs={{0,4},{2,6},{4,0},{6,2},{8,12},{10,14},{12,8},{14,10},{16,20},{18,... | collective-permute-start | bytes 1966088 | tf_op jit(solution)/shard_map/ppermute | solution.py:734
  131.8 20.4 %collective-permute-start.32 = (bf16[2,1280,128]{2,1,0:T(8,128)(2,1)S(1)}, bf16[2,1280,128]{2,1,0:T(8,128)(2,1)S(1)}, u32[]{:S(2)}, u32[]{:S(2)}) collective-permute-start(bf16[2,1280,128]{2,1,0:T(8,128)(2,1)S(1)} %copy-done.23), channel_id=1, source_target_pairs={{0,2},{2,0},{4,6},{6,4},{8,10},{10,8},{12,14},{14,12},{16,18},{18,... | collective-permute-start | bytes 1966088 | tf_op jit(solution)/shard_map/ppermute | solution.py:734
  133.5 26.4 %collective-permute-start.25 = (bf16[2,1280,128]{2,1,0:T(8,128)(2,1)S(1)}, bf16[2,1280,128]{2,1,0:T(8,128)(2,1)S(1)}, u32[]{:S(2)}, u32[]{:S(2)}) collective-permute-start(bf16[2,1280,128]{2,1,0:T(8,128)(2,1)S(1)} %copy-done.21), channel_id=1, source_target_pairs={{0,2},{2,0},{4,6},{6,4},{8,10},{10,8},{12,14},{14,12},{16,18},{18,... | collective-permute-start | bytes 1966088 | tf_op jit(solution)/shard_map/ppermute | solution.py:734
  138.9 24.5 %collective-permute-start.35 = (bf16[1280,128]{1,0:T(8,128)(2,1)S(1)}, bf16[1280,128]{1,0:T(8,128)(2,1)S(1)}, u32[]{:S(2)}, u32[]{:S(2)}) collective-permute-start(bf16[1280,128]{1,0:T(8,128)(2,1)S(1)} %slice_bitcast_fusion), channel_id=1, source_target_pairs={{0,2},{2,0},{4,6},{6,4},{8,10},{10,8},{12,14},{14,12},{16,18},{18,... | collective-permute-start | bytes 983048 | tf_op jit(solution)/shard_map/ppermute | solution.py:734
  152.4 11.3 %collective-permute-start.33 = (bf16[1280,128]{1,0:T(8,128)(2,1)S(1)}, bf16[1280,128]{1,0:T(8,128)(2,1)}, u32[]{:S(2)}, u32[]{:S(2)}) collective-permute-start(bf16[1280,128]{1,0:T(8,128)(2,1)S(1)} %slice_bitcast_fusion.2), channel_id=1, source_target_pairs={{0,4},{2,6},{4,0},{6,2},{8,12},{10,14},{12,8},{14,10},{16,20},{18,... | collective-permute-start | bytes 983048 | tf_op jit(solution)/shard_map/ppermute | solution.py:734
  168.5 11.6 %collective-permute-start.29 = (bf16[480,128]{1,0:T(8,128)(2,1)S(1)}, bf16[480,128]{1,0:T(8,128)(2,1)S(1)}, u32[]{:S(2)}, u32[]{:S(2)}) collective-permute-start(bf16[480,128]{1,0:T(8,128)(2,1)S(1)} %get-tuple-element.76), channel_id=1, source_target_pairs={{0,8},{2,10},{4,12},{6,14},{8,0},{10,2},{12,4},{14,6},{16,24},{18,... | collective-permute-start | bytes 368648 | tf_op jit(solution)/shard_map/ppermute | solution.py:734
  169.1 12.5 %collective-permute-start.30 = (bf16[480,128]{1,0:T(8,128)(2,1)S(1)}, bf16[480,128]{1,0:T(8,128)(2,1)S(1)}, u32[]{:S(2)}, u32[]{:S(2)}) collective-permute-start(bf16[480,128]{1,0:T(8,128)(2,1)S(1)} %get-tuple-element.78), channel_id=1, source_target_pairs={{0,16},{2,18},{4,20},{6,22},{8,24},{10,26},{12,28},{14,30},{16,0},... | collective-permute-start | bytes 368648 | tf_op jit(solution)/shard_map/ppermute | solution.py:734
  171.5 10.2 %collective-permute-start.31 = (bf16[480,128]{1,0:T(8,128)(2,1)S(1)}, bf16[480,128]{1,0:T(8,128)(2,1)S(1)}, u32[]{:S(2)}, u32[]{:S(2)}) collective-permute-start(bf16[480,128]{1,0:T(8,128)(2,1)S(1)} %get-tuple-element.77), channel_id=1, source_target_pairs={{0,24},{2,26},{4,28},{6,30},{8,16},{10,18},{12,20},{14,22},{16,8},... | collective-permute-start | bytes 368648 | tf_op jit(solution)/shard_map/ppermute | solution.py:734
  177.1 8.1 %collective-permute-start.37 = (bf16[640,128]{1,0:T(8,128)(2,1)S(1)}, bf16[640,128]{1,0:T(8,128)(2,1)S(1)}, u32[]{:S(2)}, u32[]{:S(2)}) collective-permute-start(bf16[640,128]{1,0:T(8,128)(2,1)S(1)} %bitcast.170), channel_id=1, source_target_pairs={{0,16},{2,18},{4,20},{6,22},{8,24},{10,26},{12,28},{14,30},{16,0},... | collective-permute-start | bytes 491528 | tf_op jit(solution)/shard_map/ppermute | solution.py:734
  180.1 7.3 %collective-permute-start.38 = (bf16[640,128]{1,0:T(8,128)(2,1)S(1)}, bf16[640,128]{1,0:T(8,128)(2,1)S(1)}, u32[]{:S(2)}, u32[]{:S(2)}) collective-permute-start(bf16[640,128]{1,0:T(8,128)(2,1)S(1)} %bitcast.171), channel_id=1, source_target_pairs={{0,24},{2,26},{4,28},{6,30},{8,16},{10,18},{12,20},{14,22},{16,8},... | collective-permute-start | bytes 491528 | tf_op jit(solution)/shard_map/ppermute | solution.py:734
  (58 other events, 463.3 us)

commit v2 on v1

--- a/solution.py
+++ b/solution.py
@@ -12,6 +12,7 @@
 WINDOW = 512
 EPS = 1e-06
 LANES = 128
+SEG_ROWS = 16
 F32 = jnp.float32
 BF16 = jnp.bfloat16
 MIB = 1 << 20
@@ -226,14 +227,6 @@
 LINE = 4
 
 
-def vmem(count):
-    return [pl.BlockSpec(memory_space=pltpu.VMEM)] * count
-
-
-def anywhere(count):
-    return [pl.BlockSpec(memory_space=pl.ANY)] * count
-
-
 def mm(a, b):
     return lax.dot_general(a, b, (((1,), (0,)), ((), ())), preferred_element_type=F32)
 
@@ -267,62 +260,123 @@
     return jnp.concatenate([a * cosine + b * sine, b * cosine - a * sine], axis=1)
 
 
-def assemble(core, pairs, sems):
-    copies = []
-    for n, (mine, theirs, full) in enumerate(pairs):
+def all_gains(core, mine, theirs):
+    a = mine[...].astype(F32)
+    b = theirs[...].astype(F32)[: a.shape[0]]
+    low, high = jnp.where(core == 0, a, b), jnp.where(core == 0, b, a)
+    rows = [half[r : r + 1, :] for half in (low, high) for r in range(a.shape[0])]
+    return jnp.concatenate(rows, axis=1)
+
+
+def row_order(table, place, core):
+    width = table.shape[0]
+    owner = table[:, :1] ^ (place * 2 + core)
+    source = owner * (width // (2 * XY * LINE)) + table[:, 1:2]
+    ranks = lax.broadcasted_iota(jnp.int32, (width, width), 1)
+    return jnp.where(ranks == source, 1.0, 0.0).astype(BF16)
+
+
+class Traffic:
+    def __init__(self, sems):
+        self.sems = sems
+        self.used = 0
+        self.pending = []
+
+    def start(self, source, target):
+        copy = pltpu.make_async_copy(source, target, self.sems.at[self.used])
+        self.used += 1
+        copy.start()
+        return copy
+
+    def fetch(self, pairs):
+        return [self.start(source, target) for source, target in pairs]
+
+    def halves(self, core, mine, pack, pieces, full):
         rows = mine.shape[0]
-        for side, (part, at) in enumerate(((mine, core), (theirs, 1 - core))):
-            begin = pl.multiple_of(at * rows, 16)
-            copy = pltpu.make_async_copy(part, full.at[pl.ds(begin, rows)], sems.at[n, side])
-            copy.start()
-            copies.append(copy)
-    return copies
-
-
-def attention_kernel(
-    reach,
-    meta,
-    *refs,
-):
-    halo = refs[: reach + 1]
-    (
-        gains,
-        cos_ref,
-        sin_ref,
-        wq_a,
-        wq_b,
-        wk_a,
-        wk_b,
-        wv_a,
-        wv_b,
-        n1_out,
-        qraw_out,
-        q_out,
-        kraw_out,
-        k_out,
-        v_out,
-        p_out,
-        ao_out,
-        wq,
-        wk,
-        wv,
-        sems,
-    ) = refs[reach + 1 :]
-    rows = halo[0].shape[0]
+        begin = pl.multiple_of(core * rows, 16)
+        copies = [self.start(mine, full.at[pl.ds(begin, rows)])]
+        for row, number, pack_row, column, cols in pieces:
+            begin = pl.multiple_of((1 - core) * rows + row, 16)
+            source = pack.at[pack_row : pack_row + number, column : column + cols]
+            copies.append(self.start(source, full.at[pl.ds(begin, number)]))
+        return copies
+
+    def emit(self, source, target):
+        self.pending.append(self.start(source, target))
+
+    def finish(self):
+        for copy in self.pending:
+            copy.wait()
+
+
+def pack_layout(rows, widths, talls):
+    layout, column = [], 0
+    for width in widths:
+        layout.append([(0, rows, 0, column, width)])
+        column += width
+    at = 0
+    for height, width in talls:
+        pieces, done = [], 0
+        while done < height:
+            take = min(height - done, rows - at % rows)
+            pieces.append((done, take, at % rows, column + at // rows * talls[0][1], width))
+            done, at = done + take, at + take
+        layout.append(pieces)
+    return layout, column + -(-at // rows) * talls[0][1]
+
+
+def prepare_kernel(layout, *refs):
+    count = len(layout)
+    tok_h, seg_h, *weights_h = refs[: count + 2]
+    ext_h, pack_h = refs[count + 2 : count + 4]
+    tok, seg, *weights = refs[count + 4 : 2 * count + 6]
+    ext, gain_s, sems = refs[2 * count + 6 :]
+    traffic = Traffic(sems)
+    first = traffic.fetch([(tok_h, tok), (seg_h, seg)])
+    rest = traffic.fetch(list(zip(weights_h, weights)))
+    wait(first)
+    rows, width = tok.shape
+    ext[:rows, :] = tok[...]
+    ext[rows:, :] = jnp.zeros((SEG_ROWS, width), BF16)
+    ids = seg[...].astype(F32)
+    ext[rows:, :rows] = jnp.broadcast_to(ids, (SEG_ROWS, rows)).astype(BF16)
+    traffic.emit(ext, ext_h)
+    for copy, source, pieces in zip(rest, weights, layout):
+        copy.wait()
+        if source is weights[-1]:
+            missing = gain_s.shape[0] - source.shape[0]
+            filled = [source[...].astype(F32), jnp.zeros((missing, LANES), F32)]
+            gain_s[...] = jnp.concatenate(filled, axis=0).astype(BF16)
+            source = gain_s
+        for row, number, pack_row, column, cols in pieces:
+            traffic.emit(
+                source.at[row : row + number, :],
+                pack_h.at[pack_row : pack_row + number, column : column + cols],
+            )
+    traffic.finish()
+
+
+def wait(copies):
+    for copy in copies:
+        copy.wait()
+
+
+def attention(reach, place, halo, gains, cos_ref, sin_ref, wq, wk, wv, outs, ready):
+    n1_out, qraw_out, q_out, kraw_out, k_out, v_out, p_out, ao_out = outs
     width = n1_out.shape[1]
+    rows = halo[0].shape[0] - SEG_ROWS
     size = k_out.shape[1]
     heads = q_out.shape[1] // size
     scale = size ** (-0.5)
-    place, core = meta[0], meta[1]
-    copies = assemble(core, ((wk_a, wk_b, wk), (wv_a, wv_b, wv), (wq_a, wq_b, wq)), sems)
+    ready("halo")
+    gains = gains()
     g_in = gains[:, :width]
     g_q = gains[:, width : width + size]
     g_k = gains[:, width + size : width + 2 * size]
     for block in range(reach + 1):
-        x = halo[block][:, :width].astype(F32)
+        x = halo[block][:rows, :].astype(F32)
         n1_out[block * rows : (block + 1) * rows, :] = (x * inverse_rms(x) * g_in).astype(BF16)
-    for copy in copies[:4]:
-        copy.wait()
+    ready("kv")
     n1 = n1_out[...]
     kraw = mm(n1, wk[...])
     kraw_out[...] = kraw
@@ -330,13 +384,13 @@
     k_out[...] = k
     v = mm(n1, wv[...]).astype(BF16)
     v_out[...] = v
-    for copy in copies[4:]:
-        copy.wait()
     keys = (reach + 1) * rows
-    lane = lax.broadcasted_iota(jnp.int32, (rows, LANES), 1)
-    pick = jnp.where(lane == 0, 1.0, 0.0).astype(BF16)
-    seg_keys = jnp.concatenate([mm_nt(pick, halo[b][:, width:]) for b in range(reach + 1)], axis=1)
-    seg_own = halo[reach][:, width : width + 1].astype(F32)
+    seg_rows = [halo[b][rows:, :rows].astype(F32)[:1] for b in range(reach + 1)]
+    seg_keys = jnp.concatenate(seg_rows, axis=1)
+    square = lax.broadcasted_iota(jnp.int32, (rows, rows), 0) == lax.broadcasted_iota(
+        jnp.int32, (rows, rows), 1
+    )
+    seg_own = jnp.sum(jnp.where(square, seg_rows[reach], 0.0), axis=1, keepdims=True)
     at_query = reach * rows + lax.broadcasted_iota(jnp.int32, (rows, keys), 0)
     at_key = lax.broadcasted_iota(jnp.int32, (rows, keys), 1)
     gap = at_query - at_key
@@ -347,6 +401,7 @@
         & (at_key >= (reach - place) * rows)
     )
     cos_own, sin_own = cos_ref[reach * rows :, :], sin_ref[reach * rows :, :]
+    ready("query")
     for h in range(heads):
         cols = slice(h * size, (h + 1) * size)
         qraw = mm(n1_out[reach * rows :, :], wq[:, cols])
@@ -375,53 +430,62 @@
     return base + rows * (value.shape[1] // LANES)
 
 
-def feed_kernel(
-    meta,
-    tok,
-    ct,
-    gains,
-    order,
-    ao_ref,
-    wo_a,
-    wo_b,
-    wg_a,
-    wg_b,
-    wu_a,
-    wu_b,
-    wd_a,
-    wd_b,
-    mixed_out,
-    dx_out,
-    dao_out,
-    dg_out,
-    keep,
-    send,
-    wo,
-    wg,
-    wu,
-    wd,
-    gate_s,
-    up_s,
-    hid_s,
-    dg_s,
-    du_s,
-    sems,
-):
-    core = meta[1]
+def forward_kernel(reach, layout, *refs):
+    halo_h, refs = refs[: reach + 1], refs[reach + 1 :]
+    ct_h, gains_h, order_h, cos_h, sin_h = refs[:5]
+    wq_a, wk_a, wv_a, wg_a, wu_a, wo_a, wd_a, pack_h = refs[5:13]
+    outs_h, refs = refs[13:27], refs[27:]
+    halo, refs = refs[: reach + 1], refs[reach + 1 :]
+    ct, gain_a, order, cos_ref, sin_ref = refs[:5]
+    outs, refs = refs[5:19], refs[19:]
+    wq, wk, wv, wo, wg, wu, wd, gate_s, up_s, hid_s, dg_s, du_s, ao_ref, gain_b, sems = refs
+    place, core = lax.axis_index("seq"), lax.axis_index("fsdp")
+    traffic = Traffic(sems)
+    waits = {}
+    _, _, pack_row, column, cols = layout[7][0]
+    gain_far = pack_h.at[pack_row : pack_row + 16, column : column + cols]
+    waits["halo"] = traffic.fetch(list(zip(halo_h, halo)))
+    waits["halo"] += traffic.fetch([(gains_h, gain_a), (gain_far, gain_b)])
+    waits["kv"] = traffic.halves(core, wk_a, pack_h, layout[1], wk)
+    waits["kv"] += traffic.halves(core, wv_a, pack_h, layout[2], wv)
+    waits["kv"] += traffic.fetch([(cos_h, cos_ref), (sin_h, sin_ref)])
+    waits["query"] = traffic.halves(core, wq_a, pack_h, layout[0], wq)
+    waits["out"] = traffic.halves(core, wo_a, pack_h, layout[5], wo)
+    waits["gate"] = traffic.halves(core, wg_a, pack_h, layout[3], wg)
+    waits["gate"] += traffic.halves(core, wu_a, pack_h, layout[4], wu)
+    waits["down"] = traffic.halves(core, wd_a, pack_h, layout[6], wd)
+    waits["rest"] = traffic.fetch([(ct_h, ct), (order_h, order)])
+
+    def ready(name):
+        wait(waits[name])
+
+    attention(
+        reach,
+        place,
+        halo,
+        lambda: all_gains(core, gain_a, gain_b),
+        cos_ref,
+        sin_ref,
+        wq,
+        wk,
+        wv,
+        (*outs[:7], ao_ref),
+        ready,
+    )
+    for source, target in zip(outs[:7], outs_h[:7]):
+        traffic.emit(source, target)
+    mixed_out, dx_out, dao_out, dg_out, keep, send, gains_out = outs[7:]
     rows, width = ct.shape
+    gains = all_gains(core, gain_a, gain_b)
+    gains_out[...] = gains
     size2 = gains.shape[1] - 4 * width
     ff = wg.shape[1]
-    copies = assemble(
-        core, ((wo_a, wo_b, wo), (wg_a, wg_b, wg), (wu_a, wu_b, wu), (wd_a, wd_b, wd)), sems
-    )
     base = width + size2
     g_pa = gains[:, base : base + width]
     g_pf = gains[:, base + width : base + 2 * width]
     g_pff = gains[:, base + 2 * width :]
-    x = tok[:, :width].astype(F32)
-    c = ct[...].astype(F32)
-    for copy in copies[:2]:
-        copy.wait()
+    x = halo[reach][:rows, :].astype(F32)
+    ready("out")
     ya = mm(ao_ref[...], wo[...])
     inv_a = inverse_rms(ya)
     hat_a = ya * inv_a
@@ -429,8 +493,10 @@
     inv_f = inverse_rms(x2)
     hat_f = x2 * inv_f
     n2 = (hat_f * g_pf).astype(BF16)
-    for copy in copies[2:]:
-        copy.wait()
+    ready("gate")
+    ready("down")
+    ready("rest")
+    c = ct[...].astype(F32)
     part = 512
     root = math.sqrt(2.0 / math.pi)
     f = jnp.zeros((rows, width), F32)
@@ -471,8 +537,7 @@
     dg_out[:, :width] = jnp.sum(dx2 * hat_a, axis=0, keepdims=True)
     dg_out[:, width : 2 * width] = jnp.sum(dn2 * hat_f, axis=0, keepdims=True)
     dg_out[:, 2 * width :] = jnp.sum(c * hat_d, axis=0, keepdims=True)
-    ranks = lax.broadcasted_iota(jnp.int32, (width, width), 1)
-    perm = jnp.where(ranks == order[...], 1.0, 0.0).astype(BF16)
+    perm = row_order(order, place, core)
     n2_t = mm_nt(perm, n2).astype(BF16)
     half = width // 2
     keep[:half, :] = n2_t[:half]
@@ -490,6 +555,9 @@
         base = store_lanes(ref, base, du_s[...])
         base = store_lanes(ref, base, df)
         store_lanes(ref, base, dya)
+    for source, target in zip(outs[7:], outs_h[7:]):
+        traffic.emit(source, target)
+    traffic.finish()
 
 
 def load_lanes(ref, base, rows, cols):
@@ -504,24 +572,38 @@
     ref[other, at : at + value.shape[0], :] = value
 
 
-def grads_kernel(
-    meta, width, ff, attn, mine, recv, gk, gs, uk, us, dk, ds, ok, os, left_s, right_s, prod_s
-):
-    place = meta[0]
+def grads_kernel(width, ff, attn, *refs):
+    sources = refs[:2]
+    outs_h = refs[2:8]
+    outs = refs[8:14]
+    gk, gs, uk, us, dk, ds = outs
+    n2_s, hid_s, ao_s, gate_s, up_s, df_s, dya_s, prod_s, sems = refs[14:]
+    traffic = Traffic(sems)
+    place = lax.axis_index("seq")
     half = width // 2
     rows = LANES
 
-    def both(base, count):
-        left_s[:count, :rows] = mine[base : base + count, :]
-        left_s[:count, rows:] = recv[base : base + count, :]
-        return left_s[:count, :]
-
-    def right(base, cols):
-        for side, ref in enumerate((mine, recv)):
-            for b in range(cols // LANES):
-                right_s[side * rows : (side + 1) * rows, b * LANES : (b + 1) * LANES] = ref[
-                    base + b * rows : base + (b + 1) * rows, :
-                ]
+    def sent(ref):
+        traffic.emit(ref, outs_h[[r is ref for r in outs].index(True)])
+
+    def lefts(base, target):
+        return [
+            traffic.start(
+                source.at[base : base + target.shape[0], :],
+                target.at[:, side * rows : (side + 1) * rows],
+            )
+            for side, source in enumerate(sources)
+        ]
+
+    def rights(base, target):
+        return [
+            traffic.start(
+                source.at[base + b * rows : base + (b + 1) * rows, :],
+                target.at[side * rows : (side + 1) * rows, b * LANES : (b + 1) * LANES],
+            )
+            for side, source in enumerate(sources)
+            for b in range(target.shape[1] // LANES)
+        ]
 
     at_hid = half
     at_ao = at_hid + ff // 2
@@ -530,11 +612,17 @@
     at_df = at_up + ff
     at_dya = at_df + width
     per = half // XY
-    n2 = both(0, half)
-    for base, (keep, send), first in ((at_gate, (gk, gs), "x"), (at_up, (uk, us), "y")):
-        right(base, ff)
+    gate_w = lefts(0, n2_s) + rights(at_gate, gate_s)
+    up_w = rights(at_up, up_s)
+    down_w = lefts(at_hid, hid_s) + rights(at_df, df_s)
+    out_w = lefts(at_ao, ao_s) + rights(at_dya, dya_s)
+    for copies, right, (keep, send), first in (
+        (gate_w, gate_s, (gk, gs), "x"),
+        (up_w, up_s, (uk, us), "y"),
+    ):
+        wait(copies)
         for col in range(0, ff, 512):
-            out = mm(n2, right_s[:, col : col + 512]).astype(BF16)
+            out = mm(n2_s[...], right[:, col : col + 512]).astype(BF16)
             for plane in range(XY):
                 for b in range(4):
                     put(
@@ -545,38 +633,42 @@
                         (col // LANES + b) * per,
                         out[plane * per : (plane + 1) * per, b * LANES : (b + 1) * LANES],
                     )
-    for base, at_left, count, (keep, send), first in (
-        (at_df, at_hid, ff // 2, (dk, ds), "x"),
-        (at_dya, at_ao, attn // 2, (ok, os), "y"),
-    ):
-        left = both(at_left, count)
-        right(base, width)
-        prod_s[:count, :] = mm(left, right_s[:, :width])
+        sent(send)
+        sent(keep)
+    row = 0
+    for copies, left, right in ((down_w, hid_s, df_s), (out_w, ao_s, dya_s)):
+        wait(copies)
+        count = left.shape[0]
+        prod_s[:count, :] = mm(left[...], right[...])
         unit = count // (XY * LINE)
         for plane in range(XY):
             for line in range(LINE):
                 whose = (place ^ (line * XY + plane)) * unit
                 block = prod_s[pl.ds(pl.multiple_of(whose, unit), unit), :].astype(BF16)
+                ref = ds if line & 1 else dk
+                chunk = (plane & 1) * 4 + (plane >> 1) * 2 + (line >> 1)
                 for b in range(width // LANES):
-                    put(
-                        keep,
-                        send,
-                        first,
-                        plane,
-                        b * unit * LINE + line * unit,
-                        block[:, b * LANES : (b + 1) * LANES],
-                    )
-
-
-def back_kernel(
-    reach,
-    meta,
-    *refs,
-):
-    halo = refs[: reach + 1]
+                    ref[chunk, row + b * unit : row + (b + 1) * unit, :] = block[
+                        :, b * LANES : (b + 1) * LANES
+                    ]
+        row += width // LANES * unit
+    sent(ds)
+    sent(dk)
+    traffic.finish()
+
+
+def back_kernel(reach, layout, *refs):
+    count = reach + 15
+    ins_h, refs = refs[:count], refs[count:]
+    _, wq_a, wk_a, wv_a, pack_h = refs[:5]
+    outs_h, refs = refs[5:9], refs[9:]
+    ins, refs = refs[:count], refs[count:]
+    halo = ins[: reach + 1]
     (
         gains,
         order,
+        scale_order,
+        dg_post,
         cos_ref,
         sin_ref,
         n1_ref,
@@ -587,48 +679,42 @@
         v_ref,
         p_ref,
         dao_ref,
-        wq_a,
-        wq_b,
-        wk_a,
-        wk_b,
-        wv_a,
-        wv_b,
-        keep,
-        send,
-        dn1_own,
-        dn1_far,
-        dg_out,
-        wq,
-        wk,
-        wv,
-        dqr_s,
-        dkv_s,
-        sems,
-    ) = refs[reach + 1 :]
-    core = meta[1]
-    rows = halo[0].shape[0]
+    ) = ins[reach + 1 :]
+    outs = keep, send, dn1_own, dn1_far = refs[:4]
+    wq, wk, wv, dqr_s, dkv_s, sems = refs[4:]
+    place, core = lax.axis_index("seq"), lax.axis_index("fsdp")
+    traffic = Traffic(sems)
+    heads = p_ref.shape[0]
+    first = traffic.fetch([(ins_h[n], ins[n]) for n in (count - 1, count - 3, count - 4)])
+    p_w = traffic.fetch([(ins_h[count - 2].at[h], p_ref.at[h]) for h in range(heads)])
+    second = traffic.fetch([(ins_h[n], ins[n]) for n in range(reach + 1, count - 4)])
+    copies = traffic.fetch(list(zip(ins_h[: reach + 1], halo)))
+    for n, (mine, full) in enumerate(((wq_a, wq), (wk_a, wk), (wv_a, wv))):
+        copies += traffic.halves(core, mine, pack_h, layout[n], full)
+    wait(first)
+    rows = halo[0].shape[0] - SEG_ROWS
     width = n1_ref.shape[1]
     size = k_ref.shape[1]
-    heads = q_ref.shape[1] // size
     scale = size ** (-0.5)
-    copies = assemble(core, ((wk_a, wk_b, wk), (wv_a, wv_b, wv), (wq_a, wq_b, wq)), sems)
-    g_in = gains[:, :width]
-    g_q = gains[:, width : width + size]
-    g_k = gains[:, width + size : width + 2 * size]
     k = k_ref[...]
     v = v_ref[...]
     keys = (reach + 1) * rows
-    cos_own, sin_own = cos_ref[reach * rows :, :], sin_ref[reach * rows :, :]
     dk = jnp.zeros((keys, size), F32)
     dv = jnp.zeros((keys, size), F32)
     dgq = jnp.zeros((1, size), F32)
     for h in range(heads):
         cols = slice(h * size, (h + 1) * size)
+        p_w[h].wait()
         p = p_ref[h]
         dao = dao_ref[:, cols]
         dp = mm_nt(dao, v)
         ds = (p * (dp - jnp.sum(p * dp, axis=-1, keepdims=True))).astype(BF16)
         dv = dv + mm_tn(p.astype(BF16), dao)
+        if h == 0:
+            wait(second)
+            g_q = gains[:, width : width + size]
+            g_k = gains[:, width + size : width + 2 * size]
+            cos_own, sin_own = cos_ref[reach * rows :, :], sin_ref[reach * rows :, :]
         dk = dk + mm_tn(ds, q_ref[:, cols])
         dq = turn_bwd(mm(ds, k) * scale, cos_own, sin_own)
         qraw = qraw_ref[:, cols]
@@ -640,17 +726,37 @@
     kraw = kraw_ref[...]
     inv = inverse_rms(kraw)
     hat = kraw * inv
-    dg_out[:, width : width + size] = dgq
-    dg_out[:, width + size :] = jnp.sum(dk * hat, axis=0, keepdims=True)
+    dgk = jnp.sum(dk * hat, axis=0, keepdims=True)
     dkv_s[:, :size] = norm_back(hat, inv, g_k, dk).astype(BF16)
     dkv_s[:, size:] = dv.astype(BF16)
-    ranks = lax.broadcasted_iota(jnp.int32, (width, width), 1)
-    perm = jnp.where(ranks == order[...], 1.0, 0.0).astype(BF16)
+    perm = row_order(order, place, core)
     n1_t = mm_nt(perm, n1_ref[...]).astype(BF16)
     half = width // 2
     per = half // XY
     attn = heads * size
-    for ref, begin in ((send, half), (keep, 0)):
+    wait(copies)
+    dgi = jnp.zeros((1, width), F32)
+    for block in range(reach + 1):
+        span = slice(block * rows, (block + 1) * rows)
+        dn1 = mm_nt(dkv_s[span, :size], wk[...]) + mm_nt(dkv_s[span, size:], wv[...])
+        if block == reach:
+            dn1 = dn1 + mm_nt(dqr_s[...], wq[...])
+        x = halo[block][:rows, :].astype(F32)
+        dgi = dgi + jnp.sum(dn1 * (x * inverse_rms(x)), axis=0, keepdims=True)
+        if block == reach:
+            dn1_own[...] = dn1
+        else:
+            bits = (place ^ (place - (reach - block))) & (XY - 1)
+            low = dn1.astype(BF16)
+            for b in range(width // LANES):
+                dn1_far[bits, b * rows : (b + 1) * rows, :] = low[:, b * LANES : (b + 1) * LANES]
+    scales = owners_rows(jnp.concatenate([dgi, dgq, dgk, dg_post[...]], axis=1))
+    owner = scale_order[:, :1] ^ (place * 2 + core)
+    mine = scale_order[:, 1:2] * 1024 + (owner & 3) * 8 + (owner >> 2)
+    columns = lax.broadcasted_iota(jnp.int32, (mine.shape[0], 2 * XY * LINE), 1)
+    scales = mm(jnp.where(columns == mine, 1.0, 0.0).astype(BF16), scales).astype(BF16)
+    rows_each = scales.shape[0] // (2 * XY)
+    for ref, begin, group in ((send, half, XY), (keep, 0, 0)):
         left = n1_t[begin : begin + half]
         own = left[:, reach * rows :]
         at = 0
@@ -668,33 +774,147 @@
                             :,
                         ] = out[plane * per : (plane + 1) * per, b * LANES : (b + 1) * LANES]
             at += total // LANES * per
-    for copy in copies:
-        copy.wait()
-    dgi = jnp.zeros((1, width), F32)
-    for block in range(reach + 1):
-        span = slice(block * rows, (block + 1) * rows)
-        dn1 = mm_nt(dkv_s[span, :size], wk[...]) + mm_nt(dkv_s[span, size:], wv[...])
-        if block == reach:
-            dn1 = dn1 + mm_nt(dqr_s[...], wq[...])
-        x = halo[block][:, :width].astype(F32)
-        dgi = dgi + jnp.sum(dn1 * (x * inverse_rms(x)), axis=0, keepdims=True)
-        if block == reach:
-            dn1_own[...] = dn1
-        else:
-            dn1_far[block] = dn1.astype(BF16)
-    dg_out[:, :width] = dgi
-
-
-def call(kernel, meta, args, specs, outs, scratch, limit, flops):
+        for plane in range(XY):
+            row = (group + plane) * rows_each
+            ref[plane, at : at + rows_each, :] = scales[row : row + rows_each]
+        traffic.emit(ref, outs_h[0 if ref is keep else 1])
+    for n in (3, 2):
+        traffic.emit(outs[n], outs_h[n])
+    traffic.finish()
+
+
+def owners_rows(line):
+    pieces = [line[:, r * LANES : (r + 1) * LANES] for r in range(line.shape[1] // LANES)]
+    first, second, third = (jnp.concatenate(pieces[n::3], axis=0) for n in range(3))
+    lane = lax.broadcasted_iota(jnp.int32, first.shape, 1)
+    quarter = LANES // 4
+    groups = [
+        first,
+        jnp.where(
+            lane < quarter, pltpu.roll(first, quarter, 1), pltpu.roll(second, quarter, 1)
+        ),
+        jnp.where(
+            lane < 2 * quarter,
+            pltpu.roll(second, 2 * quarter, 1),
+            pltpu.roll(third, 2 * quarter, 1),
+        ),
+        pltpu.roll(third, 3 * quarter, 1),
+    ]
+    return jnp.concatenate(groups, axis=0).astype(BF16)
+
+
+def collect_kernel(skip, *refs):
+    ins_h, outs_h = refs[: XY + 1], refs[XY + 1 : XY + 3]
+    ins, outs, sems = refs[XY + 3 : 2 * XY + 4], refs[2 * XY + 4 : 2 * XY + 6], refs[-1]
+    traffic = Traffic(sems)
+    own, far, *near = ins
+    near_h = [ref.at[skip:, :] for ref in ins_h[2:]]
+    wait(traffic.fetch(list(zip((ins_h[0], ins_h[1].at[0], *near_h), ins))))
+    place = lax.axis_index("seq") & (XY - 1)
+    rows = own.shape[0]
+    total = own[...]
+    below = far[...].astype(F32)
+    for bits, ref in enumerate(near, 1):
+        part = ref[...].astype(F32)
+        mine = (place ^ bits) > place
+        below = below + jnp.where(mine, 0.0, part)
+        lanes = [part[b * rows : (b + 1) * rows] for b in range(part.shape[0] // rows)]
+        total = total + jnp.where(mine, jnp.concatenate(lanes, axis=1), 0.0)
+    outs[0][...] = total
+    outs[1][...] = below.astype(BF16)
+    traffic.emit(outs[1], outs_h[1])
+    traffic.emit(outs[0], outs_h[0])
+    traffic.finish()
+
+
+def finish_kernel(*refs):
+    ins_h, out_h, ins, out, sems = refs[:5], refs[5], refs[6:11], refs[11], refs[12]
+    traffic = Traffic(sems)
+    wait(traffic.fetch(list(zip(ins_h, ins))))
+    tok, gains, dx, dn1, above = ins
+    rows, width = dx.shape
+    lanes = [above[b * rows : (b + 1) * rows, :] for b in range(width // LANES)]
+    total = dn1[...] + jnp.concatenate(lanes, axis=1).astype(F32)
+    x = tok[:rows, :].astype(F32)
+    inv = inverse_rms(x)
+    out[...] = dx[...] + norm_back(x * inv, inv, gains[:, :width], total)
+    traffic.emit(out, out_h)
+    traffic.finish()
+
+
+def line_split_kernel(groups, entries, extra, direct, *refs):
+    count = sum(groups)
+    ins_h, keep_h, send_h = refs[:count], refs[count], refs[count + 1]
+    ins = refs[count + 2 : 2 * count + 2]
+    keep, send, split, *sums, sems = refs[2 * count + 2 :]
+    traffic = Traffic(sems)
+    copies = traffic.fetch(list(zip(ins_h, ins)))
+    at = 0
+    for number, total in zip(groups, sums):
+        wait(copies[at : at + number])
+        value = ins[at][...].astype(F32)
+        for other in ins[at + 1 : at + number]:
+            value = value + other[: value.shape[0], :].astype(F32)
+        total[...] = value
+        at += number
+    at = 0
+    for group, row, blocks, unit in entries:
+        for b in range(blocks):
+            for position in range(LINE):
+                begin = row + (b * LINE + position) * unit
+                split[position, at : at + unit, :] = sums[group][begin : begin + unit, :]
+            at += unit
+    if extra:
+        group, row = extra
+        for position in range(LINE):
+            one = sums[group][row + position : row + position + 1, :]
+            split[position, at : at + 16, :] = jnp.broadcast_to(one, (16, LANES))
+    order = ((keep, (0,)), (send, (1, 2, 3))) if direct else ((keep, (0, 2)), (send, (1, 3)))
+    for ref, positions in order:
+        for n, position in enumerate(positions):
+            ref[n] = split[position].astype(ref.dtype)
+    traffic.emit(send, send_h)
+    traffic.emit(keep, keep_h)
+    traffic.finish()
+
+
+def join_kernel(parts, entries, extra, *refs):
+    count = len(entries) + extra
+    ins_h, outs_h = refs[:parts], refs[parts : parts + count]
+    ins = refs[parts + count : 2 * parts + count]
+    outs = refs[2 * parts + count : 2 * parts + 2 * count]
+    sum_s, sems = refs[2 * parts + 2 * count :]
+    traffic = Traffic(sems)
+    wait(traffic.fetch(list(zip(ins_h, ins))))
+    total = ins[0][...].astype(F32)
+    for part in ins[1:]:
+        total = total + part[...].astype(F32)
+    sum_s[...] = total
+    at = 0
+    for (blocks, unit), out in zip(entries, outs):
+        for b in range(blocks):
+            out[pl.ds(b, unit, stride=blocks), :] = sum_s[at : at + unit, :]
+            at += unit
+    if extra:
+        outs[-1][...] = sum_s[at : at + 8, :]
+    for out, out_h in zip(outs, outs_h):
+        traffic.emit(out, out_h)
+    traffic.finish()
+
+
+def call(kernel, fetched, others, outs, scratch, copies, flops, limit=56):
+    hbm = pl.BlockSpec(memory_space=pl.ANY)
     return pl.pallas_call(
         kernel,
         out_shape=outs,
-        in_specs=[pl.BlockSpec(memory_space=pltpu.SMEM)] + specs,
-        out_specs=vmem(len(outs)),
-        scratch_shapes=scratch,
+        in_specs=[hbm] * (len(fetched) + len(others)),
+        out_specs=[hbm] * len(outs),
+        scratch_shapes=[pltpu.VMEM(a.shape, a.dtype) for a in (*fetched, *outs)]
+        + scratch
+        + [pltpu.SemaphoreType.DMA((copies,))],
         compiler_params=pltpu.CompilerParams(vmem_limit_bytes=limit * MIB),
         cost_estimate=pl.CostEstimate(flops=flops, bytes_accessed=8 * MIB, transcendentals=0),
-    )(meta, *args)
+    )(*fetched, *others)
 
 
 def shape(dims, dtype):
@@ -725,7 +945,6 @@
     keys = (reach + 1) * rows
     place = lax.axis_index("seq")
     core = lax.axis_index("fsdp")
-    meta = jnp.stack([place, core]).astype(jnp.int32)
 
     def partner(value):
         return lax.ppermute(value, "fsdp", [(0, 1), (1, 0)])
@@ -733,35 +952,48 @@
     def across(value, bits):
         return lax.ppermute(value, "seq", [(i, i ^ bits) for i in range(XY * LINE)])
 
-    weights = (w_query, w_key, w_value, w_out, w_gate, w_up, w_down)
-    other = [partner(w) for w in weights]
-    gains_far = partner(norm_gains)
-    seg_cols = jnp.broadcast_to(segments[0].astype(BF16)[:, None], (rows, LANES))
-    tok = jnp.concatenate([tokens[0], seg_cols], axis=1)
+    gains_own = norm_gains.reshape(-1, LANES)
+    weights = (w_query, w_key, w_value, w_gate, w_up, w_out, w_down)
+    layout, columns = pack_layout(
+        width // 2,
+        [w.shape[1] for w in weights[:5]],
+        [w.shape for w in weights[5:]] + [(16, LANES)],
+    )
+    tok, pack = pl.pallas_call(
+        functools.partial(prepare_kernel, layout),
+        out_shape=[
+            shape((rows + SEG_ROWS, width), BF16),
+            shape((width // 2, columns), BF16),
+        ],
+        in_specs=[pl.BlockSpec(memory_space=pl.ANY)] * 10,
+        out_specs=[pl.BlockSpec(memory_space=pl.ANY)] * 2,
+        scratch_shapes=[pltpu.VMEM((rows, width), BF16), pltpu.VMEM((1, rows), jnp.int32)]
+        + [pltpu.VMEM(w.shape, BF16) for w in (*weights, gains_own)]
+        + [
+            pltpu.VMEM((rows + SEG_ROWS, width), BF16),
+            pltpu.VMEM((16, LANES), BF16),
+            pltpu.SemaphoreType.DMA((40,)),
+        ],
+        compiler_params=pltpu.CompilerParams(vmem_limit_bytes=56 * MIB),
+    )(tokens[0], segments, *weights, gains_own)
+    pack_far = partner(pack)
     halo = [shifted(tok, "seq", distance) for distance in range(reach, 0, -1)] + [tok]
 
-    gains = jnp.where(
-        core == 0,
-        jnp.concatenate([norm_gains, gains_far]),
-        jnp.concatenate([gains_far, norm_gains]),
-    ).astype(F32)[None]
     unit = width // (2 * XY * LINE)
     new = np.arange(width) // unit
     core_bit, plane, line = new // (XY * LINE), new // LINE % XY, new % LINE
-    owner = (jnp.asarray(line * XY + plane, jnp.int32) ^ place) * 2 + (
-        jnp.asarray(core_bit, jnp.int32) ^ core
-    )
-    order = (owner * unit + jnp.asarray(np.arange(width) % unit, jnp.int32))[:, None]
+    owner = (line * XY + plane) * 2 + core_bit
+    order = jnp.asarray(np.stack([owner, np.arange(width) % unit], axis=1).astype(np.int32))
     freq = np.exp(np.arange(size // 2, dtype=np.float64) * (-2.0 * math.log(10000.0) / size))
     turn = np.arange(keys, dtype=np.float64)[:, None] * freq
     cosine = jnp.asarray(np.cos(turn).astype(np.float32))
     sine = jnp.asarray(np.sin(turn).astype(np.float32))
 
-    n1, qraw, q, kraw, k, v, p, ao = call(
-        functools.partial(attention_kernel, reach),
-        meta,
-        (*halo, gains, cosine, sine, w_query, other[0], w_key, other[1], w_value, other[2]),
-        vmem(reach + 4) + anywhere(6),
+    packed = width // 2 + ff // 2 + attn // 2 + 2 * ff + 2 * width
+    n1, qraw, q, kraw, k, v, p, mixed, dx, dao, dg_post, mlp_keep, mlp_send, gains = call(
+        functools.partial(forward_kernel, reach, layout),
+        (*halo, cotangent[0], gains_own, order, cosine, sine),
+        (*weights, pack_far),
         [
             shape((keys, width), BF16),
             shape((rows, attn), F32),
@@ -770,47 +1002,18 @@
             shape((keys, size), BF16),
             shape((keys, size), BF16),
             shape((heads, rows, keys), F32),
+            shape((rows, width), BF16),
+            shape((rows, width), F32),
             shape((rows, attn), BF16),
+            shape((1, 3 * width), F32),
+            shape((packed, LANES), BF16),
+            shape((packed, LANES), BF16),
+            shape((1, count), F32),
         ],
         [
             pltpu.VMEM((width, attn), BF16),
             pltpu.VMEM((width, size), BF16),
             pltpu.VMEM((width, size), BF16),
-            pltpu.SemaphoreType.DMA((3, 2)),
-        ],
-        24,
-        3 * 10**9,
-    )
-
-    pack = width // 2 + ff // 2 + attn // 2 + 2 * ff + 2 * width
-    mixed, dx, dao, dg_post, mlp_keep, mlp_send = call(
-        feed_kernel,
-        meta,
-        (
-            tok,
-            cotangent[0],
-            gains,
-            order,
-            ao,
-            w_out,
-            other[3],
-            w_gate,
-            other[4],
-            w_up,
-            other[5],
-            w_down,
-            other[6],
-        ),
-        vmem(5) + anywhere(8),
-        [
-            shape((rows, width), BF16),
-            shape((rows, width), F32),
-            shape((rows, attn), BF16),
-            shape((1, 3 * width), F32),
-            shape((pack, LANES), BF16),
-            shape((pack, LANES), BF16),
-        ],
-        [
             pltpu.VMEM((attn, width), BF16),
             pltpu.VMEM((width, ff), BF16),
             pltpu.VMEM((width, ff), BF16),
@@ -820,68 +1023,57 @@
             pltpu.VMEM((rows, ff), BF16),
             pltpu.VMEM((rows, ff), BF16),
             pltpu.VMEM((rows, ff), BF16),
-            pltpu.SemaphoreType.DMA((4, 2)),
+            pltpu.VMEM((rows, attn), BF16),
+            pltpu.VMEM((16, LANES), BF16),
         ],
-        36,
-        4 * 10**9,
+        72,
+        7 * 10**9,
     )
     mlp_recv = partner(mlp_send)
 
     per_ff = width // 2 // XY * ff // LANES
     per_down = ff // 2 // XY * width // LANES
     per_out = attn // 2 // XY * width // LANES
-    halves = []
-    for per in (per_ff, per_ff, per_down, per_out):
-        halves += [shape((2, per, LANES), BF16)] * 2
-    gk, gs, uk, us, dk, ds, ok, os = call(
-        lambda meta_ref, *refs: grads_kernel(meta_ref, width, ff, attn, *refs),
-        meta,
+    halves = [shape((2, per_ff, LANES), BF16)] * 2
+    halves += [shape((2, per_ff, LANES), BF16)] * 2
+    halves += [shape((8, (per_down + per_out) // LINE, LANES), BF16)] * 2
+    gk, gs, uk, us, dk, ds = call(
+        functools.partial(grads_kernel, width, ff, attn),
+        (),
         (mlp_keep, mlp_recv),
-        vmem(2),
         halves,
         [
+            pltpu.VMEM((width // 2, 2 * LANES), BF16),
             pltpu.VMEM((ff // 2, 2 * LANES), BF16),
+            pltpu.VMEM((attn // 2, 2 * LANES), BF16),
             pltpu.VMEM((2 * LANES, ff), BF16),
+            pltpu.VMEM((2 * LANES, ff), BF16),
+            pltpu.VMEM((2 * LANES, width), BF16),
+            pltpu.VMEM((2 * LANES, width), BF16),
             pltpu.VMEM((ff // 2, width), F32),
         ],
+        128,
+        10**9,
         32,
-        10**9,
     )
 
     per_q = width // 2 // XY * attn // LANES
     per_k = width // 2 // XY * size // LANES
     per_back = per_q + 2 * per_k
-    back_keep, back_send, dn1_own, dn1_far, dg_pre = call(
-        functools.partial(back_kernel, reach),
-        meta,
-        (
-            *halo,
-            gains,
-            order,
-            cosine,
-            sine,
-            n1,
-            qraw,
-            q,
-            kraw,
-            k,
-            v,
-            p,
-            dao,
-            w_query,
-            other[0],
-            w_key,
-            other[1],
-            w_value,
-            other[2],
-        ),
-        vmem(reach + 13) + anywhere(6),
+    share = count // (2 * XY * LINE)
+    new = np.arange(2 * XY * 16)
+    core_bit, plane, line = new // (XY * 16), new // 16 % XY, new % 16
+    owner = (line % LINE * XY + plane) * 2 + core_bit
+    scale_order = jnp.asarray(np.stack([owner, line // LINE], axis=1).astype(np.int32))
+    back_keep, back_send, dn1_own, dn1_far = call(
+        functools.partial(back_kernel, reach, layout),
+        (*halo, gains, order, scale_order, dg_post, cosine, sine, n1, qraw, q, kraw, k, v, p, dao),
+        (gk, *weights[:3], pack_far),
         [
             shape((XY, per_back + 16, LANES), BF16),
             shape((XY, per_back + 16, LANES), BF16),
             shape((rows, width), F32),
-            shape((reach, rows, width), BF16),
-            shape((1, width + 2 * size), F32),
+            shape((XY, rows * width // LANES, LANES), BF16),
         ],
         [
             pltpu.VMEM((width, attn), BF16),
@@ -889,95 +1081,129 @@
             pltpu.VMEM((width, size), BF16),
             pltpu.VMEM((rows, attn), BF16),
             pltpu.VMEM((keys, 2 * size), BF16),
-            pltpu.SemaphoreType.DMA((3, 2)),
         ],
-        32,
+        64,
         4 * 10**9,
     )
-    share = count // (2 * XY * LINE)
-    dg = jnp.concatenate([dg_pre, dg_post], axis=1).reshape(2 * XY * LINE, share)
-    new = np.arange(2 * XY * LINE)
-    core_bit, plane, line = new // (XY * LINE), new // LINE % XY, new % LINE
-    owner = (jnp.asarray(line * XY + plane, jnp.int32) ^ place) * 2 + (
-        jnp.asarray(core_bit, jnp.int32) ^ core
-    )
-    dg = jnp.take(dg, owner, axis=0).reshape(2, XY, LINE, share).astype(BF16)
-    dg = jnp.pad(dg, ((0, 0), (0, 0), (0, 16 - LINE), (0, LANES - share)))
-    back_keep = lax.dynamic_update_slice(back_keep, dg[0], (0, per_back, 0))
-    back_send = lax.dynamic_update_slice(back_send, dg[1], (0, per_back, 0))
     back_recv = partner(back_send)
 
     def add(a, b):
         return (a.astype(F32) + b.astype(F32)).astype(BF16)
 
-    def plane_sum(keep, send, bits):
-        keep = add(keep, across(send, bits))
-        return add(keep[0], across(keep[1], 3 - bits))
-
-    def line_sum(parts):
-        total = parts[0].astype(F32)
-        for step in range(1, LINE):
-            total = total + across(parts[step], step * XY).astype(F32)
-        return total
-
-    def by_line(value, blocks):
-        unit = value.shape[0] // (blocks * LINE)
-        return value.reshape(blocks, LINE, unit, LANES).transpose(1, 0, 2, 3)
-
-    def flat(total, blocks):
-        unit = total.shape[0] // blocks
-        return total.reshape(blocks, unit, LANES).transpose(1, 0, 2).reshape(-1)
-
-    gate_sum = plane_sum(gk, gs, 1)
-    up_sum = plane_sum(uk, us, 2)
-    down_sum = plane_sum(dk, ds, 1)
-    out_sum = plane_sum(ok, os, 2)
-    mid = per_q // 2 + per_k
-    both = add(back_keep, back_recv)
-    back_x = plane_sum(both[0::2, :mid], both[1::2, :mid], 1)
-    back_y = plane_sum(both[:2, mid:], both[2:, mid:], 2)
-    back_sum = jnp.concatenate([back_x, back_y], axis=0)
-
-    def joined(*pieces):
-        return jnp.concatenate([by_line(v, b).reshape(LINE, -1, LANES) for v, b in pieces], axis=1)
-
-    wide = ff // LANES
-    narrow = width // LANES
-    first = line_sum(joined((gate_sum, wide), (up_sum, wide)))
-    second = line_sum(joined((down_sum, narrow), (out_sum, narrow)))
-    scales = back_sum[per_back : per_back + LINE].reshape(LINE, 1, LANES)
-    third = line_sum(
-        jnp.concatenate(
-            [joined((back_sum[:per_back], (attn + 2 * size) // LANES)), scales], axis=1
+    def step(keep, send, bits):
+        near = across(send, bits)
+        half = keep.shape[0] // 2
+        return add(keep[:half], near[:half]), add(keep[half:], near[half:])
+
+    def line_split(groups, entries, extra, direct):
+        part = sum(blocks * unit for _, _, blocks, unit in entries) + (16 if extra else 0)
+        stay = 1 if direct else 2
+        return call(
+            functools.partial(
+                line_split_kernel, [len(g) for g in groups], entries, extra, direct
+            ),
+            [array for g in groups for array in g],
+            (),
+            [shape((stay, part, LANES), BF16), shape((LINE - stay, part, LANES), BF16)],
+            [pltpu.VMEM((LINE, part, LANES), F32)]
+            + [pltpu.VMEM(g[0].shape, F32) for g in groups],
+            sum(len(g) for g in groups) + 2,
+            10**8,
+            24,
         )
-    )
-    own_gate = flat(first[: per_ff // LINE], wide)
-    own_up = flat(first[per_ff // LINE :], wide)
-    own_down = flat(second[: per_down // LINE], narrow)
-    own_out = flat(second[per_down // LINE :], narrow)
-    a, b = per_q // LINE, (per_q + per_k) // LINE
-    own_query = flat(third[:a], attn // LANES)
-    own_key = flat(third[a:b], size // LANES)
-    own_value = flat(third[b : per_back // LINE], size // LANES)
-    own_gains = third[per_back // LINE, :share]
-
-    dn1 = dn1_own
-    for index in range(reach):
-        dn1 = dn1 + shifted(dn1_far[index], "seq", index - reach).astype(F32)
-    x = tokens[0].astype(F32)
-    inv = inverse_rms(x)
-    input_grad = dx + norm_back(x * inv, inv, gains[:, :width], dn1)
+
+    def join(parts, entries, extra=False):
+        outs = [shape((blocks * unit, LANES), F32) for blocks, unit in entries]
+        if extra:
+            outs.append(shape((8, LANES), F32))
+        return call(
+            functools.partial(join_kernel, len(parts), entries, int(extra)),
+            parts,
+            (),
+            outs,
+            [pltpu.VMEM(parts[0].shape, F32)],
+            len(parts) + len(outs),
+            10**8,
+            24,
+        )
+
+    wide, narrow = ff // LANES, width // LANES
+    unit_out, unit_down = attn // 32, ff // 32
+
+    gate_0, gate_1 = step(gk, gs, 1)
+    up_0, up_1 = step(uk, us, 2)
+    gate_2, up_2 = across(gate_1, 2), across(up_1, 1)
+    flat = lambda value: value.reshape(value.shape[1:])
+    keep, send = line_split(
+        ((flat(gate_0), flat(gate_2)), (flat(up_0), flat(up_2))),
+        ((0, 0, wide, unit), (1, 0, wide, unit)),
+        None,
+        False,
+    )
+    mlp_0, mlp_1 = step(keep, send, XY)
+    own_gate, own_up = join(
+        (flat(mlp_0), flat(across(mlp_1, 2 * XY))), ((wide, unit), (wide, unit))
+    )
+    down_0, down_1 = step(dk, ds, XY)
+    down_0, down_1 = step(down_0, down_1, 1)
+    down_0, down_1 = step(down_0, down_1, 2)
+    own_down, own_out = join(
+        (flat(down_0), flat(across(down_1, 2 * XY))), ((narrow, unit_down), (narrow, unit_out))
+    )
+
+    planes = [add(back_keep[n], back_recv[n]) for n in range(XY)]
+    planes = [planes[0]] + [
+        across(jnp.concatenate([planes[n], dn1_far[n]]), n) for n in range(1, XY)
+    ]
+    keep, send = line_split(
+        (planes,),
+        (
+            (0, 0, attn // LANES, unit),
+            (0, per_q, size // LANES, unit),
+            (0, per_q + per_k, size // LANES, unit),
+        ),
+        (0, per_back),
+        True,
+    )
+    own_query, own_key, own_value, own_gains = join(
+        (flat(keep), *[across(send[n], (n + 1) * XY) for n in range(LINE - 1)]),
+        ((attn // LANES, unit), (size // LANES, unit), (size // LANES, unit)),
+        True,
+    )
+
+    far_shape = (rows * width // LANES, LANES)
+    dn1, below = pl.pallas_call(
+        functools.partial(collect_kernel, per_back + 16),
+        out_shape=[shape((rows, width), F32), shape(far_shape, BF16)],
+        in_specs=[pl.BlockSpec(memory_space=pl.ANY)] * (XY + 1),
+        out_specs=[pl.BlockSpec(memory_space=pl.ANY)] * 2,
+        scratch_shapes=[pltpu.VMEM((rows, width), F32)]
+        + [pltpu.VMEM(far_shape, BF16)] * XY
+        + [pltpu.VMEM((rows, width), F32), pltpu.VMEM(far_shape, BF16)]
+        + [pltpu.SemaphoreType.DMA((XY + 3,))],
+        compiler_params=pltpu.CompilerParams(vmem_limit_bytes=24 * MIB),
+    )(dn1_own, dn1_far, *planes[1:])
+    (input_grad,) = call(
+        finish_kernel,
+        (tok, gains, dx, dn1, shifted(below, "seq", -XY)),
+        (),
+        [shape((rows, width), F32)],
+        [],
+        6,
+        10**8,
+        24,
+    )
     return (
         mixed[None],
         input_grad[None],
-        own_query,
-        own_key,
-        own_value,
-        own_out,
-        own_gate,
-        own_up,
-        own_down,
-        own_gains,
+        own_query.reshape(-1),
+        own_key.reshape(-1),
+        own_value.reshape(-1),
+        own_out.reshape(-1),
+        own_gate.reshape(-1),
+        own_up.reshape(-1),
+        own_down.reshape(-1),
+        own_gains[0, :share],
     )
 
 

time: 190 us -> 138 us (0.73)
  local copies, waits for them, and re-layouts: 27.4 us -> 5.47 us
  Pallas kernels: 26.6 us -> 47.1 us
  waiting for transfers between devices: 56.8 us -> 36.3 us
  starting transfers between devices: 62 us -> 46.2 us
  other arithmetic: 14.4 us -> 1.24 us
    pallas_call x4 -> x11, Pallas kernels: 26.6 us -> 47.1 us  [the longest x9 39.9 us: call(): pl.pallas_call(kernel, out_shape=outs, in_specs=[hbm] * (len(fetched) + l...]
    ppermute x21 -> x16, waiting for transfers between devices: 43.1 us -> 27.7 us  [across(): return lax.ppermute(value, 'seq', [(i, i ^ bits) for i in range(XY * LINE)])]
    unnamed x108 -> x28, local copies, waits for them, and re-layouts: 19 us -> 4.91 us
    ppermute x21 -> x16, starting transfers between devices: 39.5 us -> 28.6 us  [across(): return lax.ppermute(value, 'seq', [(i, i ^ bits) for i in range(XY * LINE)])]
    ppermute x8 -> x5, waiting for transfers between devices: 13.7 us -> 4.57 us  [shifted(): return lax.ppermute(x, axis, pairs)]
    concatenate x5 -> x3, other arithmetic: 5.38 us -> 0.09 us  [fast(): jnp.concatenate([planes[n], dn1_far[n]])]
    ppermute x10 -> x3, waiting for transfers between devices: 0.03 us -> 4.01 us  [partner(): return lax.ppermute(value, 'fsdp', [(0, 1), (1, 0)])]
    transpose x8 -> x0, local copies, waits for them, and re-layouts: 3.64 us -> none  [the longest x5 3.28 us: flat(): return total.reshape(blocks, unit, LANES).transpose(1, 0, 2).reshape(-1)]
  transfers between devices with their start and end apart: 39 -> 24, of which waited for: 17 -> 10; matrix products, arithmetic and copies ran while one was open for 10% -> 1% of each run, Pallas kernels for 5% -> 15%
where the time goes in v2:
time: 138 us; the launch traced here: 137 us
  Pallas kernels  47.1 us (34%)
  starting transfers between devices  46.2 us (33%)
  waiting for transfers between devices  36.3 us (26%)
  local copies, waits for them, and re-layouts  5.47 us (4%)
    pallas_call x9, Pallas kernels, call(): pl.pallas_call(kernel, out_shape=outs, in_specs=[hbm] * (len(fetched) + l...  39.9 us
    ppermute x16, starting transfers between devices, across(): return lax.ppermute(value, 'seq', [(i, i ^ bits) for i in range(XY * LINE)])  28.6 us
    ppermute x16, waiting for transfers between devices, across(): return lax.ppermute(value, 'seq', [(i, i ^ bits) for i in range(XY * LINE)])  27.7 us
    ppermute x5, starting transfers between devices, shifted(): return lax.ppermute(x, axis, pairs)  17 us
    pallas_call x1, Pallas kernels, fast(): pl.pallas_call(functools.partial(prepare_kernel, layout), out_shape=[shap...  5.68 us
    unnamed x28, local copies, waits for them, and re-layouts  4.91 us
    ppermute x5, waiting for transfers between devices, shifted(): return lax.ppermute(x, axis, pairs)  4.57 us
    ppermute x3, waiting for transfers between devices, partner(): return lax.ppermute(value, 'fsdp', [(0, 1), (1, 0)])  4.01 us
  transfers between devices with their start and end apart: 24, of which 10 were waited for; matrix products, arithmetic and copies ran while one was open for 1% of the time, Pallas kernels for 15%

profile of v2, /device:TPU:0, one launch (start us, length us, event | category | flops | bytes accessed | tf_op | source)
XLA Modules:
  0.0 137.4 jit_solution(12911414308710382662)
XLA Ops:
  0.6 5.7 %shard_map.222 = (bf16[144,640]{1,0:T(8,128)(2,1)}, bf16[320,8832]{1,0:T(8,128)(2,1)}) custom-call(bf16[128,640]{1,0:T(8,128)(2,1)} %bitcast.53, s32[1,128]{1,0:T(1,128)} %refs_1_.1, bf16[320,1024]{1,0:T(8,128)(2,1)} %refs_20_.1, bf16[320,256]{1,0:T(8,128)(2,1)} %refs_21_.1, bf16[320,256]{1,0:T(8,128)(2,1)} %refs_22_.1, bf16[320,2048]{1,0:T(8,128)(2,1)} %refs_13_.1, ...), custom_call_target="tpu_custom_call" | custom-call | tf_op jit(solution)/shard_map/pallas_call | solution.py:962
  6.8 4.4 %collective-permute-start.3 = (bf16[144,640]{1,0:T(8,128)(2,1)}, bf16[144,640]{1,0:T(8,128)(2,1)S(1)}, u32[]{:S(2)}, u32[]{:S(2)}) collective-permute-start(bf16[144,640]{1,0:T(8,128)(2,1)} %get-tuple-element.50.refs_4_.refs_0_), channel_id=1, source_target_pairs={{0,2},{2,4},{4,6},{6,8},{8,10},{10,12},{12,14},{14,16},{16,18},{18... | collective-permute-start | bytes 552968 | tf_op jit(solution)/shard_map/ppermute | solution.py:24
  11.3 3.4 %collective-permute-start.2 = (bf16[144,640]{1,0:T(8,128)(2,1)}, bf16[144,640]{1,0:T(8,128)(2,1)S(1)}, u32[]{:S(2)}, u32[]{:S(2)}) collective-permute-start(bf16[144,640]{1,0:T(8,128)(2,1)} %get-tuple-element.50.refs_4_.refs_0_), channel_id=1, source_target_pairs={{0,4},{2,6},{4,8},{6,10},{8,12},{10,14},{12,16},{14,18},{16,20},{1... | collective-permute-start | bytes 552968 | tf_op jit(solution)/shard_map/ppermute | solution.py:24
  14.7 4.4 %collective-permute-start.1 = (bf16[144,640]{1,0:T(8,128)(2,1)}, bf16[144,640]{1,0:T(8,128)(2,1)S(1)}, u32[]{:S(2)}, u32[]{:S(2)}) collective-permute-start(bf16[144,640]{1,0:T(8,128)(2,1)} %get-tuple-element.50.refs_4_.refs_0_), channel_id=1, source_target_pairs={{0,6},{2,8},{4,10},{6,12},{8,14},{10,16},{12,18},{14,20},{16,22},{... | collective-permute-start | bytes 552968 | tf_op jit(solution)/shard_map/ppermute | solution.py:24
  19.1 3.5 %collective-permute-start = (bf16[144,640]{1,0:T(8,128)(2,1)}, bf16[144,640]{1,0:T(8,128)(2,1)S(1)}, u32[]{:S(2)}, u32[]{:S(2)}) collective-permute-start(bf16[144,640]{1,0:T(8,128)(2,1)} %get-tuple-element.50.refs_4_.refs_0_), channel_id=1, source_target_pairs={{0,8},{2,10},{4,12},{6,14},{8,16},{10,18},{12,20},{14,22},{16,24},... | collective-permute-start | bytes 552968 | tf_op jit(solution)/shard_map/ppermute | solution.py:24
  23.3 3.2 %collective-permute-done.refs_0_ = bf16[144,640]{1,0:T(8,128)(2,1)S(1)} collective-permute-done((bf16[144,640]{1,0:T(8,128)(2,1)}, bf16[144,640]{1,0:T(8,128)(2,1)S(1)}, u32[]{:S(2)}, u32[]{:S(2)}) %collective-permute-start) | collective-permute-done | bytes 184352 | tf_op jit(solution)/shard_map/ppermute | solution.py:24
  27.2 1.8 %copy-done.9 = bf16[320,8832]{1,0:T(8,128)(2,1)} copy-done((bf16[320,8832]{1,0:T(8,128)(2,1)}, bf16[320,8832]{1,0:T(8,128)(2,1)S(1)}, u32[]{:S(2)}) %copy-start.9) | copy-done | bytes 5652504
  29.1 14.2 %shard_map.223 = (bf16[640,640]{1,0:T(8,128)(2,1)}, f32[128,1024]{1,0:T(8,128)}, bf16[128,1024]{1,0:T(8,128)(2,1)}, f32[640,256]{1,0:T(8,128)}, bf16[640,256]{1,...) custom-call(bf16[144,640]{1,0:T(8,128)(2,1)} %copy-done.13, ...), custom_call_target="tpu_custom_call" | custom-call | flops 7000000000 | bytes 8388608 | tf_op jit(solution)/shard_map/pallas_call | solution.py:907
  43.4 4.0 %collective-permute-done.5.refs_1_ = bf16[7232,128]{1,0:T(8,128)(2,1)S(1)} collective-permute-done((bf16[7232,128]{1,0:T(8,128)(2,1)}, bf16[7232,128]{1,0:T(8,128)(2,1)S(1)}, u32[]{:S(2)}, u32[]{:S(2)}) %collective-permute-start.5) | collective-permute-done | bytes 1851424 | tf_op jit(solution)/shard_map/ppermute | solution.py:950
  47.4 1.5 %copy-done.1 = bf16[7232,128]{1,0:T(8,128)(2,1)S(1)} copy-done((bf16[7232,128]{1,0:T(8,128)(2,1)S(1)}, bf16[7232,128]{1,0:T(8,128)(2,1)}, u32[]{:S(2)}) %copy-start.1) | copy-done | bytes 1851416
  48.9 6.1 %shard_map.224 = (bf16[2,1280,128]{2,1,0:T(8,128)(2,1)S(1)}, bf16[2,1280,128]{2,1,0:T(8,128)(2,1)S(1)}, bf16[2,1280,128]{2,1,0:T(8,128)(2,1)S(1)}, bf16[2,1280,1...) custom-call(bf16[7232,128]{1,0:T(8,128)(2,1)S(1)} %copy-done.1, ...), custom_call_target="tpu_custom_call" | custom-call | flops 1000000000 | bytes 8388608 | tf_op jit(solution)/shard_map/pallas_call | solution.py:907
  55.9 1.3 collective-permute-start.18
  57.2 3.1 %collective-permute-start.20 = (bf16[2,1280,128]{2,1,0:T(8,128)(2,1)S(1)}, bf16[2,1280,128]{2,1,0:T(8,128)(2,1)S(1)}, u32[]{:S(2)}, u32[]{:S(2)}) collective-permute-start(bf16[2,1280,128]{2,1,0:T(8,128)(2,1)S(1)} %get-tuple-element.83), channel_id=1, source_target_pairs={{0,4},{2,6},{4,0},{6,2},{8,12},{10,14},{12,8},{14,10},{16,20},{18,... | collective-permute-start | bytes 1966088 | tf_op jit(solution)/shard_map/ppermute | solution.py:953
  60.3 2.4 %collective-permute-start.14 = (bf16[8,480,128]{2,1,0:T(8,128)(2,1)S(1)}, bf16[8,480,128]{2,1,0:T(8,128)(2,1)S(1)}, u32[]{:S(2)}, u32[]{:S(2)}) collective-permute-start(bf16[8,480,128]{2,1,0:T(8,128)(2,1)S(1)} %get-tuple-element.79), channel_id=1, source_target_pairs={{0,8},{2,10},{4,12},{6,14},{8,0},{10,2},{12,4},{14,6},{16,24},{18,... | collective-permute-start | bytes 2949128 | tf_op jit(solution)/shard_map/ppermute | solution.py:953
  62.6 11.9 %shard_map.225 = (bf16[4,976,128]{2,1,0:T(8,128)(2,1)}, bf16[4,976,128]{2,1,0:T(8,128)(2,1)}, f32[128,640]{1,0:T(8,128)}, bf16[4,640,128]{2,1,0:T(8,128)(2,1)}) custom-call(bf16[144,640]{1,0:T(8,128)(2,1)} %copy-done.13, bf16[144,640]{1,0:T(8,128)(2,1)} %copy-done.12, bf16[144,640]{1,0:T(8,128)(2,1)} %copy-done.11, bf16[144,640]{1,0:T(8,128)(2,1)} %copy-done.10, ...), custom_call_target="tpu_custom_call" | custom-call | flops 4000000000 | bytes 8388608 | tf_op jit(solution)/shard_map/pallas_call | solution.py:907
  74.8 1.8 %collective-permute-start.19 = (bf16[1,1280,128]{2,1,0:T(8,128)(2,1)S(1)}, bf16[1,1280,128]{2,1,0:T(8,128)(2,1)S(1)}, u32[]{:S(2)}, u32[]{:S(2)}) collective-permute-start(bf16[1,1280,128]{2,1,0:T(8,128)(2,1)S(1)} %get-tuple-element.98), channel_id=1, source_target_pairs={{0,4},{2,6},{4,0},{6,2},{8,12},{10,14},{12,8},{14,10},{16,20},{18,... | collective-permute-start | bytes 983048 | tf_op jit(solution)/shard_map/ppermute | solution.py:953
  77.6 6.6 %collective-permute-done.14 = bf16[8,480,128]{2,1,0:T(8,128)(2,1)S(1)} collective-permute-done((bf16[8,480,128]{2,1,0:T(8,128)(2,1)S(1)}, bf16[8,480,128]{2,1,0:T(8,128)(2,1)S(1)}, u32[]{:S(2)}, u32[]{:S(2)}) %collective-permute-start.14) | collective-permute-done | bytes 983072 | tf_op jit(solution)/shard_map/ppermute | solution.py:953
  84.4 1.5 %collective-permute-start.15 = (bf16[4,480,128]{2,1,0:T(8,128)(2,1)S(1)}, bf16[4,480,128]{2,1,0:T(8,128)(2,1)S(1)}, u32[]{:S(2)}, u32[]{:S(2)}) collective-permute-start(bf16[4,480,128]{2,1,0:T(8,128)(2,1)S(1)} %get-tuple-element.95), channel_id=1, source_target_pairs={{0,2},{2,0},{4,6},{6,4},{8,10},{10,8},{12,14},{14,12},{16,18},{18,... | collective-permute-start | bytes 1474568 | tf_op jit(solution)/shard_map/ppermute | solution.py:953
  86.9 2.5 %collective-permute-start.22 = (bf16[2,640,128]{2,1,0:T(8,128)(2,1)S(1)}, bf16[2,640,128]{2,1,0:T(8,128)(2,1)S(1)}, u32[]{:S(2)}, u32[]{:S(2)}) collective-permute-start(bf16[2,640,128]{2,1,0:T(8,128)(2,1)S(1)} %get-tuple-element.85), channel_id=1, source_target_pairs={{0,8},{2,10},{4,12},{6,14},{8,0},{10,2},{12,4},{14,6},{16,24},{18,... | collective-permute-start | bytes 983048 | tf_op jit(solution)/shard_map/ppermute | solution.py:953
  91.0 2.5 %collective-permute-start.9 = (bf16[1616,128]{1,0:T(8,128)(2,1)S(1)}, bf16[1616,128]{1,0:T(8,128)(2,1)S(1)}, u32[]{:S(2)}, u32[]{:S(2)}) collective-permute-start(bf16[1616,128]{1,0:T(8,128)(2,1)S(1)} %pad_maximum_fusion.2), channel_id=1, source_target_pairs={{0,6},{2,4},{4,2},{6,0},{8,14},{10,12},{12,10},{14,8},{16,22},{18,... | collective-permute-start | bytes 1241096 | tf_op jit(solution)/shard_map/ppermute | solution.py:953
  93.5 1.9 %collective-permute-done.22 = bf16[2,640,128]{2,1,0:T(8,128)(2,1)S(1)} collective-permute-done((bf16[2,640,128]{2,1,0:T(8,128)(2,1)S(1)}, bf16[2,640,128]{2,1,0:T(8,128)(2,1)S(1)}, u32[]{:S(2)}, u32[]{:S(2)}) %collective-permute-start.22) | collective-permute-done | bytes 327712 | tf_op jit(solution)/shard_map/ppermute | solution.py:953
  95.5 2.9 %collective-permute-start.23 = (bf16[1,640,128]{2,1,0:T(8,128)(2,1)S(1)}, bf16[1,640,128]{2,1,0:T(8,128)(2,1)S(1)}, u32[]{:S(2)}, u32[]{:S(2)}) collective-permute-start(bf16[1,640,128]{2,1,0:T(8,128)(2,1)S(1)} %get-tuple-element.102), channel_id=1, source_target_pairs={{0,16},{2,18},{4,20},{6,22},{8,24},{10,26},{12,28},{14,30},{16,0},... | collective-permute-start | bytes 491528 | tf_op jit(solution)/shard_map/ppermute | solution.py:953
  98.4 9.1 %collective-permute-done.7.refs_2_.refs_1_ = bf16[1616,128]{1,0:T(8,128)(2,1)S(1)} collective-permute-done((bf16[1616,128]{1,0:T(8,128)(2,1)S(1)}, bf16[1616,128]{1,0:T(8,128)(2,1)S(1)}, u32[]{:S(2)}, u32[]{:S(2)}) %collective-permute-start.7) | collective-permute-done | bytes 413728 | tf_op jit(solution)/shard_map/ppermute | solution.py:953
  107.5 7.2 %collective-permute-done.9.refs_4_.refs_3_ = bf16[1616,128]{1,0:T(8,128)(2,1)S(1)} collective-permute-done((bf16[1616,128]{1,0:T(8,128)(2,1)S(1)}, bf16[1616,128]{1,0:T(8,128)(2,1)S(1)}, u32[]{:S(2)}, u32[]{:S(2)}) %collective-permute-start.9) | collective-permute-done | bytes 413728 | tf_op jit(solution)/shard_map/ppermute | solution.py:953
  114.7 1.6 %shard_map.228 = (bf16[1,256,128]{2,1,0:T(8,128)(2,1)S(1)}, bf16[3,256,128]{2,1,0:T(8,128)(2,1)S(1)}) custom-call(bf16[976,128]{1,0:T(8,128)(2,1)S(1)} %get-tuple-element.90.refs_0_, bf16[1616,128]{1,0:T(8,128)(2,1)S(1)} %collective-permute-done.7.refs_2_.refs_1_, bf16[1616,128]{1,0:T(8,128)(2,1)S(1)} %collective-permute-done.8.refs_3_.refs_2_, ...), custom_call_target="tpu_custom_call" | custom-call | flops 100000000 | bytes 8388608 | tf_op jit(solution)/shard_map/pallas_call | solution.py:907
  117.6 4.0 %collective-permute-start.13 = (bf16[256,128]{1,0:T(8,128)(2,1)S(1)}, bf16[256,128]{1,0:T(8,128)(2,1)S(1)}, u32[]{:S(2)}, u32[]{:S(2)}) collective-permute-start(bf16[256,128]{1,0:T(8,128)(2,1)S(1)} %get-tuple-element.109), channel_id=1, source_target_pairs={{0,24},{2,26},{4,28},{6,30},{8,16},{10,18},{12,20},{14,22},{16,8},... | collective-permute-start | bytes 196616 | tf_op jit(solution)/shard_map/ppermute | solution.py:953
  122.2 1.5 %shard_map.226 = (f32[128,640]{1,0:T(8,128)S(1)}, bf16[640,128]{1,0:T(8,128)(2,1)S(1)}) custom-call(f32[128,640]{1,0:T(8,128)S(1)} %copy-done.4, bf16[4,640,128]{2,1,0:T(8,128)(2,1)S(1)} %copy-done, bf16[1616,128]{1,0:T(8,128)(2,1)S(1)} %collective-permute-done.7.refs_2_.refs_1_, bf16[1616,128]{1,0:T(8,128)(2,1)S(1)} %collective-permute-done.8.refs_3_.refs_2_, ...), custom_call_target="tpu_custom_call" | custom-call | tf_op jit(solution)/shard_map/pallas_call | solution.py:1175
  123.8 1.3 collective-permute-start.10
  125.1 1.3 shard_map.232
  128.3 2.9 %collective-permute-start.17 = (bf16[1,480,128]{2,1,0:T(8,128)(2,1)S(1)}, bf16[1,480,128]{2,1,0:T(8,128)(2,1)S(1)}, u32[]{:S(2)}, u32[]{:S(2)}) collective-permute-start(bf16[1,480,128]{2,1,0:T(8,128)(2,1)S(1)} %get-tuple-element.107), channel_id=1, source_target_pairs={{0,16},{2,18},{4,20},{6,22},{8,24},{10,26},{12,28},{14,30},{16,0},... | collective-permute-start | bytes 368648 | tf_op jit(solution)/shard_map/ppermute | solution.py:953
  132.3 1.7 %shard_map.227 = f32[128,640]{1,0:T(8,128)} custom-call(bf16[144,640]{1,0:T(8,128)(2,1)S(1)} %copy-done.6, f32[1,3072]{1,0:T(1,128)S(1)} %copy-done.7, f32[128,640]{1,0:T(8,128)S(1)} %copy-done.5, f32[128,640]{1,0:T(8,128)S(1)} %get-tuple-element.71.refs_3_, bf16[640,128]{1,0:T(8,128)(2,1)S(1)} %collective-permute-done.10.refs_4_), custom_call_target="tpu_custom_call" | custom-call | flops 100000000 | bytes 8388608 | tf_op jit(solution)/shard_map/pallas_call | solution.py:907
  134.0 2.3 %collective-permute-done.17 = bf16[1,480,128]{2,1,0:T(8,128)(2,1)S(1)} collective-permute-done((bf16[1,480,128]{2,1,0:T(8,128)(2,1)S(1)}, bf16[1,480,128]{2,1,0:T(8,128)(2,1)S(1)}, u32[]{:S(2)}, u32[]{:S(2)}) %collective-permute-start.17) | collective-permute-done | bytes 122912 | tf_op jit(solution)/shard_map/ppermute | solution.py:953
  (68 shorter events, 12.9 us)
Async XLA Ops:
  6.3 20.2 %collective-permute-start.4 = (bf16[320,8832]{1,0:T(8,128)(2,1)}, bf16[320,8832]{1,0:T(8,128)(2,1)S(1)}, u32[]{:S(2)}, u32[]{:S(2)}) collective-permute-start(bf16[320,8832]{1,0:T(8,128)(2,1)} %get-tuple-element.51), channel_id=1, source_target_pairs={{0,1},{1,0},{2,3},{3,2},{4,5},{5,4},{6,7},{7,6},{8,9},{9,8},{10,11... | collective-permute-start | bytes 16957448 | tf_op jit(solution)/shard_map/ppermute | solution.py:950
  6.8 15.7 %collective-permute-start.3 = (bf16[144,640]{1,0:T(8,128)(2,1)}, bf16[144,640]{1,0:T(8,128)(2,1)S(1)}, u32[]{:S(2)}, u32[]{:S(2)}) collective-permute-start(bf16[144,640]{1,0:T(8,128)(2,1)} %get-tuple-element.50.refs_4_.refs_0_), channel_id=1, source_target_pairs={{0,2},{2,4},{4,6},{6,8},{8,10},{10,12},{12,14},{14,16},{16,18},{18... | collective-permute-start | bytes 552968 | tf_op jit(solution)/shard_map/ppermute | solution.py:24
  11.3 11.3 %collective-permute-start.2 = (bf16[144,640]{1,0:T(8,128)(2,1)}, bf16[144,640]{1,0:T(8,128)(2,1)S(1)}, u32[]{:S(2)}, u32[]{:S(2)}) collective-permute-start(bf16[144,640]{1,0:T(8,128)(2,1)} %get-tuple-element.50.refs_4_.refs_0_), channel_id=1, source_target_pairs={{0,4},{2,6},{4,8},{6,10},{8,12},{10,14},{12,16},{14,18},{16,20},{1... | collective-permute-start | bytes 552968 | tf_op jit(solution)/shard_map/ppermute | solution.py:24
  14.7 8.6 %collective-permute-start.1 = (bf16[144,640]{1,0:T(8,128)(2,1)}, bf16[144,640]{1,0:T(8,128)(2,1)S(1)}, u32[]{:S(2)}, u32[]{:S(2)}) collective-permute-start(bf16[144,640]{1,0:T(8,128)(2,1)} %get-tuple-element.50.refs_4_.refs_0_), channel_id=1, source_target_pairs={{0,6},{2,8},{4,10},{6,12},{8,14},{10,16},{12,18},{14,20},{16,22},{... | collective-permute-start | bytes 552968 | tf_op jit(solution)/shard_map/ppermute | solution.py:24
  19.1 7.5 %collective-permute-start = (bf16[144,640]{1,0:T(8,128)(2,1)}, bf16[144,640]{1,0:T(8,128)(2,1)S(1)}, u32[]{:S(2)}, u32[]{:S(2)}) collective-permute-start(bf16[144,640]{1,0:T(8,128)(2,1)} %get-tuple-element.50.refs_4_.refs_0_), channel_id=1, source_target_pairs={{0,8},{2,10},{4,12},{6,14},{8,16},{10,18},{12,20},{14,22},{16,24},... | collective-permute-start | bytes 552968 | tf_op jit(solution)/shard_map/ppermute | solution.py:24
  22.6 4.0 %copy-start.10 = (bf16[144,640]{1,0:T(8,128)(2,1)}, bf16[144,640]{1,0:T(8,128)(2,1)S(1)}, u32[]{:S(2)}) copy-start(bf16[144,640]{1,0:T(8,128)(2,1)S(1)} %collective-permute-done.3.refs_3_) | copy-start | bytes 552964
  22.6 4.0 %copy-start.11 = (bf16[144,640]{1,0:T(8,128)(2,1)}, bf16[144,640]{1,0:T(8,128)(2,1)S(1)}, u32[]{:S(2)}) copy-start(bf16[144,640]{1,0:T(8,128)(2,1)S(1)} %collective-permute-done.2.refs_2_) | copy-start | bytes 552964
  43.3 4.1 %collective-permute-start.5 = (bf16[7232,128]{1,0:T(8,128)(2,1)}, bf16[7232,128]{1,0:T(8,128)(2,1)S(1)}, u32[]{:S(2)}, u32[]{:S(2)}) collective-permute-start(bf16[7232,128]{1,0:T(8,128)(2,1)} %get-tuple-element.65), channel_id=1, source_target_pairs={{0,1},{1,0},{2,3},{3,2},{4,5},{5,4},{6,7},{7,6},{8,9},{9,8},{10,11... | collective-permute-start | bytes 5554184 | tf_op jit(solution)/shard_map/ppermute | solution.py:950
  55.9 18.8 %collective-permute-start.18 = (bf16[2,1280,128]{2,1,0:T(8,128)(2,1)S(1)}, bf16[2,1280,128]{2,1,0:T(8,128)(2,1)S(1)}, u32[]{:S(2)}, u32[]{:S(2)}) collective-permute-start(bf16[2,1280,128]{2,1,0:T(8,128)(2,1)S(1)} %get-tuple-element.81), channel_id=1, source_target_pairs={{0,2},{2,0},{4,6},{6,4},{8,10},{10,8},{12,14},{14,12},{16,18},{18,... | collective-permute-start | bytes 1966088 | tf_op jit(solution)/shard_map/ppermute | solution.py:953
  57.2 19.5 %collective-permute-start.20 = (bf16[2,1280,128]{2,1,0:T(8,128)(2,1)S(1)}, bf16[2,1280,128]{2,1,0:T(8,128)(2,1)S(1)}, u32[]{:S(2)}, u32[]{:S(2)}) collective-permute-start(bf16[2,1280,128]{2,1,0:T(8,128)(2,1)S(1)} %get-tuple-element.83), channel_id=1, source_target_pairs={{0,4},{2,6},{4,0},{6,2},{8,12},{10,14},{12,8},{14,10},{16,20},{18,... | collective-permute-start | bytes 1966088 | tf_op jit(solution)/shard_map/ppermute | solution.py:953
  60.3 23.9 %collective-permute-start.14 = (bf16[8,480,128]{2,1,0:T(8,128)(2,1)S(1)}, bf16[8,480,128]{2,1,0:T(8,128)(2,1)S(1)}, u32[]{:S(2)}, u32[]{:S(2)}) collective-permute-start(bf16[8,480,128]{2,1,0:T(8,128)(2,1)S(1)} %get-tuple-element.79), channel_id=1, source_target_pairs={{0,8},{2,10},{4,12},{6,14},{8,0},{10,2},{12,4},{14,6},{16,24},{18,... | collective-permute-start | bytes 2949128 | tf_op jit(solution)/shard_map/ppermute | solution.py:953
  62.6 12.0 %copy-start.3 = (bf16[2,1280,128]{2,1,0:T(8,128)(2,1)S(1)}, bf16[2,1280,128]{2,1,0:T(8,128)(2,1)}, u32[]{:S(2)}) copy-start(bf16[2,1280,128]{2,1,0:T(8,128)(2,1)} %copy-done.2) | copy-start | bytes 1966084
  74.5 14.9 %collective-permute-start.6 = (bf16[4,976,128]{2,1,0:T(8,128)(2,1)}, bf16[4,976,128]{2,1,0:T(8,128)(2,1)S(1)}, u32[]{:S(2)}, u32[]{:S(2)}) collective-permute-start(bf16[4,976,128]{2,1,0:T(8,128)(2,1)} %get-tuple-element.70), channel_id=1, source_target_pairs={{0,1},{1,0},{2,3},{3,2},{4,5},{5,4},{6,7},{7,6},{8,9},{9,8},{10,11... | collective-permute-start | bytes 2998280 | tf_op jit(solution)/shard_map/ppermute | solution.py:950
  74.8 11.1 %collective-permute-start.19 = (bf16[1,1280,128]{2,1,0:T(8,128)(2,1)S(1)}, bf16[1,1280,128]{2,1,0:T(8,128)(2,1)S(1)}, u32[]{:S(2)}, u32[]{:S(2)}) collective-permute-start(bf16[1,1280,128]{2,1,0:T(8,128)(2,1)S(1)} %get-tuple-element.98), channel_id=1, source_target_pairs={{0,4},{2,6},{4,0},{6,2},{8,12},{10,14},{12,8},{14,10},{16,20},{18,... | collective-permute-start | bytes 983048 | tf_op jit(solution)/shard_map/ppermute | solution.py:953
  76.9 9.0 %collective-permute-start.21 = (bf16[1,1280,128]{2,1,0:T(8,128)(2,1)S(1)}, bf16[1,1280,128]{2,1,0:T(8,128)(2,1)S(1)}, u32[]{:S(2)}, u32[]{:S(2)}) collective-permute-start(bf16[1,1280,128]{2,1,0:T(8,128)(2,1)S(1)} %get-tuple-element.96), channel_id=1, source_target_pairs={{0,2},{2,0},{4,6},{6,4},{8,10},{10,8},{12,14},{14,12},{16,18},{18,... | collective-permute-start | bytes 983048 | tf_op jit(solution)/shard_map/ppermute | solution.py:953
  84.1 5.3 %copy-start.8 = (bf16[4,976,128]{2,1,0:T(8,128)(2,1)S(1)}, bf16[4,976,128]{2,1,0:T(8,128)(2,1)}, u32[]{:S(2)}) copy-start(bf16[4,976,128]{2,1,0:T(8,128)(2,1)} %get-tuple-element.69) | copy-start | bytes 2998276
  84.4 31.9 %collective-permute-start.15 = (bf16[4,480,128]{2,1,0:T(8,128)(2,1)S(1)}, bf16[4,480,128]{2,1,0:T(8,128)(2,1)S(1)}, u32[]{:S(2)}, u32[]{:S(2)}) collective-permute-start(bf16[4,480,128]{2,1,0:T(8,128)(2,1)S(1)} %get-tuple-element.95), channel_id=1, source_target_pairs={{0,2},{2,0},{4,6},{6,4},{8,10},{10,8},{12,14},{14,12},{16,18},{18,... | collective-permute-start | bytes 1474568 | tf_op jit(solution)/shard_map/ppermute | solution.py:953
  86.9 8.5 %collective-permute-start.22 = (bf16[2,640,128]{2,1,0:T(8,128)(2,1)S(1)}, bf16[2,640,128]{2,1,0:T(8,128)(2,1)S(1)}, u32[]{:S(2)}, u32[]{:S(2)}) collective-permute-start(bf16[2,640,128]{2,1,0:T(8,128)(2,1)S(1)} %get-tuple-element.85), channel_id=1, source_target_pairs={{0,8},{2,10},{4,12},{6,14},{8,0},{10,2},{12,4},{14,6},{16,24},{18,... | collective-permute-start | bytes 983048 | tf_op jit(solution)/shard_map/ppermute | solution.py:953
  89.8 17.7 %collective-permute-start.7 = (bf16[1616,128]{1,0:T(8,128)(2,1)S(1)}, bf16[1616,128]{1,0:T(8,128)(2,1)S(1)}, u32[]{:S(2)}, u32[]{:S(2)}) collective-permute-start(bf16[1616,128]{1,0:T(8,128)(2,1)S(1)} %pad_maximum_fusion), channel_id=1, source_target_pairs={{0,2},{2,0},{4,6},{6,4},{8,10},{10,8},{12,14},{14,12},{16,18},{18,... | collective-permute-start | bytes 1241096 | tf_op jit(solution)/shard_map/ppermute | solution.py:953
  90.0 17.4 %collective-permute-start.8 = (bf16[1616,128]{1,0:T(8,128)(2,1)S(1)}, bf16[1616,128]{1,0:T(8,128)(2,1)S(1)}, u32[]{:S(2)}, u32[]{:S(2)}) collective-permute-start(bf16[1616,128]{1,0:T(8,128)(2,1)S(1)} %pad_maximum_fusion.1), channel_id=1, source_target_pairs={{0,4},{2,6},{4,0},{6,2},{8,12},{10,14},{12,8},{14,10},{16,20},{18,... | collective-permute-start | bytes 1241096 | tf_op jit(solution)/shard_map/ppermute | solution.py:953
  91.0 23.7 %collective-permute-start.9 = (bf16[1616,128]{1,0:T(8,128)(2,1)S(1)}, bf16[1616,128]{1,0:T(8,128)(2,1)S(1)}, u32[]{:S(2)}, u32[]{:S(2)}) collective-permute-start(bf16[1616,128]{1,0:T(8,128)(2,1)S(1)} %pad_maximum_fusion.2), channel_id=1, source_target_pairs={{0,6},{2,4},{4,2},{6,0},{8,14},{10,12},{12,10},{14,8},{16,22},{18,... | collective-permute-start | bytes 1241096 | tf_op jit(solution)/shard_map/ppermute | solution.py:953
  95.5 26.7 %copy-start.4 = (f32[128,640]{1,0:T(8,128)S(1)}, f32[128,640]{1,0:T(8,128)}, u32[]{:S(2)}) copy-start(f32[128,640]{1,0:T(8,128)} %get-tuple-element.67.refs_0_) | copy-start | bytes 983044
  95.5 28.3 %collective-permute-start.23 = (bf16[1,640,128]{2,1,0:T(8,128)(2,1)S(1)}, bf16[1,640,128]{2,1,0:T(8,128)(2,1)S(1)}, u32[]{:S(2)}, u32[]{:S(2)}) collective-permute-start(bf16[1,640,128]{2,1,0:T(8,128)(2,1)S(1)} %get-tuple-element.102), channel_id=1, source_target_pairs={{0,16},{2,18},{4,20},{6,22},{8,24},{10,26},{12,28},{14,30},{16,0},... | collective-permute-start | bytes 491528 | tf_op jit(solution)/shard_map/ppermute | solution.py:953
  116.4 11.8 %collective-permute-start.16 = (bf16[2,480,128]{2,1,0:T(8,128)(2,1)S(1)}, bf16[2,480,128]{2,1,0:T(8,128)(2,1)S(1)}, u32[]{:S(2)}, u32[]{:S(2)}) collective-permute-start(bf16[2,480,128]{2,1,0:T(8,128)(2,1)S(1)} %get-tuple-element.101), channel_id=1, source_target_pairs={{0,4},{2,6},{4,0},{6,2},{8,12},{10,14},{12,8},{14,10},{16,20},{18,... | collective-permute-start | bytes 737288 | tf_op jit(solution)/shard_map/ppermute | solution.py:953
  117.6 8.8 %collective-permute-start.13 = (bf16[256,128]{1,0:T(8,128)(2,1)S(1)}, bf16[256,128]{1,0:T(8,128)(2,1)S(1)}, u32[]{:S(2)}, u32[]{:S(2)}) collective-permute-start(bf16[256,128]{1,0:T(8,128)(2,1)S(1)} %get-tuple-element.109), channel_id=1, source_target_pairs={{0,24},{2,26},{4,28},{6,30},{8,16},{10,18},{12,20},{14,22},{16,8},... | collective-permute-start | bytes 196616 | tf_op jit(solution)/shard_map/ppermute | solution.py:953
  121.6 5.5 %collective-permute-start.12 = (bf16[256,128]{1,0:T(8,128)(2,1)S(1)}, bf16[256,128]{1,0:T(8,128)(2,1)S(1)}, u32[]{:S(2)}, u32[]{:S(2)}) collective-permute-start(bf16[256,128]{1,0:T(8,128)(2,1)S(1)} %get-tuple-element.110), channel_id=1, source_target_pairs={{0,16},{2,18},{4,20},{6,22},{8,24},{10,26},{12,28},{14,30},{16,0},... | collective-permute-start | bytes 196616 | tf_op jit(solution)/shard_map/ppermute | solution.py:953
  121.6 5.5 %collective-permute-start.11 = (bf16[256,128]{1,0:T(8,128)(2,1)S(1)}, bf16[256,128]{1,0:T(8,128)(2,1)S(1)}, u32[]{:S(2)}, u32[]{:S(2)}) collective-permute-start(bf16[256,128]{1,0:T(8,128)(2,1)S(1)} %get-tuple-element.111), channel_id=1, source_target_pairs={{0,8},{2,10},{4,12},{6,14},{8,0},{10,2},{12,4},{14,6},{16,24},{18,... | collective-permute-start | bytes 196616 | tf_op jit(solution)/shard_map/ppermute | solution.py:953
  122.2 10.1 %copy-start.5 = (f32[128,640]{1,0:T(8,128)S(1)}, f32[128,640]{1,0:T(8,128)}, u32[]{:S(2)}) copy-start(f32[128,640]{1,0:T(8,128)} %get-tuple-element.54.refs_2_) | copy-start | bytes 983044
  122.2 10.1 %copy-start.6 = (bf16[144,640]{1,0:T(8,128)(2,1)S(1)}, bf16[144,640]{1,0:T(8,128)(2,1)}, u32[]{:S(2)}) copy-start(bf16[144,640]{1,0:T(8,128)(2,1)} %get-tuple-element.50.refs_4_.refs_0_) | copy-start | bytes 552964
  122.2 10.1 %copy-start.7 = (f32[1,3072]{1,0:T(1,128)S(1)}, f32[1,3072]{1,0:T(1,128)}, u32[]{:S(2)}) copy-start(f32[1,3072]{1,0:T(1,128)} %get-tuple-element.53.refs_5_.refs_1_) | copy-start | bytes 36868
  123.8 8.5 %collective-permute-start.10 = (bf16[640,128]{1,0:T(8,128)(2,1)S(1)}, bf16[640,128]{1,0:T(8,128)(2,1)S(1)}, u32[]{:S(2)}, u32[]{:S(2)}) collective-permute-start(bf16[640,128]{1,0:T(8,128)(2,1)S(1)} %get-tuple-element.72), channel_id=1, source_target_pairs={{8,0},{10,2},{12,4},{14,6},{16,8},{18,10},{20,12},{22,14},{24,16},... | collective-permute-start | bytes 491528 | tf_op jit(solution)/shard_map/ppermute | solution.py:24
  128.3 8.0 %collective-permute-start.17 = (bf16[1,480,128]{2,1,0:T(8,128)(2,1)S(1)}, bf16[1,480,128]{2,1,0:T(8,128)(2,1)S(1)}, u32[]{:S(2)}, u32[]{:S(2)}) collective-permute-start(bf16[1,480,128]{2,1,0:T(8,128)(2,1)S(1)} %get-tuple-element.107), channel_id=1, source_target_pairs={{0,16},{2,18},{4,20},{6,22},{8,24},{10,26},{12,28},{14,30},{16,0},... | collective-permute-start | bytes 368648 | tf_op jit(solution)/shard_map/ppermute | solution.py:953
  (6 other events, 11.8 us)

commit v3 on v2

--- a/solution.py
+++ b/solution.py
@@ -268,11 +268,10 @@
     return jnp.concatenate(rows, axis=1)
 
 
-def row_order(table, place, core):
-    width = table.shape[0]
+def row_order(table, width, place, core):
     owner = table[:, :1] ^ (place * 2 + core)
     source = owner * (width // (2 * XY * LINE)) + table[:, 1:2]
-    ranks = lax.broadcasted_iota(jnp.int32, (width, width), 1)
+    ranks = lax.broadcasted_iota(jnp.int32, (table.shape[0], width), 1)
     return jnp.where(ranks == source, 1.0, 0.0).astype(BF16)
 
 
@@ -411,23 +410,36 @@
         q_out[:, cols] = q
         s = jnp.where(allowed, mm_nt(q, k), -1e30)
         e = jnp.exp(s - jnp.max(s, axis=-1, keepdims=True))
-        p = e / jnp.sum(e, axis=-1, keepdims=True)
+        p = e * (1.0 / jnp.sum(e, axis=-1, keepdims=True))
         p_out[h] = p
         ao_out[:, cols] = mm(p.astype(BF16), v).astype(BF16)
 
 
-def pick_half(core, unit, width):
-    row = lax.broadcasted_iota(jnp.int32, (LANES, width), 0)
-    col = lax.broadcasted_iota(jnp.int32, (LANES, width), 1)
-    want = (lax.div(row, unit) * 2 + core) * unit + lax.rem(row, unit)
-    return jnp.where(col == want, 1.0, 0.0).astype(BF16)
-
-
-def store_lanes(ref, base, value):
-    rows = value.shape[0]
-    for b in range(value.shape[1] // LANES):
-        ref[base + b * rows : base + (b + 1) * rows, :] = value[:, b * LANES : (b + 1) * LANES]
-    return base + rows * (value.shape[1] // LANES)
+def pick_halves(core, unit):
+    row = lax.broadcasted_iota(jnp.int32, (2 * LANES, 2 * LANES), 0)
+    col = lax.broadcasted_iota(jnp.int32, (2 * LANES, 2 * LANES), 1)
+    side = jnp.where(col < LANES, core, 1 - core)
+    at = col & (LANES - 1)
+    want = (lax.div(at, unit) * 2 + side) * unit + lax.rem(at, unit)
+    return jnp.where(row == want, 1.0, 0.0).astype(BF16)
+
+
+def store_halves(keep, send, base, source, unit, core):
+    pick = pick_halves(core, unit)
+    for b in range(source.shape[1] // (2 * LANES)):
+        block = mm(source[:, 2 * b * LANES : 2 * (b + 1) * LANES], pick).astype(BF16)
+        keep[:, base + b * LANES : base + (b + 1) * LANES] = block[:, :LANES]
+        send[:, base + b * LANES : base + (b + 1) * LANES] = block[:, LANES:]
+
+
+def pair_columns(width, ff, attn):
+    sizes = (ff, ff, width, width, ff // 2, attn // 2, padded(width // 2))
+    starts = [sum(sizes[:n]) for n in range(len(sizes) + 1)]
+    return starts[:-1], starts[-1]
+
+
+def padded(columns):
+    return -(-columns // LANES) * LANES
 
 
 def forward_kernel(reach, layout, *refs):
@@ -438,7 +450,7 @@
     halo, refs = refs[: reach + 1], refs[reach + 1 :]
     ct, gain_a, order, cos_ref, sin_ref = refs[:5]
     outs, refs = refs[5:19], refs[19:]
-    wq, wk, wv, wo, wg, wu, wd, gate_s, up_s, hid_s, dg_s, du_s, ao_ref, gain_b, sems = refs
+    wq, wk, wv, wo, wg, wu, wd, act_s, slope_s, hid_s, ao_ref, gain_b, sems = refs
     place, core = lax.axis_index("seq"), lax.axis_index("fsdp")
     traffic = Traffic(sems)
     waits = {}
@@ -498,71 +510,74 @@
     ready("rest")
     c = ct[...].astype(F32)
     part = 512
+    (at_gate, at_up, at_df, at_dya, at_hid, at_ao, at_n2), end = pair_columns(
+        width, ff, ao_ref.shape[1]
+    )
+    keep_h, send_h = outs_h[11:13]
+
+    def sent(begin, stop):
+        for ref, target in ((send, send_h), (keep, keep_h)):
+            traffic.emit(ref.at[:, begin:stop], target.at[:, begin:stop])
+
+    n2_owned = mm_nt(n2, row_order(order, width, place, core)).astype(BF16)
+    half = n2_owned.shape[1] // 2
+    keep[:, at_n2:end] = n2_owned[:, :half]
+    send[:, at_n2:end] = n2_owned[:, half:]
+    store_halves(keep, send, at_ao, ao_ref, ao_ref.shape[1] // 32, core)
+    sent(at_ao, end)
     root = math.sqrt(2.0 / math.pi)
     f = jnp.zeros((rows, width), F32)
     for at in range(0, ff, part):
         cols = slice(at, at + part)
         gate = mm(n2, wg[:, cols])
         up = mm(n2, wu[:, cols])
-        gate_s[:, cols] = gate
-        up_s[:, cols] = up
-        t = jnp.tanh(root * (gate + 0.044715 * (gate * gate * gate)))
-        hid = (0.5 * gate * (1.0 + t) * up).astype(BF16)
-        hid_s[:, cols] = hid
-        f = f + mm(hid, wd[cols, :])
-    inv_d = inverse_rms(f)
-    hat_d = f * inv_d
-    mixed_out[...] = (x2 + hat_d * g_pff).astype(BF16)
-    df = norm_back(hat_d, inv_d, g_pff, c).astype(BF16)
-    dn2 = jnp.zeros((rows, width), F32)
-    for at in range(0, ff, part):
-        cols = slice(at, at + part)
-        dhid = mm_nt(df, wd[cols, :])
-        gate = gate_s[:, cols]
-        up = up_s[:, cols]
         t = jnp.tanh(root * (gate + 0.044715 * (gate * gate * gate)))
         act = 0.5 * gate * (1.0 + t)
         slope = 0.5 * (1.0 + t) + 0.5 * gate * (1.0 - t * t) * (
             root * (1.0 + 3.0 * 0.044715 * (gate * gate))
         )
-        dgate = (dhid * up * slope).astype(BF16)
-        dup = (dhid * act).astype(BF16)
-        dg_s[:, cols] = dgate
-        du_s[:, cols] = dup
+        act_s[:, cols] = act
+        slope_s[:, cols] = up * slope
+        hid = (act * up).astype(BF16)
+        hid_s[:, cols] = hid
+        f = f + mm(hid, wd[cols, :])
+    store_halves(keep, send, at_hid, hid_s, ff // 32, core)
+    sent(at_hid, at_ao)
+    inv_d = inverse_rms(f)
+    hat_d = f * inv_d
+    mixed_out[...] = (x2 + hat_d * g_pff).astype(BF16)
+    traffic.emit(mixed_out, outs_h[7])
+    df = norm_back(hat_d, inv_d, g_pff, c).astype(BF16)
+    for ref in (send, keep):
+        ref[:, at_df : at_df + width] = df
+    sent(at_df, at_df + width)
+    dn2 = jnp.zeros((rows, width), F32)
+    for at in range(0, ff, part):
+        cols = slice(at, at + part)
+        dhid = mm_nt(df, wd[cols, :])
+        dgate = (dhid * slope_s[:, cols]).astype(BF16)
+        dup = (dhid * act_s[:, cols]).astype(BF16)
+        for ref in (send, keep):
+            ref[:, at_gate + at : at_gate + at + part] = dgate
+            ref[:, at_up + at : at_up + at + part] = dup
+        sent(at_gate + at, at_gate + at + part)
+        sent(at_up + at, at_up + at + part)
         dn2 = dn2 + mm_nt(dgate, wg[:, cols]) + mm_nt(dup, wu[:, cols])
     dx2 = c + norm_back(hat_f, inv_f, g_pf, dn2)
+    dya = norm_back(hat_a, inv_a, g_pa, dx2).astype(BF16)
+    for ref in (send, keep):
+        ref[:, at_dya : at_dya + width] = dya
+    sent(at_dya, at_dya + width)
+    dao_out[...] = mm_nt(dya, wo[...]).astype(BF16)
+    traffic.emit(dao_out, outs_h[9])
     dx_out[...] = dx2
-    dya = norm_back(hat_a, inv_a, g_pa, dx2).astype(BF16)
-    dao_out[...] = mm_nt(dya, wo[...]).astype(BF16)
+    traffic.emit(dx_out, outs_h[8])
     dg_out[:, :width] = jnp.sum(dx2 * hat_a, axis=0, keepdims=True)
     dg_out[:, width : 2 * width] = jnp.sum(dn2 * hat_f, axis=0, keepdims=True)
     dg_out[:, 2 * width :] = jnp.sum(c * hat_d, axis=0, keepdims=True)
-    perm = row_order(order, place, core)
-    n2_t = mm_nt(perm, n2).astype(BF16)
-    half = width // 2
-    keep[:half, :] = n2_t[:half]
-    send[:half, :] = n2_t[half:]
-    at = half
-    for source, unit in ((hid_s, ff // 32), (ao_ref, ao_ref.shape[1] // 32)):
-        for ref, side in ((keep, core), (send, 1 - core)):
-            pick = pick_half(side, unit, 2 * LANES)
-            for b in range(source.shape[1] // (2 * LANES)):
-                block = source[:, 2 * b * LANES : 2 * (b + 1) * LANES]
-                ref[at + b * LANES : at + (b + 1) * LANES, :] = mm_nt(pick, block).astype(BF16)
-        at += source.shape[1] // 2
-    for ref in (keep, send):
-        base = store_lanes(ref, at, dg_s[...])
-        base = store_lanes(ref, base, du_s[...])
-        base = store_lanes(ref, base, df)
-        store_lanes(ref, base, dya)
-    for source, target in zip(outs[7:], outs_h[7:]):
-        traffic.emit(source, target)
+    traffic.emit(dg_out, outs_h[10])
+    traffic.emit(gains_out, outs_h[13])
     traffic.finish()
-
-
-def load_lanes(ref, base, rows, cols):
-    blocks = [ref[base + b * rows : base + (b + 1) * rows, :] for b in range(cols // LANES)]
-    return jnp.concatenate(blocks, axis=1), base + rows * (cols // LANES)
 
 
 def put(xk, xs, first, plane, at, value):
@@ -573,56 +588,34 @@
 
 
 def grads_kernel(width, ff, attn, *refs):
-    sources = refs[:2]
-    outs_h = refs[2:8]
-    outs = refs[8:14]
+    sources, outs_h, outs = refs[:2], refs[3:9], refs[9:15]
     gk, gs, uk, us, dk, ds = outs
-    n2_s, hid_s, ao_s, gate_s, up_s, df_s, dya_s, prod_s, sems = refs[14:]
+    both, prod_s, sems = refs[15:]
     traffic = Traffic(sems)
     place = lax.axis_index("seq")
-    half = width // 2
-    rows = LANES
+    (at_gate, at_up, at_df, at_dya, at_hid, at_ao, at_n2), end = pair_columns(width, ff, attn)
 
     def sent(ref):
         traffic.emit(ref, outs_h[[r is ref for r in outs].index(True)])
 
-    def lefts(base, target):
-        return [
-            traffic.start(
-                source.at[base : base + target.shape[0], :],
-                target.at[:, side * rows : (side + 1) * rows],
-            )
+    def fetch(begin, stop):
+        return traffic.fetch(
+            (source.at[:, begin:stop], both.at[side * LANES : (side + 1) * LANES, begin:stop])
             for side, source in enumerate(sources)
-        ]
-
-    def rights(base, target):
-        return [
-            traffic.start(
-                source.at[base + b * rows : base + (b + 1) * rows, :],
-                target.at[side * rows : (side + 1) * rows, b * LANES : (b + 1) * LANES],
-            )
-            for side, source in enumerate(sources)
-            for b in range(target.shape[1] // LANES)
-        ]
-
-    at_hid = half
-    at_ao = at_hid + ff // 2
-    at_gate = at_ao + attn // 2
-    at_up = at_gate + ff
-    at_df = at_up + ff
-    at_dya = at_df + width
-    per = half // XY
-    gate_w = lefts(0, n2_s) + rights(at_gate, gate_s)
-    up_w = rights(at_up, up_s)
-    down_w = lefts(at_hid, hid_s) + rights(at_df, df_s)
-    out_w = lefts(at_ao, ao_s) + rights(at_dya, dya_s)
-    for copies, right, (keep, send), first in (
-        (gate_w, gate_s, (gk, gs), "x"),
-        (up_w, up_s, (uk, us), "y"),
+        )
+
+    gate_w = fetch(at_n2, end) + fetch(at_gate, at_up)
+    up_w = fetch(at_up, at_df)
+    rest_w = fetch(at_df, at_n2)
+    per = width // 2 // XY
+    for copies, base, (keep, send), first in (
+        (gate_w, at_gate, (gk, gs), "x"),
+        (up_w, at_up, (uk, us), "y"),
     ):
         wait(copies)
         for col in range(0, ff, 512):
-            out = mm(n2_s[...], right[:, col : col + 512]).astype(BF16)
+            right = both[:, base + col : base + col + 512]
+            out = mm_tn(both[:, at_n2:end], right).astype(BF16)
             for plane in range(XY):
                 for b in range(4):
                     put(
@@ -635,18 +628,18 @@
                     )
         sent(send)
         sent(keep)
+    wait(rest_w)
     row = 0
-    for copies, left, right in ((down_w, hid_s, df_s), (out_w, ao_s, dya_s)):
-        wait(copies)
-        count = left.shape[0]
-        prod_s[:count, :] = mm(left[...], right[...])
+    for at_left, at_right, count in ((at_hid, at_df, ff // 2), (at_ao, at_dya, attn // 2)):
+        left, right = both[:, at_left : at_left + count], both[:, at_right : at_right + width]
+        prod_s[:count, :] = mm_tn(left, right)
         unit = count // (XY * LINE)
         for plane in range(XY):
             for line in range(LINE):
                 whose = (place ^ (line * XY + plane)) * unit
                 block = prod_s[pl.ds(pl.multiple_of(whose, unit), unit), :].astype(BF16)
                 ref = ds if line & 1 else dk
-                chunk = (plane & 1) * 4 + (plane >> 1) * 2 + (line >> 1)
+                chunk = (plane >> 1) * 4 + (plane & 1) * 2 + (line >> 1)
                 for b in range(width // LANES):
                     ref[chunk, row + b * unit : row + (b + 1) * unit, :] = block[
                         :, b * LANES : (b + 1) * LANES
@@ -657,48 +650,24 @@
     traffic.finish()
 
 
-def back_kernel(reach, layout, *refs):
-    count = reach + 15
-    ins_h, refs = refs[:count], refs[count:]
-    _, wq_a, wk_a, wv_a, pack_h = refs[:5]
-    outs_h, refs = refs[5:9], refs[9:]
-    ins, refs = refs[:count], refs[count:]
-    halo = ins[: reach + 1]
-    (
-        gains,
-        order,
-        scale_order,
-        dg_post,
-        cos_ref,
-        sin_ref,
-        n1_ref,
-        qraw_ref,
-        q_ref,
-        kraw_ref,
-        k_ref,
-        v_ref,
-        p_ref,
-        dao_ref,
-    ) = ins[reach + 1 :]
-    outs = keep, send, dn1_own, dn1_far = refs[:4]
-    wq, wk, wv, dqr_s, dkv_s, sems = refs[4:]
-    place, core = lax.axis_index("seq"), lax.axis_index("fsdp")
+def heads_kernel(*refs):
+    count = 9
+    ins_h, outs_h, refs = refs[:count], refs[count : count + 4], refs[count + 4 :]
+    ins, outs, sems = refs[:count], refs[count : count + 4], refs[-1]
+    gains, cos_ref, sin_ref, qraw_ref, q_ref, k_ref, v_ref, dao_ref, p_ref = ins
+    dqr, dkr, dv_out, dgq_out = outs
     traffic = Traffic(sems)
     heads = p_ref.shape[0]
-    first = traffic.fetch([(ins_h[n], ins[n]) for n in (count - 1, count - 3, count - 4)])
-    p_w = traffic.fetch([(ins_h[count - 2].at[h], p_ref.at[h]) for h in range(heads)])
-    second = traffic.fetch([(ins_h[n], ins[n]) for n in range(reach + 1, count - 4)])
-    copies = traffic.fetch(list(zip(ins_h[: reach + 1], halo)))
-    for n, (mine, full) in enumerate(((wq_a, wq), (wk_a, wk), (wv_a, wv))):
-        copies += traffic.halves(core, mine, pack_h, layout[n], full)
+    first = traffic.fetch([(ins_h[n], ins[n]) for n in (7, 6, 5)])
+    p_w = [traffic.start(ins_h[8].at[0], p_ref.at[0])]
+    second = traffic.fetch([(ins_h[n], ins[n]) for n in range(5)])
+    p_w += [traffic.start(ins_h[8].at[h], p_ref.at[h]) for h in range(1, heads)]
     wait(first)
-    rows = halo[0].shape[0] - SEG_ROWS
-    width = n1_ref.shape[1]
-    size = k_ref.shape[1]
+    rows, size = q_ref.shape[0], k_ref.shape[1]
+    keys = k_ref.shape[0]
+    width = gains.shape[1] // 4 - size // 2
     scale = size ** (-0.5)
-    k = k_ref[...]
-    v = v_ref[...]
-    keys = (reach + 1) * rows
+    k, v = k_ref[...], v_ref[...]
     dk = jnp.zeros((keys, size), F32)
     dv = jnp.zeros((keys, size), F32)
     dgq = jnp.zeros((1, size), F32)
@@ -713,34 +682,66 @@
         if h == 0:
             wait(second)
             g_q = gains[:, width : width + size]
-            g_k = gains[:, width + size : width + 2 * size]
-            cos_own, sin_own = cos_ref[reach * rows :, :], sin_ref[reach * rows :, :]
+            cos_own, sin_own = cos_ref[keys - rows :, :], sin_ref[keys - rows :, :]
         dk = dk + mm_tn(ds, q_ref[:, cols])
         dq = turn_bwd(mm(ds, k) * scale, cos_own, sin_own)
         qraw = qraw_ref[:, cols]
         inv = inverse_rms(qraw)
         hat = qraw * inv
         dgq = dgq + jnp.sum(dq * hat, axis=0, keepdims=True)
-        dqr_s[:, cols] = norm_back(hat, inv, g_q, dq).astype(BF16)
-    dk = turn_bwd(dk, cos_ref[...], sin_ref[...])
+        dqr[:, cols] = norm_back(hat, inv, g_q, dq).astype(BF16)
+    dkr[...] = turn_bwd(dk, cos_ref[...], sin_ref[...])
+    dv_out[...] = dv.astype(BF16)
+    dgq_out[...] = dgq
+    for source, target in zip(outs, outs_h):
+        traffic.emit(source, target)
+    traffic.finish()
+
+
+def back_kernel(reach, layout, *refs):
+    count = reach + 11
+    ins_h, refs = refs[:count], refs[count:]
+    _, wq_a, wk_a, wv_a, pack_h = refs[:5]
+    outs_h, refs = refs[5:9], refs[9:]
+    ins, refs = refs[:count], refs[count:]
+    halo = ins[: reach + 1]
+    gains, order, scale_order, dg_post, dgq, n1_ref, kraw_ref, dkr, dqr, dv_ref = ins[reach + 1 :]
+    outs = keep, send, dn1_own, dn1_far = refs[:4]
+    wq, wk, wv, dkv_s, sems = refs[4:]
+    place, core = lax.axis_index("seq"), lax.axis_index("fsdp")
+    traffic = Traffic(sems)
+    first = traffic.fetch([(ins_h[n], ins[n]) for n in (reach + 2, reach + 6)])
+    second = traffic.fetch([(ins_h[n], ins[n]) for n in range(reach + 7, count)])
+    second += traffic.fetch([(ins_h[reach + 1], ins[reach + 1])])
+    copies = traffic.fetch([(ins_h[n], ins[n]) for n in range(reach + 3, reach + 6)])
+    copies += traffic.fetch(list(zip(ins_h[: reach + 1], halo)))
+    for n, (mine, full) in enumerate(((wq_a, wq), (wk_a, wk), (wv_a, wv))):
+        copies += traffic.halves(core, mine, pack_h, layout[n], full)
+    rows = halo[0].shape[0] - SEG_ROWS
+    width = n1_ref.shape[1]
+    size = kraw_ref.shape[1]
+    wait(first)
+    perm = row_order(order, width, place, core)
+    n1_t = mm_nt(perm, n1_ref[...]).astype(BF16)
+    wait(second)
+    g_k = gains[:, width + size : width + 2 * size]
     kraw = kraw_ref[...]
     inv = inverse_rms(kraw)
     hat = kraw * inv
+    dk = dkr[...]
     dgk = jnp.sum(dk * hat, axis=0, keepdims=True)
     dkv_s[:, :size] = norm_back(hat, inv, g_k, dk).astype(BF16)
-    dkv_s[:, size:] = dv.astype(BF16)
-    perm = row_order(order, place, core)
-    n1_t = mm_nt(perm, n1_ref[...]).astype(BF16)
+    dkv_s[:, size:] = dv_ref[...]
     half = width // 2
     per = half // XY
-    attn = heads * size
+    attn = dqr.shape[1]
     wait(copies)
     dgi = jnp.zeros((1, width), F32)
     for block in range(reach + 1):
         span = slice(block * rows, (block + 1) * rows)
         dn1 = mm_nt(dkv_s[span, :size], wk[...]) + mm_nt(dkv_s[span, size:], wv[...])
         if block == reach:
-            dn1 = dn1 + mm_nt(dqr_s[...], wq[...])
+            dn1 = dn1 + mm_nt(dqr[...], wq[...])
         x = halo[block][:rows, :].astype(F32)
         dgi = dgi + jnp.sum(dn1 * (x * inverse_rms(x)), axis=0, keepdims=True)
         if block == reach:
@@ -750,7 +751,7 @@
             low = dn1.astype(BF16)
             for b in range(width // LANES):
                 dn1_far[bits, b * rows : (b + 1) * rows, :] = low[:, b * LANES : (b + 1) * LANES]
-    scales = owners_rows(jnp.concatenate([dgi, dgq, dgk, dg_post[...]], axis=1))
+    scales = owners_rows(jnp.concatenate([dgi, dgq[...], dgk, dg_post[...]], axis=1))
     owner = scale_order[:, :1] ^ (place * 2 + core)
     mine = scale_order[:, 1:2] * 1024 + (owner & 3) * 8 + (owner >> 2)
     columns = lax.broadcasted_iota(jnp.int32, (mine.shape[0], 2 * XY * LINE), 1)
@@ -761,7 +762,7 @@
         own = left[:, reach * rows :]
         at = 0
         for value, left_part, total in (
-            (dqr_s, own, attn),
+            (dqr, own, attn),
             (dkv_s, left, 2 * size),
         ):
             for col in range(0, total, 512):
@@ -804,34 +805,30 @@
 
 
 def collect_kernel(skip, *refs):
-    ins_h, outs_h = refs[: XY + 1], refs[XY + 1 : XY + 3]
-    ins, outs, sems = refs[XY + 3 : 2 * XY + 4], refs[2 * XY + 4 : 2 * XY + 6], refs[-1]
+    own_h, far_h, *near = refs[: XY + 1]
+    total_out, below_out, own, far, sems = refs[XY + 3 :]
     traffic = Traffic(sems)
-    own, far, *near = ins
-    near_h = [ref.at[skip:, :] for ref in ins_h[2:]]
-    wait(traffic.fetch(list(zip((ins_h[0], ins_h[1].at[0], *near_h), ins))))
+    wait(traffic.fetch([(own_h, own), (far_h.at[0], far)]))
     place = lax.axis_index("seq") & (XY - 1)
     rows = own.shape[0]
     total = own[...]
     below = far[...].astype(F32)
     for bits, ref in enumerate(near, 1):
-        part = ref[...].astype(F32)
+        part = ref[skip:, :].astype(F32)
         mine = (place ^ bits) > place
         below = below + jnp.where(mine, 0.0, part)
         lanes = [part[b * rows : (b + 1) * rows] for b in range(part.shape[0] // rows)]
         total = total + jnp.where(mine, jnp.concatenate(lanes, axis=1), 0.0)
-    outs[0][...] = total
-    outs[1][...] = below.astype(BF16)
-    traffic.emit(outs[1], outs_h[1])
-    traffic.emit(outs[0], outs_h[0])
-    traffic.finish()
+    total_out[...] = total
+    below_out[...] = below.astype(BF16)
 
 
 def finish_kernel(*refs):
-    ins_h, out_h, ins, out, sems = refs[:5], refs[5], refs[6:11], refs[11], refs[12]
+    ins_h, (dn1, above), out_h, ins = refs[:3], refs[3:5], refs[5], refs[6:9]
+    out, sems = refs[9:]
     traffic = Traffic(sems)
     wait(traffic.fetch(list(zip(ins_h, ins))))
-    tok, gains, dx, dn1, above = ins
+    tok, gains, dx = ins
     rows, width = dx.shape
     lanes = [above[b * rows : (b + 1) * rows, :] for b in range(width // LANES)]
     total = dn1[...] + jnp.concatenate(lanes, axis=1).astype(F32)
@@ -842,16 +839,11 @@
     traffic.finish()
 
 
-def line_split_kernel(groups, entries, extra, direct, *refs):
+def line_split_kernel(groups, entries, extra, direct, after, *refs):
     count = sum(groups)
-    ins_h, keep_h, send_h = refs[:count], refs[count], refs[count + 1]
-    ins = refs[count + 2 : 2 * count + 2]
-    keep, send, split, *sums, sems = refs[2 * count + 2 :]
-    traffic = Traffic(sems)
-    copies = traffic.fetch(list(zip(ins_h, ins)))
+    ins, (keep, send, split, *sums) = refs[:count], refs[count + after :]
     at = 0
     for number, total in zip(groups, sums):
-        wait(copies[at : at + number])
         value = ins[at][...].astype(F32)
         for other in ins[at + 1 : at + number]:
             value = value + other[: value.shape[0], :].astype(F32)
@@ -873,19 +865,13 @@
     for ref, positions in order:
         for n, position in enumerate(positions):
             ref[n] = split[position].astype(ref.dtype)
-    traffic.emit(send, send_h)
-    traffic.emit(keep, keep_h)
-    traffic.finish()
 
 
 def join_kernel(parts, entries, extra, *refs):
     count = len(entries) + extra
-    ins_h, outs_h = refs[:parts], refs[parts : parts + count]
-    ins = refs[parts + count : 2 * parts + count]
-    outs = refs[2 * parts + count : 2 * parts + 2 * count]
-    sum_s, sems = refs[2 * parts + 2 * count :]
+    ins, outs_h, outs = refs[:parts], refs[parts : parts + count], refs[parts + count :][:count]
+    sum_s, sems = refs[parts + 2 * count :]
     traffic = Traffic(sems)
-    wait(traffic.fetch(list(zip(ins_h, ins))))
     total = ins[0][...].astype(F32)
     for part in ins[1:]:
         total = total + part[...].astype(F32)
@@ -902,7 +888,7 @@
     traffic.finish()
 
 
-def call(kernel, fetched, others, outs, scratch, copies, flops, limit=56):
+def call(kernel, fetched, others, outs, scratch, copies, limit=61):
     hbm = pl.BlockSpec(memory_space=pl.ANY)
     return pl.pallas_call(
         kernel,
@@ -913,12 +899,16 @@
         + scratch
         + [pltpu.SemaphoreType.DMA((copies,))],
         compiler_params=pltpu.CompilerParams(vmem_limit_bytes=limit * MIB),
-        cost_estimate=pl.CostEstimate(flops=flops, bytes_accessed=8 * MIB, transcendentals=0),
+        cost_estimate=pl.CostEstimate(flops=0, bytes_accessed=0, transcendentals=0),
     )(*fetched, *others)
 
 
 def shape(dims, dtype):
     return jax.ShapeDtypeStruct(dims, dtype)
+
+
+vmem = pl.BlockSpec(memory_space=pltpu.VMEM)
+hbm = pl.BlockSpec(memory_space=pl.ANY)
 
 
 def fast(
@@ -974,7 +964,7 @@
             pltpu.VMEM((16, LANES), BF16),
             pltpu.SemaphoreType.DMA((40,)),
         ],
-        compiler_params=pltpu.CompilerParams(vmem_limit_bytes=56 * MIB),
+        compiler_params=pltpu.CompilerParams(vmem_limit_bytes=61 * MIB),
     )(tokens[0], segments, *weights, gains_own)
     pack_far = partner(pack)
     halo = [shifted(tok, "seq", distance) for distance in range(reach, 0, -1)] + [tok]
@@ -984,15 +974,18 @@
     core_bit, plane, line = new // (XY * LINE), new // LINE % XY, new % LINE
     owner = (line * XY + plane) * 2 + core_bit
     order = jnp.asarray(np.stack([owner, np.arange(width) % unit], axis=1).astype(np.int32))
+    apart = np.full((2, padded(width // 2), 2), [0, 1 << 20])
+    apart[:, : width // 2] = np.stack([owner, np.arange(width) % unit], axis=1).reshape(2, -1, 2)
+    order_pair = jnp.asarray(apart.reshape(-1, 2).astype(np.int32))
     freq = np.exp(np.arange(size // 2, dtype=np.float64) * (-2.0 * math.log(10000.0) / size))
     turn = np.arange(keys, dtype=np.float64)[:, None] * freq
     cosine = jnp.asarray(np.cos(turn).astype(np.float32))
     sine = jnp.asarray(np.sin(turn).astype(np.float32))
 
-    packed = width // 2 + ff // 2 + attn // 2 + 2 * ff + 2 * width
+    pair_end = pair_columns(width, ff, attn)[1]
     n1, qraw, q, kraw, k, v, p, mixed, dx, dao, dg_post, mlp_keep, mlp_send, gains = call(
         functools.partial(forward_kernel, reach, layout),
-        (*halo, cotangent[0], gains_own, order, cosine, sine),
+        (*halo, cotangent[0], gains_own, order_pair, cosine, sine),
         (*weights, pack_far),
         [
             shape((keys, width), BF16),
@@ -1006,8 +999,8 @@
             shape((rows, width), F32),
             shape((rows, attn), BF16),
             shape((1, 3 * width), F32),
-            shape((packed, LANES), BF16),
-            shape((packed, LANES), BF16),
+            shape((rows, pair_end), BF16),
+            shape((rows, pair_end), BF16),
             shape((1, count), F32),
         ],
         [
@@ -1021,40 +1014,41 @@
             pltpu.VMEM((rows, ff), F32),
             pltpu.VMEM((rows, ff), F32),
             pltpu.VMEM((rows, ff), BF16),
-            pltpu.VMEM((rows, ff), BF16),
-            pltpu.VMEM((rows, ff), BF16),
             pltpu.VMEM((rows, attn), BF16),
             pltpu.VMEM((16, LANES), BF16),
         ],
-        72,
-        7 * 10**9,
+        128,
     )
     mlp_recv = partner(mlp_send)
+
+    dqr, dkr, dv, dgq = call(
+        heads_kernel,
+        (gains, cosine, sine, qraw, q, k, v, dao, p),
+        (),
+        [
+            shape((rows, attn), BF16),
+            shape((keys, size), F32),
+            shape((keys, size), BF16),
+            shape((1, size), F32),
+        ],
+        [],
+        24,
+    )
 
     per_ff = width // 2 // XY * ff // LANES
     per_down = ff // 2 // XY * width // LANES
     per_out = attn // 2 // XY * width // LANES
-    halves = [shape((2, per_ff, LANES), BF16)] * 2
-    halves += [shape((2, per_ff, LANES), BF16)] * 2
-    halves += [shape((8, (per_down + per_out) // LINE, LANES), BF16)] * 2
     gk, gs, uk, us, dk, ds = call(
         functools.partial(grads_kernel, width, ff, attn),
         (),
-        (mlp_keep, mlp_recv),
-        halves,
+        (mlp_keep, mlp_recv, dgq),
+        [shape((2, per_ff, LANES), BF16)] * 4
+        + [shape((8, (per_down + per_out) // LINE, LANES), BF16)] * 2,
         [
-            pltpu.VMEM((width // 2, 2 * LANES), BF16),
-            pltpu.VMEM((ff // 2, 2 * LANES), BF16),
-            pltpu.VMEM((attn // 2, 2 * LANES), BF16),
-            pltpu.VMEM((2 * LANES, ff), BF16),
-            pltpu.VMEM((2 * LANES, ff), BF16),
-            pltpu.VMEM((2 * LANES, width), BF16),
-            pltpu.VMEM((2 * LANES, width), BF16),
+            pltpu.VMEM((2 * rows, pair_end), BF16),
             pltpu.VMEM((ff // 2, width), F32),
         ],
-        128,
-        10**9,
-        32,
+        16,
     )
 
     per_q = width // 2 // XY * attn // LANES
@@ -1067,7 +1061,7 @@
     scale_order = jnp.asarray(np.stack([owner, line // LINE], axis=1).astype(np.int32))
     back_keep, back_send, dn1_own, dn1_far = call(
         functools.partial(back_kernel, reach, layout),
-        (*halo, gains, order, scale_order, dg_post, cosine, sine, n1, qraw, q, kraw, k, v, p, dao),
+        (*halo, gains, order, scale_order, dg_post, dgq, n1, kraw, dkr, dqr, dv),
         (gk, *weights[:3], pack_far),
         [
             shape((XY, per_back + 16, LANES), BF16),
@@ -1079,56 +1073,61 @@
             pltpu.VMEM((width, attn), BF16),
             pltpu.VMEM((width, size), BF16),
             pltpu.VMEM((width, size), BF16),
-            pltpu.VMEM((rows, attn), BF16),
             pltpu.VMEM((keys, 2 * size), BF16),
         ],
         64,
-        4 * 10**9,
     )
     back_recv = partner(back_send)
 
     def add(a, b):
         return (a.astype(F32) + b.astype(F32)).astype(BF16)
 
-    def step(keep, send, bits):
-        near = across(send, bits)
+    def halves(keep, near):
         half = keep.shape[0] // 2
         return add(keep[:half], near[:half]), add(keep[half:], near[half:])
 
-    def line_split(groups, entries, extra, direct):
+    def step(keep, send, bits):
+        return halves(keep, across(send, bits))
+
+    def line_split(groups, entries, extra, direct, after=()):
         part = sum(blocks * unit for _, _, blocks, unit in entries) + (16 if extra else 0)
         stay = 1 if direct else 2
-        return call(
+        arrays = [array for g in groups for array in g]
+        return pl.pallas_call(
             functools.partial(
-                line_split_kernel, [len(g) for g in groups], entries, extra, direct
+                line_split_kernel, [len(g) for g in groups], entries, extra, direct, len(after)
             ),
-            [array for g in groups for array in g],
-            (),
-            [shape((stay, part, LANES), BF16), shape((LINE - stay, part, LANES), BF16)],
-            [pltpu.VMEM((LINE, part, LANES), F32)]
+            out_shape=[shape((n, part, LANES), BF16) for n in (stay, LINE - stay)],
+            in_specs=[vmem] * len(arrays) + [hbm] * len(after),
+            out_specs=[vmem] * 2,
+            scratch_shapes=[pltpu.VMEM((LINE, part, LANES), F32)]
             + [pltpu.VMEM(g[0].shape, F32) for g in groups],
-            sum(len(g) for g in groups) + 2,
-            10**8,
-            24,
-        )
+            compiler_params=pltpu.CompilerParams(vmem_limit_bytes=12 * MIB),
+            cost_estimate=pl.CostEstimate(flops=0, bytes_accessed=0, transcendentals=0),
+        )(*arrays, *after)
 
     def join(parts, entries, extra=False):
         outs = [shape((blocks * unit, LANES), F32) for blocks, unit in entries]
         if extra:
             outs.append(shape((8, LANES), F32))
-        return call(
+        return pl.pallas_call(
             functools.partial(join_kernel, len(parts), entries, int(extra)),
-            parts,
-            (),
-            outs,
-            [pltpu.VMEM(parts[0].shape, F32)],
-            len(parts) + len(outs),
-            10**8,
-            24,
-        )
+            out_shape=outs,
+            in_specs=[vmem] * len(parts),
+            out_specs=[hbm] * len(outs),
+            scratch_shapes=[pltpu.VMEM(a.shape, a.dtype) for a in outs]
+            + [pltpu.VMEM(parts[0].shape, F32), pltpu.SemaphoreType.DMA((len(outs),))],
+            compiler_params=pltpu.CompilerParams(vmem_limit_bytes=12 * MIB),
+            cost_estimate=pl.CostEstimate(flops=0, bytes_accessed=0, transcendentals=0),
+        )(*parts)
 
     wide, narrow = ff // LANES, width // LANES
     unit_out, unit_down = attn // 32, ff // 32
+
+    planes = [add(back_keep[n], back_recv[n]) for n in range(XY)]
+    planes = [planes[0]] + [
+        across(jnp.concatenate([planes[n], dn1_far[n]]), n) for n in range(1, XY)
+    ]
 
     gate_0, gate_1 = step(gk, gs, 1)
     up_0, up_1 = step(uk, us, 2)
@@ -1145,16 +1144,26 @@
         (flat(mlp_0), flat(across(mlp_1, 2 * XY))), ((wide, unit), (wide, unit))
     )
     down_0, down_1 = step(dk, ds, XY)
-    down_0, down_1 = step(down_0, down_1, 1)
     down_0, down_1 = step(down_0, down_1, 2)
+    down_2, down_3 = step(down_0, down_1, 1)
     own_down, own_out = join(
-        (flat(down_0), flat(across(down_1, 2 * XY))), ((narrow, unit_down), (narrow, unit_out))
-    )
-
-    planes = [add(back_keep[n], back_recv[n]) for n in range(XY)]
-    planes = [planes[0]] + [
-        across(jnp.concatenate([planes[n], dn1_far[n]]), n) for n in range(1, XY)
-    ]
+        (flat(down_2), flat(across(down_3, 2 * XY))), ((narrow, unit_down), (narrow, unit_out))
+    )
+
+    far_shape = (rows * width // LANES, LANES)
+    dn1, below = pl.pallas_call(
+        functools.partial(collect_kernel, per_back + 16),
+        out_shape=[shape((rows, width), F32), shape(far_shape, BF16)],
+        in_specs=[hbm] * 2 + [vmem] * (XY - 1) + [hbm] * 2,
+        out_specs=[vmem] * 2,
+        scratch_shapes=[
+            pltpu.VMEM((rows, width), F32),
+            pltpu.VMEM(far_shape, BF16),
+            pltpu.SemaphoreType.DMA((2,)),
+        ],
+        compiler_params=pltpu.CompilerParams(vmem_limit_bytes=12 * MIB),
+        cost_estimate=pl.CostEstimate(flops=0, bytes_accessed=0, transcendentals=0),
+    )(dn1_own, dn1_far, *planes[1:], own_gate, own_down)
     keep, send = line_split(
         (planes,),
         (
@@ -1164,6 +1173,7 @@
         ),
         (0, per_back),
         True,
+        (below,),
     )
     own_query, own_key, own_value, own_gains = join(
         (flat(keep), *[across(send[n], (n + 1) * XY) for n in range(LINE - 1)]),
@@ -1171,28 +1181,16 @@
         True,
     )
 
-    far_shape = (rows * width // LANES, LANES)
-    dn1, below = pl.pallas_call(
-        functools.partial(collect_kernel, per_back + 16),
-        out_shape=[shape((rows, width), F32), shape(far_shape, BF16)],
-        in_specs=[pl.BlockSpec(memory_space=pl.ANY)] * (XY + 1),
-        out_specs=[pl.BlockSpec(memory_space=pl.ANY)] * 2,
-        scratch_shapes=[pltpu.VMEM((rows, width), F32)]
-        + [pltpu.VMEM(far_shape, BF16)] * XY
-        + [pltpu.VMEM((rows, width), F32), pltpu.VMEM(far_shape, BF16)]
-        + [pltpu.SemaphoreType.DMA((XY + 3,))],
-        compiler_params=pltpu.CompilerParams(vmem_limit_bytes=24 * MIB),
-    )(dn1_own, dn1_far, *planes[1:])
-    (input_grad,) = call(
+    input_grad = pl.pallas_call(
         finish_kernel,
-        (tok, gains, dx, dn1, shifted(below, "seq", -XY)),
-        (),
-        [shape((rows, width), F32)],
-        [],
-        6,
-        10**8,
-        24,
-    )
+        out_shape=shape((rows, width), F32),
+        in_specs=[hbm] * 3 + [vmem] * 2,
+        out_specs=hbm,
+        scratch_shapes=[pltpu.VMEM(a.shape, a.dtype) for a in (tok, gains, dx, dx)]
+        + [pltpu.SemaphoreType.DMA((4,))],
+        compiler_params=pltpu.CompilerParams(vmem_limit_bytes=12 * MIB),
+        cost_estimate=pl.CostEstimate(flops=0, bytes_accessed=0, transcendentals=0),
+    )(tok, gains, dx, dn1, shifted(below, "seq", -XY))
     return (
         mixed[None],
         input_grad[None],

time: 138 us -> 130 us (0.942)
  Pallas kernels: 47.1 us -> 42.9 us
  waiting for transfers between devices: 36.3 us -> 34.6 us
    pallas_call x9 -> x4, Pallas kernels: 39.9 us -> 32.4 us  [call(): pl.pallas_call(kernel, out_shape=outs, in_specs=[hbm] * (len(fetched) + l...]
    pallas_call x0 -> x6, Pallas kernels: none -> 4.21 us  [the longest x3 2.31 us: join(): pl.pallas_call(functools.partial(join_kernel, len(parts), entries, int(ex...]
    ppermute x3, waiting for transfers between devices: 4.01 us -> 0.01 us  [partner(): return lax.ppermute(value, 'fsdp', [(0, 1), (1, 0)])]
    ppermute x16, waiting for transfers between devices: 27.7 us -> 29.6 us  [across(): return lax.ppermute(value, 'seq', [(i, i ^ bits) for i in range(XY * LINE)])]
    unnamed x28 -> x32, local copies, waits for them, and re-layouts: 4.91 us -> 3.82 us
  transfers between devices with their start and end apart: 24 -> 24, of which waited for: 10 -> 12; matrix products, arithmetic and copies ran while one was open for 1% -> 1% of each run, Pallas kernels for 15% -> 13%
where the time goes in v3:
time: 130 us
  starting transfers between devices  45.3 us (35%)
  Pallas kernels  42.9 us (33%)
  waiting for transfers between devices  34.6 us (27%)
  local copies, waits for them, and re-layouts  4.38 us (3%)
    pallas_call x4, Pallas kernels, call(): pl.pallas_call(kernel, out_shape=outs, in_specs=[hbm] * (len(fetched) + l...  32.4 us
    ppermute x16, waiting for transfers between devices, across(): return lax.ppermute(value, 'seq', [(i, i ^ bits) for i in range(XY * LINE)])  29.6 us
    ppermute x16, starting transfers between devices, across(): return lax.ppermute(value, 'seq', [(i, i ^ bits) for i in range(XY * LINE)])  27.7 us
    ppermute x5, starting transfers between devices, shifted(): return lax.ppermute(x, axis, pairs)  17 us
    pallas_call x1, Pallas kernels, fast(): pl.pallas_call(functools.partial(prepare_kernel, layout), out_shape=[shap...  5.73 us
    ppermute x5, waiting for transfers between devices, shifted(): return lax.ppermute(x, axis, pairs)  4.99 us
    unnamed x32, local copies, waits for them, and re-layouts  3.82 us
  transfers between devices with their start and end apart: 24, of which 12 were waited for; matrix products, arithmetic and copies ran while one was open for 1% of the time, Pallas kernels for 13%

profile of v3, /device:TPU:0, one launch (start us, length us, event | category | flops | bytes accessed | tf_op | source)
XLA Modules:
  0.0 129.6 jit_solution(17095673326235757837)
XLA Ops:
  0.6 5.7 %shard_map.231 = (bf16[144,640]{1,0:T(8,128)(2,1)}, bf16[320,8832]{1,0:T(8,128)(2,1)}) custom-call(bf16[128,640]{1,0:T(8,128)(2,1)} %bitcast.55, s32[1,128]{1,0:T(1,128)} %refs_1_.2, bf16[320,1024]{1,0:T(8,128)(2,1)} %refs_16_.3, bf16[320,256]{1,0:T(8,128)(2,1)} %refs_17_.1, bf16[320,256]{1,0:T(8,128)(2,1)} %refs_18_.1, bf16[320,2048]{1,0:T(8,128)(2,1)} %refs_13_.1, ...), custom_call_target="tpu_custom_call" | custom-call | tf_op jit(solution)/shard_map/pallas_call | solution.py:952
  6.9 4.4 %collective-permute-start.3 = (bf16[144,640]{1,0:T(8,128)(2,1)}, bf16[144,640]{1,0:T(8,128)(2,1)S(1)}, u32[]{:S(2)}, u32[]{:S(2)}) collective-permute-start(bf16[144,640]{1,0:T(8,128)(2,1)} %get-tuple-element.54.refs_4_.refs_0_), channel_id=1, source_target_pairs={{0,2},{2,4},{4,6},{6,8},{8,10},{10,12},{12,14},{14,16},{16,18},{18... | collective-permute-start | bytes 552968 | tf_op jit(solution)/shard_map/ppermute | solution.py:24
  11.3 3.4 %collective-permute-start.2 = (bf16[144,640]{1,0:T(8,128)(2,1)}, bf16[144,640]{1,0:T(8,128)(2,1)S(1)}, u32[]{:S(2)}, u32[]{:S(2)}) collective-permute-start(bf16[144,640]{1,0:T(8,128)(2,1)} %get-tuple-element.54.refs_4_.refs_0_), channel_id=1, source_target_pairs={{0,4},{2,6},{4,8},{6,10},{8,12},{10,14},{12,16},{14,18},{16,20},{1... | collective-permute-start | bytes 552968 | tf_op jit(solution)/shard_map/ppermute | solution.py:24
  14.8 4.4 %collective-permute-start.1 = (bf16[144,640]{1,0:T(8,128)(2,1)}, bf16[144,640]{1,0:T(8,128)(2,1)S(1)}, u32[]{:S(2)}, u32[]{:S(2)}) collective-permute-start(bf16[144,640]{1,0:T(8,128)(2,1)} %get-tuple-element.54.refs_4_.refs_0_), channel_id=1, source_target_pairs={{0,6},{2,8},{4,10},{6,12},{8,14},{10,16},{12,18},{14,20},{16,22},{... | collective-permute-start | bytes 552968 | tf_op jit(solution)/shard_map/ppermute | solution.py:24
  19.1 3.5 %collective-permute-start = (bf16[144,640]{1,0:T(8,128)(2,1)}, bf16[144,640]{1,0:T(8,128)(2,1)S(1)}, u32[]{:S(2)}, u32[]{:S(2)}) collective-permute-start(bf16[144,640]{1,0:T(8,128)(2,1)} %get-tuple-element.54.refs_4_.refs_0_), channel_id=1, source_target_pairs={{0,8},{2,10},{4,12},{6,14},{8,16},{10,18},{12,20},{14,22},{16,24},... | collective-permute-start | bytes 552968 | tf_op jit(solution)/shard_map/ppermute | solution.py:24
  23.4 3.2 %collective-permute-done.refs_0_ = bf16[144,640]{1,0:T(8,128)(2,1)S(1)} collective-permute-done((bf16[144,640]{1,0:T(8,128)(2,1)}, bf16[144,640]{1,0:T(8,128)(2,1)S(1)}, u32[]{:S(2)}, u32[]{:S(2)}) %collective-permute-start) | collective-permute-done | bytes 184352 | tf_op jit(solution)/shard_map/ppermute | solution.py:24
  27.3 13.7 %shard_map.232 = (bf16[640,640]{1,0:T(8,128)(2,1)}, f32[128,1024]{1,0:T(8,128)}, bf16[128,1024]{1,0:T(8,128)(2,1)}, f32[640,256]{1,0:T(8,128)}, bf16[640,256]{1,...) custom-call(bf16[144,640]{1,0:T(8,128)(2,1)} %copy-done.14, ...), custom_call_target="tpu_custom_call" | custom-call | tf_op jit(solution)/shard_map/pallas_call | solution.py:893
  41.0 5.7 %shard_map.233 = (bf16[128,1024]{1,0:T(8,128)(2,1)}, f32[640,256]{1,0:T(8,128)}, bf16[640,256]{1,0:T(8,128)(2,1)}, f32[1,256]{1,0:T(1,128)}) custom-call(f32[1,3072]{1,0:T(1,128)} %get-tuple-element.57.refs_0_.refs_5_.refs_1_, f32[640,128]{1,0:T(8,128)} %constant.12.clone.refs_8_.refs_1_, f32[640,128]{1,0:T(8,128)} %constant.13.clone.refs_9_.refs_2_, ...), custom_call_target="tpu_custom_call" | custom-call | tf_op jit(solution)/shard_map/pallas_call | solution.py:893
  46.7 1.3 copy-done.8
  48.0 5.1 %shard_map.234 = (bf16[2,1280,128]{2,1,0:T(8,128)(2,1)}, bf16[2,1280,128]{2,1,0:T(8,128)(2,1)}, bf16[2,1280,128]{2,1,0:T(8,128)(2,1)}, bf16[2,1280,128]{2,1,0:T(...) custom-call(bf16[128,7296]{1,0:T(8,128)(2,1)} %get-tuple-element.72.refs_0_, ...), custom_call_target="tpu_custom_call" | custom-call | tf_op jit(solution)/shard_map/pallas_call | solution.py:893
  53.2 1.4 %collective-permute-start.10 = (bf16[2,1280,128]{2,1,0:T(8,128)(2,1)}, bf16[2,1280,128]{2,1,0:T(8,128)(2,1)S(1)}, u32[]{:S(2)}, u32[]{:S(2)}) collective-permute-start(bf16[2,1280,128]{2,1,0:T(8,128)(2,1)} %get-tuple-element.79), channel_id=1, source_target_pairs={{0,2},{2,0},{4,6},{6,4},{8,10},{10,8},{12,14},{14,12},{16,18},{18,... | collective-permute-start | bytes 1966088 | tf_op jit(solution)/shard_map/ppermute | solution.py:943
  54.6 3.1 %collective-permute-start.12 = (bf16[2,1280,128]{2,1,0:T(8,128)(2,1)}, bf16[2,1280,128]{2,1,0:T(8,128)(2,1)S(1)}, u32[]{:S(2)}, u32[]{:S(2)}) collective-permute-start(bf16[2,1280,128]{2,1,0:T(8,128)(2,1)} %get-tuple-element.81), channel_id=1, source_target_pairs={{0,4},{2,6},{4,0},{6,2},{8,12},{10,14},{12,8},{14,10},{16,20},{18,... | collective-permute-start | bytes 1966088 | tf_op jit(solution)/shard_map/ppermute | solution.py:943
  57.7 2.4 %collective-permute-start.16 = (bf16[8,480,128]{2,1,0:T(8,128)(2,1)}, bf16[8,480,128]{2,1,0:T(8,128)(2,1)S(1)}, u32[]{:S(2)}, u32[]{:S(2)}) collective-permute-start(bf16[8,480,128]{2,1,0:T(8,128)(2,1)} %get-tuple-element.86), channel_id=1, source_target_pairs={{0,8},{2,10},{4,12},{6,14},{8,0},{10,2},{12,4},{14,6},{16,24},{18,... | collective-permute-start | bytes 2949128 | tf_op jit(solution)/shard_map/ppermute | solution.py:943
  60.0 7.9 %shard_map.235 = (bf16[4,976,128]{2,1,0:T(8,128)(2,1)}, bf16[4,976,128]{2,1,0:T(8,128)(2,1)}, f32[128,640]{1,0:T(8,128)}, bf16[4,640,128]{2,1,0:T(8,128)(2,1)}) custom-call(bf16[144,640]{1,0:T(8,128)(2,1)} %copy-done.14, bf16[144,640]{1,0:T(8,128)(2,1)} %copy-done.13, bf16[144,640]{1,0:T(8,128)(2,1)} %copy-done.12, bf16[144,640]{1,0:T(8,128)(2,1)} %copy-done.11, ...), custom_call_target="tpu_custom_call" | custom-call | tf_op jit(solution)/shard_map/pallas_call | solution.py:893
  68.1 2.5 %collective-permute-done.10 = bf16[2,1280,128]{2,1,0:T(8,128)(2,1)S(1)} collective-permute-done((bf16[2,1280,128]{2,1,0:T(8,128)(2,1)}, bf16[2,1280,128]{2,1,0:T(8,128)(2,1)S(1)}, u32[]{:S(2)}, u32[]{:S(2)}) %collective-permute-start.10) | collective-permute-done | bytes 655392 | tf_op jit(solution)/shard_map/ppermute | solution.py:943
  70.8 3.9 %collective-permute-start.11 = (bf16[1,1280,128]{2,1,0:T(8,128)(2,1)S(1)}, bf16[1,1280,128]{2,1,0:T(8,128)(2,1)S(1)}, u32[]{:S(2)}, u32[]{:S(2)}) collective-permute-start(bf16[1,1280,128]{2,1,0:T(8,128)(2,1)S(1)} %get-tuple-element.106), channel_id=1, source_target_pairs={{0,4},{2,6},{4,0},{6,2},{8,12},{10,14},{12,8},{14,10},{16,20},{18,... | collective-permute-start | bytes 983048 | tf_op jit(solution)/shard_map/ppermute | solution.py:943
  75.5 6.6 %collective-permute-done.16 = bf16[8,480,128]{2,1,0:T(8,128)(2,1)S(1)} collective-permute-done((bf16[8,480,128]{2,1,0:T(8,128)(2,1)}, bf16[8,480,128]{2,1,0:T(8,128)(2,1)S(1)}, u32[]{:S(2)}, u32[]{:S(2)}) %collective-permute-start.16) | collective-permute-done | bytes 983072 | tf_op jit(solution)/shard_map/ppermute | solution.py:943
  82.7 1.2 collective-permute-done.13
  84.3 2.4 %collective-permute-start.14 = (bf16[2,640,128]{2,1,0:T(8,128)(2,1)S(1)}, bf16[2,640,128]{2,1,0:T(8,128)(2,1)S(1)}, u32[]{:S(2)}, u32[]{:S(2)}) collective-permute-start(bf16[2,640,128]{2,1,0:T(8,128)(2,1)S(1)} %get-tuple-element.83), channel_id=1, source_target_pairs={{0,8},{2,10},{4,12},{6,14},{8,0},{10,2},{12,4},{14,6},{16,24},{18,... | collective-permute-start | bytes 983048 | tf_op jit(solution)/shard_map/ppermute | solution.py:943
  88.6 8.0 %collective-permute-done.17 = bf16[4,480,128]{2,1,0:T(8,128)(2,1)S(1)} collective-permute-done((bf16[4,480,128]{2,1,0:T(8,128)(2,1)S(1)}, bf16[4,480,128]{2,1,0:T(8,128)(2,1)S(1)}, u32[]{:S(2)}, u32[]{:S(2)}) %collective-permute-start.17) | collective-permute-done | bytes 491552 | tf_op jit(solution)/shard_map/ppermute | solution.py:943
  96.7 1.5 %collective-permute-start.18 = (bf16[2,480,128]{2,1,0:T(8,128)(2,1)S(1)}, bf16[2,480,128]{2,1,0:T(8,128)(2,1)S(1)}, u32[]{:S(2)}, u32[]{:S(2)}) collective-permute-start(bf16[2,480,128]{2,1,0:T(8,128)(2,1)S(1)} %get-tuple-element.109), channel_id=1, source_target_pairs={{0,2},{2,0},{4,6},{6,4},{8,10},{10,8},{12,14},{14,12},{16,18},{18,... | collective-permute-start | bytes 737288 | tf_op jit(solution)/shard_map/ppermute | solution.py:943
  98.7 2.9 %collective-permute-start.15 = (bf16[1,640,128]{2,1,0:T(8,128)(2,1)S(1)}, bf16[1,640,128]{2,1,0:T(8,128)(2,1)S(1)}, u32[]{:S(2)}, u32[]{:S(2)}) collective-permute-start(bf16[1,640,128]{2,1,0:T(8,128)(2,1)S(1)} %get-tuple-element.110), channel_id=1, source_target_pairs={{0,16},{2,18},{4,20},{6,22},{8,24},{10,26},{12,28},{14,30},{16,0},... | collective-permute-start | bytes 491528 | tf_op jit(solution)/shard_map/ppermute | solution.py:943
  101.6 4.2 %collective-permute-done.18 = bf16[2,480,128]{2,1,0:T(8,128)(2,1)S(1)} collective-permute-done((bf16[2,480,128]{2,1,0:T(8,128)(2,1)S(1)}, bf16[2,480,128]{2,1,0:T(8,128)(2,1)S(1)}, u32[]{:S(2)}, u32[]{:S(2)}) %collective-permute-start.18) | collective-permute-done | bytes 245792 | tf_op jit(solution)/shard_map/ppermute | solution.py:943
  105.8 2.8 %collective-permute-start.19 = (bf16[1,480,128]{2,1,0:T(8,128)(2,1)S(1)}, bf16[1,480,128]{2,1,0:T(8,128)(2,1)S(1)}, u32[]{:S(2)}, u32[]{:S(2)}) collective-permute-start(bf16[1,480,128]{2,1,0:T(8,128)(2,1)S(1)} %get-tuple-element.115), channel_id=1, source_target_pairs={{0,16},{2,18},{4,20},{6,22},{8,24},{10,26},{12,28},{14,30},{16,0},... | collective-permute-start | bytes 368648 | tf_op jit(solution)/shard_map/ppermute | solution.py:943
  110.2 2.8 %collective-permute-done.19 = bf16[1,480,128]{2,1,0:T(8,128)(2,1)S(1)} collective-permute-done((bf16[1,480,128]{2,1,0:T(8,128)(2,1)S(1)}, bf16[1,480,128]{2,1,0:T(8,128)(2,1)S(1)}, u32[]{:S(2)}, u32[]{:S(2)}) %collective-permute-start.19) | collective-permute-done | bytes 122912 | tf_op jit(solution)/shard_map/ppermute | solution.py:943
  114.7 0.9 copy-done.5
  116.4 3.4 %collective-permute-start.23 = (bf16[256,128]{1,0:T(8,128)(2,1)S(1)}, bf16[256,128]{1,0:T(8,128)(2,1)S(1)}, u32[]{:S(2)}, u32[]{:S(2)}) collective-permute-start(bf16[256,128]{1,0:T(8,128)(2,1)S(1)} %get-tuple-element.117), channel_id=1, source_target_pairs={{0,24},{2,26},{4,28},{6,30},{8,16},{10,18},{12,20},{14,22},{16,8},... | collective-permute-start | bytes 196616 | tf_op jit(solution)/shard_map/ppermute | solution.py:943
  119.8 1.0 collective-permute-start.21
  120.9 1.3 collective-permute-start.20
  122.9 2.8 %collective-permute-done.22.refs_2_ = bf16[256,128]{1,0:T(8,128)(2,1)S(1)} collective-permute-done((bf16[256,128]{1,0:T(8,128)(2,1)S(1)}, bf16[256,128]{1,0:T(8,128)(2,1)S(1)}, u32[]{:S(2)}, u32[]{:S(2)}) %collective-permute-start.22) | collective-permute-done | bytes 65568 | tf_op jit(solution)/shard_map/ppermute | solution.py:943
  127.0 1.0 collective-permute-done.20.refs_4_
  128.1 1.3 %shard_map.240 = f32[128,640]{1,0:T(8,128)} custom-call(bf16[144,640]{1,0:T(8,128)(2,1)S(1)} %copy-done.1, f32[1,3072]{1,0:T(1,128)S(1)} %copy-done.6, f32[128,640]{1,0:T(8,128)S(1)} %copy-done.3, f32[128,640]{1,0:T(8,128)S(1)} %get-tuple-element.88.refs_3_, bf16[640,128]{1,0:T(8,128)(2,1)S(1)} %collective-permute-done.20.refs_4_), custom_call_target="tpu_custom_call" | custom-call | tf_op jit(solution)/shard_map/pallas_call | solution.py:1184
  (73 shorter events, 12.8 us)
Async XLA Ops:
  6.4 20.2 %collective-permute-start.4 = (bf16[320,8832]{1,0:T(8,128)(2,1)}, bf16[320,8832]{1,0:T(8,128)(2,1)}, u32[]{:S(2)}, u32[]{:S(2)}) collective-permute-start(bf16[320,8832]{1,0:T(8,128)(2,1)} %get-tuple-element.55), channel_id=1, source_target_pairs={{0,1},{1,0},{2,3},{3,2},{4,5},{5,4},{6,7},{7,6},{8,9},{9,8},{10,11... | collective-permute-start | bytes 16957448 | tf_op jit(solution)/shard_map/ppermute | solution.py:940
  6.9 15.7 %collective-permute-start.3 = (bf16[144,640]{1,0:T(8,128)(2,1)}, bf16[144,640]{1,0:T(8,128)(2,1)S(1)}, u32[]{:S(2)}, u32[]{:S(2)}) collective-permute-start(bf16[144,640]{1,0:T(8,128)(2,1)} %get-tuple-element.54.refs_4_.refs_0_), channel_id=1, source_target_pairs={{0,2},{2,4},{4,6},{6,8},{8,10},{10,12},{12,14},{14,16},{16,18},{18... | collective-permute-start | bytes 552968 | tf_op jit(solution)/shard_map/ppermute | solution.py:24
  11.3 11.3 %collective-permute-start.2 = (bf16[144,640]{1,0:T(8,128)(2,1)}, bf16[144,640]{1,0:T(8,128)(2,1)S(1)}, u32[]{:S(2)}, u32[]{:S(2)}) collective-permute-start(bf16[144,640]{1,0:T(8,128)(2,1)} %get-tuple-element.54.refs_4_.refs_0_), channel_id=1, source_target_pairs={{0,4},{2,6},{4,8},{6,10},{8,12},{10,14},{12,16},{14,18},{16,20},{1... | collective-permute-start | bytes 552968 | tf_op jit(solution)/shard_map/ppermute | solution.py:24
  14.8 8.6 %collective-permute-start.1 = (bf16[144,640]{1,0:T(8,128)(2,1)}, bf16[144,640]{1,0:T(8,128)(2,1)S(1)}, u32[]{:S(2)}, u32[]{:S(2)}) collective-permute-start(bf16[144,640]{1,0:T(8,128)(2,1)} %get-tuple-element.54.refs_4_.refs_0_), channel_id=1, source_target_pairs={{0,6},{2,8},{4,10},{6,12},{8,14},{10,16},{12,18},{14,20},{16,22},{... | collective-permute-start | bytes 552968 | tf_op jit(solution)/shard_map/ppermute | solution.py:24
  19.1 7.5 %collective-permute-start = (bf16[144,640]{1,0:T(8,128)(2,1)}, bf16[144,640]{1,0:T(8,128)(2,1)S(1)}, u32[]{:S(2)}, u32[]{:S(2)}) collective-permute-start(bf16[144,640]{1,0:T(8,128)(2,1)} %get-tuple-element.54.refs_4_.refs_0_), channel_id=1, source_target_pairs={{0,8},{2,10},{4,12},{6,14},{8,16},{10,18},{12,20},{14,22},{16,24},... | collective-permute-start | bytes 552968 | tf_op jit(solution)/shard_map/ppermute | solution.py:24
  41.0 5.8 %collective-permute-start.5 = (bf16[128,7296]{1,0:T(8,128)(2,1)}, bf16[128,7296]{1,0:T(8,128)(2,1)S(1)}, u32[]{:S(2)}, u32[]{:S(2)}) collective-permute-start(bf16[128,7296]{1,0:T(8,128)(2,1)} %get-tuple-element.73), channel_id=1, source_target_pairs={{0,1},{1,0},{2,3},{3,2},{4,5},{5,4},{6,7},{7,6},{8,9},{9,8},{10,11... | collective-permute-start | bytes 5603336 | tf_op jit(solution)/shard_map/ppermute | solution.py:940
  53.2 17.4 %collective-permute-start.10 = (bf16[2,1280,128]{2,1,0:T(8,128)(2,1)}, bf16[2,1280,128]{2,1,0:T(8,128)(2,1)S(1)}, u32[]{:S(2)}, u32[]{:S(2)}) collective-permute-start(bf16[2,1280,128]{2,1,0:T(8,128)(2,1)} %get-tuple-element.79), channel_id=1, source_target_pairs={{0,2},{2,0},{4,6},{6,4},{8,10},{10,8},{12,14},{14,12},{16,18},{18,... | collective-permute-start | bytes 1966088 | tf_op jit(solution)/shard_map/ppermute | solution.py:943
  54.6 20.1 %collective-permute-start.12 = (bf16[2,1280,128]{2,1,0:T(8,128)(2,1)}, bf16[2,1280,128]{2,1,0:T(8,128)(2,1)S(1)}, u32[]{:S(2)}, u32[]{:S(2)}) collective-permute-start(bf16[2,1280,128]{2,1,0:T(8,128)(2,1)} %get-tuple-element.81), channel_id=1, source_target_pairs={{0,4},{2,6},{4,0},{6,2},{8,12},{10,14},{12,8},{14,10},{16,20},{18,... | collective-permute-start | bytes 1966088 | tf_op jit(solution)/shard_map/ppermute | solution.py:943
  57.7 24.4 %collective-permute-start.16 = (bf16[8,480,128]{2,1,0:T(8,128)(2,1)}, bf16[8,480,128]{2,1,0:T(8,128)(2,1)S(1)}, u32[]{:S(2)}, u32[]{:S(2)}) collective-permute-start(bf16[8,480,128]{2,1,0:T(8,128)(2,1)} %get-tuple-element.86), channel_id=1, source_target_pairs={{0,8},{2,10},{4,12},{6,14},{8,0},{10,2},{12,4},{14,6},{16,24},{18,... | collective-permute-start | bytes 2949128 | tf_op jit(solution)/shard_map/ppermute | solution.py:943
  60.0 10.6 %copy-start.7 = (bf16[2,1280,128]{2,1,0:T(8,128)(2,1)S(1)}, bf16[2,1280,128]{2,1,0:T(8,128)(2,1)}, u32[]{:S(2)}) copy-start(bf16[2,1280,128]{2,1,0:T(8,128)(2,1)} %get-tuple-element.74.refs_15_) | copy-start | bytes 1966084
  68.0 6.6 %copy-start.15 = (bf16[2,1280,128]{2,1,0:T(8,128)(2,1)S(1)}, bf16[2,1280,128]{2,1,0:T(8,128)(2,1)}, u32[]{:S(2)}) copy-start(bf16[2,1280,128]{2,1,0:T(8,128)(2,1)} %get-tuple-element.80) | copy-start | bytes 1966084
  68.0 7.5 %copy-start = (bf16[4,640,128]{2,1,0:T(8,128)(2,1)S(1)}, bf16[4,640,128]{2,1,0:T(8,128)(2,1)}, u32[]{:S(2)}) copy-start(bf16[4,640,128]{2,1,0:T(8,128)(2,1)} %get-tuple-element.76.refs_1_) | copy-start | bytes 1966084
  68.0 18.7 %collective-permute-start.6 = (bf16[4,976,128]{2,1,0:T(8,128)(2,1)}, bf16[4,976,128]{2,1,0:T(8,128)(2,1)S(1)}, u32[]{:S(2)}, u32[]{:S(2)}) collective-permute-start(bf16[4,976,128]{2,1,0:T(8,128)(2,1)} %get-tuple-element.78), channel_id=1, source_target_pairs={{0,1},{1,0},{2,3},{3,2},{4,5},{5,4},{6,7},{7,6},{8,9},{9,8},{10,11... | collective-permute-start | bytes 2998280 | tf_op jit(solution)/shard_map/ppermute | solution.py:940
  70.8 11.3 %copy-start.10 = (bf16[8,480,128]{2,1,0:T(8,128)(2,1)S(1)}, bf16[8,480,128]{2,1,0:T(8,128)(2,1)}, u32[]{:S(2)}) copy-start(bf16[8,480,128]{2,1,0:T(8,128)(2,1)} %get-tuple-element.85) | copy-start | bytes 2949124
  70.8 11.9 %collective-permute-start.11 = (bf16[1,1280,128]{2,1,0:T(8,128)(2,1)S(1)}, bf16[1,1280,128]{2,1,0:T(8,128)(2,1)S(1)}, u32[]{:S(2)}, u32[]{:S(2)}) collective-permute-start(bf16[1,1280,128]{2,1,0:T(8,128)(2,1)S(1)} %get-tuple-element.106), channel_id=1, source_target_pairs={{0,4},{2,6},{4,0},{6,2},{8,12},{10,14},{12,8},{14,10},{16,20},{18,... | collective-permute-start | bytes 983048 | tf_op jit(solution)/shard_map/ppermute | solution.py:943
  74.8 9.1 %collective-permute-start.13 = (bf16[1,1280,128]{2,1,0:T(8,128)(2,1)S(1)}, bf16[1,1280,128]{2,1,0:T(8,128)(2,1)S(1)}, u32[]{:S(2)}, u32[]{:S(2)}) collective-permute-start(bf16[1,1280,128]{2,1,0:T(8,128)(2,1)S(1)} %get-tuple-element.104), channel_id=1, source_target_pairs={{0,2},{2,0},{4,6},{6,4},{8,10},{10,8},{12,14},{14,12},{16,18},{18,... | collective-permute-start | bytes 983048 | tf_op jit(solution)/shard_map/ppermute | solution.py:943
  82.4 14.2 %collective-permute-start.17 = (bf16[4,480,128]{2,1,0:T(8,128)(2,1)S(1)}, bf16[4,480,128]{2,1,0:T(8,128)(2,1)S(1)}, u32[]{:S(2)}, u32[]{:S(2)}) collective-permute-start(bf16[4,480,128]{2,1,0:T(8,128)(2,1)S(1)} %get-tuple-element.103), channel_id=1, source_target_pairs={{0,4},{2,6},{4,0},{6,2},{8,12},{10,14},{12,8},{14,10},{16,20},{18,... | collective-permute-start | bytes 1474568 | tf_op jit(solution)/shard_map/ppermute | solution.py:943
  84.3 14.3 %collective-permute-start.14 = (bf16[2,640,128]{2,1,0:T(8,128)(2,1)S(1)}, bf16[2,640,128]{2,1,0:T(8,128)(2,1)S(1)}, u32[]{:S(2)}, u32[]{:S(2)}) collective-permute-start(bf16[2,640,128]{2,1,0:T(8,128)(2,1)S(1)} %get-tuple-element.83), channel_id=1, source_target_pairs={{0,8},{2,10},{4,12},{6,14},{8,0},{10,2},{12,4},{14,6},{16,24},{18,... | collective-permute-start | bytes 983048 | tf_op jit(solution)/shard_map/ppermute | solution.py:943
  87.0 26.7 %collective-permute-start.7 = (bf16[1616,128]{1,0:T(8,128)(2,1)S(1)}, bf16[1616,128]{1,0:T(8,128)(2,1)S(1)}, u32[]{:S(2)}, u32[]{:S(2)}) collective-permute-start(bf16[1616,128]{1,0:T(8,128)(2,1)S(1)} %pad_maximum_fusion), channel_id=1, source_target_pairs={{0,2},{2,0},{4,6},{6,4},{8,10},{10,8},{12,14},{14,12},{16,18},{18,... | collective-permute-start | bytes 1241096 | tf_op jit(solution)/shard_map/ppermute | solution.py:943
  87.7 26.0 %collective-permute-start.8 = (bf16[1616,128]{1,0:T(8,128)(2,1)S(1)}, bf16[1616,128]{1,0:T(8,128)(2,1)S(1)}, u32[]{:S(2)}, u32[]{:S(2)}) collective-permute-start(bf16[1616,128]{1,0:T(8,128)(2,1)S(1)} %pad_maximum_fusion.1), channel_id=1, source_target_pairs={{0,4},{2,6},{4,0},{6,2},{8,12},{10,14},{12,8},{14,10},{16,20},{18,... | collective-permute-start | bytes 1241096 | tf_op jit(solution)/shard_map/ppermute | solution.py:943
  96.7 17.0 %copy-start.2 = (f32[128,640]{1,0:T(8,128)S(1)}, f32[128,640]{1,0:T(8,128)}, u32[]{:S(2)}) copy-start(f32[128,640]{1,0:T(8,128)} %get-tuple-element.75.refs_0_) | copy-start | bytes 983044
  96.7 9.0 %collective-permute-start.18 = (bf16[2,480,128]{2,1,0:T(8,128)(2,1)S(1)}, bf16[2,480,128]{2,1,0:T(8,128)(2,1)S(1)}, u32[]{:S(2)}, u32[]{:S(2)}) collective-permute-start(bf16[2,480,128]{2,1,0:T(8,128)(2,1)S(1)} %get-tuple-element.109), channel_id=1, source_target_pairs={{0,2},{2,0},{4,6},{6,4},{8,10},{10,8},{12,14},{14,12},{16,18},{18,... | collective-permute-start | bytes 737288 | tf_op jit(solution)/shard_map/ppermute | solution.py:943
  98.2 15.5 %collective-permute-start.9 = (bf16[1616,128]{1,0:T(8,128)(2,1)S(1)}, bf16[1616,128]{1,0:T(8,128)(2,1)S(1)}, u32[]{:S(2)}, u32[]{:S(2)}) collective-permute-start(bf16[1616,128]{1,0:T(8,128)(2,1)S(1)} %pad_maximum_fusion.2), channel_id=1, source_target_pairs={{0,6},{2,4},{4,2},{6,0},{8,14},{10,12},{12,10},{14,8},{16,22},{18,... | collective-permute-start | bytes 1241096 | tf_op jit(solution)/shard_map/ppermute | solution.py:943
  98.7 10.6 %collective-permute-start.15 = (bf16[1,640,128]{2,1,0:T(8,128)(2,1)S(1)}, bf16[1,640,128]{2,1,0:T(8,128)(2,1)S(1)}, u32[]{:S(2)}, u32[]{:S(2)}) collective-permute-start(bf16[1,640,128]{2,1,0:T(8,128)(2,1)S(1)} %get-tuple-element.110), channel_id=1, source_target_pairs={{0,16},{2,18},{4,20},{6,22},{8,24},{10,26},{12,28},{14,30},{16,0},... | collective-permute-start | bytes 491528 | tf_op jit(solution)/shard_map/ppermute | solution.py:943
  105.8 7.2 %collective-permute-start.19 = (bf16[1,480,128]{2,1,0:T(8,128)(2,1)S(1)}, bf16[1,480,128]{2,1,0:T(8,128)(2,1)S(1)}, u32[]{:S(2)}, u32[]{:S(2)}) collective-permute-start(bf16[1,480,128]{2,1,0:T(8,128)(2,1)S(1)} %get-tuple-element.115), channel_id=1, source_target_pairs={{0,16},{2,18},{4,20},{6,22},{8,24},{10,26},{12,28},{14,30},{16,0},... | collective-permute-start | bytes 368648 | tf_op jit(solution)/shard_map/ppermute | solution.py:943
  115.6 12.5 %copy-start.1 = (bf16[144,640]{1,0:T(8,128)(2,1)S(1)}, bf16[144,640]{1,0:T(8,128)(2,1)}, u32[]{:S(2)}) copy-start(bf16[144,640]{1,0:T(8,128)(2,1)} %get-tuple-element.54.refs_4_.refs_0_) | copy-start | bytes 552964
  115.6 12.5 %copy-start.3 = (f32[128,640]{1,0:T(8,128)S(1)}, f32[128,640]{1,0:T(8,128)}, u32[]{:S(2)}) copy-start(f32[128,640]{1,0:T(8,128)} %get-tuple-element.58.refs_2_) | copy-start | bytes 983044
  115.6 12.5 %copy-start.6 = (f32[1,3072]{1,0:T(1,128)S(1)}, f32[1,3072]{1,0:T(1,128)}, u32[]{:S(2)}) copy-start(f32[1,3072]{1,0:T(1,128)} %get-tuple-element.57.refs_0_.refs_5_.refs_1_) | copy-start | bytes 36868
  116.4 6.5 %collective-permute-start.23 = (bf16[256,128]{1,0:T(8,128)(2,1)S(1)}, bf16[256,128]{1,0:T(8,128)(2,1)S(1)}, u32[]{:S(2)}, u32[]{:S(2)}) collective-permute-start(bf16[256,128]{1,0:T(8,128)(2,1)S(1)} %get-tuple-element.117), channel_id=1, source_target_pairs={{0,24},{2,26},{4,28},{6,30},{8,16},{10,18},{12,20},{14,22},{16,8},... | collective-permute-start | bytes 196616 | tf_op jit(solution)/shard_map/ppermute | solution.py:943
  119.8 5.9 %collective-permute-start.22 = (bf16[256,128]{1,0:T(8,128)(2,1)S(1)}, bf16[256,128]{1,0:T(8,128)(2,1)S(1)}, u32[]{:S(2)}, u32[]{:S(2)}) collective-permute-start(bf16[256,128]{1,0:T(8,128)(2,1)S(1)} %get-tuple-element.118), channel_id=1, source_target_pairs={{0,16},{2,18},{4,20},{6,22},{8,24},{10,26},{12,28},{14,30},{16,0},... | collective-permute-start | bytes 196616 | tf_op jit(solution)/shard_map/ppermute | solution.py:943
  119.8 5.9 %collective-permute-start.21 = (bf16[256,128]{1,0:T(8,128)(2,1)S(1)}, bf16[256,128]{1,0:T(8,128)(2,1)S(1)}, u32[]{:S(2)}, u32[]{:S(2)}) collective-permute-start(bf16[256,128]{1,0:T(8,128)(2,1)S(1)} %get-tuple-element.119), channel_id=1, source_target_pairs={{0,8},{2,10},{4,12},{6,14},{8,0},{10,2},{12,4},{14,6},{16,24},{18,... | collective-permute-start | bytes 196616 | tf_op jit(solution)/shard_map/ppermute | solution.py:943
  120.9 7.2 %collective-permute-start.20 = (bf16[640,128]{1,0:T(8,128)(2,1)S(1)}, bf16[640,128]{1,0:T(8,128)(2,1)S(1)}, u32[]{:S(2)}, u32[]{:S(2)}) collective-permute-start(bf16[640,128]{1,0:T(8,128)(2,1)S(1)} %get-tuple-element.89.refs_4_), channel_id=1, source_target_pairs={{8,0},{10,2},{12,4},{14,6},{16,8},{18,10},{20,12},{22,14},{24,16},... | collective-permute-start | bytes 491528 | tf_op jit(solution)/shard_map/ppermute | solution.py:24
  (8 other events, 19.6 us)

commit v4 on v3

--- a/solution.py
+++ b/solution.py
@@ -446,10 +446,10 @@
     halo_h, refs = refs[: reach + 1], refs[reach + 1 :]
     ct_h, gains_h, order_h, cos_h, sin_h = refs[:5]
     wq_a, wk_a, wv_a, wg_a, wu_a, wo_a, wd_a, pack_h = refs[5:13]
-    outs_h, refs = refs[13:27], refs[27:]
+    outs_h, refs = refs[13:28], refs[28:]
     halo, refs = refs[: reach + 1], refs[reach + 1 :]
     ct, gain_a, order, cos_ref, sin_ref = refs[:5]
-    outs, refs = refs[5:19], refs[19:]
+    outs, refs = refs[5:20], refs[20:]
     wq, wk, wv, wo, wg, wu, wd, act_s, slope_s, hid_s, ao_ref, gain_b, sems = refs
     place, core = lax.axis_index("seq"), lax.axis_index("fsdp")
     traffic = Traffic(sems)
@@ -486,7 +486,9 @@
     )
     for source, target in zip(outs[:7], outs_h[:7]):
         traffic.emit(source, target)
-    mixed_out, dx_out, dao_out, dg_out, keep, send, gains_out = outs[7:]
+    mixed_out, dx_out, dao_out, dg_out, keep, send, gains_out, _ = outs[7:]
+    for block in range(reach):
+        traffic.emit(halo[block], outs_h[14].at[block])
     rows, width = ct.shape
     gains = all_gains(core, gain_a, gain_b)
     gains_out[...] = gains
@@ -699,25 +701,23 @@
 
 
 def back_kernel(reach, layout, *refs):
-    count = reach + 11
+    count = 12
     ins_h, refs = refs[:count], refs[count:]
     _, wq_a, wk_a, wv_a, pack_h = refs[:5]
     outs_h, refs = refs[5:9], refs[9:]
     ins, refs = refs[:count], refs[count:]
-    halo = ins[: reach + 1]
-    gains, order, scale_order, dg_post, dgq, n1_ref, kraw_ref, dkr, dqr, dv_ref = ins[reach + 1 :]
+    toks, tok, gains, order, scale_order, dg_post, dgq, n1_ref, kraw_ref, dkr, dqr, dv_ref = ins
+    halo = [toks.at[n] for n in range(reach)] + [tok]
     outs = keep, send, dn1_own, dn1_far = refs[:4]
     wq, wk, wv, dkv_s, sems = refs[4:]
     place, core = lax.axis_index("seq"), lax.axis_index("fsdp")
     traffic = Traffic(sems)
-    first = traffic.fetch([(ins_h[n], ins[n]) for n in (reach + 2, reach + 6)])
-    second = traffic.fetch([(ins_h[n], ins[n]) for n in range(reach + 7, count)])
-    second += traffic.fetch([(ins_h[reach + 1], ins[reach + 1])])
-    copies = traffic.fetch([(ins_h[n], ins[n]) for n in range(reach + 3, reach + 6)])
-    copies += traffic.fetch(list(zip(ins_h[: reach + 1], halo)))
+    first = traffic.fetch([(ins_h[n], ins[n]) for n in (3, 7)])
+    second = traffic.fetch([(ins_h[n], ins[n]) for n in (8, 9, 10, 11, 2)])
+    copies = traffic.fetch([(ins_h[n], ins[n]) for n in (4, 5, 6, 0, 1)])
     for n, (mine, full) in enumerate(((wq_a, wq), (wk_a, wk), (wv_a, wv))):
         copies += traffic.halves(core, mine, pack_h, layout[n], full)
-    rows = halo[0].shape[0] - SEG_ROWS
+    rows = tok.shape[0] - SEG_ROWS
     width = n1_ref.shape[1]
     size = kraw_ref.shape[1]
     wait(first)
@@ -869,8 +869,9 @@
 
 def join_kernel(parts, entries, extra, *refs):
     count = len(entries) + extra
-    ins, outs_h, outs = refs[:parts], refs[parts : parts + count], refs[parts + count :][:count]
-    sum_s, sems = refs[parts + 2 * count :]
+    ins, outs_h, refs = refs[:parts], refs[parts : parts + count], refs[parts + count :]
+    flag, outs, (sum_s, sems) = refs[0], refs[1 : count + 1], refs[count + 1 :]
+    flag[...] = jnp.zeros_like(flag)
     traffic = Traffic(sems)
     total = ins[0][...].astype(F32)
     for part in ins[1:]:
@@ -882,7 +883,7 @@
             out[pl.ds(b, unit, stride=blocks), :] = sum_s[at : at + unit, :]
             at += unit
     if extra:
-        outs[-1][...] = sum_s[at : at + 8, :]
+        outs[-1][...] = sum_s[at : at + 8, :][:1, : outs[-1].shape[1]]
     for out, out_h in zip(outs, outs_h):
         traffic.emit(out, out_h)
     traffic.finish()
@@ -983,7 +984,7 @@
     sine = jnp.asarray(np.sin(turn).astype(np.float32))
 
     pair_end = pair_columns(width, ff, attn)[1]
-    n1, qraw, q, kraw, k, v, p, mixed, dx, dao, dg_post, mlp_keep, mlp_send, gains = call(
+    n1, qraw, q, kraw, k, v, p, mixed, dx, dao, dg_post, mlp_keep, mlp_send, gains, toks = call(
         functools.partial(forward_kernel, reach, layout),
         (*halo, cotangent[0], gains_own, order_pair, cosine, sine),
         (*weights, pack_far),
@@ -1002,6 +1003,7 @@
             shape((rows, pair_end), BF16),
             shape((rows, pair_end), BF16),
             shape((1, count), F32),
+            shape((reach, rows + SEG_ROWS, width), BF16),
         ],
         [
             pltpu.VMEM((width, attn), BF16),
@@ -1033,6 +1035,7 @@
         ],
         [],
         24,
+        63,
     )
 
     per_ff = width // 2 // XY * ff // LANES
@@ -1061,7 +1064,7 @@
     scale_order = jnp.asarray(np.stack([owner, line // LINE], axis=1).astype(np.int32))
     back_keep, back_send, dn1_own, dn1_far = call(
         functools.partial(back_kernel, reach, layout),
-        (*halo, gains, order, scale_order, dg_post, dgq, n1, kraw, dkr, dqr, dv),
+        (toks, tok, gains, order, scale_order, dg_post, dgq, n1, kraw, dkr, dqr, dv),
         (gk, *weights[:3], pack_far),
         [
             shape((XY, per_back + 16, LANES), BF16),
@@ -1098,7 +1101,7 @@
                 line_split_kernel, [len(g) for g in groups], entries, extra, direct, len(after)
             ),
             out_shape=[shape((n, part, LANES), BF16) for n in (stay, LINE - stay)],
-            in_specs=[vmem] * len(arrays) + [hbm] * len(after),
+            in_specs=[vmem] * (len(arrays) + len(after)),
             out_specs=[vmem] * 2,
             scratch_shapes=[pltpu.VMEM((LINE, part, LANES), F32)]
             + [pltpu.VMEM(g[0].shape, F32) for g in groups],
@@ -1109,17 +1112,18 @@
     def join(parts, entries, extra=False):
         outs = [shape((blocks * unit, LANES), F32) for blocks, unit in entries]
         if extra:
-            outs.append(shape((8, LANES), F32))
-        return pl.pallas_call(
+            outs.append(shape((1, share), F32))
+        *arrays, flag = pl.pallas_call(
             functools.partial(join_kernel, len(parts), entries, int(extra)),
-            out_shape=outs,
+            out_shape=outs + [shape((8, LANES), F32)],
             in_specs=[vmem] * len(parts),
-            out_specs=[hbm] * len(outs),
+            out_specs=[hbm] * len(outs) + [vmem],
             scratch_shapes=[pltpu.VMEM(a.shape, a.dtype) for a in outs]
             + [pltpu.VMEM(parts[0].shape, F32), pltpu.SemaphoreType.DMA((len(outs),))],
             compiler_params=pltpu.CompilerParams(vmem_limit_bytes=12 * MIB),
             cost_estimate=pl.CostEstimate(flops=0, bytes_accessed=0, transcendentals=0),
         )(*parts)
+        return arrays, flag
 
     wide, narrow = ff // LANES, width // LANES
     unit_out, unit_down = attn // 32, ff // 32
@@ -1140,13 +1144,13 @@
         False,
     )
     mlp_0, mlp_1 = step(keep, send, XY)
-    own_gate, own_up = join(
+    (own_gate, own_up), mlp_done = join(
         (flat(mlp_0), flat(across(mlp_1, 2 * XY))), ((wide, unit), (wide, unit))
     )
     down_0, down_1 = step(dk, ds, XY)
     down_0, down_1 = step(down_0, down_1, 2)
     down_2, down_3 = step(down_0, down_1, 1)
-    own_down, own_out = join(
+    (own_down, own_out), down_done = join(
         (flat(down_2), flat(across(down_3, 2 * XY))), ((narrow, unit_down), (narrow, unit_out))
     )
 
@@ -1154,7 +1158,7 @@
     dn1, below = pl.pallas_call(
         functools.partial(collect_kernel, per_back + 16),
         out_shape=[shape((rows, width), F32), shape(far_shape, BF16)],
-        in_specs=[hbm] * 2 + [vmem] * (XY - 1) + [hbm] * 2,
+        in_specs=[hbm] * 2 + [vmem] * (XY + 1),
         out_specs=[vmem] * 2,
         scratch_shapes=[
             pltpu.VMEM((rows, width), F32),
@@ -1163,7 +1167,7 @@
         ],
         compiler_params=pltpu.CompilerParams(vmem_limit_bytes=12 * MIB),
         cost_estimate=pl.CostEstimate(flops=0, bytes_accessed=0, transcendentals=0),
-    )(dn1_own, dn1_far, *planes[1:], own_gate, own_down)
+    )(dn1_own, dn1_far, *planes[1:], mlp_done, down_done)
     keep, send = line_split(
         (planes,),
         (
@@ -1175,7 +1179,7 @@
         True,
         (below,),
     )
-    own_query, own_key, own_value, own_gains = join(
+    (own_query, own_key, own_value, own_gains), _ = join(
         (flat(keep), *[across(send[n], (n + 1) * XY) for n in range(LINE - 1)]),
         ((attn // LANES, unit), (size // LANES, unit), (size // LANES, unit)),
         True,
@@ -1201,7 +1205,7 @@
         own_gate.reshape(-1),
         own_up.reshape(-1),
         own_down.reshape(-1),
-        own_gains[0, :share],
+        own_gains.reshape(-1),
     )
 
 

time: 130 us -> 128 us (0.985)
  local copies, waits for them, and re-layouts: 4.38 us -> 0.75 us
    unnamed x32 -> x26, local copies, waits for them, and re-layouts: 3.82 us -> 0.7 us
    ppermute x16, waiting for transfers between devices: 29.6 us -> 31.4 us  [across(): return lax.ppermute(value, 'seq', [(i, i ^ bits) for i in range(XY * LINE)])]
  transfers between devices with their start and end apart: 24 -> 24, of which waited for: 12 -> 11; matrix products, arithmetic and copies ran while one was open for 1% -> 1% of each run, Pallas kernels for 13% -> 13%
where the time goes in v4:
time: 128 us; the launch traced here: 127 us
  starting transfers between devices  45.3 us (35%)
  Pallas kernels  43.6 us (34%)
  waiting for transfers between devices  35.4 us (28%)
    pallas_call x4, Pallas kernels, call(): pl.pallas_call(kernel, out_shape=outs, in_specs=[hbm] * (len(fetched) + l...  32.5 us
    ppermute x16, waiting for transfers between devices, across(): return lax.ppermute(value, 'seq', [(i, i ^ bits) for i in range(XY * LINE)])  31.4 us
    ppermute x16, starting transfers between devices, across(): return lax.ppermute(value, 'seq', [(i, i ^ bits) for i in range(XY * LINE)])  27.7 us
    ppermute x5, starting transfers between devices, shifted(): return lax.ppermute(x, axis, pairs)  17 us
    pallas_call x1, Pallas kernels, fast(): pl.pallas_call(functools.partial(prepare_kernel, layout), out_shape=[shap...  5.71 us
    ppermute x5, waiting for transfers between devices, shifted(): return lax.ppermute(x, axis, pairs)  3.96 us
    pallas_call x3, Pallas kernels, join(): pl.pallas_call(functools.partial(join_kernel, len(parts), entries, int(ex...  2.9 us
  transfers between devices with their start and end apart: 24, of which 11 were waited for; matrix products, arithmetic and copies ran while one was open for 1% of the time, Pallas kernels for 13%

profile of v4, /device:TPU:0, one launch (start us, length us, event | category | flops | bytes accessed | tf_op | source)
XLA Modules:
  0.0 127.5 jit_solution(8945666071541571699)
XLA Ops:
  0.6 5.7 %shard_map.231 = (bf16[144,640]{1,0:T(8,128)(2,1)}, bf16[320,8832]{1,0:T(8,128)(2,1)}) custom-call(bf16[128,640]{1,0:T(8,128)(2,1)} %bitcast.52, s32[1,128]{1,0:T(1,128)} %refs_1_.2, bf16[320,1024]{1,0:T(8,128)(2,1)} %refs_13_.3, bf16[320,256]{1,0:T(8,128)(2,1)} %refs_14_.3, bf16[320,256]{1,0:T(8,128)(2,1)} %refs_15_.3, bf16[320,2048]{1,0:T(8,128)(2,1)} %refs_13_.2, ...), custom_call_target="tpu_custom_call" | custom-call | tf_op jit(solution)/shard_map/pallas_call | solution.py:953
  6.9 4.4 %collective-permute-start.3 = (bf16[144,640]{1,0:T(8,128)(2,1)}, bf16[144,640]{1,0:T(8,128)(2,1)S(1)}, u32[]{:S(2)}, u32[]{:S(2)}) collective-permute-start(bf16[144,640]{1,0:T(8,128)(2,1)} %get-tuple-element.57.refs_4_.refs_1_.refs_0_), channel_id=1, source_target_pairs={{0,2},{2,4},{4,6},{6,8},{8,10},{10,12},{12,14},{14,16},{16,18},{18... | collective-permute-start | bytes 552968 | tf_op jit(solution)/shard_map/ppermute | solution.py:24
  11.3 3.4 %collective-permute-start.2 = (bf16[144,640]{1,0:T(8,128)(2,1)}, bf16[144,640]{1,0:T(8,128)(2,1)S(1)}, u32[]{:S(2)}, u32[]{:S(2)}) collective-permute-start(bf16[144,640]{1,0:T(8,128)(2,1)} %get-tuple-element.57.refs_4_.refs_1_.refs_0_), channel_id=1, source_target_pairs={{0,4},{2,6},{4,8},{6,10},{8,12},{10,14},{12,16},{14,18},{16,20},{1... | collective-permute-start | bytes 552968 | tf_op jit(solution)/shard_map/ppermute | solution.py:24
  14.7 4.4 %collective-permute-start.1 = (bf16[144,640]{1,0:T(8,128)(2,1)}, bf16[144,640]{1,0:T(8,128)(2,1)S(1)}, u32[]{:S(2)}, u32[]{:S(2)}) collective-permute-start(bf16[144,640]{1,0:T(8,128)(2,1)} %get-tuple-element.57.refs_4_.refs_1_.refs_0_), channel_id=1, source_target_pairs={{0,6},{2,8},{4,10},{6,12},{8,14},{10,16},{12,18},{14,20},{16,22},{... | collective-permute-start | bytes 552968 | tf_op jit(solution)/shard_map/ppermute | solution.py:24
  19.1 3.5 %collective-permute-start = (bf16[144,640]{1,0:T(8,128)(2,1)}, bf16[144,640]{1,0:T(8,128)(2,1)S(1)}, u32[]{:S(2)}, u32[]{:S(2)}) collective-permute-start(bf16[144,640]{1,0:T(8,128)(2,1)} %get-tuple-element.57.refs_4_.refs_1_.refs_0_), channel_id=1, source_target_pairs={{0,8},{2,10},{4,12},{6,14},{8,16},{10,18},{12,20},{14,22},{16,24},... | collective-permute-start | bytes 552968 | tf_op jit(solution)/shard_map/ppermute | solution.py:24
  23.4 3.2 %collective-permute-done.refs_0_ = bf16[144,640]{1,0:T(8,128)(2,1)S(1)} collective-permute-done((bf16[144,640]{1,0:T(8,128)(2,1)}, bf16[144,640]{1,0:T(8,128)(2,1)S(1)}, u32[]{:S(2)}, u32[]{:S(2)}) %collective-permute-start) | collective-permute-done | bytes 184352 | tf_op jit(solution)/shard_map/ppermute | solution.py:24
  27.2 13.7 %shard_map.232 = (bf16[640,640]{1,0:T(8,128)(2,1)}, f32[128,1024]{1,0:T(8,128)}, bf16[128,1024]{1,0:T(8,128)(2,1)}, f32[640,256]{1,0:T(8,128)}, bf16[640,256]{1,...) custom-call(bf16[144,640]{1,0:T(8,128)(2,1)} %copy-done.12, ...), custom_call_target="tpu_custom_call" | custom-call | tf_op jit(solution)/shard_map/pallas_call | solution.py:894
  41.0 5.6 %shard_map.233 = (bf16[128,1024]{1,0:T(8,128)(2,1)}, f32[640,256]{1,0:T(8,128)}, bf16[640,256]{1,0:T(8,128)(2,1)}, f32[1,256]{1,0:T(1,128)}) custom-call(f32[1,3072]{1,0:T(1,128)} %get-tuple-element.60.refs_0_.refs_2_.refs_1_, f32[640,128]{1,0:T(8,128)} %constant.12.clone.refs_8_.refs_1_, f32[640,128]{1,0:T(8,128)} %constant.13.clone.refs_9_.refs_2_, ...), custom_call_target="tpu_custom_call" | custom-call | tf_op jit(solution)/shard_map/pallas_call | solution.py:894
  46.7 5.2 %shard_map.234 = (bf16[2,1280,128]{2,1,0:T(8,128)(2,1)}, bf16[2,1280,128]{2,1,0:T(8,128)(2,1)}, bf16[2,1280,128]{2,1,0:T(8,128)(2,1)}, bf16[2,1280,128]{2,1,0:T(...) custom-call(bf16[128,7296]{1,0:T(8,128)(2,1)} %get-tuple-element.76.refs_0_, ...), custom_call_target="tpu_custom_call" | custom-call | tf_op jit(solution)/shard_map/pallas_call | solution.py:894
  51.9 1.4 %collective-permute-start.10 = (bf16[2,1280,128]{2,1,0:T(8,128)(2,1)}, bf16[2,1280,128]{2,1,0:T(8,128)(2,1)S(1)}, u32[]{:S(2)}, u32[]{:S(2)}) collective-permute-start(bf16[2,1280,128]{2,1,0:T(8,128)(2,1)} %get-tuple-element.83), channel_id=1, source_target_pairs={{0,2},{2,0},{4,6},{6,4},{8,10},{10,8},{12,14},{14,12},{16,18},{18,... | collective-permute-start | bytes 1966088 | tf_op jit(solution)/shard_map/ppermute | solution.py:944
  53.3 3.1 %collective-permute-start.12 = (bf16[2,1280,128]{2,1,0:T(8,128)(2,1)}, bf16[2,1280,128]{2,1,0:T(8,128)(2,1)S(1)}, u32[]{:S(2)}, u32[]{:S(2)}) collective-permute-start(bf16[2,1280,128]{2,1,0:T(8,128)(2,1)} %get-tuple-element.85), channel_id=1, source_target_pairs={{0,4},{2,6},{4,0},{6,2},{8,12},{10,14},{12,8},{14,10},{16,20},{18,... | collective-permute-start | bytes 1966088 | tf_op jit(solution)/shard_map/ppermute | solution.py:944
  56.4 2.4 %collective-permute-start.16 = (bf16[8,480,128]{2,1,0:T(8,128)(2,1)}, bf16[8,480,128]{2,1,0:T(8,128)(2,1)S(1)}, u32[]{:S(2)}, u32[]{:S(2)}) collective-permute-start(bf16[8,480,128]{2,1,0:T(8,128)(2,1)} %get-tuple-element.90), channel_id=1, source_target_pairs={{0,8},{2,10},{4,12},{6,14},{8,0},{10,2},{12,4},{14,6},{16,24},{18,... | collective-permute-start | bytes 2949128 | tf_op jit(solution)/shard_map/ppermute | solution.py:944
  58.8 7.9 %shard_map.235 = (bf16[4,976,128]{2,1,0:T(8,128)(2,1)}, bf16[4,976,128]{2,1,0:T(8,128)(2,1)}, f32[128,640]{1,0:T(8,128)}, bf16[4,640,128]{2,1,0:T(8,128)(2,1)}) custom-call(bf16[4,144,640]{2,1,0:T(8,128)(2,1)} %get-tuple-element.62.refs_0_, bf16[144,640]{1,0:T(8,128)(2,1)} %get-tuple-element.57.refs_4_.refs_1_.refs_0_, ...), custom_call_target="tpu_custom_call" | custom-call | tf_op jit(solution)/shard_map/pallas_call | solution.py:894
  66.8 2.5 %collective-permute-done.10 = bf16[2,1280,128]{2,1,0:T(8,128)(2,1)S(1)} collective-permute-done((bf16[2,1280,128]{2,1,0:T(8,128)(2,1)}, bf16[2,1280,128]{2,1,0:T(8,128)(2,1)S(1)}, u32[]{:S(2)}, u32[]{:S(2)}) %collective-permute-start.10) | collective-permute-done | bytes 655392 | tf_op jit(solution)/shard_map/ppermute | solution.py:944
  69.5 3.8 %collective-permute-start.11 = (bf16[1,1280,128]{2,1,0:T(8,128)(2,1)S(1)}, bf16[1,1280,128]{2,1,0:T(8,128)(2,1)S(1)}, u32[]{:S(2)}, u32[]{:S(2)}) collective-permute-start(bf16[1,1280,128]{2,1,0:T(8,128)(2,1)S(1)} %get-tuple-element.112), channel_id=1, source_target_pairs={{0,4},{2,6},{4,0},{6,2},{8,12},{10,14},{12,8},{14,10},{16,20},{18,... | collective-permute-start | bytes 983048 | tf_op jit(solution)/shard_map/ppermute | solution.py:944
  74.3 6.6 %collective-permute-done.16 = bf16[8,480,128]{2,1,0:T(8,128)(2,1)S(1)} collective-permute-done((bf16[8,480,128]{2,1,0:T(8,128)(2,1)}, bf16[8,480,128]{2,1,0:T(8,128)(2,1)S(1)}, u32[]{:S(2)}, u32[]{:S(2)}) %collective-permute-start.16) | collective-permute-done | bytes 983072 | tf_op jit(solution)/shard_map/ppermute | solution.py:944
  81.4 1.2 collective-permute-done.13
  83.0 2.4 %collective-permute-start.14 = (bf16[2,640,128]{2,1,0:T(8,128)(2,1)S(1)}, bf16[2,640,128]{2,1,0:T(8,128)(2,1)S(1)}, u32[]{:S(2)}, u32[]{:S(2)}) collective-permute-start(bf16[2,640,128]{2,1,0:T(8,128)(2,1)S(1)} %get-tuple-element.87), channel_id=1, source_target_pairs={{0,8},{2,10},{4,12},{6,14},{8,0},{10,2},{12,4},{14,6},{16,24},{18,... | collective-permute-start | bytes 983048 | tf_op jit(solution)/shard_map/ppermute | solution.py:944
  86.4 0.9 collective-permute-start.8
  87.3 8.0 %collective-permute-done.17 = bf16[4,480,128]{2,1,0:T(8,128)(2,1)S(1)} collective-permute-done((bf16[4,480,128]{2,1,0:T(8,128)(2,1)S(1)}, bf16[4,480,128]{2,1,0:T(8,128)(2,1)S(1)}, u32[]{:S(2)}, u32[]{:S(2)}) %collective-permute-start.17) | collective-permute-done | bytes 491552 | tf_op jit(solution)/shard_map/ppermute | solution.py:944
  95.5 1.5 %collective-permute-start.18 = (bf16[2,480,128]{2,1,0:T(8,128)(2,1)S(1)}, bf16[2,480,128]{2,1,0:T(8,128)(2,1)S(1)}, u32[]{:S(2)}, u32[]{:S(2)}) collective-permute-start(bf16[2,480,128]{2,1,0:T(8,128)(2,1)S(1)} %get-tuple-element.115), channel_id=1, source_target_pairs={{0,2},{2,0},{4,6},{6,4},{8,10},{10,8},{12,14},{14,12},{16,18},{18,... | collective-permute-start | bytes 737288 | tf_op jit(solution)/shard_map/ppermute | solution.py:944
  97.4 2.9 %collective-permute-start.15 = (bf16[1,640,128]{2,1,0:T(8,128)(2,1)S(1)}, bf16[1,640,128]{2,1,0:T(8,128)(2,1)S(1)}, u32[]{:S(2)}, u32[]{:S(2)}) collective-permute-start(bf16[1,640,128]{2,1,0:T(8,128)(2,1)S(1)} %get-tuple-element.116), channel_id=1, source_target_pairs={{0,16},{2,18},{4,20},{6,22},{8,24},{10,26},{12,28},{14,30},{16,0},... | collective-permute-start | bytes 491528 | tf_op jit(solution)/shard_map/ppermute | solution.py:944
  100.3 4.2 %collective-permute-done.18 = bf16[2,480,128]{2,1,0:T(8,128)(2,1)S(1)} collective-permute-done((bf16[2,480,128]{2,1,0:T(8,128)(2,1)S(1)}, bf16[2,480,128]{2,1,0:T(8,128)(2,1)S(1)}, u32[]{:S(2)}, u32[]{:S(2)}) %collective-permute-start.18) | collective-permute-done | bytes 245792 | tf_op jit(solution)/shard_map/ppermute | solution.py:944
  104.5 2.8 %collective-permute-start.19 = (bf16[1,480,128]{2,1,0:T(8,128)(2,1)S(1)}, bf16[1,480,128]{2,1,0:T(8,128)(2,1)S(1)}, u32[]{:S(2)}, u32[]{:S(2)}) collective-permute-start(bf16[1,480,128]{2,1,0:T(8,128)(2,1)S(1)} %get-tuple-element.121), channel_id=1, source_target_pairs={{0,16},{2,18},{4,20},{6,22},{8,24},{10,26},{12,28},{14,30},{16,0},... | collective-permute-start | bytes 368648 | tf_op jit(solution)/shard_map/ppermute | solution.py:944
  108.0 0.9 shard_map.237
  108.9 2.8 %collective-permute-done.19 = bf16[1,480,128]{2,1,0:T(8,128)(2,1)S(1)} collective-permute-done((bf16[1,480,128]{2,1,0:T(8,128)(2,1)S(1)}, bf16[1,480,128]{2,1,0:T(8,128)(2,1)S(1)}, u32[]{:S(2)}, u32[]{:S(2)}) %collective-permute-start.19) | collective-permute-done | bytes 122912 | tf_op jit(solution)/shard_map/ppermute | solution.py:944
  113.1 1.3 %collective-permute-start.20 = (bf16[640,128]{1,0:T(8,128)(2,1)S(1)}, bf16[640,128]{1,0:T(8,128)(2,1)S(1)}, u32[]{:S(2)}, u32[]{:S(2)}) collective-permute-start(bf16[640,128]{1,0:T(8,128)(2,1)S(1)} %get-tuple-element.93.refs_4_), channel_id=1, source_target_pairs={{8,0},{10,2},{12,4},{14,6},{16,8},{18,10},{20,12},{22,14},{24,16},... | collective-permute-start | bytes 491528 | tf_op jit(solution)/shard_map/ppermute | solution.py:24
  114.6 3.7 %collective-permute-start.23 = (bf16[256,128]{1,0:T(8,128)(2,1)S(1)}, bf16[256,128]{1,0:T(8,128)(2,1)S(1)}, u32[]{:S(2)}, u32[]{:S(2)}) collective-permute-start(bf16[256,128]{1,0:T(8,128)(2,1)S(1)} %get-tuple-element.123), channel_id=1, source_target_pairs={{0,24},{2,26},{4,28},{6,30},{8,16},{10,18},{12,20},{14,22},{16,8},... | collective-permute-start | bytes 196616 | tf_op jit(solution)/shard_map/ppermute | solution.py:944
  119.1 3.7 %collective-permute-done.23.refs_3_ = bf16[256,128]{1,0:T(8,128)(2,1)S(1)} collective-permute-done((bf16[256,128]{1,0:T(8,128)(2,1)S(1)}, bf16[256,128]{1,0:T(8,128)(2,1)S(1)}, u32[]{:S(2)}, u32[]{:S(2)}) %collective-permute-start.23) | collective-permute-done | bytes 65568 | tf_op jit(solution)/shard_map/ppermute | solution.py:944
  122.8 1.8 %collective-permute-done.22.refs_2_ = bf16[256,128]{1,0:T(8,128)(2,1)S(1)} collective-permute-done((bf16[256,128]{1,0:T(8,128)(2,1)S(1)}, bf16[256,128]{1,0:T(8,128)(2,1)S(1)}, u32[]{:S(2)}, u32[]{:S(2)}) %collective-permute-start.22) | collective-permute-done | bytes 65568 | tf_op jit(solution)/shard_map/ppermute | solution.py:944
  124.6 1.3 %shard_map.242 = (f32[160,128]{1,0:T(8,128)}, f32[40,128]{1,0:T(8,128)}, f32[40,128]{1,0:T(8,128)}, f32[1,96]{1,0:T(1,128)}, f32[8,128]{1,0:T(8,128)}) custom-call(bf16[256,128]{1,0:T(8,128)(2,1)S(1)} %bitcast.50, bf16[256,128]{1,0:T(8,128)(2,1)S(1)} %collective-permute-done.21.refs_1_, bf16[256,128]{1,0:T(8,128)(2,1)S(1)} %collective-permute-done.22.refs_2_, ...), custom_call_target="tpu_custom_call" | custom-call | tf_op jit(solution)/shard_map/pallas_call | solution.py:1116
  126.0 1.3 %shard_map.240 = f32[128,640]{1,0:T(8,128)} custom-call(bf16[144,640]{1,0:T(8,128)(2,1)S(1)} %copy-done.1, f32[1,3072]{1,0:T(1,128)S(1)} %copy-done.4, f32[128,640]{1,0:T(8,128)S(1)} %copy-done.3, f32[128,640]{1,0:T(8,128)S(1)} %get-tuple-element.92.refs_3_, bf16[640,128]{1,0:T(8,128)(2,1)S(1)} %collective-permute-done.20.refs_4_), custom_call_target="tpu_custom_call" | custom-call | tf_op jit(solution)/shard_map/pallas_call | solution.py:1188
  (66 shorter events, 8.8 us)
Async XLA Ops:
  6.4 20.2 %collective-permute-start.4 = (bf16[320,8832]{1,0:T(8,128)(2,1)}, bf16[320,8832]{1,0:T(8,128)(2,1)}, u32[]{:S(2)}, u32[]{:S(2)}) collective-permute-start(bf16[320,8832]{1,0:T(8,128)(2,1)} %get-tuple-element.58), channel_id=1, source_target_pairs={{0,1},{1,0},{2,3},{3,2},{4,5},{5,4},{6,7},{7,6},{8,9},{9,8},{10,11... | collective-permute-start | bytes 16957448 | tf_op jit(solution)/shard_map/ppermute | solution.py:941
  6.9 15.7 %collective-permute-start.3 = (bf16[144,640]{1,0:T(8,128)(2,1)}, bf16[144,640]{1,0:T(8,128)(2,1)S(1)}, u32[]{:S(2)}, u32[]{:S(2)}) collective-permute-start(bf16[144,640]{1,0:T(8,128)(2,1)} %get-tuple-element.57.refs_4_.refs_1_.refs_0_), channel_id=1, source_target_pairs={{0,2},{2,4},{4,6},{6,8},{8,10},{10,12},{12,14},{14,16},{16,18},{18... | collective-permute-start | bytes 552968 | tf_op jit(solution)/shard_map/ppermute | solution.py:24
  11.3 11.3 %collective-permute-start.2 = (bf16[144,640]{1,0:T(8,128)(2,1)}, bf16[144,640]{1,0:T(8,128)(2,1)S(1)}, u32[]{:S(2)}, u32[]{:S(2)}) collective-permute-start(bf16[144,640]{1,0:T(8,128)(2,1)} %get-tuple-element.57.refs_4_.refs_1_.refs_0_), channel_id=1, source_target_pairs={{0,4},{2,6},{4,8},{6,10},{8,12},{10,14},{12,16},{14,18},{16,20},{1... | collective-permute-start | bytes 552968 | tf_op jit(solution)/shard_map/ppermute | solution.py:24
  14.7 8.6 %collective-permute-start.1 = (bf16[144,640]{1,0:T(8,128)(2,1)}, bf16[144,640]{1,0:T(8,128)(2,1)S(1)}, u32[]{:S(2)}, u32[]{:S(2)}) collective-permute-start(bf16[144,640]{1,0:T(8,128)(2,1)} %get-tuple-element.57.refs_4_.refs_1_.refs_0_), channel_id=1, source_target_pairs={{0,6},{2,8},{4,10},{6,12},{8,14},{10,16},{12,18},{14,20},{16,22},{... | collective-permute-start | bytes 552968 | tf_op jit(solution)/shard_map/ppermute | solution.py:24
  19.1 7.5 %collective-permute-start = (bf16[144,640]{1,0:T(8,128)(2,1)}, bf16[144,640]{1,0:T(8,128)(2,1)S(1)}, u32[]{:S(2)}, u32[]{:S(2)}) collective-permute-start(bf16[144,640]{1,0:T(8,128)(2,1)} %get-tuple-element.57.refs_4_.refs_1_.refs_0_), channel_id=1, source_target_pairs={{0,8},{2,10},{4,12},{6,14},{8,16},{10,18},{12,20},{14,22},{16,24},... | collective-permute-start | bytes 552968 | tf_op jit(solution)/shard_map/ppermute | solution.py:24
  40.9 5.7 %collective-permute-start.5 = (bf16[128,7296]{1,0:T(8,128)(2,1)}, bf16[128,7296]{1,0:T(8,128)(2,1)}, u32[]{:S(2)}, u32[]{:S(2)}) collective-permute-start(bf16[128,7296]{1,0:T(8,128)(2,1)} %get-tuple-element.77), channel_id=1, source_target_pairs={{0,1},{1,0},{2,3},{3,2},{4,5},{5,4},{6,7},{7,6},{8,9},{9,8},{10,11... | collective-permute-start | bytes 5603336 | tf_op jit(solution)/shard_map/ppermute | solution.py:941
  51.9 17.4 %collective-permute-start.10 = (bf16[2,1280,128]{2,1,0:T(8,128)(2,1)}, bf16[2,1280,128]{2,1,0:T(8,128)(2,1)S(1)}, u32[]{:S(2)}, u32[]{:S(2)}) collective-permute-start(bf16[2,1280,128]{2,1,0:T(8,128)(2,1)} %get-tuple-element.83), channel_id=1, source_target_pairs={{0,2},{2,0},{4,6},{6,4},{8,10},{10,8},{12,14},{14,12},{16,18},{18,... | collective-permute-start | bytes 1966088 | tf_op jit(solution)/shard_map/ppermute | solution.py:944
  53.3 20.0 %collective-permute-start.12 = (bf16[2,1280,128]{2,1,0:T(8,128)(2,1)}, bf16[2,1280,128]{2,1,0:T(8,128)(2,1)S(1)}, u32[]{:S(2)}, u32[]{:S(2)}) collective-permute-start(bf16[2,1280,128]{2,1,0:T(8,128)(2,1)} %get-tuple-element.85), channel_id=1, source_target_pairs={{0,4},{2,6},{4,0},{6,2},{8,12},{10,14},{12,8},{14,10},{16,20},{18,... | collective-permute-start | bytes 1966088 | tf_op jit(solution)/shard_map/ppermute | solution.py:944
  56.4 24.4 %collective-permute-start.16 = (bf16[8,480,128]{2,1,0:T(8,128)(2,1)}, bf16[8,480,128]{2,1,0:T(8,128)(2,1)S(1)}, u32[]{:S(2)}, u32[]{:S(2)}) collective-permute-start(bf16[8,480,128]{2,1,0:T(8,128)(2,1)} %get-tuple-element.90), channel_id=1, source_target_pairs={{0,8},{2,10},{4,12},{6,14},{8,0},{10,2},{12,4},{14,6},{16,24},{18,... | collective-permute-start | bytes 2949128 | tf_op jit(solution)/shard_map/ppermute | solution.py:944
  58.8 10.6 %copy-start.5 = (bf16[2,1280,128]{2,1,0:T(8,128)(2,1)S(1)}, bf16[2,1280,128]{2,1,0:T(8,128)(2,1)}, u32[]{:S(2)}) copy-start(bf16[2,1280,128]{2,1,0:T(8,128)(2,1)} %get-tuple-element.78.refs_12_) | copy-start | bytes 1966084
  66.7 6.6 %copy-start.8 = (bf16[2,1280,128]{2,1,0:T(8,128)(2,1)S(1)}, bf16[2,1280,128]{2,1,0:T(8,128)(2,1)}, u32[]{:S(2)}) copy-start(bf16[2,1280,128]{2,1,0:T(8,128)(2,1)} %get-tuple-element.84) | copy-start | bytes 1966084
  66.7 7.5 %copy-start = (bf16[4,640,128]{2,1,0:T(8,128)(2,1)S(1)}, bf16[4,640,128]{2,1,0:T(8,128)(2,1)}, u32[]{:S(2)}) copy-start(bf16[4,640,128]{2,1,0:T(8,128)(2,1)} %get-tuple-element.80.refs_1_) | copy-start | bytes 1966084
  66.7 18.7 %collective-permute-start.6 = (bf16[4,976,128]{2,1,0:T(8,128)(2,1)}, bf16[4,976,128]{2,1,0:T(8,128)(2,1)S(1)}, u32[]{:S(2)}, u32[]{:S(2)}) collective-permute-start(bf16[4,976,128]{2,1,0:T(8,128)(2,1)} %get-tuple-element.82), channel_id=1, source_target_pairs={{0,1},{1,0},{2,3},{3,2},{4,5},{5,4},{6,7},{7,6},{8,9},{9,8},{10,11... | collective-permute-start | bytes 2998280 | tf_op jit(solution)/shard_map/ppermute | solution.py:941
  69.5 11.3 %copy-start.7 = (bf16[8,480,128]{2,1,0:T(8,128)(2,1)S(1)}, bf16[8,480,128]{2,1,0:T(8,128)(2,1)}, u32[]{:S(2)}) copy-start(bf16[8,480,128]{2,1,0:T(8,128)(2,1)} %get-tuple-element.89) | copy-start | bytes 2949124
  69.5 11.9 %collective-permute-start.11 = (bf16[1,1280,128]{2,1,0:T(8,128)(2,1)S(1)}, bf16[1,1280,128]{2,1,0:T(8,128)(2,1)S(1)}, u32[]{:S(2)}, u32[]{:S(2)}) collective-permute-start(bf16[1,1280,128]{2,1,0:T(8,128)(2,1)S(1)} %get-tuple-element.112), channel_id=1, source_target_pairs={{0,4},{2,6},{4,0},{6,2},{8,12},{10,14},{12,8},{14,10},{16,20},{18,... | collective-permute-start | bytes 983048 | tf_op jit(solution)/shard_map/ppermute | solution.py:944
  73.5 9.1 %collective-permute-start.13 = (bf16[1,1280,128]{2,1,0:T(8,128)(2,1)S(1)}, bf16[1,1280,128]{2,1,0:T(8,128)(2,1)S(1)}, u32[]{:S(2)}, u32[]{:S(2)}) collective-permute-start(bf16[1,1280,128]{2,1,0:T(8,128)(2,1)S(1)} %get-tuple-element.110), channel_id=1, source_target_pairs={{0,2},{2,0},{4,6},{6,4},{8,10},{10,8},{12,14},{14,12},{16,18},{18,... | collective-permute-start | bytes 983048 | tf_op jit(solution)/shard_map/ppermute | solution.py:944
  81.1 14.2 %collective-permute-start.17 = (bf16[4,480,128]{2,1,0:T(8,128)(2,1)S(1)}, bf16[4,480,128]{2,1,0:T(8,128)(2,1)S(1)}, u32[]{:S(2)}, u32[]{:S(2)}) collective-permute-start(bf16[4,480,128]{2,1,0:T(8,128)(2,1)S(1)} %get-tuple-element.109), channel_id=1, source_target_pairs={{0,4},{2,6},{4,0},{6,2},{8,12},{10,14},{12,8},{14,10},{16,20},{18,... | collective-permute-start | bytes 1474568 | tf_op jit(solution)/shard_map/ppermute | solution.py:944
  83.0 14.4 %collective-permute-start.14 = (bf16[2,640,128]{2,1,0:T(8,128)(2,1)S(1)}, bf16[2,640,128]{2,1,0:T(8,128)(2,1)S(1)}, u32[]{:S(2)}, u32[]{:S(2)}) collective-permute-start(bf16[2,640,128]{2,1,0:T(8,128)(2,1)S(1)} %get-tuple-element.87), channel_id=1, source_target_pairs={{0,8},{2,10},{4,12},{6,14},{8,0},{10,2},{12,4},{14,6},{16,24},{18,... | collective-permute-start | bytes 983048 | tf_op jit(solution)/shard_map/ppermute | solution.py:944
  85.7 26.7 %collective-permute-start.7 = (bf16[1616,128]{1,0:T(8,128)(2,1)S(1)}, bf16[1616,128]{1,0:T(8,128)(2,1)S(1)}, u32[]{:S(2)}, u32[]{:S(2)}) collective-permute-start(bf16[1616,128]{1,0:T(8,128)(2,1)S(1)} %pad_maximum_fusion), channel_id=1, source_target_pairs={{0,2},{2,0},{4,6},{6,4},{8,10},{10,8},{12,14},{14,12},{16,18},{18,... | collective-permute-start | bytes 1241096 | tf_op jit(solution)/shard_map/ppermute | solution.py:944
  86.4 26.0 %collective-permute-start.8 = (bf16[1616,128]{1,0:T(8,128)(2,1)S(1)}, bf16[1616,128]{1,0:T(8,128)(2,1)S(1)}, u32[]{:S(2)}, u32[]{:S(2)}) collective-permute-start(bf16[1616,128]{1,0:T(8,128)(2,1)S(1)} %pad_maximum_fusion.1), channel_id=1, source_target_pairs={{0,4},{2,6},{4,0},{6,2},{8,12},{10,14},{12,8},{14,10},{16,20},{18,... | collective-permute-start | bytes 1241096 | tf_op jit(solution)/shard_map/ppermute | solution.py:944
  95.4 17.0 %copy-start.2 = (f32[128,640]{1,0:T(8,128)S(1)}, f32[128,640]{1,0:T(8,128)}, u32[]{:S(2)}) copy-start(f32[128,640]{1,0:T(8,128)} %get-tuple-element.79.refs_0_) | copy-start | bytes 983044
  95.5 9.0 %collective-permute-start.18 = (bf16[2,480,128]{2,1,0:T(8,128)(2,1)S(1)}, bf16[2,480,128]{2,1,0:T(8,128)(2,1)S(1)}, u32[]{:S(2)}, u32[]{:S(2)}) collective-permute-start(bf16[2,480,128]{2,1,0:T(8,128)(2,1)S(1)} %get-tuple-element.115), channel_id=1, source_target_pairs={{0,2},{2,0},{4,6},{6,4},{8,10},{10,8},{12,14},{14,12},{16,18},{18,... | collective-permute-start | bytes 737288 | tf_op jit(solution)/shard_map/ppermute | solution.py:944
  97.0 15.5 %collective-permute-start.9 = (bf16[1616,128]{1,0:T(8,128)(2,1)S(1)}, bf16[1616,128]{1,0:T(8,128)(2,1)S(1)}, u32[]{:S(2)}, u32[]{:S(2)}) collective-permute-start(bf16[1616,128]{1,0:T(8,128)(2,1)S(1)} %pad_maximum_fusion.2), channel_id=1, source_target_pairs={{0,6},{2,4},{4,2},{6,0},{8,14},{10,12},{12,10},{14,8},{16,22},{18,... | collective-permute-start | bytes 1241096 | tf_op jit(solution)/shard_map/ppermute | solution.py:944
  97.4 10.6 %collective-permute-start.15 = (bf16[1,640,128]{2,1,0:T(8,128)(2,1)S(1)}, bf16[1,640,128]{2,1,0:T(8,128)(2,1)S(1)}, u32[]{:S(2)}, u32[]{:S(2)}) collective-permute-start(bf16[1,640,128]{2,1,0:T(8,128)(2,1)S(1)} %get-tuple-element.116), channel_id=1, source_target_pairs={{0,16},{2,18},{4,20},{6,22},{8,24},{10,26},{12,28},{14,30},{16,0},... | collective-permute-start | bytes 491528 | tf_op jit(solution)/shard_map/ppermute | solution.py:944
  104.5 7.2 %collective-permute-start.19 = (bf16[1,480,128]{2,1,0:T(8,128)(2,1)S(1)}, bf16[1,480,128]{2,1,0:T(8,128)(2,1)S(1)}, u32[]{:S(2)}, u32[]{:S(2)}) collective-permute-start(bf16[1,480,128]{2,1,0:T(8,128)(2,1)S(1)} %get-tuple-element.121), channel_id=1, source_target_pairs={{0,16},{2,18},{4,20},{6,22},{8,24},{10,26},{12,28},{14,30},{16,0},... | collective-permute-start | bytes 368648 | tf_op jit(solution)/shard_map/ppermute | solution.py:944
  112.5 13.5 %copy-start.1 = (bf16[144,640]{1,0:T(8,128)(2,1)S(1)}, bf16[144,640]{1,0:T(8,128)(2,1)}, u32[]{:S(2)}) copy-start(bf16[144,640]{1,0:T(8,128)(2,1)} %get-tuple-element.57.refs_4_.refs_1_.refs_0_) | copy-start | bytes 552964
  112.5 13.5 %copy-start.3 = (f32[128,640]{1,0:T(8,128)S(1)}, f32[128,640]{1,0:T(8,128)}, u32[]{:S(2)}) copy-start(f32[128,640]{1,0:T(8,128)} %get-tuple-element.61.refs_2_) | copy-start | bytes 983044
  112.5 13.5 %copy-start.4 = (f32[1,3072]{1,0:T(1,128)S(1)}, f32[1,3072]{1,0:T(1,128)}, u32[]{:S(2)}) copy-start(f32[1,3072]{1,0:T(1,128)} %get-tuple-element.60.refs_0_.refs_2_.refs_1_) | copy-start | bytes 36868
  113.1 12.9 %collective-permute-start.20 = (bf16[640,128]{1,0:T(8,128)(2,1)S(1)}, bf16[640,128]{1,0:T(8,128)(2,1)S(1)}, u32[]{:S(2)}, u32[]{:S(2)}) collective-permute-start(bf16[640,128]{1,0:T(8,128)(2,1)S(1)} %get-tuple-element.93.refs_4_), channel_id=1, source_target_pairs={{8,0},{10,2},{12,4},{14,6},{16,8},{18,10},{20,12},{22,14},{24,16},... | collective-permute-start | bytes 491528 | tf_op jit(solution)/shard_map/ppermute | solution.py:24
  114.6 8.1 %collective-permute-start.23 = (bf16[256,128]{1,0:T(8,128)(2,1)S(1)}, bf16[256,128]{1,0:T(8,128)(2,1)S(1)}, u32[]{:S(2)}, u32[]{:S(2)}) collective-permute-start(bf16[256,128]{1,0:T(8,128)(2,1)S(1)} %get-tuple-element.123), channel_id=1, source_target_pairs={{0,24},{2,26},{4,28},{6,30},{8,16},{10,18},{12,20},{14,22},{16,8},... | collective-permute-start | bytes 196616 | tf_op jit(solution)/shard_map/ppermute | solution.py:944
  118.3 6.3 %collective-permute-start.22 = (bf16[256,128]{1,0:T(8,128)(2,1)S(1)}, bf16[256,128]{1,0:T(8,128)(2,1)S(1)}, u32[]{:S(2)}, u32[]{:S(2)}) collective-permute-start(bf16[256,128]{1,0:T(8,128)(2,1)S(1)} %get-tuple-element.124), channel_id=1, source_target_pairs={{0,16},{2,18},{4,20},{6,22},{8,24},{10,26},{12,28},{14,30},{16,0},... | collective-permute-start | bytes 196616 | tf_op jit(solution)/shard_map/ppermute | solution.py:944
  118.8 5.8 %collective-permute-start.21 = (bf16[256,128]{1,0:T(8,128)(2,1)S(1)}, bf16[256,128]{1,0:T(8,128)(2,1)S(1)}, u32[]{:S(2)}, u32[]{:S(2)}) collective-permute-start(bf16[256,128]{1,0:T(8,128)(2,1)S(1)} %get-tuple-element.125), channel_id=1, source_target_pairs={{0,8},{2,10},{4,12},{6,14},{8,0},{10,2},{12,4},{14,6},{16,24},{18,... | collective-permute-start | bytes 196616 | tf_op jit(solution)/shard_map/ppermute | solution.py:944
  (5 other events, 16.5 us)

commit v5 on v4

--- a/solution.py
+++ b/solution.py
@@ -518,7 +518,8 @@
     keep_h, send_h = outs_h[11:13]
 
     def sent(begin, stop):
-        for ref, target in ((send, send_h), (keep, keep_h)):
+        both = ((send, send_h), (keep, keep_h)) if begin >= at_hid else ((send, send_h),)
+        for ref, target in both:
             traffic.emit(ref.at[:, begin:stop], target.at[:, begin:stop])
 
     n2_owned = mm_nt(n2, row_order(order, width, place, core)).astype(BF16)
@@ -550,8 +551,7 @@
     mixed_out[...] = (x2 + hat_d * g_pff).astype(BF16)
     traffic.emit(mixed_out, outs_h[7])
     df = norm_back(hat_d, inv_d, g_pff, c).astype(BF16)
-    for ref in (send, keep):
-        ref[:, at_df : at_df + width] = df
+    send[:, at_df : at_df + width] = df
     sent(at_df, at_df + width)
     dn2 = jnp.zeros((rows, width), F32)
     for at in range(0, ff, part):
@@ -559,16 +559,14 @@
         dhid = mm_nt(df, wd[cols, :])
         dgate = (dhid * slope_s[:, cols]).astype(BF16)
         dup = (dhid * act_s[:, cols]).astype(BF16)
-        for ref in (send, keep):
-            ref[:, at_gate + at : at_gate + at + part] = dgate
-            ref[:, at_up + at : at_up + at + part] = dup
+        send[:, at_gate + at : at_gate + at + part] = dgate
+        send[:, at_up + at : at_up + at + part] = dup
         sent(at_gate + at, at_gate + at + part)
         sent(at_up + at, at_up + at + part)
         dn2 = dn2 + mm_nt(dgate, wg[:, cols]) + mm_nt(dup, wu[:, cols])
     dx2 = c + norm_back(hat_f, inv_f, g_pf, dn2)
     dya = norm_back(hat_a, inv_a, g_pa, dx2).astype(BF16)
-    for ref in (send, keep):
-        ref[:, at_dya : at_dya + width] = dya
+    send[:, at_dya : at_dya + width] = dya
     sent(at_dya, at_dya + width)
     dao_out[...] = mm_nt(dya, wo[...]).astype(BF16)
     traffic.emit(dao_out, outs_h[9])
@@ -590,9 +588,10 @@
 
 
 def grads_kernel(width, ff, attn, *refs):
-    sources, outs_h, outs = refs[:2], refs[3:9], refs[9:15]
+    keep_h, send_h, recv_h = refs[:3]
+    outs_h, outs = refs[4:10], refs[10:16]
     gk, gs, uk, us, dk, ds = outs
-    both, prod_s, sems = refs[15:]
+    both, prod_s, sems = refs[16:]
     traffic = Traffic(sems)
     place = lax.axis_index("seq")
     (at_gate, at_up, at_df, at_dya, at_hid, at_ao, at_n2), end = pair_columns(width, ff, attn)
@@ -601,14 +600,15 @@
         traffic.emit(ref, outs_h[[r is ref for r in outs].index(True)])
 
     def fetch(begin, stop):
+        own_h = keep_h if begin >= at_hid else send_h
         return traffic.fetch(
             (source.at[:, begin:stop], both.at[side * LANES : (side + 1) * LANES, begin:stop])
-            for side, source in enumerate(sources)
+            for side, source in enumerate((own_h, recv_h))
         )
 
     gate_w = fetch(at_n2, end) + fetch(at_gate, at_up)
     up_w = fetch(at_up, at_df)
-    rest_w = fetch(at_df, at_n2)
+    rest_w = fetch(at_df, at_hid) + fetch(at_hid, at_n2)
     per = width // 2 // XY
     for copies, base, (keep, send), first in (
         (gate_w, at_gate, (gk, gs), "x"),
@@ -653,68 +653,56 @@
 
 
 def heads_kernel(*refs):
-    count = 9
-    ins_h, outs_h, refs = refs[:count], refs[count : count + 4], refs[count + 4 :]
-    ins, outs, sems = refs[:count], refs[count : count + 4], refs[-1]
-    gains, cos_ref, sin_ref, qraw_ref, q_ref, k_ref, v_ref, dao_ref, p_ref = ins
-    dqr, dkr, dv_out, dgq_out = outs
+    count = 5
+    ins_h, outs_h, refs = refs[:count], refs[count : count + 3], refs[count + 3 :]
+    ins, outs, sems = refs[:count], refs[count : count + 3], refs[-1]
+    q_ref, k_ref, v_ref, dao_ref, p_ref = ins
+    dq_out, dk_out, done = outs
     traffic = Traffic(sems)
     heads = p_ref.shape[0]
-    first = traffic.fetch([(ins_h[n], ins[n]) for n in (7, 6, 5)])
-    p_w = [traffic.start(ins_h[8].at[0], p_ref.at[0])]
-    second = traffic.fetch([(ins_h[n], ins[n]) for n in range(5)])
-    p_w += [traffic.start(ins_h[8].at[h], p_ref.at[h]) for h in range(1, heads)]
+    first = traffic.fetch([(ins_h[n], ins[n]) for n in (3, 2)])
+    p_w = [traffic.start(ins_h[4].at[0], p_ref.at[0])]
+    second = traffic.fetch([(ins_h[n], ins[n]) for n in (1, 0)])
+    p_w += [traffic.start(ins_h[4].at[h], p_ref.at[h]) for h in range(1, heads)]
+    keys, size = k_ref.shape
     wait(first)
-    rows, size = q_ref.shape[0], k_ref.shape[1]
-    keys = k_ref.shape[0]
-    width = gains.shape[1] // 4 - size // 2
-    scale = size ** (-0.5)
-    k, v = k_ref[...], v_ref[...]
+    v = v_ref[...]
     dk = jnp.zeros((keys, size), F32)
-    dv = jnp.zeros((keys, size), F32)
-    dgq = jnp.zeros((1, size), F32)
     for h in range(heads):
         cols = slice(h * size, (h + 1) * size)
+        dp = mm_nt(dao_ref[:, cols], v)
         p_w[h].wait()
         p = p_ref[h]
-        dao = dao_ref[:, cols]
-        dp = mm_nt(dao, v)
         ds = (p * (dp - jnp.sum(p * dp, axis=-1, keepdims=True))).astype(BF16)
-        dv = dv + mm_tn(p.astype(BF16), dao)
         if h == 0:
             wait(second)
-            g_q = gains[:, width : width + size]
-            cos_own, sin_own = cos_ref[keys - rows :, :], sin_ref[keys - rows :, :]
+            k = k_ref[...]
         dk = dk + mm_tn(ds, q_ref[:, cols])
-        dq = turn_bwd(mm(ds, k) * scale, cos_own, sin_own)
-        qraw = qraw_ref[:, cols]
-        inv = inverse_rms(qraw)
-        hat = qraw * inv
-        dgq = dgq + jnp.sum(dq * hat, axis=0, keepdims=True)
-        dqr[:, cols] = norm_back(hat, inv, g_q, dq).astype(BF16)
-    dkr[...] = turn_bwd(dk, cos_ref[...], sin_ref[...])
-    dv_out[...] = dv.astype(BF16)
-    dgq_out[...] = dgq
+        dq_out[:, cols] = mm(ds, k)
+    dk_out[...] = dk
+    done[...] = jnp.zeros_like(done)
     for source, target in zip(outs, outs_h):
         traffic.emit(source, target)
     traffic.finish()
 
 
 def back_kernel(reach, layout, *refs):
-    count = 12
+    count = 15
     ins_h, refs = refs[:count], refs[count:]
     _, wq_a, wk_a, wv_a, pack_h = refs[:5]
     outs_h, refs = refs[5:9], refs[9:]
     ins, refs = refs[:count], refs[count:]
-    toks, tok, gains, order, scale_order, dg_post, dgq, n1_ref, kraw_ref, dkr, dqr, dv_ref = ins
+    toks, tok, gains, order, scale_order, dg_post, cos_ref, sin_ref, *more = ins
+    n1_ref, dao_ref, p_ref, qraw_ref, kraw_ref, dq_ref, dk_ref = more
     halo = [toks.at[n] for n in range(reach)] + [tok]
     outs = keep, send, dn1_own, dn1_far = refs[:4]
-    wq, wk, wv, dkv_s, sems = refs[4:]
+    wq, wk, wv, dkv_s, dqr, sems = refs[4:]
     place, core = lax.axis_index("seq"), lax.axis_index("fsdp")
     traffic = Traffic(sems)
-    first = traffic.fetch([(ins_h[n], ins[n]) for n in (3, 7)])
-    second = traffic.fetch([(ins_h[n], ins[n]) for n in (8, 9, 10, 11, 2)])
-    copies = traffic.fetch([(ins_h[n], ins[n]) for n in (4, 5, 6, 0, 1)])
+    first = traffic.fetch([(ins_h[n], ins[n]) for n in (3, 8)])
+    second = traffic.fetch([(ins_h[n], ins[n]) for n in (9, 10)])
+    third = traffic.fetch([(ins_h[n], ins[n]) for n in (2, 6, 7, 11, 12, 13, 14)])
+    copies = traffic.fetch([(ins_h[n], ins[n]) for n in (4, 5, 0, 1)])
     for n, (mine, full) in enumerate(((wq_a, wq), (wk_a, wk), (wv_a, wv))):
         copies += traffic.halves(core, mine, pack_h, layout[n], full)
     rows = tok.shape[0] - SEG_ROWS
@@ -724,14 +712,30 @@
     perm = row_order(order, width, place, core)
     n1_t = mm_nt(perm, n1_ref[...]).astype(BF16)
     wait(second)
+    heads = p_ref.shape[0]
+    dv = jnp.zeros((n1_ref.shape[0], size), F32)
+    for h in range(heads):
+        dv = dv + mm_tn(p_ref[h].astype(BF16), dao_ref[:, h * size : (h + 1) * size])
+    dkv_s[:, size:] = dv.astype(BF16)
+    wait(third)
+    g_q = gains[:, width : width + size]
+    cos_own, sin_own = cos_ref[reach * rows :, :], sin_ref[reach * rows :, :]
+    dgq = jnp.zeros((1, size), F32)
+    for h in range(heads):
+        cols = slice(h * size, (h + 1) * size)
+        dq = turn_bwd(dq_ref[:, cols] * size ** (-0.5), cos_own, sin_own)
+        qraw = qraw_ref[:, cols]
+        inv = inverse_rms(qraw)
+        hat = qraw * inv
+        dgq = dgq + jnp.sum(dq * hat, axis=0, keepdims=True)
+        dqr[:, cols] = norm_back(hat, inv, g_q, dq).astype(BF16)
     g_k = gains[:, width + size : width + 2 * size]
     kraw = kraw_ref[...]
     inv = inverse_rms(kraw)
     hat = kraw * inv
-    dk = dkr[...]
+    dk = turn_bwd(dk_ref[...], cos_ref[...], sin_ref[...])
     dgk = jnp.sum(dk * hat, axis=0, keepdims=True)
     dkv_s[:, :size] = norm_back(hat, inv, g_k, dk).astype(BF16)
-    dkv_s[:, size:] = dv_ref[...]
     half = width // 2
     per = half // XY
     attn = dqr.shape[1]
@@ -751,7 +755,7 @@
             low = dn1.astype(BF16)
             for b in range(width // LANES):
                 dn1_far[bits, b * rows : (b + 1) * rows, :] = low[:, b * LANES : (b + 1) * LANES]
-    scales = owners_rows(jnp.concatenate([dgi, dgq[...], dgk, dg_post[...]], axis=1))
+    scales = owners_rows(jnp.concatenate([dgi, dgq, dgk, dg_post[...]], axis=1))
     owner = scale_order[:, :1] ^ (place * 2 + core)
     mine = scale_order[:, 1:2] * 1024 + (owner & 3) * 8 + (owner >> 2)
     columns = lax.broadcasted_iota(jnp.int32, (mine.shape[0], 2 * XY * LINE), 1)
@@ -1023,28 +1027,23 @@
     )
     mlp_recv = partner(mlp_send)
 
-    dqr, dkr, dv, dgq = call(
+    dq, dk, heads_done = call(
         heads_kernel,
-        (gains, cosine, sine, qraw, q, k, v, dao, p),
+        (q, k, v, dao, p),
         (),
-        [
-            shape((rows, attn), BF16),
-            shape((keys, size), F32),
-            shape((keys, size), BF16),
-            shape((1, size), F32),
-        ],
+        [shape((rows, attn), F32), shape((keys, size), F32), shape((8, LANES), F32)],
         [],
-        24,
+        16,
         63,
     )
 
     per_ff = width // 2 // XY * ff // LANES
     per_down = ff // 2 // XY * width // LANES
     per_out = attn // 2 // XY * width // LANES
-    gk, gs, uk, us, dk, ds = call(
+    gk, gs, uk, us, tk, ts = call(
         functools.partial(grads_kernel, width, ff, attn),
         (),
-        (mlp_keep, mlp_recv, dgq),
+        (mlp_keep, mlp_send, mlp_recv, heads_done),
         [shape((2, per_ff, LANES), BF16)] * 4
         + [shape((8, (per_down + per_out) // LINE, LANES), BF16)] * 2,
         [
@@ -1064,7 +1063,23 @@
     scale_order = jnp.asarray(np.stack([owner, line // LINE], axis=1).astype(np.int32))
     back_keep, back_send, dn1_own, dn1_far = call(
         functools.partial(back_kernel, reach, layout),
-        (toks, tok, gains, order, scale_order, dg_post, dgq, n1, kraw, dkr, dqr, dv),
+        (
+            toks,
+            tok,
+            gains,
+            order,
+            scale_order,
+            dg_post,
+            cosine,
+            sine,
+            n1,
+            dao,
+            p,
+            qraw,
+            kraw,
+            dq,
+            dk,
+        ),
         (gk, *weights[:3], pack_far),
         [
             shape((XY, per_back + 16, LANES), BF16),
@@ -1077,6 +1092,7 @@
             pltpu.VMEM((width, size), BF16),
             pltpu.VMEM((width, size), BF16),
             pltpu.VMEM((keys, 2 * size), BF16),
+            pltpu.VMEM((rows, attn), BF16),
         ],
         64,
     )
@@ -1147,7 +1163,7 @@
     (own_gate, own_up), mlp_done = join(
         (flat(mlp_0), flat(across(mlp_1, 2 * XY))), ((wide, unit), (wide, unit))
     )
-    down_0, down_1 = step(dk, ds, XY)
+    down_0, down_1 = step(tk, ts, XY)
     down_0, down_1 = step(down_0, down_1, 2)
     down_2, down_3 = step(down_0, down_1, 1)
     (own_down, own_out), down_done = join(

time: 128 us -> 126 us (0.984)
  no operation moved by 1% of the time
where the time goes in v5:
time: 126 us
  starting transfers between devices  45.3 us (36%)
  Pallas kernels  43 us (34%)
  waiting for transfers between devices  34.4 us (27%)
    pallas_call x4, Pallas kernels, call(): pl.pallas_call(kernel, out_shape=outs, in_specs=[hbm] * (len(fetched) + l...  31.9 us
    ppermute x16, waiting for transfers between devices, across(): return lax.ppermute(value, 'seq', [(i, i ^ bits) for i in range(XY * LINE)])  30.4 us
    ppermute x16, starting transfers between devices, across(): return lax.ppermute(value, 'seq', [(i, i ^ bits) for i in range(XY * LINE)])  27.7 us
    ppermute x5, starting transfers between devices, shifted(): return lax.ppermute(x, axis, pairs)  17 us
    pallas_call x1, Pallas kernels, fast(): pl.pallas_call(functools.partial(prepare_kernel, layout), out_shape=[shap...  5.72 us
    ppermute x5, waiting for transfers between devices, shifted(): return lax.ppermute(x, axis, pairs)  3.96 us
    pallas_call x3, Pallas kernels, join(): pl.pallas_call(functools.partial(join_kernel, len(parts), entries, int(ex...  2.9 us
  transfers between devices with their start and end apart: 24, of which 11 were waited for; matrix products, arithmetic and copies ran while one was open for 1% of the time, Pallas kernels for 13%

profile of v5, /device:TPU:0, one launch (start us, length us, event | category | flops | bytes accessed | tf_op | source)
XLA Modules:
  0.0 125.9 jit_solution(7849331883581651264)
XLA Ops:
  0.6 5.7 %shard_map.231 = (bf16[144,640]{1,0:T(8,128)(2,1)}, bf16[320,8832]{1,0:T(8,128)(2,1)}) custom-call(bf16[128,640]{1,0:T(8,128)(2,1)} %bitcast.52, s32[1,128]{1,0:T(1,128)} %refs_1_.1, bf16[320,1024]{1,0:T(8,128)(2,1)} %refs_16_.3, bf16[320,256]{1,0:T(8,128)(2,1)} %refs_17_.1, bf16[320,256]{1,0:T(8,128)(2,1)} %refs_18_.1, bf16[320,2048]{1,0:T(8,128)(2,1)} %refs_13_.1, ...), custom_call_target="tpu_custom_call" | custom-call | tf_op jit(solution)/shard_map/pallas_call | solution.py:957
  6.9 4.4 %collective-permute-start.3 = (bf16[144,640]{1,0:T(8,128)(2,1)}, bf16[144,640]{1,0:T(8,128)(2,1)S(1)}, u32[]{:S(2)}, u32[]{:S(2)}) collective-permute-start(bf16[144,640]{1,0:T(8,128)(2,1)} %get-tuple-element.56.refs_4_.refs_1_.refs_0_), channel_id=1, source_target_pairs={{0,2},{2,4},{4,6},{6,8},{8,10},{10,12},{12,14},{14,16},{16,18},{18... | collective-permute-start | bytes 552968 | tf_op jit(solution)/shard_map/ppermute | solution.py:24
  11.3 3.4 %collective-permute-start.2 = (bf16[144,640]{1,0:T(8,128)(2,1)}, bf16[144,640]{1,0:T(8,128)(2,1)S(1)}, u32[]{:S(2)}, u32[]{:S(2)}) collective-permute-start(bf16[144,640]{1,0:T(8,128)(2,1)} %get-tuple-element.56.refs_4_.refs_1_.refs_0_), channel_id=1, source_target_pairs={{0,4},{2,6},{4,8},{6,10},{8,12},{10,14},{12,16},{14,18},{16,20},{1... | collective-permute-start | bytes 552968 | tf_op jit(solution)/shard_map/ppermute | solution.py:24
  14.7 4.4 %collective-permute-start.1 = (bf16[144,640]{1,0:T(8,128)(2,1)}, bf16[144,640]{1,0:T(8,128)(2,1)S(1)}, u32[]{:S(2)}, u32[]{:S(2)}) collective-permute-start(bf16[144,640]{1,0:T(8,128)(2,1)} %get-tuple-element.56.refs_4_.refs_1_.refs_0_), channel_id=1, source_target_pairs={{0,6},{2,8},{4,10},{6,12},{8,14},{10,16},{12,18},{14,20},{16,22},{... | collective-permute-start | bytes 552968 | tf_op jit(solution)/shard_map/ppermute | solution.py:24
  19.1 3.5 %collective-permute-start = (bf16[144,640]{1,0:T(8,128)(2,1)}, bf16[144,640]{1,0:T(8,128)(2,1)S(1)}, u32[]{:S(2)}, u32[]{:S(2)}) collective-permute-start(bf16[144,640]{1,0:T(8,128)(2,1)} %get-tuple-element.56.refs_4_.refs_1_.refs_0_), channel_id=1, source_target_pairs={{0,8},{2,10},{4,12},{6,14},{8,16},{10,18},{12,20},{14,22},{16,24},... | collective-permute-start | bytes 552968 | tf_op jit(solution)/shard_map/ppermute | solution.py:24
  23.4 3.2 %collective-permute-done.refs_0_ = bf16[144,640]{1,0:T(8,128)(2,1)S(1)} collective-permute-done((bf16[144,640]{1,0:T(8,128)(2,1)}, bf16[144,640]{1,0:T(8,128)(2,1)S(1)}, u32[]{:S(2)}, u32[]{:S(2)}) %collective-permute-start) | collective-permute-done | bytes 184352 | tf_op jit(solution)/shard_map/ppermute | solution.py:24
  27.3 13.7 %shard_map.232 = (bf16[640,640]{1,0:T(8,128)(2,1)}, f32[128,1024]{1,0:T(8,128)}, bf16[128,1024]{1,0:T(8,128)(2,1)}, f32[640,256]{1,0:T(8,128)}, bf16[640,256]{1,...) custom-call(bf16[144,640]{1,0:T(8,128)(2,1)} %copy-done.12, ...), custom_call_target="tpu_custom_call" | custom-call | tf_op jit(solution)/shard_map/pallas_call | solution.py:898
  41.0 4.2 %shard_map.233 = (f32[128,1024]{1,0:T(8,128)}, f32[640,256]{1,0:T(8,128)}, f32[8,128]{1,0:T(8,128)}) custom-call(bf16[128,1024]{1,0:T(8,128)(2,1)} %get-tuple-element.68.refs_0_, bf16[640,256]{1,0:T(8,128)(2,1)} %get-tuple-element.69.refs_1_, bf16[640,256]{1,0:T(8,128)(2,1)} %get-tuple-element.70.refs_2_, ...), custom_call_target="tpu_custom_call" | custom-call | tf_op jit(solution)/shard_map/pallas_call | solution.py:898
  45.3 5.0 %shard_map.234 = (bf16[2,1280,128]{2,1,0:T(8,128)(2,1)}, bf16[2,1280,128]{2,1,0:T(8,128)(2,1)}, bf16[2,1280,128]{2,1,0:T(8,128)(2,1)}, bf16[2,1280,128]{2,1,0:T(...) custom-call(bf16[128,7296]{1,0:T(8,128)(2,1)} %get-tuple-element.73.refs_0_, ...), custom_call_target="tpu_custom_call" | custom-call | tf_op jit(solution)/shard_map/pallas_call | solution.py:898
  50.3 1.4 %collective-permute-start.10 = (bf16[2,1280,128]{2,1,0:T(8,128)(2,1)}, bf16[2,1280,128]{2,1,0:T(8,128)(2,1)S(1)}, u32[]{:S(2)}, u32[]{:S(2)}) collective-permute-start(bf16[2,1280,128]{2,1,0:T(8,128)(2,1)} %get-tuple-element.81), channel_id=1, source_target_pairs={{0,2},{2,0},{4,6},{6,4},{8,10},{10,8},{12,14},{14,12},{16,18},{18,... | collective-permute-start | bytes 1966088 | tf_op jit(solution)/shard_map/ppermute | solution.py:948
  51.6 3.1 %collective-permute-start.12 = (bf16[2,1280,128]{2,1,0:T(8,128)(2,1)}, bf16[2,1280,128]{2,1,0:T(8,128)(2,1)S(1)}, u32[]{:S(2)}, u32[]{:S(2)}) collective-permute-start(bf16[2,1280,128]{2,1,0:T(8,128)(2,1)} %get-tuple-element.83), channel_id=1, source_target_pairs={{0,4},{2,6},{4,0},{6,2},{8,12},{10,14},{12,8},{14,10},{16,20},{18,... | collective-permute-start | bytes 1966088 | tf_op jit(solution)/shard_map/ppermute | solution.py:948
  54.7 2.4 %collective-permute-start.16 = (bf16[8,480,128]{2,1,0:T(8,128)(2,1)}, bf16[8,480,128]{2,1,0:T(8,128)(2,1)S(1)}, u32[]{:S(2)}, u32[]{:S(2)}) collective-permute-start(bf16[8,480,128]{2,1,0:T(8,128)(2,1)} %get-tuple-element.88), channel_id=1, source_target_pairs={{0,8},{2,10},{4,12},{6,14},{8,0},{10,2},{12,4},{14,6},{16,24},{18,... | collective-permute-start | bytes 2949128 | tf_op jit(solution)/shard_map/ppermute | solution.py:948
  57.1 9.0 %shard_map.235 = (bf16[4,976,128]{2,1,0:T(8,128)(2,1)}, bf16[4,976,128]{2,1,0:T(8,128)(2,1)}, f32[128,640]{1,0:T(8,128)}, bf16[4,640,128]{2,1,0:T(8,128)(2,1)}) custom-call(bf16[4,144,640]{2,1,0:T(8,128)(2,1)} %get-tuple-element.61.refs_0_, bf16[144,640]{1,0:T(8,128)(2,1)} %get-tuple-element.56.refs_4_.refs_1_.refs_0_, ...), custom_call_target="tpu_custom_call" | custom-call | tf_op jit(solution)/shard_map/pallas_call | solution.py:898
  66.2 1.5 %collective-permute-done.10 = bf16[2,1280,128]{2,1,0:T(8,128)(2,1)S(1)} collective-permute-done((bf16[2,1280,128]{2,1,0:T(8,128)(2,1)}, bf16[2,1280,128]{2,1,0:T(8,128)(2,1)S(1)}, u32[]{:S(2)}, u32[]{:S(2)}) %collective-permute-start.10) | collective-permute-done | bytes 655392 | tf_op jit(solution)/shard_map/ppermute | solution.py:948
  67.8 3.9 %collective-permute-start.11 = (bf16[1,1280,128]{2,1,0:T(8,128)(2,1)S(1)}, bf16[1,1280,128]{2,1,0:T(8,128)(2,1)S(1)}, u32[]{:S(2)}, u32[]{:S(2)}) collective-permute-start(bf16[1,1280,128]{2,1,0:T(8,128)(2,1)S(1)} %get-tuple-element.110), channel_id=1, source_target_pairs={{0,4},{2,6},{4,0},{6,2},{8,12},{10,14},{12,8},{14,10},{16,20},{18,... | collective-permute-start | bytes 983048 | tf_op jit(solution)/shard_map/ppermute | solution.py:948
  72.6 6.6 %collective-permute-done.16 = bf16[8,480,128]{2,1,0:T(8,128)(2,1)S(1)} collective-permute-done((bf16[8,480,128]{2,1,0:T(8,128)(2,1)}, bf16[8,480,128]{2,1,0:T(8,128)(2,1)S(1)}, u32[]{:S(2)}, u32[]{:S(2)}) %collective-permute-start.16) | collective-permute-done | bytes 983072 | tf_op jit(solution)/shard_map/ppermute | solution.py:948
  79.8 1.2 collective-permute-done.13
  81.4 2.4 %collective-permute-start.14 = (bf16[2,640,128]{2,1,0:T(8,128)(2,1)S(1)}, bf16[2,640,128]{2,1,0:T(8,128)(2,1)S(1)}, u32[]{:S(2)}, u32[]{:S(2)}) collective-permute-start(bf16[2,640,128]{2,1,0:T(8,128)(2,1)S(1)} %get-tuple-element.85), channel_id=1, source_target_pairs={{0,8},{2,10},{4,12},{6,14},{8,0},{10,2},{12,4},{14,6},{16,24},{18,... | collective-permute-start | bytes 983048 | tf_op jit(solution)/shard_map/ppermute | solution.py:948
  84.8 0.9 collective-permute-start.8
  85.7 7.9 %collective-permute-done.17 = bf16[4,480,128]{2,1,0:T(8,128)(2,1)S(1)} collective-permute-done((bf16[4,480,128]{2,1,0:T(8,128)(2,1)S(1)}, bf16[4,480,128]{2,1,0:T(8,128)(2,1)S(1)}, u32[]{:S(2)}, u32[]{:S(2)}) %collective-permute-start.17) | collective-permute-done | bytes 491552 | tf_op jit(solution)/shard_map/ppermute | solution.py:948
  93.8 1.5 %collective-permute-start.18 = (bf16[2,480,128]{2,1,0:T(8,128)(2,1)S(1)}, bf16[2,480,128]{2,1,0:T(8,128)(2,1)S(1)}, u32[]{:S(2)}, u32[]{:S(2)}) collective-permute-start(bf16[2,480,128]{2,1,0:T(8,128)(2,1)S(1)} %get-tuple-element.113), channel_id=1, source_target_pairs={{0,2},{2,0},{4,6},{6,4},{8,10},{10,8},{12,14},{14,12},{16,18},{18,... | collective-permute-start | bytes 737288 | tf_op jit(solution)/shard_map/ppermute | solution.py:948
  95.8 2.9 %collective-permute-start.15 = (bf16[1,640,128]{2,1,0:T(8,128)(2,1)S(1)}, bf16[1,640,128]{2,1,0:T(8,128)(2,1)S(1)}, u32[]{:S(2)}, u32[]{:S(2)}) collective-permute-start(bf16[1,640,128]{2,1,0:T(8,128)(2,1)S(1)} %get-tuple-element.114), channel_id=1, source_target_pairs={{0,16},{2,18},{4,20},{6,22},{8,24},{10,26},{12,28},{14,30},{16,0},... | collective-permute-start | bytes 491528 | tf_op jit(solution)/shard_map/ppermute | solution.py:948
  98.6 4.2 %collective-permute-done.18 = bf16[2,480,128]{2,1,0:T(8,128)(2,1)S(1)} collective-permute-done((bf16[2,480,128]{2,1,0:T(8,128)(2,1)S(1)}, bf16[2,480,128]{2,1,0:T(8,128)(2,1)S(1)}, u32[]{:S(2)}, u32[]{:S(2)}) %collective-permute-start.18) | collective-permute-done | bytes 245792 | tf_op jit(solution)/shard_map/ppermute | solution.py:948
  102.9 2.8 %collective-permute-start.19 = (bf16[1,480,128]{2,1,0:T(8,128)(2,1)S(1)}, bf16[1,480,128]{2,1,0:T(8,128)(2,1)S(1)}, u32[]{:S(2)}, u32[]{:S(2)}) collective-permute-start(bf16[1,480,128]{2,1,0:T(8,128)(2,1)S(1)} %get-tuple-element.119), channel_id=1, source_target_pairs={{0,16},{2,18},{4,20},{6,22},{8,24},{10,26},{12,28},{14,30},{16,0},... | collective-permute-start | bytes 368648 | tf_op jit(solution)/shard_map/ppermute | solution.py:948
  106.4 0.9 shard_map.237
  107.2 2.8 %collective-permute-done.19 = bf16[1,480,128]{2,1,0:T(8,128)(2,1)S(1)} collective-permute-done((bf16[1,480,128]{2,1,0:T(8,128)(2,1)S(1)}, bf16[1,480,128]{2,1,0:T(8,128)(2,1)S(1)}, u32[]{:S(2)}, u32[]{:S(2)}) %collective-permute-start.19) | collective-permute-done | bytes 122912 | tf_op jit(solution)/shard_map/ppermute | solution.py:948
  111.4 1.3 %collective-permute-start.20 = (bf16[640,128]{1,0:T(8,128)(2,1)S(1)}, bf16[640,128]{1,0:T(8,128)(2,1)S(1)}, u32[]{:S(2)}, u32[]{:S(2)}) collective-permute-start(bf16[640,128]{1,0:T(8,128)(2,1)S(1)} %get-tuple-element.91.refs_4_), channel_id=1, source_target_pairs={{8,0},{10,2},{12,4},{14,6},{16,8},{18,10},{20,12},{22,14},{24,16},... | collective-permute-start | bytes 491528 | tf_op jit(solution)/shard_map/ppermute | solution.py:24
  113.0 3.6 %collective-permute-start.23 = (bf16[256,128]{1,0:T(8,128)(2,1)S(1)}, bf16[256,128]{1,0:T(8,128)(2,1)S(1)}, u32[]{:S(2)}, u32[]{:S(2)}) collective-permute-start(bf16[256,128]{1,0:T(8,128)(2,1)S(1)} %get-tuple-element.121), channel_id=1, source_target_pairs={{0,24},{2,26},{4,28},{6,30},{8,16},{10,18},{12,20},{14,22},{16,8},... | collective-permute-start | bytes 196616 | tf_op jit(solution)/shard_map/ppermute | solution.py:948
  117.4 3.7 %collective-permute-done.23.refs_3_ = bf16[256,128]{1,0:T(8,128)(2,1)S(1)} collective-permute-done((bf16[256,128]{1,0:T(8,128)(2,1)S(1)}, bf16[256,128]{1,0:T(8,128)(2,1)S(1)}, u32[]{:S(2)}, u32[]{:S(2)}) %collective-permute-start.23) | collective-permute-done | bytes 65568 | tf_op jit(solution)/shard_map/ppermute | solution.py:948
  121.1 1.9 %collective-permute-done.22.refs_2_ = bf16[256,128]{1,0:T(8,128)(2,1)S(1)} collective-permute-done((bf16[256,128]{1,0:T(8,128)(2,1)S(1)}, bf16[256,128]{1,0:T(8,128)(2,1)S(1)}, u32[]{:S(2)}, u32[]{:S(2)}) %collective-permute-start.22) | collective-permute-done | bytes 65568 | tf_op jit(solution)/shard_map/ppermute | solution.py:948
  123.0 1.3 %shard_map.242 = (f32[160,128]{1,0:T(8,128)}, f32[40,128]{1,0:T(8,128)}, f32[40,128]{1,0:T(8,128)}, f32[1,96]{1,0:T(1,128)}, f32[8,128]{1,0:T(8,128)}) custom-call(bf16[256,128]{1,0:T(8,128)(2,1)S(1)} %bitcast.50, bf16[256,128]{1,0:T(8,128)(2,1)S(1)} %collective-permute-done.21.refs_1_, bf16[256,128]{1,0:T(8,128)(2,1)S(1)} %collective-permute-done.22.refs_2_, ...), custom_call_target="tpu_custom_call" | custom-call | tf_op jit(solution)/shard_map/pallas_call | solution.py:1132
  124.4 1.3 %shard_map.240 = f32[128,640]{1,0:T(8,128)} custom-call(bf16[144,640]{1,0:T(8,128)(2,1)S(1)} %copy-done.1, f32[1,3072]{1,0:T(1,128)S(1)} %copy-done.4, f32[128,640]{1,0:T(8,128)S(1)} %copy-done.3, f32[128,640]{1,0:T(8,128)S(1)} %get-tuple-element.90.refs_3_, bf16[640,128]{1,0:T(8,128)(2,1)S(1)} %collective-permute-done.20.refs_4_), custom_call_target="tpu_custom_call" | custom-call | tf_op jit(solution)/shard_map/pallas_call | solution.py:1204
  (66 shorter events, 8.9 us)
Async XLA Ops:
  6.4 20.2 %collective-permute-start.4 = (bf16[320,8832]{1,0:T(8,128)(2,1)}, bf16[320,8832]{1,0:T(8,128)(2,1)}, u32[]{:S(2)}, u32[]{:S(2)}) collective-permute-start(bf16[320,8832]{1,0:T(8,128)(2,1)} %get-tuple-element.57), channel_id=1, source_target_pairs={{0,1},{1,0},{2,3},{3,2},{4,5},{5,4},{6,7},{7,6},{8,9},{9,8},{10,11... | collective-permute-start | bytes 16957448 | tf_op jit(solution)/shard_map/ppermute | solution.py:945
  6.9 15.7 %collective-permute-start.3 = (bf16[144,640]{1,0:T(8,128)(2,1)}, bf16[144,640]{1,0:T(8,128)(2,1)S(1)}, u32[]{:S(2)}, u32[]{:S(2)}) collective-permute-start(bf16[144,640]{1,0:T(8,128)(2,1)} %get-tuple-element.56.refs_4_.refs_1_.refs_0_), channel_id=1, source_target_pairs={{0,2},{2,4},{4,6},{6,8},{8,10},{10,12},{12,14},{14,16},{16,18},{18... | collective-permute-start | bytes 552968 | tf_op jit(solution)/shard_map/ppermute | solution.py:24
  11.3 11.3 %collective-permute-start.2 = (bf16[144,640]{1,0:T(8,128)(2,1)}, bf16[144,640]{1,0:T(8,128)(2,1)S(1)}, u32[]{:S(2)}, u32[]{:S(2)}) collective-permute-start(bf16[144,640]{1,0:T(8,128)(2,1)} %get-tuple-element.56.refs_4_.refs_1_.refs_0_), channel_id=1, source_target_pairs={{0,4},{2,6},{4,8},{6,10},{8,12},{10,14},{12,16},{14,18},{16,20},{1... | collective-permute-start | bytes 552968 | tf_op jit(solution)/shard_map/ppermute | solution.py:24
  14.7 8.6 %collective-permute-start.1 = (bf16[144,640]{1,0:T(8,128)(2,1)}, bf16[144,640]{1,0:T(8,128)(2,1)S(1)}, u32[]{:S(2)}, u32[]{:S(2)}) collective-permute-start(bf16[144,640]{1,0:T(8,128)(2,1)} %get-tuple-element.56.refs_4_.refs_1_.refs_0_), channel_id=1, source_target_pairs={{0,6},{2,8},{4,10},{6,12},{8,14},{10,16},{12,18},{14,20},{16,22},{... | collective-permute-start | bytes 552968 | tf_op jit(solution)/shard_map/ppermute | solution.py:24
  19.1 7.5 %collective-permute-start = (bf16[144,640]{1,0:T(8,128)(2,1)}, bf16[144,640]{1,0:T(8,128)(2,1)S(1)}, u32[]{:S(2)}, u32[]{:S(2)}) collective-permute-start(bf16[144,640]{1,0:T(8,128)(2,1)} %get-tuple-element.56.refs_4_.refs_1_.refs_0_), channel_id=1, source_target_pairs={{0,8},{2,10},{4,12},{6,14},{8,16},{10,18},{12,20},{14,22},{16,24},... | collective-permute-start | bytes 552968 | tf_op jit(solution)/shard_map/ppermute | solution.py:24
  40.9 4.3 %collective-permute-start.5 = (bf16[128,7296]{1,0:T(8,128)(2,1)}, bf16[128,7296]{1,0:T(8,128)(2,1)}, u32[]{:S(2)}, u32[]{:S(2)}) collective-permute-start(bf16[128,7296]{1,0:T(8,128)(2,1)} %get-tuple-element.74.refs_1_), channel_id=1, source_target_pairs={{0,1},{1,0},{2,3},{3,2},{4,5},{5,4},{6,7},{7,6},{8,9},{9,8},{10,11... | collective-permute-start | bytes 5603336 | tf_op jit(solution)/shard_map/ppermute | solution.py:945
  50.3 17.4 %collective-permute-start.10 = (bf16[2,1280,128]{2,1,0:T(8,128)(2,1)}, bf16[2,1280,128]{2,1,0:T(8,128)(2,1)S(1)}, u32[]{:S(2)}, u32[]{:S(2)}) collective-permute-start(bf16[2,1280,128]{2,1,0:T(8,128)(2,1)} %get-tuple-element.81), channel_id=1, source_target_pairs={{0,2},{2,0},{4,6},{6,4},{8,10},{10,8},{12,14},{14,12},{16,18},{18,... | collective-permute-start | bytes 1966088 | tf_op jit(solution)/shard_map/ppermute | solution.py:948
  51.6 20.1 %collective-permute-start.12 = (bf16[2,1280,128]{2,1,0:T(8,128)(2,1)}, bf16[2,1280,128]{2,1,0:T(8,128)(2,1)S(1)}, u32[]{:S(2)}, u32[]{:S(2)}) collective-permute-start(bf16[2,1280,128]{2,1,0:T(8,128)(2,1)} %get-tuple-element.83), channel_id=1, source_target_pairs={{0,4},{2,6},{4,0},{6,2},{8,12},{10,14},{12,8},{14,10},{16,20},{18,... | collective-permute-start | bytes 1966088 | tf_op jit(solution)/shard_map/ppermute | solution.py:948
  54.7 24.4 %collective-permute-start.16 = (bf16[8,480,128]{2,1,0:T(8,128)(2,1)}, bf16[8,480,128]{2,1,0:T(8,128)(2,1)S(1)}, u32[]{:S(2)}, u32[]{:S(2)}) collective-permute-start(bf16[8,480,128]{2,1,0:T(8,128)(2,1)} %get-tuple-element.88), channel_id=1, source_target_pairs={{0,8},{2,10},{4,12},{6,14},{8,0},{10,2},{12,4},{14,6},{16,24},{18,... | collective-permute-start | bytes 2949128 | tf_op jit(solution)/shard_map/ppermute | solution.py:948
  57.1 10.6 %copy-start.5 = (bf16[2,1280,128]{2,1,0:T(8,128)(2,1)S(1)}, bf16[2,1280,128]{2,1,0:T(8,128)(2,1)}, u32[]{:S(2)}) copy-start(bf16[2,1280,128]{2,1,0:T(8,128)(2,1)} %get-tuple-element.76.refs_15_) | copy-start | bytes 1966084
  66.1 5.6 %copy-start.8 = (bf16[2,1280,128]{2,1,0:T(8,128)(2,1)S(1)}, bf16[2,1280,128]{2,1,0:T(8,128)(2,1)}, u32[]{:S(2)}) copy-start(bf16[2,1280,128]{2,1,0:T(8,128)(2,1)} %get-tuple-element.82) | copy-start | bytes 1966084
  66.1 6.5 %copy-start = (bf16[4,640,128]{2,1,0:T(8,128)(2,1)S(1)}, bf16[4,640,128]{2,1,0:T(8,128)(2,1)}, u32[]{:S(2)}) copy-start(bf16[4,640,128]{2,1,0:T(8,128)(2,1)} %get-tuple-element.78.refs_1_) | copy-start | bytes 1966084
  66.1 17.7 %collective-permute-start.6 = (bf16[4,976,128]{2,1,0:T(8,128)(2,1)}, bf16[4,976,128]{2,1,0:T(8,128)(2,1)S(1)}, u32[]{:S(2)}, u32[]{:S(2)}) collective-permute-start(bf16[4,976,128]{2,1,0:T(8,128)(2,1)} %get-tuple-element.80), channel_id=1, source_target_pairs={{0,1},{1,0},{2,3},{3,2},{4,5},{5,4},{6,7},{7,6},{8,9},{9,8},{10,11... | collective-permute-start | bytes 2998280 | tf_op jit(solution)/shard_map/ppermute | solution.py:945
  67.8 11.3 %copy-start.7 = (bf16[8,480,128]{2,1,0:T(8,128)(2,1)S(1)}, bf16[8,480,128]{2,1,0:T(8,128)(2,1)}, u32[]{:S(2)}) copy-start(bf16[8,480,128]{2,1,0:T(8,128)(2,1)} %get-tuple-element.87) | copy-start | bytes 2949124
  67.8 11.9 %collective-permute-start.11 = (bf16[1,1280,128]{2,1,0:T(8,128)(2,1)S(1)}, bf16[1,1280,128]{2,1,0:T(8,128)(2,1)S(1)}, u32[]{:S(2)}, u32[]{:S(2)}) collective-permute-start(bf16[1,1280,128]{2,1,0:T(8,128)(2,1)S(1)} %get-tuple-element.110), channel_id=1, source_target_pairs={{0,4},{2,6},{4,0},{6,2},{8,12},{10,14},{12,8},{14,10},{16,20},{18,... | collective-permute-start | bytes 983048 | tf_op jit(solution)/shard_map/ppermute | solution.py:948
  71.9 9.1 %collective-permute-start.13 = (bf16[1,1280,128]{2,1,0:T(8,128)(2,1)S(1)}, bf16[1,1280,128]{2,1,0:T(8,128)(2,1)S(1)}, u32[]{:S(2)}, u32[]{:S(2)}) collective-permute-start(bf16[1,1280,128]{2,1,0:T(8,128)(2,1)S(1)} %get-tuple-element.108), channel_id=1, source_target_pairs={{0,2},{2,0},{4,6},{6,4},{8,10},{10,8},{12,14},{14,12},{16,18},{18,... | collective-permute-start | bytes 983048 | tf_op jit(solution)/shard_map/ppermute | solution.py:948
  79.4 14.2 %collective-permute-start.17 = (bf16[4,480,128]{2,1,0:T(8,128)(2,1)S(1)}, bf16[4,480,128]{2,1,0:T(8,128)(2,1)S(1)}, u32[]{:S(2)}, u32[]{:S(2)}) collective-permute-start(bf16[4,480,128]{2,1,0:T(8,128)(2,1)S(1)} %get-tuple-element.107), channel_id=1, source_target_pairs={{0,4},{2,6},{4,0},{6,2},{8,12},{10,14},{12,8},{14,10},{16,20},{18,... | collective-permute-start | bytes 1474568 | tf_op jit(solution)/shard_map/ppermute | solution.py:948
  81.4 14.3 %collective-permute-start.14 = (bf16[2,640,128]{2,1,0:T(8,128)(2,1)S(1)}, bf16[2,640,128]{2,1,0:T(8,128)(2,1)S(1)}, u32[]{:S(2)}, u32[]{:S(2)}) collective-permute-start(bf16[2,640,128]{2,1,0:T(8,128)(2,1)S(1)} %get-tuple-element.85), channel_id=1, source_target_pairs={{0,8},{2,10},{4,12},{6,14},{8,0},{10,2},{12,4},{14,6},{16,24},{18,... | collective-permute-start | bytes 983048 | tf_op jit(solution)/shard_map/ppermute | solution.py:948
  84.1 26.7 %collective-permute-start.7 = (bf16[1616,128]{1,0:T(8,128)(2,1)S(1)}, bf16[1616,128]{1,0:T(8,128)(2,1)S(1)}, u32[]{:S(2)}, u32[]{:S(2)}) collective-permute-start(bf16[1616,128]{1,0:T(8,128)(2,1)S(1)} %pad_maximum_fusion), channel_id=1, source_target_pairs={{0,2},{2,0},{4,6},{6,4},{8,10},{10,8},{12,14},{14,12},{16,18},{18,... | collective-permute-start | bytes 1241096 | tf_op jit(solution)/shard_map/ppermute | solution.py:948
  84.8 26.0 %collective-permute-start.8 = (bf16[1616,128]{1,0:T(8,128)(2,1)S(1)}, bf16[1616,128]{1,0:T(8,128)(2,1)S(1)}, u32[]{:S(2)}, u32[]{:S(2)}) collective-permute-start(bf16[1616,128]{1,0:T(8,128)(2,1)S(1)} %pad_maximum_fusion.1), channel_id=1, source_target_pairs={{0,4},{2,6},{4,0},{6,2},{8,12},{10,14},{12,8},{14,10},{16,20},{18,... | collective-permute-start | bytes 1241096 | tf_op jit(solution)/shard_map/ppermute | solution.py:948
  93.8 17.0 %copy-start.2 = (f32[128,640]{1,0:T(8,128)S(1)}, f32[128,640]{1,0:T(8,128)}, u32[]{:S(2)}) copy-start(f32[128,640]{1,0:T(8,128)} %get-tuple-element.77.refs_0_) | copy-start | bytes 983044
  93.8 9.0 %collective-permute-start.18 = (bf16[2,480,128]{2,1,0:T(8,128)(2,1)S(1)}, bf16[2,480,128]{2,1,0:T(8,128)(2,1)S(1)}, u32[]{:S(2)}, u32[]{:S(2)}) collective-permute-start(bf16[2,480,128]{2,1,0:T(8,128)(2,1)S(1)} %get-tuple-element.113), channel_id=1, source_target_pairs={{0,2},{2,0},{4,6},{6,4},{8,10},{10,8},{12,14},{14,12},{16,18},{18,... | collective-permute-start | bytes 737288 | tf_op jit(solution)/shard_map/ppermute | solution.py:948
  95.3 15.5 %collective-permute-start.9 = (bf16[1616,128]{1,0:T(8,128)(2,1)S(1)}, bf16[1616,128]{1,0:T(8,128)(2,1)S(1)}, u32[]{:S(2)}, u32[]{:S(2)}) collective-permute-start(bf16[1616,128]{1,0:T(8,128)(2,1)S(1)} %pad_maximum_fusion.2), channel_id=1, source_target_pairs={{0,6},{2,4},{4,2},{6,0},{8,14},{10,12},{12,10},{14,8},{16,22},{18,... | collective-permute-start | bytes 1241096 | tf_op jit(solution)/shard_map/ppermute | solution.py:948
  95.8 10.6 %collective-permute-start.15 = (bf16[1,640,128]{2,1,0:T(8,128)(2,1)S(1)}, bf16[1,640,128]{2,1,0:T(8,128)(2,1)S(1)}, u32[]{:S(2)}, u32[]{:S(2)}) collective-permute-start(bf16[1,640,128]{2,1,0:T(8,128)(2,1)S(1)} %get-tuple-element.114), channel_id=1, source_target_pairs={{0,16},{2,18},{4,20},{6,22},{8,24},{10,26},{12,28},{14,30},{16,0},... | collective-permute-start | bytes 491528 | tf_op jit(solution)/shard_map/ppermute | solution.py:948
  102.9 7.2 %collective-permute-start.19 = (bf16[1,480,128]{2,1,0:T(8,128)(2,1)S(1)}, bf16[1,480,128]{2,1,0:T(8,128)(2,1)S(1)}, u32[]{:S(2)}, u32[]{:S(2)}) collective-permute-start(bf16[1,480,128]{2,1,0:T(8,128)(2,1)S(1)} %get-tuple-element.119), channel_id=1, source_target_pairs={{0,16},{2,18},{4,20},{6,22},{8,24},{10,26},{12,28},{14,30},{16,0},... | collective-permute-start | bytes 368648 | tf_op jit(solution)/shard_map/ppermute | solution.py:948
  110.8 13.5 %copy-start.1 = (bf16[144,640]{1,0:T(8,128)(2,1)S(1)}, bf16[144,640]{1,0:T(8,128)(2,1)}, u32[]{:S(2)}) copy-start(bf16[144,640]{1,0:T(8,128)(2,1)} %get-tuple-element.56.refs_4_.refs_1_.refs_0_) | copy-start | bytes 552964
  110.8 13.5 %copy-start.3 = (f32[128,640]{1,0:T(8,128)S(1)}, f32[128,640]{1,0:T(8,128)}, u32[]{:S(2)}) copy-start(f32[128,640]{1,0:T(8,128)} %get-tuple-element.60.refs_2_) | copy-start | bytes 983044
  110.8 13.5 %copy-start.4 = (f32[1,3072]{1,0:T(1,128)S(1)}, f32[1,3072]{1,0:T(1,128)}, u32[]{:S(2)}) copy-start(f32[1,3072]{1,0:T(1,128)} %get-tuple-element.59.refs_2_.refs_1_) | copy-start | bytes 36868
  111.4 12.9 %collective-permute-start.20 = (bf16[640,128]{1,0:T(8,128)(2,1)S(1)}, bf16[640,128]{1,0:T(8,128)(2,1)S(1)}, u32[]{:S(2)}, u32[]{:S(2)}) collective-permute-start(bf16[640,128]{1,0:T(8,128)(2,1)S(1)} %get-tuple-element.91.refs_4_), channel_id=1, source_target_pairs={{8,0},{10,2},{12,4},{14,6},{16,8},{18,10},{20,12},{22,14},{24,16},... | collective-permute-start | bytes 491528 | tf_op jit(solution)/shard_map/ppermute | solution.py:24
  113.0 8.1 %collective-permute-start.23 = (bf16[256,128]{1,0:T(8,128)(2,1)S(1)}, bf16[256,128]{1,0:T(8,128)(2,1)S(1)}, u32[]{:S(2)}, u32[]{:S(2)}) collective-permute-start(bf16[256,128]{1,0:T(8,128)(2,1)S(1)} %get-tuple-element.121), channel_id=1, source_target_pairs={{0,24},{2,26},{4,28},{6,30},{8,16},{10,18},{12,20},{14,22},{16,8},... | collective-permute-start | bytes 196616 | tf_op jit(solution)/shard_map/ppermute | solution.py:948
  116.6 6.4 %collective-permute-start.22 = (bf16[256,128]{1,0:T(8,128)(2,1)S(1)}, bf16[256,128]{1,0:T(8,128)(2,1)S(1)}, u32[]{:S(2)}, u32[]{:S(2)}) collective-permute-start(bf16[256,128]{1,0:T(8,128)(2,1)S(1)} %get-tuple-element.122), channel_id=1, source_target_pairs={{0,16},{2,18},{4,20},{6,22},{8,24},{10,26},{12,28},{14,30},{16,0},... | collective-permute-start | bytes 196616 | tf_op jit(solution)/shard_map/ppermute | solution.py:948
  117.1 5.8 %collective-permute-start.21 = (bf16[256,128]{1,0:T(8,128)(2,1)S(1)}, bf16[256,128]{1,0:T(8,128)(2,1)S(1)}, u32[]{:S(2)}, u32[]{:S(2)}) collective-permute-start(bf16[256,128]{1,0:T(8,128)(2,1)S(1)} %get-tuple-element.123), channel_id=1, source_target_pairs={{0,8},{2,10},{4,12},{6,14},{8,0},{10,2},{12,4},{14,6},{16,24},{18,... | collective-permute-start | bytes 196616 | tf_op jit(solution)/shard_map/ppermute | solution.py:948
  (5 other events, 16.5 us)

commit v6 on v5

--- a/solution.py
+++ b/solution.py
@@ -511,7 +511,7 @@
     ready("down")
     ready("rest")
     c = ct[...].astype(F32)
-    part = 512
+    part = 1024
     (at_gate, at_up, at_df, at_dya, at_hid, at_ao, at_n2), end = pair_columns(
         width, ff, ao_ref.shape[1]
     )

time: 126 us -> 126 us (level)
  no operation moved by 1% of the time
where the time goes in v6:
time: 126 us; the launch traced here: 125 us
  starting transfers between devices  45.3 us (36%)
  Pallas kernels  42.5 us (34%)
  waiting for transfers between devices  34.4 us (27%)
    pallas_call x4, Pallas kernels, call(): pl.pallas_call(kernel, out_shape=outs, in_specs=[hbm] * (len(fetched) + l...  31.4 us
    ppermute x16, waiting for transfers between devices, across(): return lax.ppermute(value, 'seq', [(i, i ^ bits) for i in range(XY * LINE)])  30.4 us
    ppermute x16, starting transfers between devices, across(): return lax.ppermute(value, 'seq', [(i, i ^ bits) for i in range(XY * LINE)])  27.7 us
    ppermute x5, starting transfers between devices, shifted(): return lax.ppermute(x, axis, pairs)  17 us
    pallas_call x1, Pallas kernels, fast(): pl.pallas_call(functools.partial(prepare_kernel, layout), out_shape=[shap...  5.72 us
    ppermute x5, waiting for transfers between devices, shifted(): return lax.ppermute(x, axis, pairs)  3.96 us
    pallas_call x3, Pallas kernels, join(): pl.pallas_call(functools.partial(join_kernel, len(parts), entries, int(ex...  2.9 us
  transfers between devices with their start and end apart: 24, of which 11 were waited for; matrix products, arithmetic and copies ran while one was open for 1% of the time, Pallas kernels for 13%

profile of v6, /device:TPU:0, one launch (start us, length us, event | category | flops | bytes accessed | tf_op | source)
XLA Modules:
  0.0 125.4 jit_solution(5184617035325536289)
XLA Ops:
  0.6 5.7 %shard_map.231 = (bf16[144,640]{1,0:T(8,128)(2,1)}, bf16[320,8832]{1,0:T(8,128)(2,1)}) custom-call(bf16[128,640]{1,0:T(8,128)(2,1)} %bitcast.52, s32[1,128]{1,0:T(1,128)} %refs_1_.1, bf16[320,1024]{1,0:T(8,128)(2,1)} %refs_16_.3, bf16[320,256]{1,0:T(8,128)(2,1)} %refs_17_.1, bf16[320,256]{1,0:T(8,128)(2,1)} %refs_18_.1, bf16[320,2048]{1,0:T(8,128)(2,1)} %refs_13_.1, ...), custom_call_target="tpu_custom_call" | custom-call | tf_op jit(solution)/shard_map/pallas_call | solution.py:957
  6.9 4.4 %collective-permute-start.3 = (bf16[144,640]{1,0:T(8,128)(2,1)}, bf16[144,640]{1,0:T(8,128)(2,1)S(1)}, u32[]{:S(2)}, u32[]{:S(2)}) collective-permute-start(bf16[144,640]{1,0:T(8,128)(2,1)} %get-tuple-element.56.refs_4_.refs_1_.refs_0_), channel_id=1, source_target_pairs={{0,2},{2,4},{4,6},{6,8},{8,10},{10,12},{12,14},{14,16},{16,18},{18... | collective-permute-start | bytes 552968 | tf_op jit(solution)/shard_map/ppermute | solution.py:24
  11.3 3.4 %collective-permute-start.2 = (bf16[144,640]{1,0:T(8,128)(2,1)}, bf16[144,640]{1,0:T(8,128)(2,1)S(1)}, u32[]{:S(2)}, u32[]{:S(2)}) collective-permute-start(bf16[144,640]{1,0:T(8,128)(2,1)} %get-tuple-element.56.refs_4_.refs_1_.refs_0_), channel_id=1, source_target_pairs={{0,4},{2,6},{4,8},{6,10},{8,12},{10,14},{12,16},{14,18},{16,20},{1... | collective-permute-start | bytes 552968 | tf_op jit(solution)/shard_map/ppermute | solution.py:24
  14.7 4.4 %collective-permute-start.1 = (bf16[144,640]{1,0:T(8,128)(2,1)}, bf16[144,640]{1,0:T(8,128)(2,1)S(1)}, u32[]{:S(2)}, u32[]{:S(2)}) collective-permute-start(bf16[144,640]{1,0:T(8,128)(2,1)} %get-tuple-element.56.refs_4_.refs_1_.refs_0_), channel_id=1, source_target_pairs={{0,6},{2,8},{4,10},{6,12},{8,14},{10,16},{12,18},{14,20},{16,22},{... | collective-permute-start | bytes 552968 | tf_op jit(solution)/shard_map/ppermute | solution.py:24
  19.1 3.5 %collective-permute-start = (bf16[144,640]{1,0:T(8,128)(2,1)}, bf16[144,640]{1,0:T(8,128)(2,1)S(1)}, u32[]{:S(2)}, u32[]{:S(2)}) collective-permute-start(bf16[144,640]{1,0:T(8,128)(2,1)} %get-tuple-element.56.refs_4_.refs_1_.refs_0_), channel_id=1, source_target_pairs={{0,8},{2,10},{4,12},{6,14},{8,16},{10,18},{12,20},{14,22},{16,24},... | collective-permute-start | bytes 552968 | tf_op jit(solution)/shard_map/ppermute | solution.py:24
  23.4 3.2 %collective-permute-done.refs_0_ = bf16[144,640]{1,0:T(8,128)(2,1)S(1)} collective-permute-done((bf16[144,640]{1,0:T(8,128)(2,1)}, bf16[144,640]{1,0:T(8,128)(2,1)S(1)}, u32[]{:S(2)}, u32[]{:S(2)}) %collective-permute-start) | collective-permute-done | bytes 184352 | tf_op jit(solution)/shard_map/ppermute | solution.py:24
  27.3 13.2 %shard_map.232 = (bf16[640,640]{1,0:T(8,128)(2,1)}, f32[128,1024]{1,0:T(8,128)}, bf16[128,1024]{1,0:T(8,128)(2,1)}, f32[640,256]{1,0:T(8,128)}, bf16[640,256]{1,...) custom-call(bf16[144,640]{1,0:T(8,128)(2,1)} %copy-done.12, ...), custom_call_target="tpu_custom_call" | custom-call | tf_op jit(solution)/shard_map/pallas_call | solution.py:898
  40.6 4.2 %shard_map.233 = (f32[128,1024]{1,0:T(8,128)}, f32[640,256]{1,0:T(8,128)}, f32[8,128]{1,0:T(8,128)}) custom-call(bf16[128,1024]{1,0:T(8,128)(2,1)} %get-tuple-element.68.refs_0_, bf16[640,256]{1,0:T(8,128)(2,1)} %get-tuple-element.69.refs_1_, bf16[640,256]{1,0:T(8,128)(2,1)} %get-tuple-element.70.refs_2_, ...), custom_call_target="tpu_custom_call" | custom-call | tf_op jit(solution)/shard_map/pallas_call | solution.py:898
  44.8 5.0 %shard_map.234 = (bf16[2,1280,128]{2,1,0:T(8,128)(2,1)}, bf16[2,1280,128]{2,1,0:T(8,128)(2,1)}, bf16[2,1280,128]{2,1,0:T(8,128)(2,1)}, bf16[2,1280,128]{2,1,0:T(...) custom-call(bf16[128,7296]{1,0:T(8,128)(2,1)} %get-tuple-element.73.refs_0_, ...), custom_call_target="tpu_custom_call" | custom-call | tf_op jit(solution)/shard_map/pallas_call | solution.py:898
  49.8 1.4 %collective-permute-start.10 = (bf16[2,1280,128]{2,1,0:T(8,128)(2,1)}, bf16[2,1280,128]{2,1,0:T(8,128)(2,1)S(1)}, u32[]{:S(2)}, u32[]{:S(2)}) collective-permute-start(bf16[2,1280,128]{2,1,0:T(8,128)(2,1)} %get-tuple-element.81), channel_id=1, source_target_pairs={{0,2},{2,0},{4,6},{6,4},{8,10},{10,8},{12,14},{14,12},{16,18},{18,... | collective-permute-start | bytes 1966088 | tf_op jit(solution)/shard_map/ppermute | solution.py:948
  51.2 3.1 %collective-permute-start.12 = (bf16[2,1280,128]{2,1,0:T(8,128)(2,1)}, bf16[2,1280,128]{2,1,0:T(8,128)(2,1)S(1)}, u32[]{:S(2)}, u32[]{:S(2)}) collective-permute-start(bf16[2,1280,128]{2,1,0:T(8,128)(2,1)} %get-tuple-element.83), channel_id=1, source_target_pairs={{0,4},{2,6},{4,0},{6,2},{8,12},{10,14},{12,8},{14,10},{16,20},{18,... | collective-permute-start | bytes 1966088 | tf_op jit(solution)/shard_map/ppermute | solution.py:948
  54.3 2.4 %collective-permute-start.16 = (bf16[8,480,128]{2,1,0:T(8,128)(2,1)}, bf16[8,480,128]{2,1,0:T(8,128)(2,1)S(1)}, u32[]{:S(2)}, u32[]{:S(2)}) collective-permute-start(bf16[8,480,128]{2,1,0:T(8,128)(2,1)} %get-tuple-element.88), channel_id=1, source_target_pairs={{0,8},{2,10},{4,12},{6,14},{8,0},{10,2},{12,4},{14,6},{16,24},{18,... | collective-permute-start | bytes 2949128 | tf_op jit(solution)/shard_map/ppermute | solution.py:948
  56.7 9.0 %shard_map.235 = (bf16[4,976,128]{2,1,0:T(8,128)(2,1)}, bf16[4,976,128]{2,1,0:T(8,128)(2,1)}, f32[128,640]{1,0:T(8,128)}, bf16[4,640,128]{2,1,0:T(8,128)(2,1)}) custom-call(bf16[4,144,640]{2,1,0:T(8,128)(2,1)} %get-tuple-element.61.refs_0_, bf16[144,640]{1,0:T(8,128)(2,1)} %get-tuple-element.56.refs_4_.refs_1_.refs_0_, ...), custom_call_target="tpu_custom_call" | custom-call | tf_op jit(solution)/shard_map/pallas_call | solution.py:898
  65.8 1.4 %collective-permute-done.10 = bf16[2,1280,128]{2,1,0:T(8,128)(2,1)S(1)} collective-permute-done((bf16[2,1280,128]{2,1,0:T(8,128)(2,1)}, bf16[2,1280,128]{2,1,0:T(8,128)(2,1)S(1)}, u32[]{:S(2)}, u32[]{:S(2)}) %collective-permute-start.10) | collective-permute-done | bytes 655392 | tf_op jit(solution)/shard_map/ppermute | solution.py:948
  67.4 3.9 %collective-permute-start.11 = (bf16[1,1280,128]{2,1,0:T(8,128)(2,1)S(1)}, bf16[1,1280,128]{2,1,0:T(8,128)(2,1)S(1)}, u32[]{:S(2)}, u32[]{:S(2)}) collective-permute-start(bf16[1,1280,128]{2,1,0:T(8,128)(2,1)S(1)} %get-tuple-element.110), channel_id=1, source_target_pairs={{0,4},{2,6},{4,0},{6,2},{8,12},{10,14},{12,8},{14,10},{16,20},{18,... | collective-permute-start | bytes 983048 | tf_op jit(solution)/shard_map/ppermute | solution.py:948
  72.2 6.6 %collective-permute-done.16 = bf16[8,480,128]{2,1,0:T(8,128)(2,1)S(1)} collective-permute-done((bf16[8,480,128]{2,1,0:T(8,128)(2,1)}, bf16[8,480,128]{2,1,0:T(8,128)(2,1)S(1)}, u32[]{:S(2)}, u32[]{:S(2)}) %collective-permute-start.16) | collective-permute-done | bytes 983072 | tf_op jit(solution)/shard_map/ppermute | solution.py:948
  79.3 1.2 collective-permute-done.13
  80.9 2.4 %collective-permute-start.14 = (bf16[2,640,128]{2,1,0:T(8,128)(2,1)S(1)}, bf16[2,640,128]{2,1,0:T(8,128)(2,1)S(1)}, u32[]{:S(2)}, u32[]{:S(2)}) collective-permute-start(bf16[2,640,128]{2,1,0:T(8,128)(2,1)S(1)} %get-tuple-element.85), channel_id=1, source_target_pairs={{0,8},{2,10},{4,12},{6,14},{8,0},{10,2},{12,4},{14,6},{16,24},{18,... | collective-permute-start | bytes 983048 | tf_op jit(solution)/shard_map/ppermute | solution.py:948
  84.4 0.9 collective-permute-start.8
  85.2 8.0 %collective-permute-done.17 = bf16[4,480,128]{2,1,0:T(8,128)(2,1)S(1)} collective-permute-done((bf16[4,480,128]{2,1,0:T(8,128)(2,1)S(1)}, bf16[4,480,128]{2,1,0:T(8,128)(2,1)S(1)}, u32[]{:S(2)}, u32[]{:S(2)}) %collective-permute-start.17) | collective-permute-done | bytes 491552 | tf_op jit(solution)/shard_map/ppermute | solution.py:948
  93.4 1.5 %collective-permute-start.18 = (bf16[2,480,128]{2,1,0:T(8,128)(2,1)S(1)}, bf16[2,480,128]{2,1,0:T(8,128)(2,1)S(1)}, u32[]{:S(2)}, u32[]{:S(2)}) collective-permute-start(bf16[2,480,128]{2,1,0:T(8,128)(2,1)S(1)} %get-tuple-element.113), channel_id=1, source_target_pairs={{0,2},{2,0},{4,6},{6,4},{8,10},{10,8},{12,14},{14,12},{16,18},{18,... | collective-permute-start | bytes 737288 | tf_op jit(solution)/shard_map/ppermute | solution.py:948
  95.3 2.9 %collective-permute-start.15 = (bf16[1,640,128]{2,1,0:T(8,128)(2,1)S(1)}, bf16[1,640,128]{2,1,0:T(8,128)(2,1)S(1)}, u32[]{:S(2)}, u32[]{:S(2)}) collective-permute-start(bf16[1,640,128]{2,1,0:T(8,128)(2,1)S(1)} %get-tuple-element.114), channel_id=1, source_target_pairs={{0,16},{2,18},{4,20},{6,22},{8,24},{10,26},{12,28},{14,30},{16,0},... | collective-permute-start | bytes 491528 | tf_op jit(solution)/shard_map/ppermute | solution.py:948
  98.2 4.2 %collective-permute-done.18 = bf16[2,480,128]{2,1,0:T(8,128)(2,1)S(1)} collective-permute-done((bf16[2,480,128]{2,1,0:T(8,128)(2,1)S(1)}, bf16[2,480,128]{2,1,0:T(8,128)(2,1)S(1)}, u32[]{:S(2)}, u32[]{:S(2)}) %collective-permute-start.18) | collective-permute-done | bytes 245792 | tf_op jit(solution)/shard_map/ppermute | solution.py:948
  102.4 2.8 %collective-permute-start.19 = (bf16[1,480,128]{2,1,0:T(8,128)(2,1)S(1)}, bf16[1,480,128]{2,1,0:T(8,128)(2,1)S(1)}, u32[]{:S(2)}, u32[]{:S(2)}) collective-permute-start(bf16[1,480,128]{2,1,0:T(8,128)(2,1)S(1)} %get-tuple-element.119), channel_id=1, source_target_pairs={{0,16},{2,18},{4,20},{6,22},{8,24},{10,26},{12,28},{14,30},{16,0},... | collective-permute-start | bytes 368648 | tf_op jit(solution)/shard_map/ppermute | solution.py:948
  105.9 0.9 shard_map.237
  106.7 2.8 %collective-permute-done.19 = bf16[1,480,128]{2,1,0:T(8,128)(2,1)S(1)} collective-permute-done((bf16[1,480,128]{2,1,0:T(8,128)(2,1)S(1)}, bf16[1,480,128]{2,1,0:T(8,128)(2,1)S(1)}, u32[]{:S(2)}, u32[]{:S(2)}) %collective-permute-start.19) | collective-permute-done | bytes 122912 | tf_op jit(solution)/shard_map/ppermute | solution.py:948
  111.0 1.3 %collective-permute-start.20 = (bf16[640,128]{1,0:T(8,128)(2,1)S(1)}, bf16[640,128]{1,0:T(8,128)(2,1)S(1)}, u32[]{:S(2)}, u32[]{:S(2)}) collective-permute-start(bf16[640,128]{1,0:T(8,128)(2,1)S(1)} %get-tuple-element.91.refs_4_), channel_id=1, source_target_pairs={{8,0},{10,2},{12,4},{14,6},{16,8},{18,10},{20,12},{22,14},{24,16},... | collective-permute-start | bytes 491528 | tf_op jit(solution)/shard_map/ppermute | solution.py:24
  112.5 3.7 %collective-permute-start.23 = (bf16[256,128]{1,0:T(8,128)(2,1)S(1)}, bf16[256,128]{1,0:T(8,128)(2,1)S(1)}, u32[]{:S(2)}, u32[]{:S(2)}) collective-permute-start(bf16[256,128]{1,0:T(8,128)(2,1)S(1)} %get-tuple-element.121), channel_id=1, source_target_pairs={{0,24},{2,26},{4,28},{6,30},{8,16},{10,18},{12,20},{14,22},{16,8},... | collective-permute-start | bytes 196616 | tf_op jit(solution)/shard_map/ppermute | solution.py:948
  117.0 3.7 %collective-permute-done.23.refs_3_ = bf16[256,128]{1,0:T(8,128)(2,1)S(1)} collective-permute-done((bf16[256,128]{1,0:T(8,128)(2,1)S(1)}, bf16[256,128]{1,0:T(8,128)(2,1)S(1)}, u32[]{:S(2)}, u32[]{:S(2)}) %collective-permute-start.23) | collective-permute-done | bytes 65568 | tf_op jit(solution)/shard_map/ppermute | solution.py:948
  120.7 1.8 %collective-permute-done.22.refs_2_ = bf16[256,128]{1,0:T(8,128)(2,1)S(1)} collective-permute-done((bf16[256,128]{1,0:T(8,128)(2,1)S(1)}, bf16[256,128]{1,0:T(8,128)(2,1)S(1)}, u32[]{:S(2)}, u32[]{:S(2)}) %collective-permute-start.22) | collective-permute-done | bytes 65568 | tf_op jit(solution)/shard_map/ppermute | solution.py:948
  122.5 1.3 %shard_map.242 = (f32[160,128]{1,0:T(8,128)}, f32[40,128]{1,0:T(8,128)}, f32[40,128]{1,0:T(8,128)}, f32[1,96]{1,0:T(1,128)}, f32[8,128]{1,0:T(8,128)}) custom-call(bf16[256,128]{1,0:T(8,128)(2,1)S(1)} %bitcast.50, bf16[256,128]{1,0:T(8,128)(2,1)S(1)} %collective-permute-done.21.refs_1_, bf16[256,128]{1,0:T(8,128)(2,1)S(1)} %collective-permute-done.22.refs_2_, ...), custom_call_target="tpu_custom_call" | custom-call | tf_op jit(solution)/shard_map/pallas_call | solution.py:1132
  123.9 1.3 %shard_map.240 = f32[128,640]{1,0:T(8,128)} custom-call(bf16[144,640]{1,0:T(8,128)(2,1)S(1)} %copy-done.1, f32[1,3072]{1,0:T(1,128)S(1)} %copy-done.4, f32[128,640]{1,0:T(8,128)S(1)} %copy-done.3, f32[128,640]{1,0:T(8,128)S(1)} %get-tuple-element.90.refs_3_, bf16[640,128]{1,0:T(8,128)(2,1)S(1)} %collective-permute-done.20.refs_4_), custom_call_target="tpu_custom_call" | custom-call | tf_op jit(solution)/shard_map/pallas_call | solution.py:1204
  (66 shorter events, 8.8 us)
Async XLA Ops:
  6.4 20.2 %collective-permute-start.4 = (bf16[320,8832]{1,0:T(8,128)(2,1)}, bf16[320,8832]{1,0:T(8,128)(2,1)}, u32[]{:S(2)}, u32[]{:S(2)}) collective-permute-start(bf16[320,8832]{1,0:T(8,128)(2,1)} %get-tuple-element.57), channel_id=1, source_target_pairs={{0,1},{1,0},{2,3},{3,2},{4,5},{5,4},{6,7},{7,6},{8,9},{9,8},{10,11... | collective-permute-start | bytes 16957448 | tf_op jit(solution)/shard_map/ppermute | solution.py:945
  6.9 15.7 %collective-permute-start.3 = (bf16[144,640]{1,0:T(8,128)(2,1)}, bf16[144,640]{1,0:T(8,128)(2,1)S(1)}, u32[]{:S(2)}, u32[]{:S(2)}) collective-permute-start(bf16[144,640]{1,0:T(8,128)(2,1)} %get-tuple-element.56.refs_4_.refs_1_.refs_0_), channel_id=1, source_target_pairs={{0,2},{2,4},{4,6},{6,8},{8,10},{10,12},{12,14},{14,16},{16,18},{18... | collective-permute-start | bytes 552968 | tf_op jit(solution)/shard_map/ppermute | solution.py:24
  11.3 11.3 %collective-permute-start.2 = (bf16[144,640]{1,0:T(8,128)(2,1)}, bf16[144,640]{1,0:T(8,128)(2,1)S(1)}, u32[]{:S(2)}, u32[]{:S(2)}) collective-permute-start(bf16[144,640]{1,0:T(8,128)(2,1)} %get-tuple-element.56.refs_4_.refs_1_.refs_0_), channel_id=1, source_target_pairs={{0,4},{2,6},{4,8},{6,10},{8,12},{10,14},{12,16},{14,18},{16,20},{1... | collective-permute-start | bytes 552968 | tf_op jit(solution)/shard_map/ppermute | solution.py:24
  14.7 8.6 %collective-permute-start.1 = (bf16[144,640]{1,0:T(8,128)(2,1)}, bf16[144,640]{1,0:T(8,128)(2,1)S(1)}, u32[]{:S(2)}, u32[]{:S(2)}) collective-permute-start(bf16[144,640]{1,0:T(8,128)(2,1)} %get-tuple-element.56.refs_4_.refs_1_.refs_0_), channel_id=1, source_target_pairs={{0,6},{2,8},{4,10},{6,12},{8,14},{10,16},{12,18},{14,20},{16,22},{... | collective-permute-start | bytes 552968 | tf_op jit(solution)/shard_map/ppermute | solution.py:24
  19.1 7.5 %collective-permute-start = (bf16[144,640]{1,0:T(8,128)(2,1)}, bf16[144,640]{1,0:T(8,128)(2,1)S(1)}, u32[]{:S(2)}, u32[]{:S(2)}) collective-permute-start(bf16[144,640]{1,0:T(8,128)(2,1)} %get-tuple-element.56.refs_4_.refs_1_.refs_0_), channel_id=1, source_target_pairs={{0,8},{2,10},{4,12},{6,14},{8,16},{10,18},{12,20},{14,22},{16,24},... | collective-permute-start | bytes 552968 | tf_op jit(solution)/shard_map/ppermute | solution.py:24
  40.5 4.3 %collective-permute-start.5 = (bf16[128,7296]{1,0:T(8,128)(2,1)}, bf16[128,7296]{1,0:T(8,128)(2,1)}, u32[]{:S(2)}, u32[]{:S(2)}) collective-permute-start(bf16[128,7296]{1,0:T(8,128)(2,1)} %get-tuple-element.74.refs_1_), channel_id=1, source_target_pairs={{0,1},{1,0},{2,3},{3,2},{4,5},{5,4},{6,7},{7,6},{8,9},{9,8},{10,11... | collective-permute-start | bytes 5603336 | tf_op jit(solution)/shard_map/ppermute | solution.py:945
  49.8 17.4 %collective-permute-start.10 = (bf16[2,1280,128]{2,1,0:T(8,128)(2,1)}, bf16[2,1280,128]{2,1,0:T(8,128)(2,1)S(1)}, u32[]{:S(2)}, u32[]{:S(2)}) collective-permute-start(bf16[2,1280,128]{2,1,0:T(8,128)(2,1)} %get-tuple-element.81), channel_id=1, source_target_pairs={{0,2},{2,0},{4,6},{6,4},{8,10},{10,8},{12,14},{14,12},{16,18},{18,... | collective-permute-start | bytes 1966088 | tf_op jit(solution)/shard_map/ppermute | solution.py:948
  51.2 20.1 %collective-permute-start.12 = (bf16[2,1280,128]{2,1,0:T(8,128)(2,1)}, bf16[2,1280,128]{2,1,0:T(8,128)(2,1)S(1)}, u32[]{:S(2)}, u32[]{:S(2)}) collective-permute-start(bf16[2,1280,128]{2,1,0:T(8,128)(2,1)} %get-tuple-element.83), channel_id=1, source_target_pairs={{0,4},{2,6},{4,0},{6,2},{8,12},{10,14},{12,8},{14,10},{16,20},{18,... | collective-permute-start | bytes 1966088 | tf_op jit(solution)/shard_map/ppermute | solution.py:948
  54.3 24.4 %collective-permute-start.16 = (bf16[8,480,128]{2,1,0:T(8,128)(2,1)}, bf16[8,480,128]{2,1,0:T(8,128)(2,1)S(1)}, u32[]{:S(2)}, u32[]{:S(2)}) collective-permute-start(bf16[8,480,128]{2,1,0:T(8,128)(2,1)} %get-tuple-element.88), channel_id=1, source_target_pairs={{0,8},{2,10},{4,12},{6,14},{8,0},{10,2},{12,4},{14,6},{16,24},{18,... | collective-permute-start | bytes 2949128 | tf_op jit(solution)/shard_map/ppermute | solution.py:948
  56.7 10.6 %copy-start.5 = (bf16[2,1280,128]{2,1,0:T(8,128)(2,1)S(1)}, bf16[2,1280,128]{2,1,0:T(8,128)(2,1)}, u32[]{:S(2)}) copy-start(bf16[2,1280,128]{2,1,0:T(8,128)(2,1)} %get-tuple-element.76.refs_15_) | copy-start | bytes 1966084
  65.7 5.6 %copy-start.8 = (bf16[2,1280,128]{2,1,0:T(8,128)(2,1)S(1)}, bf16[2,1280,128]{2,1,0:T(8,128)(2,1)}, u32[]{:S(2)}) copy-start(bf16[2,1280,128]{2,1,0:T(8,128)(2,1)} %get-tuple-element.82) | copy-start | bytes 1966084
  65.7 6.4 %copy-start = (bf16[4,640,128]{2,1,0:T(8,128)(2,1)S(1)}, bf16[4,640,128]{2,1,0:T(8,128)(2,1)}, u32[]{:S(2)}) copy-start(bf16[4,640,128]{2,1,0:T(8,128)(2,1)} %get-tuple-element.78.refs_1_) | copy-start | bytes 1966084
  65.7 17.6 %collective-permute-start.6 = (bf16[4,976,128]{2,1,0:T(8,128)(2,1)}, bf16[4,976,128]{2,1,0:T(8,128)(2,1)S(1)}, u32[]{:S(2)}, u32[]{:S(2)}) collective-permute-start(bf16[4,976,128]{2,1,0:T(8,128)(2,1)} %get-tuple-element.80), channel_id=1, source_target_pairs={{0,1},{1,0},{2,3},{3,2},{4,5},{5,4},{6,7},{7,6},{8,9},{9,8},{10,11... | collective-permute-start | bytes 2998280 | tf_op jit(solution)/shard_map/ppermute | solution.py:945
  67.4 11.3 %copy-start.7 = (bf16[8,480,128]{2,1,0:T(8,128)(2,1)S(1)}, bf16[8,480,128]{2,1,0:T(8,128)(2,1)}, u32[]{:S(2)}) copy-start(bf16[8,480,128]{2,1,0:T(8,128)(2,1)} %get-tuple-element.87) | copy-start | bytes 2949124
  67.4 11.9 %collective-permute-start.11 = (bf16[1,1280,128]{2,1,0:T(8,128)(2,1)S(1)}, bf16[1,1280,128]{2,1,0:T(8,128)(2,1)S(1)}, u32[]{:S(2)}, u32[]{:S(2)}) collective-permute-start(bf16[1,1280,128]{2,1,0:T(8,128)(2,1)S(1)} %get-tuple-element.110), channel_id=1, source_target_pairs={{0,4},{2,6},{4,0},{6,2},{8,12},{10,14},{12,8},{14,10},{16,20},{18,... | collective-permute-start | bytes 983048 | tf_op jit(solution)/shard_map/ppermute | solution.py:948
  71.5 9.1 %collective-permute-start.13 = (bf16[1,1280,128]{2,1,0:T(8,128)(2,1)S(1)}, bf16[1,1280,128]{2,1,0:T(8,128)(2,1)S(1)}, u32[]{:S(2)}, u32[]{:S(2)}) collective-permute-start(bf16[1,1280,128]{2,1,0:T(8,128)(2,1)S(1)} %get-tuple-element.108), channel_id=1, source_target_pairs={{0,2},{2,0},{4,6},{6,4},{8,10},{10,8},{12,14},{14,12},{16,18},{18,... | collective-permute-start | bytes 983048 | tf_op jit(solution)/shard_map/ppermute | solution.py:948
  79.0 14.2 %collective-permute-start.17 = (bf16[4,480,128]{2,1,0:T(8,128)(2,1)S(1)}, bf16[4,480,128]{2,1,0:T(8,128)(2,1)S(1)}, u32[]{:S(2)}, u32[]{:S(2)}) collective-permute-start(bf16[4,480,128]{2,1,0:T(8,128)(2,1)S(1)} %get-tuple-element.107), channel_id=1, source_target_pairs={{0,4},{2,6},{4,0},{6,2},{8,12},{10,14},{12,8},{14,10},{16,20},{18,... | collective-permute-start | bytes 1474568 | tf_op jit(solution)/shard_map/ppermute | solution.py:948
  80.9 14.3 %collective-permute-start.14 = (bf16[2,640,128]{2,1,0:T(8,128)(2,1)S(1)}, bf16[2,640,128]{2,1,0:T(8,128)(2,1)S(1)}, u32[]{:S(2)}, u32[]{:S(2)}) collective-permute-start(bf16[2,640,128]{2,1,0:T(8,128)(2,1)S(1)} %get-tuple-element.85), channel_id=1, source_target_pairs={{0,8},{2,10},{4,12},{6,14},{8,0},{10,2},{12,4},{14,6},{16,24},{18,... | collective-permute-start | bytes 983048 | tf_op jit(solution)/shard_map/ppermute | solution.py:948
  83.6 26.7 %collective-permute-start.7 = (bf16[1616,128]{1,0:T(8,128)(2,1)S(1)}, bf16[1616,128]{1,0:T(8,128)(2,1)S(1)}, u32[]{:S(2)}, u32[]{:S(2)}) collective-permute-start(bf16[1616,128]{1,0:T(8,128)(2,1)S(1)} %pad_maximum_fusion), channel_id=1, source_target_pairs={{0,2},{2,0},{4,6},{6,4},{8,10},{10,8},{12,14},{14,12},{16,18},{18,... | collective-permute-start | bytes 1241096 | tf_op jit(solution)/shard_map/ppermute | solution.py:948
  84.4 26.0 %collective-permute-start.8 = (bf16[1616,128]{1,0:T(8,128)(2,1)S(1)}, bf16[1616,128]{1,0:T(8,128)(2,1)S(1)}, u32[]{:S(2)}, u32[]{:S(2)}) collective-permute-start(bf16[1616,128]{1,0:T(8,128)(2,1)S(1)} %pad_maximum_fusion.1), channel_id=1, source_target_pairs={{0,4},{2,6},{4,0},{6,2},{8,12},{10,14},{12,8},{14,10},{16,20},{18,... | collective-permute-start | bytes 1241096 | tf_op jit(solution)/shard_map/ppermute | solution.py:948
  93.3 17.0 %copy-start.2 = (f32[128,640]{1,0:T(8,128)S(1)}, f32[128,640]{1,0:T(8,128)}, u32[]{:S(2)}) copy-start(f32[128,640]{1,0:T(8,128)} %get-tuple-element.77.refs_0_) | copy-start | bytes 983044
  93.4 9.0 %collective-permute-start.18 = (bf16[2,480,128]{2,1,0:T(8,128)(2,1)S(1)}, bf16[2,480,128]{2,1,0:T(8,128)(2,1)S(1)}, u32[]{:S(2)}, u32[]{:S(2)}) collective-permute-start(bf16[2,480,128]{2,1,0:T(8,128)(2,1)S(1)} %get-tuple-element.113), channel_id=1, source_target_pairs={{0,2},{2,0},{4,6},{6,4},{8,10},{10,8},{12,14},{14,12},{16,18},{18,... | collective-permute-start | bytes 737288 | tf_op jit(solution)/shard_map/ppermute | solution.py:948
  94.9 15.5 %collective-permute-start.9 = (bf16[1616,128]{1,0:T(8,128)(2,1)S(1)}, bf16[1616,128]{1,0:T(8,128)(2,1)S(1)}, u32[]{:S(2)}, u32[]{:S(2)}) collective-permute-start(bf16[1616,128]{1,0:T(8,128)(2,1)S(1)} %pad_maximum_fusion.2), channel_id=1, source_target_pairs={{0,6},{2,4},{4,2},{6,0},{8,14},{10,12},{12,10},{14,8},{16,22},{18,... | collective-permute-start | bytes 1241096 | tf_op jit(solution)/shard_map/ppermute | solution.py:948
  95.3 10.6 %collective-permute-start.15 = (bf16[1,640,128]{2,1,0:T(8,128)(2,1)S(1)}, bf16[1,640,128]{2,1,0:T(8,128)(2,1)S(1)}, u32[]{:S(2)}, u32[]{:S(2)}) collective-permute-start(bf16[1,640,128]{2,1,0:T(8,128)(2,1)S(1)} %get-tuple-element.114), channel_id=1, source_target_pairs={{0,16},{2,18},{4,20},{6,22},{8,24},{10,26},{12,28},{14,30},{16,0},... | collective-permute-start | bytes 491528 | tf_op jit(solution)/shard_map/ppermute | solution.py:948
  102.4 7.2 %collective-permute-start.19 = (bf16[1,480,128]{2,1,0:T(8,128)(2,1)S(1)}, bf16[1,480,128]{2,1,0:T(8,128)(2,1)S(1)}, u32[]{:S(2)}, u32[]{:S(2)}) collective-permute-start(bf16[1,480,128]{2,1,0:T(8,128)(2,1)S(1)} %get-tuple-element.119), channel_id=1, source_target_pairs={{0,16},{2,18},{4,20},{6,22},{8,24},{10,26},{12,28},{14,30},{16,0},... | collective-permute-start | bytes 368648 | tf_op jit(solution)/shard_map/ppermute | solution.py:948
  110.4 13.5 %copy-start.1 = (bf16[144,640]{1,0:T(8,128)(2,1)S(1)}, bf16[144,640]{1,0:T(8,128)(2,1)}, u32[]{:S(2)}) copy-start(bf16[144,640]{1,0:T(8,128)(2,1)} %get-tuple-element.56.refs_4_.refs_1_.refs_0_) | copy-start | bytes 552964
  110.4 13.5 %copy-start.3 = (f32[128,640]{1,0:T(8,128)S(1)}, f32[128,640]{1,0:T(8,128)}, u32[]{:S(2)}) copy-start(f32[128,640]{1,0:T(8,128)} %get-tuple-element.60.refs_2_) | copy-start | bytes 983044
  110.4 13.5 %copy-start.4 = (f32[1,3072]{1,0:T(1,128)S(1)}, f32[1,3072]{1,0:T(1,128)}, u32[]{:S(2)}) copy-start(f32[1,3072]{1,0:T(1,128)} %get-tuple-element.59.refs_2_.refs_1_) | copy-start | bytes 36868
  111.0 12.9 %collective-permute-start.20 = (bf16[640,128]{1,0:T(8,128)(2,1)S(1)}, bf16[640,128]{1,0:T(8,128)(2,1)S(1)}, u32[]{:S(2)}, u32[]{:S(2)}) collective-permute-start(bf16[640,128]{1,0:T(8,128)(2,1)S(1)} %get-tuple-element.91.refs_4_), channel_id=1, source_target_pairs={{8,0},{10,2},{12,4},{14,6},{16,8},{18,10},{20,12},{22,14},{24,16},... | collective-permute-start | bytes 491528 | tf_op jit(solution)/shard_map/ppermute | solution.py:24
  112.5 8.1 %collective-permute-start.23 = (bf16[256,128]{1,0:T(8,128)(2,1)S(1)}, bf16[256,128]{1,0:T(8,128)(2,1)S(1)}, u32[]{:S(2)}, u32[]{:S(2)}) collective-permute-start(bf16[256,128]{1,0:T(8,128)(2,1)S(1)} %get-tuple-element.121), channel_id=1, source_target_pairs={{0,24},{2,26},{4,28},{6,30},{8,16},{10,18},{12,20},{14,22},{16,8},... | collective-permute-start | bytes 196616 | tf_op jit(solution)/shard_map/ppermute | solution.py:948
  116.2 6.3 %collective-permute-start.22 = (bf16[256,128]{1,0:T(8,128)(2,1)S(1)}, bf16[256,128]{1,0:T(8,128)(2,1)S(1)}, u32[]{:S(2)}, u32[]{:S(2)}) collective-permute-start(bf16[256,128]{1,0:T(8,128)(2,1)S(1)} %get-tuple-element.122), channel_id=1, source_target_pairs={{0,16},{2,18},{4,20},{6,22},{8,24},{10,26},{12,28},{14,30},{16,0},... | collective-permute-start | bytes 196616 | tf_op jit(solution)/shard_map/ppermute | solution.py:948
  116.7 5.8 %collective-permute-start.21 = (bf16[256,128]{1,0:T(8,128)(2,1)S(1)}, bf16[256,128]{1,0:T(8,128)(2,1)S(1)}, u32[]{:S(2)}, u32[]{:S(2)}) collective-permute-start(bf16[256,128]{1,0:T(8,128)(2,1)S(1)} %get-tuple-element.123), channel_id=1, source_target_pairs={{0,8},{2,10},{4,12},{6,14},{8,0},{10,2},{12,4},{14,6},{16,24},{18,... | collective-permute-start | bytes 196616 | tf_op jit(solution)/shard_map/ppermute | solution.py:948
  (5 other events, 16.5 us)
